TPU v7x, 32 devices: a whole 2x2x4 slice. The times are simulated.
32 devices in a mesh: dp: 4 (over x, core), ctx: 2 (over y), fsdp: 4 (over z).
Axes of the slice: x: 2, y: 2, z: 4, core: 2. Of those that a mesh axis runs over, the one named last changes fastest.
Arguments:
- tokens: float32 [4, 1024, 768], P('dp', ('ctx', 'fsdp')), may hold values from -6 to 6
- cotangent: float32 [4, 1024, 768], P('dp', ('ctx', 'fsdp')), may hold values from -6 to 6
- ln1_gain: float32 [768], P(('dp', 'fsdp')), may hold values from 0.5 to 1.5
- ln1_bias: float32 [768], P(('dp', 'fsdp')), may hold values from -3 to 3
- qkv_weight: float32 [768, 2304], P(('dp', 'fsdp')), may hold values from -0.3125 to 0.3125
- q_bias: float32 [768], P(('dp', 'fsdp')), may hold values from -4 to 4
- v_bias: float32 [768], P(('dp', 'fsdp')), may hold values from -4 to 4
- out_weight: float32 [768, 768], P(('dp', 'fsdp')), may hold values from -1.75 to 1.75
- out_bias: float32 [768], P(('dp', 'fsdp')), may hold values from -4 to 4
- ln2_gain: float32 [768], P(('dp', 'fsdp')), may hold values from 0.5 to 1.5
- ln2_bias: float32 [768], P(('dp', 'fsdp')), may hold values from -3 to 3
- fc1_weight: float32 [768, 3072], P(('dp', 'fsdp')), may hold values from -0.21875 to 0.21875
- fc1_bias: float32 [3072], P(('dp', 'fsdp')), may hold values from -4 to 4
- fc2_weight: float32 [3072, 768], P(('dp', 'fsdp')), may hold values from -0.109375 to 0.109375
- fc2_bias: float32 [768], P(('dp', 'fsdp')), may hold values from -4 to 4
Outputs:
- output: float32 [4, 1024, 768], P('dp', ('ctx', 'fsdp'))
- input_grad: float32 [4, 1024, 768], P('dp', ('ctx', 'fsdp'))
- ln1_gain_grad: float32 [768], P(('dp', 'fsdp'))
- ln1_bias_grad: float32 [768], P(('dp', 'fsdp'))
- qkv_weight_grad: float32 [768, 2304], P(('dp', 'fsdp'))
- q_bias_grad: float32 [768], P(('dp', 'fsdp'))
- v_bias_grad: float32 [768], P(('dp', 'fsdp'))
- out_weight_grad: float32 [768, 768], P(('dp', 'fsdp'))
- out_bias_grad: float32 [768], P(('dp', 'fsdp'))
- ln2_gain_grad: float32 [768], P(('dp', 'fsdp'))
- ln2_bias_grad: float32 [768], P(('dp', 'fsdp'))
- fc1_weight_grad: float32 [768, 3072], P(('dp', 'fsdp'))
- fc1_bias_grad: float32 [3072], P(('dp', 'fsdp'))
- fc2_weight_grad: float32 [3072, 768], P(('dp', 'fsdp'))
- fc2_bias_grad: float32 [768], P(('dp', 'fsdp'))
All inputs are finite; a program needn't handle non-finite values.
Results may differ from a plain program's by a relative error of at most 0.02.
Values may be sent and summed in bfloat16 or wider, within the bound.
No kernel may reach another device: no remote copies, remote signals or barrier semaphores. Data moves between devices by JAX's collectives and lax.ppermute only.
A program may use at most 256 MiB of HBM per device.

v0:
```python
import math

import jax
import jax.numpy as jnp
from jax import lax
from jax.sharding import PartitionSpec as P

HEAD_DIM = 64


EPSILON = 1e-05
start_floor = -1e30


def layer_norm(values, norm_gain, norm_shift):
    centered = values - jnp.mean(values, axis=-1, keepdims=True)
    spread = jnp.mean(centered * centered, axis=-1, keepdims=True)
    return centered * lax.rsqrt(spread + EPSILON) * norm_gain + norm_shift


def split_heads(values):
    return values.reshape(values.shape[0], values.shape[1] // HEAD_DIM, HEAD_DIM)


def to_rows(values):
    return jnp.transpose(values, (1, 0, 2)).reshape(
        values.shape[1], values.shape[0] * values.shape[2]
    )


def head_slices(head_count):
    head_group = math.gcd(head_count, 4)
    return [
        (head_first, head_first + head_group) for head_first in range(0, head_count, head_group)
    ]


def keep_state(carried):
    return carried


def forward_fold(query_heads, query_pos, score_scale):
    head_count = query_heads.shape[1]

    def forward_fold_step(carried, arriving, first_index):
        key_rows, value_rows = arriving
        arrived_rows = key_rows.shape[0]
        key_pos = jnp.arange(arrived_rows, dtype=jnp.int32)
        visible = key_pos[None, :] <= query_pos[:, None]
        key_heads = split_heads(key_rows)
        value_heads = split_heads(value_rows)

        def forward_visit_piece(current):
            running_max, running_sum, weighted = current
            new_maxima, new_sums, new_weighted = ([], [], [])
            for head_first, head_end in head_slices(head_count):
                raw_scores = jnp.einsum(
                    "qhd,khd->hqk",
                    query_heads[:, head_first:head_end],
                    key_heads[:, head_first:head_end],
                    preferred_element_type=jnp.float32,
                )
                scores = jnp.where(visible[None], raw_scores * score_scale, -jnp.inf)
                old_max = running_max[head_first:head_end]
                new_max = jnp.maximum(old_max, jnp.max(scores, axis=-1))
                fading = jnp.exp(old_max - new_max)
                exponent = jnp.exp(scores - new_max[..., None])
                added = jnp.einsum(
                    "hqk,khd->hqd",
                    exponent.astype(jnp.bfloat16),
                    value_heads[:, head_first:head_end],
                    preferred_element_type=jnp.float32,
                )
                new_maxima.append(new_max)
                new_sums.append(jnp.sum(exponent, axis=-1))
                new_weighted.append(added)
            return (
                jnp.concatenate(new_maxima, 0),
                jnp.concatenate(new_sums, 0),
                jnp.concatenate(new_weighted, 0),
            )

        return lax.cond(key_pos[0] <= query_pos[-1], forward_visit_piece, keep_state, carried)

    return forward_fold_step


def query_grad_fold(query_heads, query_pos, grad_heads, log_total, grad_delta, score_scale):
    head_count = query_heads.shape[1]

    def query_fold_step(carried, arriving, first_index):
        key_rows, value_rows = arriving
        arrived_rows = key_rows.shape[0]
        key_pos = jnp.arange(arrived_rows, dtype=jnp.int32)
        visible = key_pos[None, :] <= query_pos[:, None]
        key_heads = split_heads(key_rows)
        value_heads = split_heads(value_rows)

        def query_visit_piece(current):
            collected = []
            for head_first, head_end in head_slices(head_count):
                raw_scores = jnp.einsum(
                    "qhd,khd->hqk",
                    query_heads[:, head_first:head_end],
                    key_heads[:, head_first:head_end],
                    preferred_element_type=jnp.float32,
                )
                scores = jnp.where(visible[None], raw_scores * score_scale, -jnp.inf)
                normalized = jnp.exp(scores - log_total[head_first:head_end][..., None])
                grad_dots = jnp.einsum(
                    "qhd,khd->hqk",
                    grad_heads[:, head_first:head_end],
                    value_heads[:, head_first:head_end],
                    preferred_element_type=jnp.float32,
                )
                score_grad = (
                    normalized
                    * (grad_dots - grad_delta[head_first:head_end][..., None])
                    * score_scale
                ).astype(jnp.bfloat16)
                collected.append(
                    current[head_first:head_end]
                    + jnp.einsum(
                        "hqk,khd->hqd",
                        score_grad,
                        key_heads[:, head_first:head_end],
                        preferred_element_type=jnp.float32,
                    )
                )
            return jnp.concatenate(collected, 0)

        return lax.cond(key_pos[0] <= query_pos[-1], query_visit_piece, keep_state, carried)

    return query_fold_step


def key_grad_fold(key_heads, value_heads, key_pos, row_count, stride, offset, score_scale):
    head_count = key_heads.shape[1]

    def key_fold_step(carried, arriving, first_index):
        query_piece, grad_piece, total_piece, delta_piece = arriving
        arrived_rows = query_piece.shape[0]
        gathered_index = jnp.arange(arrived_rows, dtype=jnp.int32)
        query_pos = gathered_index // row_count * stride + offset + gathered_index % row_count
        visible = key_pos[None, :] <= query_pos[:, None]
        query_heads = split_heads(query_piece)
        grad_heads = split_heads(grad_piece)

        def key_visit_piece(current):
            key_acc, value_acc = current
            key_parts, value_parts = ([], [])
            for head_first, head_end in head_slices(head_count):
                raw_scores = jnp.einsum(
                    "qhd,khd->hqk",
                    query_heads[:, head_first:head_end],
                    key_heads[:, head_first:head_end],
                    preferred_element_type=jnp.float32,
                )
                scores = jnp.where(visible[None], raw_scores * score_scale, -jnp.inf)
                normalized = jnp.exp(
                    scores - jnp.transpose(total_piece[:, head_first:head_end])[..., None]
                )
                grad_dots = jnp.einsum(
                    "qhd,khd->hqk",
                    grad_heads[:, head_first:head_end],
                    value_heads[:, head_first:head_end],
                    preferred_element_type=jnp.float32,
                )
                score_grad = (
                    normalized
                    * (grad_dots - jnp.transpose(delta_piece[:, head_first:head_end])[..., None])
                    * score_scale
                ).astype(jnp.bfloat16)
                key_parts.append(
                    key_acc[head_first:head_end]
                    + jnp.einsum(
                        "hqk,qhd->hkd",
                        score_grad,
                        query_heads[:, head_first:head_end],
                        preferred_element_type=jnp.float32,
                    )
                )
                value_parts.append(
                    value_acc[head_first:head_end]
                    + jnp.einsum(
                        "hqk,qhd->hkd",
                        normalized.astype(jnp.bfloat16),
                        grad_heads[:, head_first:head_end],
                        preferred_element_type=jnp.float32,
                    )
                )
            return (jnp.concatenate(key_parts, 0), jnp.concatenate(value_parts, 0))

        return lax.cond(jnp.max(query_pos) >= key_pos[0], key_visit_piece, keep_state, carried)

    return key_fold_step


def local(
    tokens,
    cotangent,
    ln1_gain,
    ln1_bias,
    qkv_weight,
    q_bias,
    v_bias,
    out_weight,
    out_bias,
    ln2_gain,
    ln2_bias,
    fc1_weight,
    fc1_bias,
    fc2_weight,
    fc2_bias,
):
    gathered = (
        lax.all_gather(ln1_gain.astype(jnp.bfloat16), ("dp", "fsdp"), axis=0, tiled=True),
        lax.all_gather(ln1_bias.astype(jnp.bfloat16), ("dp", "fsdp"), axis=0, tiled=True),
        lax.all_gather(qkv_weight.astype(jnp.bfloat16), ("dp", "fsdp"), axis=0, tiled=True),
        lax.all_gather(q_bias.astype(jnp.bfloat16), ("dp", "fsdp"), axis=0, tiled=True),
        lax.all_gather(v_bias.astype(jnp.bfloat16), ("dp", "fsdp"), axis=0, tiled=True),
        lax.all_gather(out_weight.astype(jnp.bfloat16), ("dp", "fsdp"), axis=0, tiled=True),
        lax.all_gather(out_bias.astype(jnp.bfloat16), ("dp", "fsdp"), axis=0, tiled=True),
        lax.all_gather(ln2_gain.astype(jnp.bfloat16), ("dp", "fsdp"), axis=0, tiled=True),
        lax.all_gather(ln2_bias.astype(jnp.bfloat16), ("dp", "fsdp"), axis=0, tiled=True),
        lax.all_gather(fc1_weight.astype(jnp.bfloat16), ("dp", "fsdp"), axis=0, tiled=True),
        lax.all_gather(fc1_bias.astype(jnp.bfloat16), ("dp", "fsdp"), axis=0, tiled=True),
        lax.all_gather(fc2_weight.astype(jnp.bfloat16), ("dp", "fsdp"), axis=0, tiled=True),
        lax.all_gather(fc2_bias.astype(jnp.bfloat16), ("dp", "fsdp"), axis=0, tiled=True),
    )
    first_gain = gathered[0].astype(jnp.float32)
    first_shift = gathered[1].astype(jnp.float32)
    qkv_matrix = gathered[2]
    query_shift = gathered[3].astype(jnp.float32)
    value_shift = gathered[4].astype(jnp.float32)
    out_matrix = gathered[5]
    out_shift = gathered[6].astype(jnp.float32)
    second_gain = gathered[7].astype(jnp.float32)
    second_shift = gathered[8].astype(jnp.float32)
    up_matrix = gathered[9]
    up_shift = gathered[10].astype(jnp.float32)
    down_matrix = gathered[11]
    down_shift = gathered[12].astype(jnp.float32)
    token_rows = tokens[0]
    row_count = token_rows.shape[0]
    model_width = token_rows.shape[1]
    head_count = model_width // HEAD_DIM
    score_scale = HEAD_DIM ** (-0.5)
    fsdp_count = lax.axis_size("fsdp")
    my_first = (lax.axis_index("ctx") * fsdp_count + lax.axis_index("fsdp")) * row_count
    query_pos = my_first + jnp.arange(row_count, dtype=jnp.int32)
    norm1, norm1_back = jax.vjp(layer_norm, token_rows, first_gain, first_shift)
    norm1_low = norm1.astype(jnp.bfloat16)
    projected = jnp.dot(norm1_low, qkv_matrix, preferred_element_type=jnp.float32)
    queries = (projected[:, :model_width] + query_shift).astype(jnp.bfloat16)
    key_rows = projected[:, model_width : 2 * model_width].astype(jnp.bfloat16)
    value_rows = (projected[:, 2 * model_width :] + value_shift).astype(jnp.bfloat16)
    query_heads = split_heads(queries)
    state_init = (
        jnp.full((head_count, row_count), start_floor, jnp.float32),
        jnp.zeros((head_count, row_count), jnp.float32),
        jnp.zeros((head_count, row_count, HEAD_DIM), jnp.float32),
    )
    forward_step = forward_fold(query_heads, query_pos, score_scale)
    block_keys, block_values = (
        lax.all_gather(key_rows, "fsdp", axis=0, tiled=True),
        lax.all_gather(value_rows, "fsdp", axis=0, tiled=True),
    )
    running_max, running_sum, weighted = forward_step(
        state_init,
        (
            lax.all_gather(block_keys, "ctx", axis=0, tiled=True),
            lax.all_gather(block_values, "ctx", axis=0, tiled=True),
        ),
        jnp.int32(0),
    )
    log_total = running_max + jnp.log(running_sum)
    context = to_rows(weighted / running_sum[..., None])
    context_low = context.astype(jnp.bfloat16)
    mixed = (
        token_rows
        + jnp.dot(context_low, out_matrix, preferred_element_type=jnp.float32)
        + out_shift
    )
    norm2, norm2_back = jax.vjp(layer_norm, mixed, second_gain, second_shift)
    norm2_low = norm2.astype(jnp.bfloat16)
    inner = jnp.dot(norm2_low, up_matrix, preferred_element_type=jnp.float32) + up_shift
    activated, gelu_back = jax.vjp(jax.nn.gelu, inner)
    hidden = activated.astype(jnp.bfloat16)
    output = mixed + jnp.dot(hidden, down_matrix, preferred_element_type=jnp.float32) + down_shift
    back_qkv, back_out, back_up, back_down = (qkv_matrix, out_matrix, up_matrix, down_matrix)
    grad_rows = cotangent[0]
    branch_grad = grad_rows.astype(jnp.bfloat16)
    fc2_bias_grad = jnp.sum(branch_grad.astype(jnp.float32), axis=0)
    fc2_weight_grad = jnp.einsum(
        "tf,td->fd", hidden, branch_grad, preferred_element_type=jnp.float32
    )
    hidden_grad = jnp.einsum(
        "td,fd->tf", branch_grad, back_down, preferred_element_type=jnp.float32
    )
    inner_grad = gelu_back(hidden_grad)[0].astype(jnp.bfloat16)
    fc1_bias_grad = jnp.sum(inner_grad.astype(jnp.float32), axis=0)
    fc1_weight_grad = jnp.einsum(
        "td,tf->df", norm2_low, inner_grad, preferred_element_type=jnp.float32
    )
    norm2_grad = jnp.einsum("tf,df->td", inner_grad, back_up, preferred_element_type=jnp.float32)
    mixed_part, ln2_gain_grad, ln2_bias_grad = norm2_back(norm2_grad)
    mixed_grad = grad_rows + mixed_part
    attn_grad = mixed_grad.astype(jnp.bfloat16)
    out_bias_grad = jnp.sum(attn_grad.astype(jnp.float32), axis=0)
    out_weight_grad = jnp.einsum(
        "td,te->de", context_low, attn_grad, preferred_element_type=jnp.float32
    )
    context_grad = jnp.einsum(
        "te,de->td", attn_grad, back_out, preferred_element_type=jnp.float32
    ).astype(jnp.bfloat16)
    grad_delta = jnp.sum(
        (context_grad.astype(jnp.float32) * context).reshape(row_count, head_count, HEAD_DIM),
        axis=-1,
    )
    total_rows = jnp.transpose(log_total)
    grad_heads = split_heads(context_grad)
    query_step = query_grad_fold(
        query_heads, query_pos, grad_heads, log_total, jnp.transpose(grad_delta), score_scale
    )
    query_init = jnp.zeros((head_count, row_count, HEAD_DIM), jnp.float32)
    block_rows = block_keys.shape[0]
    block_pos = lax.axis_index("ctx") * block_rows + jnp.arange(block_rows, dtype=jnp.int32)
    query_acc = query_step(
        query_init,
        (
            lax.all_gather(block_keys, "ctx", axis=0, tiled=True),
            lax.all_gather(block_values, "ctx", axis=0, tiled=True),
        ),
        jnp.int32(0),
    )
    key_step = key_grad_fold(
        split_heads(block_keys),
        split_heads(block_values),
        block_pos,
        row_count,
        block_rows,
        lax.axis_index("fsdp") * row_count,
        score_scale,
    )
    key_init = (
        jnp.zeros((head_count, block_rows, HEAD_DIM), jnp.float32),
        jnp.zeros((head_count, block_rows, HEAD_DIM), jnp.float32),
    )
    key_acc, value_acc = key_step(
        key_init,
        (
            lax.all_gather(queries.astype(jnp.float32), "ctx", axis=0, tiled=True).astype(
                jnp.bfloat16
            ),
            lax.all_gather(context_grad.astype(jnp.float32), "ctx", axis=0, tiled=True).astype(
                jnp.bfloat16
            ),
            lax.all_gather(total_rows, "ctx", axis=0, tiled=True),
            lax.all_gather(grad_delta, "ctx", axis=0, tiled=True),
        ),
        jnp.int32(0),
    )
    key_sum, value_sum = (
        lax.psum_scatter(to_rows(key_acc), "fsdp", scatter_dimension=0, tiled=True),
        lax.psum_scatter(to_rows(value_acc), "fsdp", scatter_dimension=0, tiled=True),
    )
    query_grad = to_rows(query_acc).astype(jnp.bfloat16)
    key_grad = key_sum.astype(jnp.bfloat16)
    value_grad = value_sum.astype(jnp.bfloat16)
    stacked_grad = jnp.concatenate([query_grad, key_grad, value_grad], axis=1)
    q_bias_grad = jnp.sum(query_grad.astype(jnp.float32), axis=0)
    v_bias_grad = jnp.sum(value_grad.astype(jnp.float32), axis=0)
    qkv_weight_grad = jnp.einsum(
        "td,te->de", norm1_low, stacked_grad, preferred_element_type=jnp.float32
    )
    norm1_grad = jnp.einsum("te,de->td", stacked_grad, back_qkv, preferred_element_type=jnp.float32)
    rows_part, ln1_gain_grad, ln1_bias_grad = norm1_back(norm1_grad)
    input_grad = mixed_grad + rows_part
    shares = (
        lax.psum_scatter(ln1_gain_grad, ("dp", "fsdp"), scatter_dimension=0, tiled=True),
        lax.psum_scatter(ln1_bias_grad, ("dp", "fsdp"), scatter_dimension=0, tiled=True),
        lax.psum_scatter(qkv_weight_grad, ("dp", "fsdp"), scatter_dimension=0, tiled=True),
        lax.psum_scatter(q_bias_grad, ("dp", "fsdp"), scatter_dimension=0, tiled=True),
        lax.psum_scatter(v_bias_grad, ("dp", "fsdp"), scatter_dimension=0, tiled=True),
        lax.psum_scatter(out_weight_grad, ("dp", "fsdp"), scatter_dimension=0, tiled=True),
        lax.psum_scatter(out_bias_grad, ("dp", "fsdp"), scatter_dimension=0, tiled=True),
        lax.psum_scatter(ln2_gain_grad, ("dp", "fsdp"), scatter_dimension=0, tiled=True),
        lax.psum_scatter(ln2_bias_grad, ("dp", "fsdp"), scatter_dimension=0, tiled=True),
        lax.psum_scatter(fc1_weight_grad, ("dp", "fsdp"), scatter_dimension=0, tiled=True),
        lax.psum_scatter(fc1_bias_grad, ("dp", "fsdp"), scatter_dimension=0, tiled=True),
        lax.psum_scatter(fc2_weight_grad, ("dp", "fsdp"), scatter_dimension=0, tiled=True),
        lax.psum_scatter(fc2_bias_grad, ("dp", "fsdp"), scatter_dimension=0, tiled=True),
    )
    totals = lax.psum(
        (
            shares[0],
            shares[1],
            shares[2],
            shares[3],
            shares[4],
            shares[5],
            shares[6],
            shares[7],
            shares[8],
            shares[9],
            shares[10],
            shares[11],
            shares[12],
        ),
        "ctx",
    )
    return (output[None], input_grad[None]) + tuple(totals)


def solution(mesh):
    placed = (
        P("dp", ("ctx", "fsdp"), None),
        P("dp", ("ctx", "fsdp"), None),
        P(("dp", "fsdp")),
        P(("dp", "fsdp")),
        P(("dp", "fsdp"), None),
        P(("dp", "fsdp")),
        P(("dp", "fsdp")),
        P(("dp", "fsdp"), None),
        P(("dp", "fsdp")),
        P(("dp", "fsdp")),
        P(("dp", "fsdp")),
        P(("dp", "fsdp"), None),
        P(("dp", "fsdp")),
        P(("dp", "fsdp"), None),
        P(("dp", "fsdp")),
    )
    return jax.shard_map(
        local,
        mesh=mesh,
        in_specs=placed,
        out_specs=(
            P("dp", ("ctx", "fsdp"), None),
            P("dp", ("ctx", "fsdp"), None),
            P(("dp", "fsdp")),
            P(("dp", "fsdp")),
            P(("dp", "fsdp"), None),
            P(("dp", "fsdp")),
            P(("dp", "fsdp")),
            P(("dp", "fsdp"), None),
            P(("dp", "fsdp")),
            P(("dp", "fsdp")),
            P(("dp", "fsdp")),
            P(("dp", "fsdp"), None),
            P(("dp", "fsdp")),
            P(("dp", "fsdp"), None),
            P(("dp", "fsdp")),
        ),
        check_vma=False,
    )
```

profile of v0, /device:TPU:0, one launch (start us, length us, event | category | flops | bytes accessed | tf_op | source)
XLA Modules:
  0.0 915.1 jit_solution(6084197832530870177)
XLA Ops:
  19.4 63.9 %all-reduce.21 = (bf16[768]{0:T(1024)(128)(2,1)S(1)}, bf16[768]{0:T(1024)(128)(2,1)S(1)}, bf16[768]{0:T(1024)(128)(2,1)S(1)}, bf16[768]{0:T(1024)(128)(2,1)S(1)}...) all-reduce(bf16[768]{0:T(1024)(128)(2,1)S(1)} %dynamic-update-slice, ...), channel_id=1, replica_groups=mesh['dp'=4,'ctx'=2,'fsdp'=4] {'dp','fsdp'}, use_global_device_ids=true, to_apply=%add.4 | all-reduce | flops 9216 | bytes 36864
  86.1 2.8 fusion.100
  89.0 18.2 %all_gather.69 = bf16[512,768]{1,0:T(8,128)(2,1)} all-gather(bf16[128,768]{1,0:T(8,128)(2,1)S(1)} %slice.313), channel_id=1, replica_groups=mesh['dp'=4,'ctx'=2,'fsdp'=4] {'fsdp'}, dimensions={0}, use_global_device_ids=true | all-gather | bytes 983040 | tf_op jit(solution)/shard_map/all_gather | solution.py:266
  107.4 18.0 %all_gather.72 = bf16[512,768]{1,0:T(8,128)(2,1)} all-gather(bf16[128,768]{1,0:T(8,128)(2,1)S(1)} %get-tuple-element.374), channel_id=1, replica_groups=mesh['dp'=4,'ctx'=2,'fsdp'=4] {'fsdp'}, dimensions={0}, use_global_device_ids=true | all-gather | bytes 983040 | tf_op jit(solution)/shard_map/all_gather | solution.py:267
  133.2 6.5 all_gather.82
  142.2 22.9 %all-gather.11.cloned.1.call-done = bf16[1024,768]{1,0:T(8,128)(2,1)} async-done(((bf16[512,768]{1,0:T(8,128)(2,1)}), bf16[1024,768]{1,0:T(8,128)(2,1)}) %all-gather.11.cloned.1.call-update) | async-done | bytes 1572880 | tf_op jit(solution)/shard_map/all_gather | solution.py:273
  167.7 12.1 %conditional.3 = (f32[12,128]{1,0:T(8,128)S(1)}, f32[12,128]{1,0:T(8,128)S(1)}, f32[12,128,64]{1,2,0:T(8,128)S(1)}, f32[12,128]{1,0:T(8,128)S(1)}) conditional(s32[]{:T(128)} %bitcast.14, () %tuple.38, (pred[128,1024]{1,0:T(8,128)(4,1)S(1)}, bf16[128,12,64]{0,2,1:T(8,128)(2,1)S(1)}, bf16[1024,12,64]{0,2,1:T(8,128)(2,1)}, ...), branch_computations={%region_2.0_spmd, %region_3.10_spmd} | conditional | flops 420155904 | bytes 26740768 | solution.py:83
  180.8 4.6 all_gather.83
  185.4 20.8 %all-gather.13.cloned.1.call-done = bf16[768,768]{1,0:T(8,128)(2,1)} async-done(((bf16[48,768]{1,0:T(8,128)(2,1)}), bf16[768,768]{1,0:T(8,128)(2,1)}) %all-gather.13.cloned.1.call-update) | async-done | bytes 1179664 | tf_op jit(solution)/shard_map/all_gather | solution.py:222
  208.2 53.2 %all-gather.15.cloned.1.call-done = bf16[768,3072]{1,0:T(8,128)(2,1)} async-done(((bf16[48,3072]{1,0:T(8,128)(2,1)}), bf16[768,3072]{1,0:T(8,128)(2,1)}) %all-gather.15.cloned.1.call-update) | async-done | bytes 4718608 | tf_op jit(solution)/shard_map/all_gather | solution.py:226
  261.4 3.2 convolution_add_fusion
  264.6 51.5 %all-gather.17.cloned.1.call-done = bf16[3072,768]{1,0:T(8,128)(2,1)} async-done(((bf16[192,768]{1,0:T(8,128)(2,1)}), bf16[3072,768]{1,0:T(8,128)(2,1)}) %all-gather.17.cloned.1.call-update) | async-done | bytes 4718608 | tf_op jit(solution)/shard_map/all_gather | solution.py:228
  316.1 5.0 convert_reduce_fusion
  327.2 7.8 all_gather.84
  338.6 5.4 all_gather.85
  345.1 23.3 %conditional.5 = (f32[12,512,64]{1,2,0:T(8,128)}, f32[12,512,64]{1,2,0:T(8,128)}) conditional(s32[]{:T(128)} %convert_element_type.240, () %tuple.42, (s32[]{:T(128)}, s32[1,512]{1,0:T(1,128)}, s32[256,1]{0,1:T(1,128)}, s32[]{:T(128)}, s32[256,1]{0,1:T(1,128)}, /*index=5*/bf16[256,768]{1,0:T(8,128)(2,1)}, bf16[512,768]{1,0:T(8,128)(2,1)S(1)}, ...), branch_computations={%region_18.19_spmd, %region_19.20_spmd} | conditional | flops 819598080 | bytes 66210124 | solution.py:194
  351.8 3.1 subtract_exponential_fusion.3
  371.3 18.0 %conditional.4 = (bf16[12,128,64]{1,2,0:T(8,128)(2,1)S(1)}) conditional(s32[]{:T(128)} %bitcast.14, () %tuple.40, (pred[128,1024]{1,0:T(8,128)(4,1)}, bf16[128,12,64]{0,2,1:T(8,128)(2,1)S(1)}, bf16[1024,12,64]{0,2,1:T(8,128)(2,1)}, f32[12,128]{1,0:T(8,128)}, bf16[128,768]{1,0:T(8,128)(2,1)S(1)}, /*index=5*/bf16[1024,12,64]{0,2,1:T(8,128)(2,1)}, ...), branch_computations={%region_15.16_spmd, %region_16.17_spmd} | conditional | flops 615186432 | bytes 26759260 | solution.py:132
  371.6 3.0 fusion.38
  374.8 2.7 multiply_convert_fusion
  389.3 12.4 %reduce-scatter.7.cloned.1.call-done = f32[128,768]{0,1:T(8,128)} async-done(((f32[512,768]{0,1:T(8,128)}), f32[128,768]{0,1:T(8,128)}) %reduce-scatter.7.cloned.1.call-update) | async-done | bytes 393232 | tf_op jit(solution)/shard_map/reduce_scatter | solution.py:365
  402.7 35.6 %reduce-scatter.9.cloned.1.call-done = f32[128,768]{0,1:T(8,128)} async-done(((f32[512,768]{0,1:T(8,128)}), f32[128,768]{0,1:T(8,128)}) %reduce-scatter.9.cloned.1.call-update) | async-done | bytes 393232 | tf_op jit(solution)/shard_map/reduce_scatter | solution.py:366
  440.1 4.1 fusion.82
  445.4 5.8 fusion.101
  452.2 5.2 fusion.96
  459.4 44.7 %reduce-scatter.13.cloned.1.call-done = f32[48,768]{1,0:T(8,128)} async-done(((f32[768,768]{1,0:T(8,128)}), f32[48,768]{1,0:T(8,128)}) %reduce-scatter.13.cloned.1.call-update) | async-done | bytes 147472 | tf_op jit(solution)/shard_map/reduce_scatter | solution.py:386
  504.1 93.4 %reduce-scatter.11.cloned.1.call-done = f32[48,2304]{1,0:T(8,128)} async-done(((f32[768,2304]{1,0:T(8,128)}), f32[48,2304]{1,0:T(8,128)}) %reduce-scatter.11.cloned.1.call-update) | async-done | bytes 442384 | tf_op jit(solution)/shard_map/reduce_scatter | solution.py:383
  597.5 115.0 %reduce-scatter.15.cloned.1.call-done = f32[48,3072]{1,0:T(8,128)} async-done(((f32[768,3072]{1,0:T(8,128)}), f32[48,3072]{1,0:T(8,128)}) %reduce-scatter.15.cloned.1.call-update) | async-done | bytes 589840 | tf_op jit(solution)/shard_map/reduce_scatter | solution.py:390
  712.5 115.7 %reduce-scatter.17.cloned.1.call-done = f32[192,768]{1,0:T(8,128)} async-done(((f32[3072,768]{1,0:T(8,128)}), f32[192,768]{1,0:T(8,128)}) %reduce-scatter.17.cloned.1.call-update) | async-done | bytes 589840 | tf_op jit(solution)/shard_map/reduce_scatter | solution.py:392
  828.5 4.3 fusion.79
  835.5 60.7 %all-reduce.18 = (f32[768]{0:T(1024)S(1)}, f32[768]{0:T(1024)S(1)}, f32[768]{0:T(1024)S(1)}, f32[768]{0:T(1024)S(1)}, f32[768]{0:T(1024)S(1)}, /*index=5*/f32[76...) all-reduce(f32[768]{0:T(1024)S(1)} %get-tuple-element.306, ...), channel_id=4, replica_groups=mesh['dp'=4,'ctx'=2,'fsdp'=4] {'dp','fsdp'}, use_global_device_ids=true, to_apply=%region_25.26.clone | all-reduce | flops 9216 | bytes 73728
  896.9 5.6 all-reduce.19
  (288 shorter events, 99.6 us)
Async XLA Ops:
  7.2 78.5 %all-gather.7.cloned.1.call-start = ((), (), s32[]{:S(2)}) async-start(), calls=%async_computation.6 | async-start | bytes 3760128 | tf_op jit(solution)/shard_map/all_gather | solution.py:219
  9.0 130.6 %all-gather.9.cloned.1.call-start = ((), (), s32[]{:S(2)}) async-start(), calls=%async_computation.7 | async-start | bytes 2359296 | tf_op jit(solution)/shard_map/all_gather | solution.py:272
  84.4 4.5 copy-start.42
  107.2 18.3 %copy-start.31 = (f32[48,768]{1,0:T(8,128)S(1)}, f32[48,768]{1,0:T(8,128)}, u32[]{:S(2)}) copy-start(f32[48,768]{1,0:T(8,128)} %param.28) | copy-start | bytes 442372
  107.2 19.0 %copy-start.26 = (f32[48,3072]{1,0:T(8,128)S(1)}, f32[48,3072]{1,0:T(8,128)}, u32[]{:S(2)}) copy-start(f32[48,3072]{1,0:T(8,128)} %param.32) | copy-start | bytes 1769476
  107.3 57.9 %all-gather.11.cloned.1.call-start = ((), (), s32[]{:S(2)}) async-start(), calls=%async_computation.8 | async-start | bytes 2359296 | tf_op jit(solution)/shard_map/all_gather | solution.py:273
  107.3 19.7 %copy-start.27 = (f32[192,768]{1,0:T(8,128)S(1)}, f32[192,768]{1,0:T(8,128)}, u32[]{:S(2)}) copy-start(f32[192,768]{1,0:T(8,128)} %param.34) | copy-start | bytes 1769476
  125.5 80.7 %all-gather.13.cloned.1.call-start = ((), (), s32[]{:S(2)}) async-start(), calls=%async_computation.9 | async-start | bytes 1253376 | tf_op jit(solution)/shard_map/all_gather | solution.py:222
  126.2 135.2 %all-gather.15.cloned.1.call-start = ((), (), s32[]{:S(2)}) async-start(), calls=%async_computation.10 | async-start | bytes 5013504 | tf_op jit(solution)/shard_map/all_gather | solution.py:226
  127.0 189.1 %all-gather.17.cloned.1.call-start = ((), (), s32[]{:S(2)}) async-start(), calls=%async_computation.11 | async-start | bytes 5013504 | tf_op jit(solution)/shard_map/all_gather | solution.py:228
  127.8 273.9 %reduce-scatter.7.cloned.1.call-start = ((), (), s32[]{:S(2)}) async-start(), calls=%async_computation.12 | async-start | bytes 1966080 | tf_op jit(solution)/shard_map/reduce_scatter | solution.py:365
  133.0 34.7 %copy-start.29 = (pred[128,1024]{1,0:T(8,128)(4,1)}, pred[128,1024]{1,0:T(8,128)(4,1)S(1)}, u32[]{:S(2)}) copy-start(pred[128,1024]{1,0:T(8,128)(4,1)S(1)} %iota_compare_fusion) | copy-start | bytes 393220
  133.1 34.6 %copy-start.5 = (bf16[128,768]{0,1:T(8,128)(2,1)}, bf16[128,768]{0,1:T(8,128)(2,1)S(1)}, u32[]{:S(2)}) copy-start(bf16[128,768]{0,1:T(8,128)(2,1)S(1)} %copy.50) | copy-start | bytes 589828
  167.7 38.5 %copy-start.1 = (f32[1,128,768]{2,1,0:T(8,128)S(1)}, f32[1,128,768]{2,1,0:T(8,128)}, u32[]{:S(2)}) copy-start(f32[1,128,768]{2,1,0:T(8,128)} %param.21) | copy-start | bytes 1179652
  180.8 27.4 %copy-start.33 = (f32[12,128]{1,0:T(8,128)}, f32[12,128]{1,0:T(8,128)S(1)}, u32[]{:S(2)}) copy-start(f32[12,128]{1,0:T(8,128)S(1)} %add.245) | copy-start | bytes 18436
  207.9 115.5 %copy-start.36 = (f32[128]{0:T(128)}, f32[128]{0:T(128)S(1)}, u32[]{:S(2)}) copy-start(f32[128]{0:T(128)S(1)} %broadcast_multiply_fusion) | copy-start | bytes 1540
  208.2 115.3 %copy-start.45 = (f32[128]{0:T(128)}, f32[128]{0:T(128)S(1)}, u32[]{:S(2)}) copy-start(f32[128]{0:T(128)S(1)} %fusion.95) | copy-start | bytes 1540
  208.2 107.9 %copy-start.10 = (f32[1,128,768]{2,1,0:T(8,128)S(1)}, f32[1,128,768]{2,1,0:T(8,128)}, u32[]{:S(2)}) copy-start(f32[1,128,768]{2,1,0:T(8,128)} %param.22) | copy-start | bytes 1179652
  316.1 5.1 copy-start
  325.2 19.9 %copy-start.2 = (bf16[512,768]{1,0:T(8,128)(2,1)S(1)}, bf16[512,768]{1,0:T(8,128)(2,1)}, u32[]{:S(2)}) copy-start(bf16[512,768]{1,0:T(8,128)(2,1)} %all_gather.69) | copy-start | bytes 2359300
  351.8 5.1 copy-start.3
  368.4 69.9 %reduce-scatter.9.cloned.1.call-start = ((), (), s32[]{:S(2)}) async-start(), calls=%async_computation.13 | async-start | bytes 1966080 | tf_op jit(solution)/shard_map/reduce_scatter | solution.py:366
  369.2 134.8 %reduce-scatter.13.cloned.1.call-start = ((), (), s32[]{:S(2)}) async-start(), calls=%async_computation.15 | async-start | bytes 2506752 | tf_op jit(solution)/shard_map/reduce_scatter | solution.py:386
  371.2 226.3 %reduce-scatter.11.cloned.1.call-start = ((), (), s32[]{:S(2)}) async-start(), calls=%async_computation.14 | async-start | bytes 7520256 | tf_op jit(solution)/shard_map/reduce_scatter | solution.py:383
  371.3 68.8 %copy-start.43 = (f32[128]{0:T(128)S(1)}, f32[128]{0:T(128)}, u32[]{:S(2)}) copy-start(f32[128]{0:T(128)} %copy-done.42) | copy-start | bytes 1540
  371.3 68.8 %copy-start.48 = (f32[128]{0:T(128)S(1)}, f32[128]{0:T(128)}, u32[]{:S(2)}) copy-start(f32[128]{0:T(128)} %copy-done.47) | copy-start | bytes 1540
  444.3 268.2 %reduce-scatter.15.cloned.1.call-start = ((), (), s32[]{:S(2)}) async-start(), calls=%async_computation.16 | async-start | bytes 10027008 | tf_op jit(solution)/shard_map/reduce_scatter | solution.py:390
  451.2 376.9 %reduce-scatter.17.cloned.1.call-start = ((), (), s32[]{:S(2)}) async-start(), calls=%async_computation.17 | async-start | bytes 10027008 | tf_op jit(solution)/shard_map/reduce_scatter | solution.py:392
  457.5 445.0 %all-reduce.24.cloned.1.call-start = ((), (), s32[]{:S(2)}) async-start(), calls=%async_computation.18 | async-start | bytes 3538944 | tf_op jit(solution)/shard_map/psum | solution.py:395
  828.5 4.3 copy-start.44
  828.5 4.3 copy-start.49
  902.4 5.4 copy-start.28
  (40 other events, 74.0 us)
Sparse Core Ops, SparseCore 0:
  10.9 50.5 all-gather.6
  107.4 28.3 all-gather.8
  137.3 27.7 all-gather.10
  167.8 38.3 all-gather.12
  208.9 52.4 all-gather.14
  264.1 51.9 all-gather.16
  368.6 33.1 reduce-scatter.6
  404.0 34.2 reduce-scatter.8
  442.1 61.9 reduce-scatter.12
  508.5 89.0 reduce-scatter.10
  601.6 110.8 reduce-scatter.14
  717.0 111.1 reduce-scatter.16
  830.7 56.0 all-reduce.23
where the time goes:
time: 917 us; the launch traced here: 915 us
  waiting for transfers between devices  566 us (62%)
  blocking collectives  191 us (21%)
  matrix products  77.1 us (8%)
  local copies, waits for them, and re-layouts  34.4 us (4%)
  other arithmetic  25.9 us (3%)
  between operations  19.7 us (2%)
    unnamed x2, blocking collectives  125 us
    reduce_scatter x1, waiting for transfers between devices, local(): lax.psum_scatter(fc2_weight_grad, ('dp', 'fsdp'), scatter_dimension=0, ti...  116 us
    reduce_scatter x1, waiting for transfers between devices, local(): lax.psum_scatter(fc1_weight_grad, ('dp', 'fsdp'), scatter_dimension=0, ti...  115 us
    reduce_scatter x1, waiting for transfers between devices, local(): lax.psum_scatter(qkv_weight_grad, ('dp', 'fsdp'), scatter_dimension=0, ti...  93.4 us
    all_gather x1, waiting for transfers between devices, local(): lax.all_gather(fc1_weight.astype(jnp.bfloat16), ('dp', 'fsdp'), axis=0, t...  53.2 us
    all_gather x1, waiting for transfers between devices, local(): lax.all_gather(fc2_weight.astype(jnp.bfloat16), ('dp', 'fsdp'), axis=0, t...  51.5 us
    reduce_scatter x1, waiting for transfers between devices, local(): lax.psum_scatter(out_weight_grad, ('dp', 'fsdp'), scatter_dimension=0, ti...  44.7 us
    reduce_scatter x1, waiting for transfers between devices, local(): lax.psum_scatter(to_rows(value_acc), 'fsdp', scatter_dimension=0, tiled=T...  35.6 us
  transfers between devices with their start and end apart: 13, of which 10 were waited for; matrix products, arithmetic and copies ran while one was open for 9% of the time, Pallas kernels for 0%

commit v1 on v0

v1 whole, which is shorter than its diff:
```python
import functools

import jax
import jax.numpy as jnp
from jax import lax
from jax.experimental import pallas as pl
from jax.experimental.pallas import tpu as pltpu
from jax.sharding import PartitionSpec as P

HEAD_DIM = 64
EPSILON = 1e-05
SCALE = HEAD_DIM ** (-0.5)
MASKED = -1e30
CHUNK = 64
LOW = jnp.bfloat16
WIDE = jnp.float32


def swap(value, axis, bit):
    count = lax.axis_size(axis)
    return lax.ppermute(value, axis, [(at, at ^ bit) for at in range(count)])


def shift(value, axis, by):
    count = lax.axis_size(axis)
    return lax.ppermute(value, axis, [(at, (at + by) % count) for at in range(count)])


def transpose_homes(value):
    side = lax.axis_size("dp")
    pairs = [(a * side + b, b * side + a) for a in range(side) for b in range(side)]
    return lax.ppermute(value, ("dp", "fsdp"), pairs)


def slot_order(count):
    order = [0]
    bit = count // 2
    while bit:
        order = order + [slot ^ bit for slot in order]
        bit //= 2
    return order


def gather_rows(block):
    bit = lax.axis_size("dp") // 2
    while bit:
        block = jnp.concatenate([block, swap(block, "dp", bit)], axis=0)
        bit //= 2
    return block


def scatter_rows(partial):
    bit = 1
    count = lax.axis_size("dp")
    while bit < count:
        half = partial.shape[0] // 2
        arrived = swap(partial[half:].astype(LOW), "dp", bit)
        partial = partial[:half].astype(WIDE) + arrived.astype(WIDE)
        bit *= 2
    return partial


def pick(stack, at):
    return lax.dynamic_index_in_dim(stack, at, 0, keepdims=False)


def exchange(stack, axis):
    mine = lax.axis_index(axis)
    count = lax.axis_size(axis)
    relative = [pick(stack, mine)]
    for bit in range(1, count):
        relative.append(swap(pick(stack, mine ^ bit), axis, bit))
    relative = jnp.stack(relative)
    return jnp.stack([pick(relative, mine ^ source) for source in range(count)])


def exchange_sum(stack, axis):
    mine = lax.axis_index(axis)
    total = pick(stack, mine).astype(WIDE)
    for bit in range(1, lax.axis_size(axis)):
        total += swap(pick(stack, mine ^ bit).astype(LOW), axis, bit).astype(WIDE)
    return total


def sum_replicas(value):
    low = value.astype(LOW)
    if lax.axis_size("ctx") == 2:
        return low.astype(WIDE) + shift(low, "ctx", 1).astype(WIDE)
    return jnp.sum(lax.all_gather(low, "ctx").astype(WIDE), axis=0)


def matmul_nt(left, right):
    return lax.dot_general(left, right, (((1,), (1,)), ((), ())), preferred_element_type=WIDE)


def matmul_nn(left, right):
    return lax.dot_general(left, right, (((1,), (0,)), ((), ())), preferred_element_type=WIDE)


def matmul_tn(left, right):
    return lax.dot_general(left, right, (((0,), (0,)), ((), ())), preferred_element_type=WIDE)


def visible_block(place_ref, start, block_rows, columns):
    slot = start // block_rows
    query_pos = place_ref[slot] * block_rows + start % block_rows
    query_pos = query_pos + lax.broadcasted_iota(jnp.int32, (CHUNK, columns), 0)
    lane = lax.broadcasted_iota(jnp.int32, (CHUNK, columns), 1)
    key_pos = lane
    for at in range(columns // block_rows):
        inside = (lane >= at * block_rows) & (lane < (at + 1) * block_rows)
        key_pos = jnp.where(inside, place_ref[at] * block_rows + lane - at * block_rows, key_pos)
    return key_pos <= query_pos


def columns_of(head):
    return slice(head * HEAD_DIM, (head + 1) * HEAD_DIM)


def own_forward(heads, block_rows, place_ref, kvq_ref, acc_ref, stat_ref, score, prob):
    width = heads * HEAD_DIM
    rows = kvq_ref.shape[0]
    for head in range(heads):
        query = kvq_ref[:, 2 * width + head * HEAD_DIM : 2 * width + (head + 1) * HEAD_DIM]
        score[...] = matmul_nt(query, kvq_ref[:, columns_of(head)])

        def chunk(step, carry):
            start = pl.multiple_of(step * CHUNK, CHUNK)
            seen = visible_block(place_ref, start, block_rows, rows)
            scores = jnp.where(seen, score[pl.ds(start, CHUNK), :] * SCALE, MASKED)
            highest = jnp.max(scores, axis=1, keepdims=True)
            weight = jnp.exp(scores - highest)
            stat_ref[pl.ds(start, CHUNK), head : head + 1] = highest
            stat_ref[pl.ds(start, CHUNK), heads + head : heads + head + 1] = jnp.sum(
                weight, axis=1, keepdims=True
            )
            prob[pl.ds(start, CHUNK), :] = weight.astype(LOW)
            return carry

        lax.fori_loop(0, rows // CHUNK, chunk, 0)
        value = kvq_ref[:, width + head * HEAD_DIM : width + (head + 1) * HEAD_DIM]
        acc_ref[:, columns_of(head)] = matmul_nn(prob[...], value)


def earlier_forward(
    heads, place_ref, kvq_ref, kv_ref, acc_in, stat_in, acc_ref, low_ref, stat_ref, score, prob, fade
):
    width = heads * HEAD_DIM
    rows = kvq_ref.shape[0]
    slots = place_ref.shape[0] - 1
    acc_ref[...] = acc_in[...]
    stat_ref[...] = stat_in[...]
    for piece in range(kv_ref.shape[0]):

        @pl.when(place_ref[slots] > piece)
        def _visit(piece=piece):
            for head in range(heads):
                query = kvq_ref[:, 2 * width + head * HEAD_DIM : 2 * width + (head + 1) * HEAD_DIM]
                score[...] = matmul_nt(query, kv_ref[piece, :, columns_of(head)])

                def chunk(step, carry):
                    here = pl.ds(pl.multiple_of(step * CHUNK, CHUNK), CHUNK)
                    scores = score[here, :] * SCALE
                    old = stat_ref[here, head : head + 1]
                    highest = jnp.maximum(old, jnp.max(scores, axis=1, keepdims=True))
                    weight = jnp.exp(scores - highest)
                    fading = jnp.exp(old - highest)
                    stat_ref[here, head : head + 1] = highest
                    total = stat_ref[here, heads + head : heads + head + 1]
                    stat_ref[here, heads + head : heads + head + 1] = total * fading + jnp.sum(
                        weight, axis=1, keepdims=True
                    )
                    fade[here, :] = jnp.broadcast_to(fading, (CHUNK, HEAD_DIM))
                    prob[here, :] = weight.astype(LOW)
                    return carry

                lax.fori_loop(0, rows // CHUNK, chunk, 0)
                value = kv_ref[piece, :, width + head * HEAD_DIM : width + (head + 1) * HEAD_DIM]
                acc_ref[:, columns_of(head)] = acc_ref[:, columns_of(head)] * fade[
                    ...
                ] + matmul_nn(prob[...], value)

    for head in range(heads):
        total = stat_ref[:, heads + head : heads + head + 1]
        context = acc_ref[:, columns_of(head)] / total
        acc_ref[:, columns_of(head)] = context
        low_ref[:, columns_of(head)] = context.astype(LOW)
        stat_ref[:, head : head + 1] = stat_ref[:, head : head + 1] + jnp.log(total)


def score_grads(here, seen, head, total, delta, score, dots, prob, grad):
    scores = score[here, :] * SCALE
    weight = jnp.exp(scores - total)
    if seen is not None:
        weight = jnp.where(seen, weight, 0.0)
    prob[here, :] = weight.astype(LOW)
    grad[here, :] = (weight * (dots[here, :] - delta) * SCALE).astype(LOW)


def delta_of(here, head, context_ref, ctx_grad_ref):
    product = context_ref[here, columns_of(head)] * ctx_grad_ref[here, columns_of(head)].astype(WIDE)
    return jnp.sum(product, axis=1, keepdims=True)


def earlier_backward(
    heads, place_ref, kvq_ref, kv_ref, ctx_grad_ref, context_ref, stat_ref, query_grad_ref,
    kv_grad_ref, score, dots, prob, grad
):
    width = heads * HEAD_DIM
    rows = kvq_ref.shape[0]
    slots = place_ref.shape[0] - 1
    query_grad_ref[...] = jnp.zeros_like(query_grad_ref)
    for piece in range(kv_ref.shape[0]):

        @pl.when(place_ref[slots] <= piece)
        def _skip(piece=piece):
            kv_grad_ref[piece] = jnp.zeros(kv_grad_ref.shape[1:], kv_grad_ref.dtype)

        @pl.when(place_ref[slots] > piece)
        def _visit(piece=piece):
            for head in range(heads):
                query = kvq_ref[:, 2 * width + head * HEAD_DIM : 2 * width + (head + 1) * HEAD_DIM]
                value_at = slice(width + head * HEAD_DIM, width + (head + 1) * HEAD_DIM)
                key = kv_ref[piece, :, columns_of(head)]
                out_grad = ctx_grad_ref[:, columns_of(head)]
                score[...] = matmul_nt(query, key)
                dots[...] = matmul_nt(out_grad, kv_ref[piece, :, value_at])

                def chunk(step, carry):
                    here = pl.ds(pl.multiple_of(step * CHUNK, CHUNK), CHUNK)
                    total = stat_ref[here, head : head + 1]
                    delta = delta_of(here, head, context_ref, ctx_grad_ref)
                    score_grads(here, None, head, total, delta, score, dots, prob, grad)
                    return carry

                lax.fori_loop(0, rows // CHUNK, chunk, 0)
                kv_grad_ref[piece, :, columns_of(head)] = matmul_tn(grad[...], query).astype(LOW)
                kv_grad_ref[piece, :, value_at] = matmul_tn(prob[...], out_grad).astype(LOW)
                query_grad_ref[:, columns_of(head)] += matmul_nn(grad[...], key)


def own_backward(
    heads, block_rows, place_ref, kvq_ref, ctx_grad_ref, context_ref, stat_ref, query_grad_in,
    grad_ref, score, dots, prob, grad
):
    width = heads * HEAD_DIM
    rows = kvq_ref.shape[0]
    for head in range(heads):
        query_at = slice(2 * width + head * HEAD_DIM, 2 * width + (head + 1) * HEAD_DIM)
        value_at = slice(width + head * HEAD_DIM, width + (head + 1) * HEAD_DIM)
        query = kvq_ref[:, query_at]
        key = kvq_ref[:, columns_of(head)]
        out_grad = ctx_grad_ref[:, columns_of(head)]
        score[...] = matmul_nt(query, key)
        dots[...] = matmul_nt(out_grad, kvq_ref[:, value_at])

        def chunk(step, carry):
            start = pl.multiple_of(step * CHUNK, CHUNK)
            here = pl.ds(start, CHUNK)
            seen = visible_block(place_ref, start, block_rows, rows)
            total = stat_ref[here, head : head + 1]
            delta = delta_of(here, head, context_ref, ctx_grad_ref)
            score_grads(here, seen, head, total, delta, score, dots, prob, grad)
            return carry

        lax.fori_loop(0, rows // CHUNK, chunk, 0)
        grad_ref[:, columns_of(head)] = matmul_tn(grad[...], query)
        grad_ref[:, value_at] = matmul_tn(prob[...], out_grad)
        grad_ref[:, query_at] = query_grad_in[:, columns_of(head)] + matmul_nn(grad[...], key)


def attention_call(kernel, operands, results, square, low_squares, wide_squares, extra=()):
    smem = pl.BlockSpec(memory_space=pltpu.SMEM)
    vmem = pl.BlockSpec(memory_space=pltpu.VMEM)
    return pl.pallas_call(
        kernel,
        out_shape=results,
        in_specs=[smem] + [vmem] * (len(operands) - 1),
        out_specs=[vmem] * len(results),
        scratch_shapes=[pltpu.VMEM((square, square), WIDE)] * wide_squares
        + [pltpu.VMEM((square, square), LOW)] * low_squares
        + list(extra),
        compiler_params=pltpu.CompilerParams(vmem_limit_bytes=48 * 1024 * 1024),
        cost_estimate=pl.CostEstimate(
            flops=2 * 6 * square * square * HEAD_DIM * 4, bytes_accessed=8 * 1024 * 1024,
            transcendentals=3 * square * square,
        ),
    )(*operands)


def normalize(values):
    centered = values - jnp.mean(values, axis=-1, keepdims=True)
    spread = jnp.mean(centered * centered, axis=-1, keepdims=True)
    inverse = lax.rsqrt(spread + EPSILON)
    return centered * inverse, inverse


def normalize_back(grad, gain, hat, inverse):
    scaled = grad * gain
    mean_scaled = jnp.mean(scaled, axis=-1, keepdims=True)
    mean_product = jnp.mean(scaled * hat, axis=-1, keepdims=True)
    part = inverse * (scaled - mean_scaled - hat * mean_product)
    return part, jnp.sum(grad * hat, axis=0), jnp.sum(grad, axis=0)


def local(
    tokens, cotangent, ln1_gain, ln1_bias, qkv_weight, q_bias, v_bias, out_weight, out_bias,
    ln2_gain, ln2_bias, fc1_weight, fc1_bias, fc2_weight, fc2_bias,
):
    parts = lax.axis_size("dp")
    depth = lax.axis_size("fsdp")
    contexts = lax.axis_size("ctx")
    assert parts == depth
    mine = lax.axis_index("dp")
    rows, model = tokens.shape[1:]
    shard = ln1_gain.shape[0]
    heads = model // HEAD_DIM // parts
    width = heads * HEAD_DIM
    hidden_shard = fc1_bias.shape[0]
    hidden_part = hidden_shard * depth
    group_rows = parts * rows

    token_rows = transpose_homes(tokens[0].astype(LOW)).astype(WIDE)

    vector_rows = [ln1_gain, ln1_bias, ln2_gain, ln2_bias, out_bias, fc2_bias, q_bias, v_bias]
    per_hidden = hidden_shard // shard
    packed = jnp.concatenate(
        [jnp.stack(vector_rows), fc1_bias.reshape(per_hidden, shard)], axis=0
    )
    packed = jnp.pad(packed, ((0, 16 - packed.shape[0]), (0, 128 - shard))).astype(LOW)
    vectors = lax.all_gather(packed, ("dp", "fsdp"), axis=0)
    vectors = vectors[:, : 8 + per_hidden, :shard].astype(WIDE)
    whole = jnp.transpose(vectors[:, :8], (1, 0, 2)).reshape(8, model)
    gain1, bias1, gain2, bias2, out_shift, down_shift = [whole[at] for at in range(6)]
    query_shift = lax.dynamic_slice_in_dim(whole[6], mine * width, width)
    value_shift = lax.dynamic_slice_in_dim(whole[7], mine * width, width)
    up_shift = lax.dynamic_slice_in_dim(vectors[:, 8:], mine * depth, depth, axis=0).reshape(-1)

    qkv_split = qkv_weight.astype(LOW).reshape(shard, 3, parts, width)
    qkv_split = jnp.stack([qkv_split[:, 1], qkv_split[:, 2], qkv_split[:, 0]], axis=1)
    qkv_split = jnp.transpose(qkv_split, (2, 0, 1, 3)).reshape(parts, shard, 3 * width)
    up_split = fc1_weight.astype(LOW).reshape(shard, parts, hidden_part)
    up_split = jnp.transpose(up_split, (1, 0, 2))

    def gather_columns(split):
        gathered = lax.all_gather(exchange(split, "dp"), "fsdp", axis=0)
        return jnp.transpose(gathered, (1, 0, 2, 3)).reshape(model, split.shape[-1])

    kvq_matrix = gather_columns(qkv_split)
    out_matrix = lax.all_gather(out_weight.astype(LOW), "fsdp", axis=0, tiled=True)
    up_matrix = gather_columns(up_split)
    down_matrix = lax.all_gather(fc2_weight.astype(LOW), "fsdp", axis=0, tiled=True)

    grad_rows = transpose_homes(cotangent[0].astype(LOW))

    hat1, inverse1 = normalize(token_rows)
    norm1 = gather_rows((hat1 * gain1 + bias1).astype(LOW))
    kvq_shift = jnp.concatenate([jnp.zeros((width,), WIDE), value_shift, query_shift])
    kvq = (matmul_nn(norm1, kvq_matrix) + kvq_shift).astype(LOW)
    kv = kvq[:, : 2 * width]
    kv_earlier = jnp.stack([shift(kv, "ctx", by) for by in range(1, contexts)])
    order = slot_order(parts)
    place = jnp.stack(
        [(mine ^ slot).astype(jnp.int32) for slot in order]
        + [lax.axis_index("ctx").astype(jnp.int32)]
    )
    like = jax.ShapeDtypeStruct
    acc, stat = attention_call(
        functools.partial(own_forward, heads, rows),
        (place, kvq),
        (like((group_rows, width), WIDE), like((group_rows, 128), WIDE)),
        group_rows, 1, 1,
    )
    context, context_low, stat = attention_call(
        functools.partial(earlier_forward, heads),
        (place, kvq, kv_earlier, acc, stat),
        (
            like((group_rows, width), WIDE),
            like((group_rows, width), LOW),
            like((group_rows, 128), WIDE),
        ),
        group_rows, 1, 1, (pltpu.VMEM((group_rows, HEAD_DIM), WIDE),),
    )
    attended = scatter_rows(matmul_nn(context_low, out_matrix)) + out_shift
    mixed = token_rows + attended

    hat2, inverse2 = normalize(mixed)
    norm2 = gather_rows((hat2 * gain2 + bias2).astype(LOW))
    inner = matmul_nn(norm2, up_matrix) + up_shift
    activated, gelu_back = jax.vjp(jax.nn.gelu, inner)
    hidden = activated.astype(LOW)
    branch = gather_rows(grad_rows)
    hidden_grad = matmul_nt(branch, down_matrix)
    inner_grad = gelu_back(hidden_grad)[0].astype(LOW)
    norm2_grad = scatter_rows(matmul_nt(inner_grad, up_matrix))
    mixed_part, gain2_grad, bias2_grad = normalize_back(norm2_grad, gain2, hat2, inverse2)
    attn_grad = (grad_rows.astype(WIDE) + mixed_part).astype(LOW)
    attn_grads = gather_rows(attn_grad)
    context_grad = matmul_nt(attn_grads, out_matrix).astype(LOW)

    fed = scatter_rows(matmul_nn(hidden, down_matrix)) + down_shift
    output = tokens[0] + transpose_homes((attended + fed).astype(LOW)).astype(WIDE)
    down_grad = matmul_tn(hidden, branch)
    up_grad = matmul_tn(norm2, inner_grad)
    out_grad = matmul_tn(context_low, attn_grads)

    def to_owner_rows(grad):
        return sum_replicas(exchange_sum(grad, "fsdp"))

    def by_owner(grad):
        return jnp.transpose(grad.reshape(parts, depth, shard, grad.shape[-1]), (1, 0, 2, 3))

    down_total = to_owner_rows(down_grad.reshape(depth, hidden_shard, model))
    up_total = to_owner_rows(by_owner(up_grad))
    up_total = exchange(up_total.astype(LOW), "dp")
    up_total = jnp.transpose(up_total, (1, 0, 2)).reshape(shard, parts * hidden_part)
    out_total = to_owner_rows(out_grad.reshape(depth, shard, model))

    query_grad, kv_grad = attention_call(
        functools.partial(earlier_backward, heads),
        (place, kvq, kv_earlier, context_grad, context, stat),
        (like((group_rows, width), WIDE), like(kv_earlier.shape, LOW)),
        group_rows, 2, 2,
    )
    arrived = sum(
        shift(kv_grad[by - 1], "ctx", -by).astype(WIDE) for by in range(1, contexts)
    )
    (kvq_own,) = attention_call(
        functools.partial(own_backward, heads, rows),
        (place, kvq, context_grad, context, stat, query_grad),
        (like((group_rows, 3 * width), WIDE),),
        group_rows, 2, 2,
    )
    kvq_grad = jnp.concatenate(
        [kvq_own[:, : 2 * width] + arrived, kvq_own[:, 2 * width :]], axis=1
    ).astype(LOW)
    norm1_grad = scatter_rows(matmul_nt(kvq_grad, kvq_matrix))
    rows_part, gain1_grad, bias1_grad = normalize_back(norm1_grad, gain1, hat1, inverse1)
    input_grad = cotangent[0] + transpose_homes((mixed_part + rows_part).astype(LOW)).astype(WIDE)

    kvq_total = to_owner_rows(by_owner(matmul_tn(norm1, kvq_grad)))
    kvq_total = exchange(kvq_total.astype(LOW), "dp").reshape(parts, shard, 3, width)
    qkv_total = jnp.stack([kvq_total[:, :, 2], kvq_total[:, :, 0], kvq_total[:, :, 1]], axis=0)
    qkv_total = jnp.transpose(qkv_total, (2, 0, 1, 3)).reshape(shard, 3 * model)

    kvq_bias = jnp.sum(kvq_grad.astype(WIDE), axis=0)
    up_bias = jnp.sum(inner_grad.astype(WIDE), axis=0)
    full = jnp.stack(
        [
            gain1_grad,
            bias1_grad,
            gain2_grad,
            bias2_grad,
            jnp.sum(attn_grad.astype(WIDE), axis=0),
            jnp.sum(grad_rows.astype(WIDE), axis=0),
        ]
    ).reshape(6, parts, depth, shard)
    full = jnp.transpose(full, (2, 1, 0, 3))
    part = jnp.concatenate(
        [
            kvq_bias[2 * width :].reshape(depth, 1, shard),
            kvq_bias[width : 2 * width].reshape(depth, 1, shard),
            up_bias.reshape(depth, per_hidden, shard),
        ],
        axis=1,
    )
    owned = (jnp.arange(parts) == mine)[None, :, None, None]
    part = jnp.where(owned, part[:, None], 0.0)
    vector_grads = jnp.concatenate([full, part], axis=2)
    vector_grads = jnp.pad(
        vector_grads, ((0, 0), (0, 0), (0, 16 - vector_grads.shape[2]), (0, 128 - shard))
    )
    vector_total = exchange_sum(vector_grads, "fsdp")
    vector_total = exchange_sum(vector_total, "dp")
    vector_total = sum_replicas(vector_total)[:, :shard]

    return (
        output[None],
        input_grad[None],
        vector_total[0],
        vector_total[1],
        qkv_total.astype(WIDE),
        vector_total[6],
        vector_total[7],
        out_total,
        vector_total[4],
        vector_total[2],
        vector_total[3],
        up_total.astype(WIDE),
        vector_total[8 : 8 + per_hidden].reshape(-1),
        down_total,
        vector_total[5],
    )


def solution(mesh):
    rows = P("dp", ("ctx", "fsdp"), None)
    vector = P(("dp", "fsdp"))
    matrix = P(("dp", "fsdp"), None)
    parameters = (
        vector, vector, matrix, vector, vector, matrix, vector, vector, vector, matrix, vector,
        matrix, vector,
    )
    return jax.shard_map(
        local,
        mesh=mesh,
        in_specs=(rows, rows) + parameters,
        out_specs=(rows, rows) + parameters,
        check_vma=False,
    )
```

time: 917 us -> 361 us (0.39)
  the two profiles are of different devices: /device:TPU:0 before, /device:TPU:2 now
where the time goes in v1:
time: 361 us; the launch traced here: 359 us
  waiting for transfers between devices  99 us (27%)
  starting transfers between devices  83.8 us (23%)
  blocking collectives  69.5 us (19%)
  local copies, waits for them, and re-layouts  33.3 us (9%)
  other arithmetic  24.7 us (7%)
  matrix products  18.2 us (5%)
  between operations  15.6 us (4%)
  Pallas kernels  15.4 us (4%)
    ppermute x46, waiting for transfers between devices, swap(): return lax.ppermute(value, axis, [(at, at ^ bit) for at in range(count)])  64.5 us
    ppermute x46, starting transfers between devices, swap(): return lax.ppermute(value, axis, [(at, at ^ bit) for at in range(count)])  47.1 us
    all_gather x1, blocking collectives, local(): vectors = lax.all_gather(packed, ('dp', 'fsdp'), axis=0)  32.2 us
    ppermute x7, starting transfers between devices, shift(): lax.ppermute(value, axis, [(at, (at + by) % count) for at in range(count)])  21 us
    all_gather x1, blocking collectives, gather_columns(): gathered = lax.all_gather(exchange(split, 'dp'), 'fsdp', axis=0)  21 us
    ppermute x4, waiting for transfers between devices, transpose_homes(): return lax.ppermute(value, ('dp', 'fsdp'), pairs)  17.4 us
    all_gather x1, blocking collectives, local(): lax.all_gather(out_weight.astype(LOW), 'fsdp', axis=0, tiled=True)  16.3 us
    ppermute x4, starting transfers between devices, transpose_homes(): return lax.ppermute(value, ('dp', 'fsdp'), pairs)  15.5 us
  transfers between devices with their start and end apart: 59, of which 23 were waited for; matrix products, arithmetic and copies ran while one was open for 16% of the time, Pallas kernels for 4%

profile of v1, /device:TPU:2, one launch (start us, length us, event | category | flops | bytes accessed | tf_op | source)
XLA Modules:
  0.0 359.5 jit_solution(1746865568534131032)
XLA Ops:
  13.1 5.8 %collective-permute-start = (bf16[128,768]{1,0:T(8,128)(2,1)S(1)}, bf16[128,768]{1,0:T(8,128)(2,1)S(1)}, u32[]{:S(2)}, u32[]{:S(2)}) collective-permute-start(bf16[128,768]{1,0:T(8,128)(2,1)S(1)} %bitcast_convert_fusion.4), channel_id=1, source_target_pairs={{0,0},{1,8},{2,16},{3,24},{8,1},{9,9},{10,17},{11,25},{16,2},{17,1... | collective-permute-start | bytes 589832 | tf_op jit(solution)/shard_map/ppermute | solution.py:32
  19.1 32.2 %all-gather = bf16[256,128]{1,0:T(8,128)(2,1)S(1)} all-gather(bf16[16,128]{1,0:T(8,128)(2,1)S(1)} %pad.9), channel_id=2, replica_groups=mesh['dp'=4,'ctx'=2,'fsdp'=4] {'dp','fsdp'}, dimensions={0}, use_global_device_ids=true | all-gather | bytes 69632 | tf_op jit(solution)/shard_map/all_gather | solution.py:331
  55.3 6.6 %collective-permute-done.1 = bf16[128,768]{1,0:T(8,128)(2,1)S(1)} collective-permute-done((bf16[128,768]{1,0:T(8,128)(2,1)S(1)}, bf16[128,768]{1,0:T(8,128)(2,1)S(1)}, u32[]{:S(2)}, u32[]{:S(2)}) %collective-permute-start.1) | collective-permute-done | bytes 196640 | tf_op jit(solution)/shard_map/ppermute | solution.py:21
  62.0 21.0 %all-gather.1 = bf16[16,48,576]{2,1,0:T(8,128)(2,1)S(1)} all-gather(bf16[4,48,576]{2,1,0:T(8,128)(2,1)S(1)} %pad_maximum_fusion.18), channel_id=3, replica_groups=mesh['dp'=4,'ctx'=2,'fsdp'=4] {'fsdp'}, dimensions={0}, use_global_device_ids=true | all-gather | bytes 1105920 | tf_op jit(solution)/shard_map/all_gather | solution.py:346
  86.9 16.3 %all_gather.28 = bf16[192,768]{1,0:T(8,128)(2,1)S(1)} all-gather(bf16[48,768]{1,0:T(8,128)(2,1)S(1)} %convert_element_type.348), channel_id=1, replica_groups=mesh['dp'=4,'ctx'=2,'fsdp'=4] {'fsdp'}, dimensions={0}, use_global_device_ids=true | all-gather | bytes 368640 | tf_op jit(solution)/shard_map/all_gather | solution.py:350
  103.2 6.8 %shard_map.262 = (f32[512,192]{1,0:T(8,128)S(1)}, f32[512,128]{1,0:T(8,128)S(1)}) custom-call(s32[5]{0:T(128)S(1)} %stack.166.place_ref, bf16[512,576]{1,0:T(8,128)(2,1)S(1)} %fusion.7.kvq_ref), custom_call_target="tpu_custom_call" | custom-call | flops 805306368 | bytes 8388608 | tf_op jit(solution)/shard_map/pallas_call | solution.py:275
  112.8 3.1 collective-permute-start.17
  117.7 7.7 %collective-permute-done.17 = bf16[128,768]{1,0:T(8,128)(2,1)} collective-permute-done((bf16[128,768]{1,0:T(8,128)(2,1)}, bf16[128,768]{1,0:T(8,128)(2,1)}, u32[]{:S(2)}, u32[]{:S(2)}) %collective-permute-start.17) | collective-permute-done | bytes 196640 | tf_op jit(solution)/shard_map/ppermute | solution.py:32
  125.4 2.7 collective-permute-done.8
  147.6 3.5 fusion.81
  151.1 4.9 %all-gather.6.cloned.1.call-done = bf16[768,768]{1,0:T(8,128)(2,1)} async-done(((bf16[192,768]{1,0:T(8,128)(2,1)}), bf16[768,768]{1,0:T(8,128)(2,1)}) %all-gather.6.cloned.1.call-update) | async-done | bytes 1179664 | tf_op jit(solution)/shard_map/all_gather | solution.py:352
  155.9 3.6 convert_reduce_fusion
  171.7 2.4 collective-permute-done.48
  174.9 13.2 %collective-permute-start.53 = (bf16[192,768]{1,0:T(8,128)(2,1)}, bf16[192,768]{1,0:T(8,128)(2,1)}, u32[]{:S(2)}, u32[]{:S(2)}) collective-permute-start(bf16[192,768]{1,0:T(8,128)(2,1)} %get-tuple-element.52), channel_id=1, source_target_pairs={{0,1},{1,0},{2,3},{3,2},{4,5},{5,4},{6,7},{7,6},{8,9},{9,8},{10,11... | collective-permute-start | bytes 884744 | tf_op jit(solution)/shard_map/ppermute | solution.py:21
  191.7 12.4 %collective-permute-done.47 = bf16[4,48,768]{2,1,0:T(8,128)(2,1)} collective-permute-done((bf16[4,48,768]{2,1,0:T(8,128)(2,1)}, bf16[4,48,768]{2,1,0:T(8,128)(2,1)}, u32[]{:S(2)}, u32[]{:S(2)}) %collective-permute-start.47) | collective-permute-done | bytes 294944 | tf_op jit(solution)/shard_map/ppermute | solution.py:21
  206.1 4.4 %collective-permute-start.49 = (bf16[4,48,768]{2,1,0:T(8,128)(2,1)S(1)}, bf16[4,48,768]{2,1,0:T(8,128)(2,1)S(1)}, u32[]{:S(2)}, u32[]{:S(2)}) collective-permute-start(bf16[4,48,768]{2,1,0:T(8,128)(2,1)S(1)} %fusion.14), channel_id=1, source_target_pairs={{0,4},{4,0},{1,5},{5,1},{2,6},{6,2},{3,7},{7,3},{8,12},{12,8},{9,1... | collective-permute-start | bytes 884744 | tf_op jit(solution)/shard_map/ppermute | solution.py:26
  210.6 5.0 %collective-permute-done.54 = bf16[192,768]{1,0:T(8,128)(2,1)} collective-permute-done((bf16[192,768]{1,0:T(8,128)(2,1)}, bf16[192,768]{1,0:T(8,128)(2,1)}, u32[]{:S(2)}, u32[]{:S(2)}) %collective-permute-start.54) | collective-permute-done | bytes 294944 | tf_op jit(solution)/shard_map/ppermute | solution.py:21
  217.1 5.2 %collective-permute-start.56 = (bf16[192,768]{1,0:T(8,128)(2,1)S(1)}, bf16[192,768]{1,0:T(8,128)(2,1)S(1)}, u32[]{:S(2)}, u32[]{:S(2)}) collective-permute-start(bf16[192,768]{1,0:T(8,128)(2,1)S(1)} %fusion.11), channel_id=1, source_target_pairs={{0,4},{4,0},{1,5},{5,1},{2,6},{6,2},{3,7},{7,3},{8,12},{12,8},{9,1... | collective-permute-start | bytes 884744 | tf_op jit(solution)/shard_map/ppermute | solution.py:26
  226.0 3.2 collective-permute-done.56
  230.1 4.4 %collective-permute-done.21 = bf16[128,768]{1,0:T(8,128)(2,1)S(1)} collective-permute-done((bf16[128,768]{1,0:T(8,128)(2,1)S(1)}, bf16[128,768]{1,0:T(8,128)(2,1)S(1)}, u32[]{:S(2)}, u32[]{:S(2)}) %collective-permute-start.21) | collective-permute-done | bytes 196640 | tf_op jit(solution)/shard_map/ppermute | solution.py:21
  235.3 2.5 convert_reduce_fusion.4
  239.3 2.6 collective-permute-start.16
  255.3 3.4 collective-permute-start.42
  260.8 6.1 %collective-permute-start.24 = (bf16[512,384]{1,0:T(8,128)(2,1)S(1)}, bf16[512,384]{1,0:T(8,128)(2,1)S(1)}, u32[]{:S(2)}, u32[]{:S(2)}) collective-permute-start(bf16[512,384]{1,0:T(8,128)(2,1)S(1)} %bitcast.243), channel_id=1, source_target_pairs={{0,4},{4,0},{1,5},{5,1},{2,6},{6,2},{3,7},{7,3},{8,12},{12,8},{9,1... | collective-permute-start | bytes 1179656 | tf_op jit(solution)/shard_map/ppermute | solution.py:26
  267.1 6.6 %shard_map.265 = f32[512,576]{1,0:T(8,128)S(1)} custom-call(s32[5]{0:T(128)S(1)} %stack.166.place_ref, bf16[512,576]{1,0:T(8,128)(2,1)S(1)} %fusion.7.kvq_ref, bf16[512,192]{1,0:T(8,128)(2,1)S(1)} %convolution_convert_fusion.ctx_grad_ref, f32[512,192]{1,0:T(8,128)S(1)} %get-tuple-element.25.context_ref, f32[512,128]{1,0:T(8,128)S(1)} %get-tuple-element.26.stat_ref, ...), custom_call_target="tpu_custom_call" | custom-call | flops 805306368 | bytes 8388608 | tf_op jit(solution)/shard_map/pallas_call | solution.py:275
  273.7 3.2 collective-permute-done.45
  282.9 2.7 collective-permute-start.35
  285.9 6.1 %collective-permute-done.37 = bf16[4,48,576]{2,1,0:T(8,128)(2,1)} collective-permute-done((bf16[4,48,576]{2,1,0:T(8,128)(2,1)S(1)}, bf16[4,48,576]{2,1,0:T(8,128)(2,1)}, u32[]{:S(2)}, u32[]{:S(2)}) %collective-permute-start.37) | collective-permute-done | bytes 221216 | tf_op jit(solution)/shard_map/ppermute | solution.py:21
  292.0 13.1 %collective-permute-done.36 = bf16[4,48,576]{2,1,0:T(8,128)(2,1)} collective-permute-done((bf16[4,48,576]{2,1,0:T(8,128)(2,1)S(1)}, bf16[4,48,576]{2,1,0:T(8,128)(2,1)}, u32[]{:S(2)}, u32[]{:S(2)}) %collective-permute-start.36) | collective-permute-done | bytes 221216 | tf_op jit(solution)/shard_map/ppermute | solution.py:21
  308.5 5.7 %collective-permute-done.38 = bf16[4,48,576]{2,1,0:T(8,128)(2,1)S(1)} collective-permute-done((bf16[4,48,576]{2,1,0:T(8,128)(2,1)S(1)}, bf16[4,48,576]{2,1,0:T(8,128)(2,1)S(1)}, u32[]{:S(2)}, u32[]{:S(2)}) %collective-permute-start.38) | collective-permute-done | bytes 221216 | tf_op jit(solution)/shard_map/ppermute | solution.py:26
  336.8 4.2 %collective-permute-start.27 = (bf16[128,768]{1,0:T(8,128)(2,1)S(1)}, bf16[128,768]{1,0:T(8,128)(2,1)S(1)}, u32[]{:S(2)}, u32[]{:S(2)}) collective-permute-start(bf16[128,768]{1,0:T(8,128)(2,1)S(1)} %fusion.30), channel_id=1, source_target_pairs={{0,0},{1,8},{2,16},{3,24},{8,1},{9,9},{10,17},{11,25},{16,2},{17,1... | collective-permute-start | bytes 589832 | tf_op jit(solution)/shard_map/ppermute | solution.py:32
  342.1 9.7 %collective-permute-done.27 = bf16[128,768]{1,0:T(8,128)(2,1)S(1)} collective-permute-done((bf16[128,768]{1,0:T(8,128)(2,1)S(1)}, bf16[128,768]{1,0:T(8,128)(2,1)S(1)}, u32[]{:S(2)}, u32[]{:S(2)}) %collective-permute-start.27) | collective-permute-done | bytes 196640 | tf_op jit(solution)/shard_map/ppermute | solution.py:32
  (398 shorter events, 113.4 us)
Async XLA Ops:
  7.2 135.7 %all-gather.8.cloned.1.call-start = ((), (), s32[]{:S(2)}) async-start(), calls=%async_computation.1 | async-start | bytes 1474560 | tf_op jit(solution)/shard_map/all_gather | solution.py:346
  9.3 73.9 %collective-permute-start.13 = (bf16[48,768]{1,0:T(8,128)(2,1)S(1)}, bf16[48,768]{1,0:T(8,128)(2,1)S(1)}, u32[]{:S(2)}, u32[]{:S(2)}) collective-permute-start(bf16[48,768]{1,0:T(8,128)(2,1)S(1)} %bitcast.267), channel_id=1, source_target_pairs={{0,24},{8,16},{16,8},{24,0},{1,25},{9,17},{17,9},{25,1},{2,26},{10... | collective-permute-start | bytes 221192 | tf_op jit(solution)/shard_map/ppermute | solution.py:21
  11.1 41.1 %collective-permute-start.5 = (bf16[48,576]{1,0:T(8,128)(2,1)S(1)}, bf16[48,576]{1,0:T(8,128)(2,1)S(1)}, u32[]{:S(2)}, u32[]{:S(2)}) collective-permute-start(bf16[48,576]{1,0:T(8,128)(2,1)S(1)} %get-tuple-element.96), channel_id=1, source_target_pairs={{0,24},{8,16},{16,8},{24,0},{1,25},{9,17},{17,9},{25,1},{2,26},{10... | collective-permute-start | bytes 165896 | tf_op jit(solution)/shard_map/ppermute | solution.py:21
  12.9 40.8 %collective-permute-start.4 = (bf16[48,576]{1,0:T(8,128)(2,1)S(1)}, bf16[48,576]{1,0:T(8,128)(2,1)S(1)}, u32[]{:S(2)}, u32[]{:S(2)}) collective-permute-start(bf16[48,576]{1,0:T(8,128)(2,1)S(1)} %get-tuple-element.97), channel_id=1, source_target_pairs={{0,16},{8,24},{16,0},{24,8},{1,17},{9,25},{17,1},{25,9},{2,18},{10... | collective-permute-start | bytes 165896 | tf_op jit(solution)/shard_map/ppermute | solution.py:21
  12.9 40.8 %collective-permute-start.3 = (bf16[48,576]{1,0:T(8,128)(2,1)S(1)}, bf16[48,576]{1,0:T(8,128)(2,1)S(1)}, u32[]{:S(2)}, u32[]{:S(2)}) collective-permute-start(bf16[48,576]{1,0:T(8,128)(2,1)S(1)} %get-tuple-element.98), channel_id=1, source_target_pairs={{0,8},{8,0},{16,24},{24,16},{1,9},{9,1},{17,25},{25,17},{2,10},{10... | collective-permute-start | bytes 165896 | tf_op jit(solution)/shard_map/ppermute | solution.py:21
  13.1 40.7 %collective-permute-start = (bf16[128,768]{1,0:T(8,128)(2,1)S(1)}, bf16[128,768]{1,0:T(8,128)(2,1)S(1)}, u32[]{:S(2)}, u32[]{:S(2)}) collective-permute-start(bf16[128,768]{1,0:T(8,128)(2,1)S(1)} %bitcast_convert_fusion.4), channel_id=1, source_target_pairs={{0,0},{1,8},{2,16},{3,24},{8,1},{9,9},{10,17},{11,25},{16,2},{17,1... | collective-permute-start | bytes 589832 | tf_op jit(solution)/shard_map/ppermute | solution.py:32
  52.2 31.0 %collective-permute-start.12 = (bf16[48,768]{1,0:T(8,128)(2,1)S(1)}, bf16[48,768]{1,0:T(8,128)(2,1)S(1)}, u32[]{:S(2)}, u32[]{:S(2)}) collective-permute-start(bf16[48,768]{1,0:T(8,128)(2,1)S(1)} %bitcast.269), channel_id=1, source_target_pairs={{0,16},{8,24},{16,0},{24,8},{1,17},{9,25},{17,1},{25,9},{2,18},{10... | collective-permute-start | bytes 221192 | tf_op jit(solution)/shard_map/ppermute | solution.py:21
  53.7 29.5 %collective-permute-start.11 = (bf16[48,768]{1,0:T(8,128)(2,1)S(1)}, bf16[48,768]{1,0:T(8,128)(2,1)S(1)}, u32[]{:S(2)}, u32[]{:S(2)}) collective-permute-start(bf16[48,768]{1,0:T(8,128)(2,1)S(1)} %bitcast.268), channel_id=1, source_target_pairs={{0,8},{8,0},{16,24},{24,16},{1,9},{9,1},{17,25},{25,17},{2,10},{10... | collective-permute-start | bytes 221192 | tf_op jit(solution)/shard_map/ppermute | solution.py:21
  62.0 22.3 %collective-permute-start.2 = (bf16[256,768]{1,0:T(8,128)(2,1)S(1)}, bf16[256,768]{1,0:T(8,128)(2,1)S(1)}, u32[]{:S(2)}, u32[]{:S(2)}) collective-permute-start(bf16[256,768]{1,0:T(8,128)(2,1)S(1)} %pad_maximum_fusion.4), channel_id=1, source_target_pairs={{0,8},{8,0},{16,24},{24,16},{1,9},{9,1},{17,25},{25,17},{2,10},{10... | collective-permute-start | bytes 1179656 | tf_op jit(solution)/shard_map/ppermute | solution.py:21
  84.2 71.7 %all-gather.6.cloned.1.call-start = ((), (), s32[]{:S(2)}) async-start(), calls=%async_computation | async-start | bytes 1474560 | tf_op jit(solution)/shard_map/all_gather | solution.py:352
  85.2 24.8 %collective-permute-start.6 = (bf16[512,384]{1,0:T(8,128)(2,1)S(1)}, bf16[512,384]{1,0:T(8,128)(2,1)S(1)}, u32[]{:S(2)}, u32[]{:S(2)}) collective-permute-start(bf16[512,384]{1,0:T(8,128)(2,1)S(1)} %slice.237), channel_id=1, source_target_pairs={{0,4},{4,0},{1,5},{5,1},{2,6},{6,2},{3,7},{7,3},{8,12},{12,8},{9,1... | collective-permute-start | bytes 1179656 | tf_op jit(solution)/shard_map/ppermute | solution.py:26
  112.8 12.6 %collective-permute-start.17 = (bf16[128,768]{1,0:T(8,128)(2,1)}, bf16[128,768]{1,0:T(8,128)(2,1)}, u32[]{:S(2)}, u32[]{:S(2)}) collective-permute-start(bf16[128,768]{1,0:T(8,128)(2,1)} %bitcast_convert_fusion.3), channel_id=1, source_target_pairs={{0,0},{1,8},{2,16},{3,24},{8,1},{9,9},{10,17},{11,25},{16,2},{17,1... | collective-permute-start | bytes 589832 | tf_op jit(solution)/shard_map/ppermute | solution.py:32
  163.8 40.3 %collective-permute-start.47 = (bf16[4,48,768]{2,1,0:T(8,128)(2,1)}, bf16[4,48,768]{2,1,0:T(8,128)(2,1)}, u32[]{:S(2)}, u32[]{:S(2)}) collective-permute-start(bf16[4,48,768]{2,1,0:T(8,128)(2,1)} %get-tuple-element.57), channel_id=1, source_target_pairs={{0,2},{1,3},{2,0},{3,1},{4,6},{5,7},{6,4},{7,5},{8,10},{9,11},{10,... | collective-permute-start | bytes 884744 | tf_op jit(solution)/shard_map/ppermute | solution.py:21
  164.8 39.4 %collective-permute-start.46 = (bf16[4,48,768]{2,1,0:T(8,128)(2,1)}, bf16[4,48,768]{2,1,0:T(8,128)(2,1)}, u32[]{:S(2)}, u32[]{:S(2)}) collective-permute-start(bf16[4,48,768]{2,1,0:T(8,128)(2,1)} %get-tuple-element.55), channel_id=1, source_target_pairs={{0,1},{1,0},{2,3},{3,2},{4,5},{5,4},{6,7},{7,6},{8,9},{9,8},{10,11... | collective-permute-start | bytes 884744 | tf_op jit(solution)/shard_map/ppermute | solution.py:21
  169.1 37.0 %collective-permute-start.55 = (bf16[192,768]{1,0:T(8,128)(2,1)}, bf16[192,768]{1,0:T(8,128)(2,1)}, u32[]{:S(2)}, u32[]{:S(2)}) collective-permute-start(bf16[192,768]{1,0:T(8,128)(2,1)} %get-tuple-element.53), channel_id=1, source_target_pairs={{0,3},{1,2},{2,1},{3,0},{4,7},{5,6},{6,5},{7,4},{8,11},{9,10},{10,... | collective-permute-start | bytes 884744 | tf_op jit(solution)/shard_map/ppermute | solution.py:21
  170.6 45.0 %collective-permute-start.54 = (bf16[192,768]{1,0:T(8,128)(2,1)}, bf16[192,768]{1,0:T(8,128)(2,1)}, u32[]{:S(2)}, u32[]{:S(2)}) collective-permute-start(bf16[192,768]{1,0:T(8,128)(2,1)} %get-tuple-element.54), channel_id=1, source_target_pairs={{0,2},{1,3},{2,0},{3,1},{4,6},{5,7},{6,4},{7,5},{8,10},{9,11},{10,... | collective-permute-start | bytes 884744 | tf_op jit(solution)/shard_map/ppermute | solution.py:21
  174.9 40.7 %collective-permute-start.53 = (bf16[192,768]{1,0:T(8,128)(2,1)}, bf16[192,768]{1,0:T(8,128)(2,1)}, u32[]{:S(2)}, u32[]{:S(2)}) collective-permute-start(bf16[192,768]{1,0:T(8,128)(2,1)} %get-tuple-element.52), channel_id=1, source_target_pairs={{0,1},{1,0},{2,3},{3,2},{4,5},{5,4},{6,7},{7,6},{8,9},{9,8},{10,11... | collective-permute-start | bytes 884744 | tf_op jit(solution)/shard_map/ppermute | solution.py:21
  204.1 18.2 %collective-permute-start.14 = (bf16[256,768]{1,0:T(8,128)(2,1)}, bf16[256,768]{1,0:T(8,128)(2,1)S(1)}, u32[]{:S(2)}, u32[]{:S(2)}) collective-permute-start(bf16[256,768]{1,0:T(8,128)(2,1)} %slice.345), channel_id=1, source_target_pairs={{0,8},{8,0},{16,24},{24,16},{1,9},{9,1},{17,25},{25,17},{2,10},{10... | collective-permute-start | bytes 1179656 | tf_op jit(solution)/shard_map/ppermute | solution.py:21
  204.2 18.7 %collective-permute-start.20 = (bf16[256,768]{1,0:T(8,128)(2,1)}, bf16[256,768]{1,0:T(8,128)(2,1)S(1)}, u32[]{:S(2)}, u32[]{:S(2)}) collective-permute-start(bf16[256,768]{1,0:T(8,128)(2,1)} %slice.344), channel_id=1, source_target_pairs={{0,8},{8,0},{16,24},{24,16},{1,9},{9,1},{17,25},{25,17},{2,10},{10... | collective-permute-start | bytes 1179656 | tf_op jit(solution)/shard_map/ppermute | solution.py:21
  206.1 18.6 %collective-permute-start.49 = (bf16[4,48,768]{2,1,0:T(8,128)(2,1)S(1)}, bf16[4,48,768]{2,1,0:T(8,128)(2,1)S(1)}, u32[]{:S(2)}, u32[]{:S(2)}) collective-permute-start(bf16[4,48,768]{2,1,0:T(8,128)(2,1)S(1)} %fusion.14), channel_id=1, source_target_pairs={{0,4},{4,0},{1,5},{5,1},{2,6},{6,2},{3,7},{7,3},{8,12},{12,8},{9,1... | collective-permute-start | bytes 884744 | tf_op jit(solution)/shard_map/ppermute | solution.py:26
  222.4 15.8 %collective-permute-start.15 = (bf16[128,768]{1,0:T(8,128)(2,1)S(1)}, bf16[128,768]{1,0:T(8,128)(2,1)S(1)}, u32[]{:S(2)}, u32[]{:S(2)}) collective-permute-start(bf16[128,768]{1,0:T(8,128)(2,1)S(1)} %slice.350), channel_id=1, source_target_pairs={{0,16},{8,24},{16,0},{24,8},{1,17},{9,25},{17,1},{25,9},{2,18},{10... | collective-permute-start | bytes 589832 | tf_op jit(solution)/shard_map/ppermute | solution.py:21
  225.5 21.8 %collective-permute-start.52 = (bf16[48,768]{1,0:T(8,128)(2,1)}, bf16[48,768]{1,0:T(8,128)(2,1)}, u32[]{:S(2)}, u32[]{:S(2)}) collective-permute-start(bf16[48,768]{1,0:T(8,128)(2,1)} %get-tuple-element.72), channel_id=1, source_target_pairs={{0,24},{8,16},{16,8},{24,0},{1,25},{9,17},{17,9},{25,1},{2,26},{10... | collective-permute-start | bytes 221192 | tf_op jit(solution)/shard_map/ppermute | solution.py:21
  225.5 21.8 %collective-permute-start.51 = (bf16[48,768]{1,0:T(8,128)(2,1)}, bf16[48,768]{1,0:T(8,128)(2,1)}, u32[]{:S(2)}, u32[]{:S(2)}) collective-permute-start(bf16[48,768]{1,0:T(8,128)(2,1)} %get-tuple-element.73), channel_id=1, source_target_pairs={{0,16},{8,24},{16,0},{24,8},{1,17},{9,25},{17,1},{25,9},{2,18},{10... | collective-permute-start | bytes 221192 | tf_op jit(solution)/shard_map/ppermute | solution.py:21
  229.2 18.1 %collective-permute-start.50 = (bf16[48,768]{1,0:T(8,128)(2,1)}, bf16[48,768]{1,0:T(8,128)(2,1)}, u32[]{:S(2)}, u32[]{:S(2)}) collective-permute-start(bf16[48,768]{1,0:T(8,128)(2,1)} %get-tuple-element.74), channel_id=1, source_target_pairs={{0,8},{8,0},{16,24},{24,16},{1,9},{9,1},{17,25},{25,17},{2,10},{10... | collective-permute-start | bytes 221192 | tf_op jit(solution)/shard_map/ppermute | solution.py:21
  239.3 12.8 %collective-permute-start.16 = (bf16[128,768]{1,0:T(8,128)(2,1)S(1)}, bf16[128,768]{1,0:T(8,128)(2,1)S(1)}, u32[]{:S(2)}, u32[]{:S(2)}) collective-permute-start(bf16[128,768]{1,0:T(8,128)(2,1)S(1)} %fusion.36), channel_id=1, source_target_pairs={{0,0},{1,8},{2,16},{3,24},{8,1},{9,9},{10,17},{11,25},{16,2},{17,1... | collective-permute-start | bytes 589832 | tf_op jit(solution)/shard_map/ppermute | solution.py:32
  254.2 12.7 %collective-permute-start.44 = (bf16[48,768]{1,0:T(8,128)(2,1)S(1)}, bf16[48,768]{1,0:T(8,128)(2,1)S(1)}, u32[]{:S(2)}, u32[]{:S(2)}) collective-permute-start(bf16[48,768]{1,0:T(8,128)(2,1)S(1)} %get-tuple-element.62), channel_id=1, source_target_pairs={{0,3},{1,2},{2,1},{3,0},{4,7},{5,6},{6,5},{7,4},{8,11},{9,10},{10,... | collective-permute-start | bytes 221192 | tf_op jit(solution)/shard_map/ppermute | solution.py:21
  254.6 12.4 %collective-permute-start.43 = (bf16[48,768]{1,0:T(8,128)(2,1)S(1)}, bf16[48,768]{1,0:T(8,128)(2,1)S(1)}, u32[]{:S(2)}, u32[]{:S(2)}) collective-permute-start(bf16[48,768]{1,0:T(8,128)(2,1)S(1)} %get-tuple-element.63), channel_id=1, source_target_pairs={{0,2},{1,3},{2,0},{3,1},{4,6},{5,7},{6,4},{7,5},{8,10},{9,11},{10,... | collective-permute-start | bytes 221192 | tf_op jit(solution)/shard_map/ppermute | solution.py:21
  260.8 16.8 %collective-permute-start.24 = (bf16[512,384]{1,0:T(8,128)(2,1)S(1)}, bf16[512,384]{1,0:T(8,128)(2,1)S(1)}, u32[]{:S(2)}, u32[]{:S(2)}) collective-permute-start(bf16[512,384]{1,0:T(8,128)(2,1)S(1)} %bitcast.243), channel_id=1, source_target_pairs={{0,4},{4,0},{1,5},{5,1},{2,6},{6,2},{3,7},{7,3},{8,12},{12,8},{9,1... | collective-permute-start | bytes 1179656 | tf_op jit(solution)/shard_map/ppermute | solution.py:26
  278.8 37.4 %collective-permute-start.25 = (bf16[256,768]{1,0:T(8,128)(2,1)S(1)}, bf16[256,768]{1,0:T(8,128)(2,1)S(1)}, u32[]{:S(2)}, u32[]{:S(2)}) collective-permute-start(bf16[256,768]{1,0:T(8,128)(2,1)S(1)} %slice.343), channel_id=1, source_target_pairs={{0,8},{8,0},{16,24},{24,16},{1,9},{9,1},{17,25},{25,17},{2,10},{10... | collective-permute-start | bytes 1179656 | tf_op jit(solution)/shard_map/ppermute | solution.py:21
  281.9 23.2 %collective-permute-start.36 = (bf16[4,48,576]{2,1,0:T(8,128)(2,1)S(1)}, bf16[4,48,576]{2,1,0:T(8,128)(2,1)}, u32[]{:S(2)}, u32[]{:S(2)}) collective-permute-start(bf16[4,48,576]{2,1,0:T(8,128)(2,1)S(1)} %get-tuple-element.60), channel_id=1, source_target_pairs={{0,2},{1,3},{2,0},{3,1},{4,6},{5,7},{6,4},{7,5},{8,10},{9,11},{10,... | collective-permute-start | bytes 663560 | tf_op jit(solution)/shard_map/ppermute | solution.py:21
  282.9 22.2 %collective-permute-start.35 = (bf16[4,48,576]{2,1,0:T(8,128)(2,1)S(1)}, bf16[4,48,576]{2,1,0:T(8,128)(2,1)}, u32[]{:S(2)}, u32[]{:S(2)}) collective-permute-start(bf16[4,48,576]{2,1,0:T(8,128)(2,1)S(1)} %get-tuple-element.58), channel_id=1, source_target_pairs={{0,1},{1,0},{2,3},{3,2},{4,5},{5,4},{6,7},{7,6},{8,9},{9,8},{10,11... | collective-permute-start | bytes 663560 | tf_op jit(solution)/shard_map/ppermute | solution.py:21
  336.8 15.1 %collective-permute-start.27 = (bf16[128,768]{1,0:T(8,128)(2,1)S(1)}, bf16[128,768]{1,0:T(8,128)(2,1)S(1)}, u32[]{:S(2)}, u32[]{:S(2)}) collective-permute-start(bf16[128,768]{1,0:T(8,128)(2,1)S(1)} %fusion.30), channel_id=1, source_target_pairs={{0,0},{1,8},{2,16},{3,24},{8,1},{9,9},{10,17},{11,25},{16,2},{17,1... | collective-permute-start | bytes 589832 | tf_op jit(solution)/shard_map/ppermute | solution.py:32
  (92 other events, 693.4 us)
Sparse Core Ops, SparseCore 0:
  84.3 31.3 all-gather.7
  117.9 38.0 all-gather.5

commit v2 on v1

v2 whole, which is shorter than its diff:
```python
import functools

import jax
import jax.numpy as jnp
from jax import lax
from jax.experimental import pallas as pl
from jax.experimental.pallas import tpu as pltpu
from jax.sharding import PartitionSpec as P

HEAD_DIM = 64
EPSILON = 1e-05
SCALE = HEAD_DIM ** (-0.5)
MASKED = -1e30
CHUNK = 64
GELU_SCALE = 0.7978845608
GELU_CUBE = 0.044715
LOW = jnp.bfloat16
WIDE = jnp.float32


def swap(value, axis, bit):
    count = lax.axis_size(axis)
    return lax.ppermute(value, axis, [(at, at ^ bit) for at in range(count)])


def shift(value, axis, by):
    count = lax.axis_size(axis)
    return lax.ppermute(value, axis, [(at, (at + by) % count) for at in range(count)])


def transpose_homes(value):
    side = lax.axis_size("dp")
    pairs = [(a * side + b, b * side + a) for a in range(side) for b in range(side)]
    return lax.ppermute(value, ("dp", "fsdp"), pairs)


def after(value, *others):
    return lax.optimization_barrier((value,) + others)[0]


def gather_pieces(block):
    pieces = [block]
    for slot in range(1, lax.axis_size("dp")):
        low_bit = slot & -slot
        pieces.append(swap(pieces[slot ^ low_bit], "dp", low_bit))
    return pieces


def send_pieces(sends, axis):
    return [swap(send, axis, slot) for slot, send in enumerate(sends, 1)]


def gather_direct(block, axis):
    return [block] + [swap(block, axis, slot) for slot in range(1, lax.axis_size(axis))]


def sum_all(kept, arrived):
    total = kept
    for piece in arrived:
        total = total + piece.astype(WIDE)
    return total


def sum_replicas(value):
    if lax.axis_size("ctx") == 2:
        return value.astype(WIDE) + shift(value, "ctx", 1).astype(WIDE)
    return jnp.sum(lax.all_gather(value, "ctx").astype(WIDE), axis=0)


def matmul_nt(left, right):
    return lax.dot_general(left, right, (((1,), (1,)), ((), ())), preferred_element_type=WIDE)


def matmul_nn(left, right):
    return lax.dot_general(left, right, (((1,), (0,)), ((), ())), preferred_element_type=WIDE)


def matmul_tn(left, right):
    return lax.dot_general(left, right, (((0,), (0,)), ((), ())), preferred_element_type=WIDE)


def visible_block(place_ref, start, block_rows, columns):
    slot = start // block_rows
    query_pos = place_ref[slot] * block_rows + start % block_rows
    query_pos = query_pos + lax.broadcasted_iota(jnp.int32, (CHUNK, columns), 0)
    lane = lax.broadcasted_iota(jnp.int32, (CHUNK, columns), 1)
    key_pos = lane
    for at in range(columns // block_rows):
        inside = (lane >= at * block_rows) & (lane < (at + 1) * block_rows)
        key_pos = jnp.where(inside, place_ref[at] * block_rows + lane - at * block_rows, key_pos)
    return key_pos <= query_pos


def columns_of(head):
    return slice(head * HEAD_DIM, (head + 1) * HEAD_DIM)


def own_forward(heads, block_rows, place_ref, kvq_ref, acc_ref, stat_ref, score, prob):
    width = heads * HEAD_DIM
    rows = kvq_ref.shape[0]
    for head in range(heads):
        query = kvq_ref[:, 2 * width + head * HEAD_DIM : 2 * width + (head + 1) * HEAD_DIM]
        score[...] = matmul_nt(query, kvq_ref[:, columns_of(head)])

        def chunk(step, carry):
            start = pl.multiple_of(step * CHUNK, CHUNK)
            seen = visible_block(place_ref, start, block_rows, rows)
            scores = jnp.where(seen, score[pl.ds(start, CHUNK), :] * SCALE, MASKED)
            highest = jnp.max(scores, axis=1, keepdims=True)
            weight = jnp.exp(scores - highest)
            stat_ref[pl.ds(start, CHUNK), head : head + 1] = highest
            stat_ref[pl.ds(start, CHUNK), heads + head : heads + head + 1] = jnp.sum(
                weight, axis=1, keepdims=True
            )
            prob[pl.ds(start, CHUNK), :] = weight.astype(LOW)
            return carry

        lax.fori_loop(0, rows // CHUNK, chunk, 0)
        value = kvq_ref[:, width + head * HEAD_DIM : width + (head + 1) * HEAD_DIM]
        acc_ref[:, columns_of(head)] = matmul_nn(prob[...], value)


def earlier_forward(
    heads, slots, place_ref, kvq_ref, kv_ref, acc_in, stat_in, acc_ref, low_ref, stat_ref, score,
    prob, fade
):
    width = heads * HEAD_DIM
    rows = kvq_ref.shape[0]
    acc_ref[...] = acc_in[...]
    stat_ref[...] = stat_in[...]
    for piece in range(kv_ref.shape[0]):

        @pl.when(place_ref[slots] > piece)
        def _visit(piece=piece):
            for head in range(heads):
                query = kvq_ref[:, 2 * width + head * HEAD_DIM : 2 * width + (head + 1) * HEAD_DIM]
                score[...] = matmul_nt(query, kv_ref[piece, :, columns_of(head)])

                def chunk(step, carry):
                    here = pl.ds(pl.multiple_of(step * CHUNK, CHUNK), CHUNK)
                    scores = score[here, :] * SCALE
                    old = stat_ref[here, head : head + 1]
                    highest = jnp.maximum(old, jnp.max(scores, axis=1, keepdims=True))
                    weight = jnp.exp(scores - highest)
                    fading = jnp.exp(old - highest)
                    stat_ref[here, head : head + 1] = highest
                    total = stat_ref[here, heads + head : heads + head + 1]
                    stat_ref[here, heads + head : heads + head + 1] = total * fading + jnp.sum(
                        weight, axis=1, keepdims=True
                    )
                    fade[here, :] = jnp.broadcast_to(fading, (CHUNK, HEAD_DIM))
                    prob[here, :] = weight.astype(LOW)
                    return carry

                lax.fori_loop(0, rows // CHUNK, chunk, 0)
                value = kv_ref[piece, :, width + head * HEAD_DIM : width + (head + 1) * HEAD_DIM]
                acc_ref[:, columns_of(head)] = acc_ref[:, columns_of(head)] * fade[
                    ...
                ] + matmul_nn(prob[...], value)

    for head in range(heads):
        total = stat_ref[:, heads + head : heads + head + 1]
        context = acc_ref[:, columns_of(head)] / total
        acc_ref[:, columns_of(head)] = context
        low_ref[:, columns_of(head)] = context.astype(LOW)
        stat_ref[:, head : head + 1] = stat_ref[:, head : head + 1] + jnp.log(total)


def score_grads(here, seen, head, total, delta, score, dots, prob, grad):
    scores = score[here, :] * SCALE
    weight = jnp.exp(scores - total)
    if seen is not None:
        weight = jnp.where(seen, weight, 0.0)
    prob[here, :] = weight.astype(LOW)
    grad[here, :] = (weight * (dots[here, :] - delta) * SCALE).astype(LOW)


def delta_of(here, head, context_ref, ctx_grad_ref):
    product = context_ref[here, columns_of(head)] * ctx_grad_ref[here, columns_of(head)].astype(WIDE)
    return jnp.sum(product, axis=1, keepdims=True)


def earlier_backward(
    heads, slots, place_ref, kvq_ref, kv_ref, ctx_grad_ref, context_ref, stat_ref, query_grad_ref,
    kv_grad_ref, score, dots, prob, grad
):
    width = heads * HEAD_DIM
    rows = kvq_ref.shape[0]
    query_grad_ref[...] = jnp.zeros_like(query_grad_ref)
    for piece in range(kv_ref.shape[0]):

        @pl.when(place_ref[slots] <= piece)
        def _skip(piece=piece):
            kv_grad_ref[piece] = jnp.zeros(kv_grad_ref.shape[1:], kv_grad_ref.dtype)

        @pl.when(place_ref[slots] > piece)
        def _visit(piece=piece):
            for head in range(heads):
                query = kvq_ref[:, 2 * width + head * HEAD_DIM : 2 * width + (head + 1) * HEAD_DIM]
                value_at = slice(width + head * HEAD_DIM, width + (head + 1) * HEAD_DIM)
                key = kv_ref[piece, :, columns_of(head)]
                out_grad = ctx_grad_ref[:, columns_of(head)]
                score[...] = matmul_nt(query, key)
                dots[...] = matmul_nt(out_grad, kv_ref[piece, :, value_at])

                def chunk(step, carry):
                    here = pl.ds(pl.multiple_of(step * CHUNK, CHUNK), CHUNK)
                    total = stat_ref[here, head : head + 1]
                    delta = delta_of(here, head, context_ref, ctx_grad_ref)
                    score_grads(here, None, head, total, delta, score, dots, prob, grad)
                    return carry

                lax.fori_loop(0, rows // CHUNK, chunk, 0)
                kv_grad_ref[piece, :, columns_of(head)] = matmul_tn(grad[...], query).astype(LOW)
                kv_grad_ref[piece, :, value_at] = matmul_tn(prob[...], out_grad).astype(LOW)
                query_grad_ref[:, columns_of(head)] += matmul_nn(grad[...], key)


def own_backward(
    heads, block_rows, place_ref, kvq_ref, ctx_grad_ref, context_ref, stat_ref, query_grad_in,
    grad_ref, score, dots, prob, grad
):
    width = heads * HEAD_DIM
    rows = kvq_ref.shape[0]
    for head in range(heads):
        query_at = slice(2 * width + head * HEAD_DIM, 2 * width + (head + 1) * HEAD_DIM)
        value_at = slice(width + head * HEAD_DIM, width + (head + 1) * HEAD_DIM)
        query = kvq_ref[:, query_at]
        key = kvq_ref[:, columns_of(head)]
        out_grad = ctx_grad_ref[:, columns_of(head)]
        score[...] = matmul_nt(query, key)
        dots[...] = matmul_nt(out_grad, kvq_ref[:, value_at])

        def chunk(step, carry):
            start = pl.multiple_of(step * CHUNK, CHUNK)
            here = pl.ds(start, CHUNK)
            seen = visible_block(place_ref, start, block_rows, rows)
            total = stat_ref[here, head : head + 1]
            delta = delta_of(here, head, context_ref, ctx_grad_ref)
            score_grads(here, seen, head, total, delta, score, dots, prob, grad)
            return carry

        lax.fori_loop(0, rows // CHUNK, chunk, 0)
        grad_ref[:, columns_of(head)] = matmul_tn(grad[...], query)
        grad_ref[:, value_at] = matmul_tn(prob[...], out_grad)
        grad_ref[:, query_at] = query_grad_in[:, columns_of(head)] + matmul_nn(grad[...], key)


def normalize(values):
    centered = values - jnp.mean(values, axis=-1, keepdims=True)
    spread = jnp.mean(centered * centered, axis=-1, keepdims=True)
    inverse = lax.rsqrt(spread + EPSILON)
    return centered * inverse, inverse


def normalize_back(grad, gain, hat, inverse):
    scaled = grad * gain
    mean_scaled = jnp.mean(scaled, axis=-1, keepdims=True)
    mean_product = jnp.mean(scaled * hat, axis=-1, keepdims=True)
    part = inverse * (scaled - mean_scaled - hat * mean_product)
    gain_grad = jnp.sum(grad * hat, axis=0, keepdims=True)
    return part, gain_grad, jnp.sum(grad, axis=0, keepdims=True)


def take(refs, *counts):
    groups, at = [], 0
    for count in counts:
        if count is None:
            groups.append(refs[at])
            at += 1
        else:
            groups.append(refs[at : at + count])
            at += count
    return groups


def place_blocks(meta_ref, parts, depth, pieces, out_ref):
    rows = pieces[0].shape[1]
    for deep in range(depth):
        member = meta_ref[parts + 1] ^ deep
        for slot in range(parts):
            start = pl.multiple_of((meta_ref[slot] * depth + member) * rows, 16)
            out_ref[pl.ds(start, rows), :] = pieces[deep][slot]


def place_shards(meta_ref, parts, pieces, out_ref):
    rows = pieces[0].shape[0]
    for deep, piece in enumerate(pieces):
        start = pl.multiple_of((meta_ref[parts + 1] ^ deep) * rows, 16)
        out_ref[pl.ds(start, rows), :] = piece[...]


def stack_rows(pieces, out_ref):
    rows = pieces[0].shape[0]
    for slot, piece in enumerate(pieces):
        out_ref[slot * rows : (slot + 1) * rows, :] = piece[...]


def emit_rows(partial, keep_ref, send_refs):
    rows = keep_ref.shape[0]
    keep_ref[...] = partial[:rows]
    for slot, send in enumerate(send_refs, 1):
        send[...] = partial[slot * rows : (slot + 1) * rows].astype(LOW)


def emit_blocks(meta_ref, parts, depth, whole_ref, keep_ref, send_refs):
    rows = keep_ref.shape[1]
    for deep in range(depth):
        member = meta_ref[parts + 1] ^ deep
        for slot in range(parts):
            start = pl.multiple_of((meta_ref[slot] * depth + member) * rows, 16)
            block = whole_ref[pl.ds(start, rows), :]
            if deep:
                send_refs[deep - 1][slot] = block.astype(LOW)
            else:
                keep_ref[slot] = block


def emit_shards(meta_ref, parts, whole_ref, keep_ref, send_refs):
    rows = keep_ref.shape[0]
    for deep in range(len(send_refs) + 1):
        start = pl.multiple_of((meta_ref[parts + 1] ^ deep) * rows, 16)
        block = whole_ref[pl.ds(start, rows), :]
        if deep:
            send_refs[deep - 1][...] = block.astype(LOW)
        else:
            keep_ref[...] = block


def split_kernel(parts, width, meta_ref, qkv_ref, up_ref, *outs):
    kvq_outs, up_outs = take(outs, parts, parts)
    model = parts * width
    part = up_ref.shape[1] // parts
    for case in range(parts):

        @pl.when(meta_ref[0] == case)
        def _case(case=case):
            for slot in range(parts):
                owner = case ^ slot
                for at, first in enumerate((model, 2 * model, 0)):
                    start = first + owner * width
                    kvq_outs[slot][:, at * width : (at + 1) * width] = qkv_ref[
                        :, start : start + width
                    ].astype(LOW)
                up_outs[slot][...] = up_ref[:, owner * part : (owner + 1) * part].astype(LOW)


def join_qkv_kernel(parts, width, meta_ref, *refs):
    pieces, out_ref = refs[:parts], refs[parts]
    model = parts * width
    for case in range(parts):

        @pl.when(meta_ref[0] == case)
        def _case(case=case):
            for slot in range(parts):
                owner = case ^ slot
                for at, first in enumerate((model, 2 * model, 0)):
                    start = first + owner * width
                    out_ref[:, start : start + width] = pieces[slot][
                        :, at * width : (at + 1) * width
                    ].astype(WIDE)


def join_up_kernel(parts, meta_ref, *refs):
    pieces, out_ref = refs[:parts], refs[parts]
    part = pieces[0].shape[1]
    for slot in range(parts):
        start = pl.multiple_of(meta_ref[slot] * part, 128)
        out_ref[:, pl.ds(start, part)] = pieces[slot][...].astype(WIDE)


def first_norm_kernel(meta_ref, tokens_ref, vectors_ref, out_ref):
    hat, _ = normalize(tokens_ref[...].astype(WIDE))
    out_ref[...] = (hat * vectors_ref[0:1, :] + vectors_ref[1:2, :]).astype(LOW)


def project_kernel(parts, depth, meta_ref, *refs):
    norm, weight, vectors_ref, kvq_ref, kv_ref, matrix_ref, norm_ref = take(
        refs, parts, depth, None, None, None, None, None
    )
    columns = kvq_ref.shape[1]
    place_blocks(meta_ref, parts, depth, weight, matrix_ref)
    stack_rows(norm, norm_ref)
    low = (matmul_nn(norm_ref[...], matrix_ref[...]) + vectors_ref[6:7, :columns]).astype(LOW)
    kvq_ref[...] = low
    kv_ref[...] = low[:, : kv_ref.shape[1]]


def context_kernel(parts, depth, heads, meta_ref, *refs):
    (
        kvq, kv, acc_in, stat_in, weight, context, low, stat, matrix, keep, sends, score, prob, fade
    ) = take(
        refs, None, None, None, None, depth, None, None, None, None, None, parts - 1, None, None,
        None,
    )
    place_shards(meta_ref, parts, weight, matrix)
    earlier_forward(
        heads, parts, meta_ref, kvq, kv, acc_in, stat_in, context, low, stat, score, prob, fade
    )
    emit_rows(matmul_nn(low[...], matrix[...]), keep, sends)


def second_norm_kernel(parts, meta_ref, *refs):
    keep, arrived, tokens, vectors, out, attended_ref = take(
        refs, None, parts - 1, None, None, None, None
    )
    attended = sum_all(keep[...], [piece[...] for piece in arrived]) + vectors[4:5, :]
    attended_ref[...] = attended
    hat, _ = normalize(tokens[...].astype(WIDE) + attended)
    out[...] = (hat * vectors[2:3, :] + vectors[3:4, :]).astype(LOW)


def feed_kernel(parts, depth, meta_ref, *refs):
    (
        norm, branch, up, down, vectors, keep, sends, hidden, inner_grad, norm_all, branch_all,
        down_all, up_bias, up_all, inner, grad,
    ) = take(
        refs, parts, parts, depth, depth, None, None, parts - 1, None, None, None, None, None,
        None, None, None, None,
    )
    place_blocks(meta_ref, parts, depth, up, up_all)
    place_shards(meta_ref, parts, down, down_all)
    stack_rows(norm, norm_all)
    stack_rows(branch, branch_all)
    inner[...] = matmul_nn(norm_all[...], up_all[...])
    grad[...] = matmul_nt(branch_all[...], down_all[...])
    up_bias[...] = jnp.zeros_like(up_bias)

    def chunk(step, carry):
        here = pl.ds(pl.multiple_of(step * CHUNK, CHUNK), CHUNK)
        value = inner[here, :] + vectors[7:8, :]
        square = value * value
        bent = jnp.tanh(GELU_SCALE * (value + GELU_CUBE * square * value))
        hidden[here, :] = (0.5 * value * (1.0 + bent)).astype(LOW)
        slope = 0.5 * (1.0 + bent) + 0.5 * value * (1.0 - bent * bent) * GELU_SCALE * (
            1.0 + 3.0 * GELU_CUBE * square
        )
        low = (grad[here, :] * slope).astype(LOW)
        inner_grad[here, :] = low
        up_bias[...] += jnp.sum(low.astype(WIDE), axis=0, keepdims=True)
        return carry

    lax.fori_loop(0, inner.shape[0] // CHUNK, chunk, 0)
    emit_rows(matmul_nt(inner_grad[...], up_all[...]), keep, sends)


def feed_grad_kernel(parts, depth, meta_ref, *refs):
    (
        hidden, inner_grad, norm_all, branch_all, down_all, down_keep, down_sends, up_keep,
        up_sends, fed_keep, fed_sends, whole,
    ) = take(
        refs, None, None, None, None, None, None, depth - 1, None, depth - 1, None, parts - 1, None
    )
    whole[...] = matmul_tn(hidden[...], branch_all[...])
    emit_shards(meta_ref, parts, whole, down_keep, down_sends)
    whole[...] = matmul_tn(norm_all[...], inner_grad[...])
    emit_blocks(meta_ref, parts, depth, whole, up_keep, up_sends)
    emit_rows(matmul_nn(hidden[...], down_all[...]), fed_keep, fed_sends)


def second_norm_grad_kernel(parts, meta_ref, *refs):
    keep, arrived, tokens, attended, branch, vectors, attn_grad, mixed_part, sums = take(
        refs, None, parts - 1, None, None, None, None, None, None, None
    )
    grad = sum_all(keep[...], [piece[...] for piece in arrived])
    hat, inverse = normalize(tokens[...].astype(WIDE) + attended[...])
    part, gain_grad, bias_grad = normalize_back(grad, vectors[2:3, :], hat, inverse)
    mixed_part[...] = part
    branch_rows = branch[...].astype(WIDE)
    low = (branch_rows + part).astype(LOW)
    attn_grad[...] = low
    sums[...] = jnp.zeros_like(sums)
    sums[2:3, :] = gain_grad
    sums[3:4, :] = bias_grad
    sums[4:5, :] = jnp.sum(low.astype(WIDE), axis=0, keepdims=True)
    sums[5:6, :] = jnp.sum(branch_rows, axis=0, keepdims=True)


def context_grad_kernel(parts, heads, meta_ref, *refs):
    (
        attn, matrix, kvq, kv, context, stat, ctx_grad, attn_all, query_grad, kv_grad, score, dots,
        prob, grad,
    ) = take(refs, parts, *([None] * 13))
    stack_rows(attn, attn_all)
    ctx_grad[...] = matmul_nt(attn_all[...], matrix[...]).astype(LOW)
    earlier_backward(
        heads, parts, meta_ref, kvq, kv, ctx_grad, context, stat, query_grad, kv_grad, score, dots,
        prob, grad,
    )


def own_grad_kernel(parts, depth, heads, rows, meta_ref, *refs):
    (
        kvq, ctx_grad, context, stat, query_grad, low, attn_all, kvq_grad, out_keep, out_sends,
        whole, score, dots, prob, grad,
    ) = take(refs, *([None] * 9), depth - 1, *([None] * 5))
    own_backward(
        heads, rows, meta_ref, kvq, ctx_grad, context, stat, query_grad, kvq_grad, score, dots,
        prob, grad,
    )
    whole[...] = matmul_tn(low[...], attn_all[...])
    emit_shards(meta_ref, parts, whole, out_keep, out_sends)


def projection_back_kernel(parts, meta_ref, *refs):
    own, arrived, matrix, kvq_grad, keep, sends, bias = take(
        refs, None, None, None, None, None, parts - 1, None
    )
    kv_width = arrived.shape[2]
    total = own[:, :kv_width]
    for piece in range(arrived.shape[0]):
        total = total + arrived[piece].astype(WIDE)
    kvq_grad[:, :kv_width] = total.astype(LOW)
    kvq_grad[:, kv_width:] = own[:, kv_width:].astype(LOW)
    emit_rows(matmul_nt(kvq_grad[...], matrix[...]), keep, sends)
    bias[...] = jnp.sum(kvq_grad[...].astype(WIDE), axis=0, keepdims=True)


def projection_grad_kernel(parts, depth, meta_ref, *refs):
    norm, kvq_grad, keep, sends, whole = take(refs, None, None, None, depth - 1, None)
    whole[...] = matmul_tn(norm[...], kvq_grad[...])
    emit_blocks(meta_ref, parts, depth, whole, keep, sends)


def first_norm_grad_kernel(parts, meta_ref, *refs):
    keep, arrived, tokens, vectors, mixed_part, sums_in, kvq_bias, up_bias, out, sums = take(
        refs, None, parts - 1, *([None] * 8)
    )
    grad = sum_all(keep[...], [piece[...] for piece in arrived])
    hat, inverse = normalize(tokens[...].astype(WIDE))
    part, gain_grad, bias_grad = normalize_back(grad, vectors[0:1, :], hat, inverse)
    out[...] = (mixed_part[...] + part).astype(LOW)
    sums[...] = sums_in[...]
    sums[0:1, :] = gain_grad
    sums[1:2, :] = bias_grad
    sums[6:7, : kvq_bias.shape[1]] = kvq_bias[...]
    sums[7:8, :] = up_bias[...]


def local_call(kernel, operands, results, scratch=(), flops=0):
    smem = pl.BlockSpec(memory_space=pltpu.SMEM)
    vmem = pl.BlockSpec(memory_space=pltpu.VMEM)
    moved = sum(each.size * each.dtype.itemsize for each in tuple(operands) + tuple(results))
    return pl.pallas_call(
        kernel,
        out_shape=tuple(results),
        in_specs=[smem] + [vmem] * (len(operands) - 1),
        out_specs=tuple([vmem] * len(results)),
        scratch_shapes=list(scratch),
        compiler_params=pltpu.CompilerParams(vmem_limit_bytes=48 * 1024 * 1024),
        cost_estimate=pl.CostEstimate(flops=flops, bytes_accessed=moved, transcendentals=0),
    )(*operands)


def low_like(*shape):
    return jax.ShapeDtypeStruct(shape, LOW)


def wide_like(*shape):
    return jax.ShapeDtypeStruct(shape, WIDE)


def local(
    tokens, cotangent, ln1_gain, ln1_bias, qkv_weight, q_bias, v_bias, out_weight, out_bias,
    ln2_gain, ln2_bias, fc1_weight, fc1_bias, fc2_weight, fc2_bias,
):
    parts = lax.axis_size("dp")
    depth = lax.axis_size("fsdp")
    contexts = lax.axis_size("ctx")
    assert parts == depth
    mine = lax.axis_index("dp")
    deep = lax.axis_index("fsdp")
    rows, model = tokens.shape[1:]
    shard = ln1_gain.shape[0]
    heads = model // HEAD_DIM // parts
    width = heads * HEAD_DIM
    hidden_shard = fc1_bias.shape[0]
    hidden_part = hidden_shard * depth
    group = parts * rows
    meta = jnp.stack(
        [mine ^ slot for slot in range(parts)] + [lax.axis_index("ctx"), deep]
    ).astype(jnp.int32)

    token_rows = transpose_homes(tokens[0].astype(LOW))

    split = local_call(
        functools.partial(split_kernel, parts, width),
        (meta, qkv_weight, fc1_weight),
        [low_like(shard, 3 * width)] * parts + [low_like(shard, hidden_part)] * parts,
    )
    kvq_split, up_split = split[:parts], split[parts:]
    kvq_rows = jnp.stack([kvq_split[0]] + send_pieces(kvq_split[1:], "dp"))
    kvq_pieces = gather_direct(kvq_rows, "fsdp")

    low_vectors = [
        each.astype(LOW).astype(WIDE)
        for each in (ln1_gain, ln1_bias, ln2_gain, ln2_bias, out_bias, fc2_bias)
    ]
    vectors = jnp.zeros((8, model), WIDE)
    vectors = lax.dynamic_update_slice(
        vectors, jnp.stack(low_vectors), (0, (mine * depth + deep) * shard)
    )
    for row, first, part in (
        (6, width, v_bias), (6, 2 * width, q_bias), (7, 0, fc1_bias),
    ):
        part = part.astype(LOW).astype(WIDE)[None]
        vectors = lax.dynamic_update_slice(vectors, part, (row, first + deep * part.shape[1]))
    vectors = sum_all(vectors, gather_direct(vectors, "fsdp")[1:])
    everywhere = sum_all(vectors, gather_direct(vectors, "dp")[1:])
    vectors = jnp.where(jnp.arange(8)[:, None] < 6, everywhere, vectors)

    up_rows = jnp.stack([up_split[0]] + send_pieces(up_split[1:], "dp"))
    out_pieces = gather_direct(after(out_weight.astype(LOW), kvq_pieces[-1]), "fsdp")
    up_pieces = gather_direct(after(up_rows, kvq_pieces[-1]), "fsdp")
    down_pieces = gather_direct(after(fc2_weight.astype(LOW), kvq_pieces[-1]), "fsdp")

    (norm1,) = local_call(
        first_norm_kernel, (meta, token_rows, vectors), [low_like(rows, model)]
    )
    norm1_pieces = gather_pieces(norm1)
    kvq, kv, kvq_matrix, norm1_all = local_call(
        functools.partial(project_kernel, parts, depth),
        (meta, *norm1_pieces, *kvq_pieces, vectors),
        [
            low_like(group, 3 * width),
            low_like(group, 2 * width),
            low_like(model, 3 * width),
            low_like(group, model),
        ],
        flops=2 * group * model * 3 * width,
    )
    kv_earlier = jnp.stack([shift(kv, "ctx", by) for by in range(1, contexts)])

    grad_rows = transpose_homes(after(cotangent[0].astype(LOW), token_rows))
    branch_pieces = gather_pieces(after(grad_rows, norm1_pieces[-1]))

    score_flops = 2 * group * group * width
    wide_square = pltpu.VMEM((group, group), WIDE)
    low_square = pltpu.VMEM((group, group), LOW)
    acc, stat = local_call(
        functools.partial(own_forward, heads, rows),
        (meta, kvq),
        [wide_like(group, width), wide_like(group, 128)],
        [wide_square, low_square],
        flops=2 * score_flops,
    )
    context, context_low, stat, out_matrix, attended_keep, *attended_sends = local_call(
        functools.partial(context_kernel, parts, depth, heads),
        (meta, kvq, kv_earlier, acc, stat, *out_pieces),
        [
            wide_like(group, width),
            low_like(group, width),
            wide_like(group, 128),
            low_like(width, model),
            wide_like(rows, model),
        ]
        + [low_like(rows, model)] * (parts - 1),
        [wide_square, low_square, pltpu.VMEM((group, HEAD_DIM), WIDE)],
        flops=2 * score_flops,
    )
    arrived = send_pieces(attended_sends, "dp")
    norm2, attended = local_call(
        functools.partial(second_norm_kernel, parts),
        (meta, attended_keep, *arrived, token_rows, vectors),
        [low_like(rows, model), wide_like(rows, model)],
    )

    norm2_pieces = gather_pieces(norm2)
    norm2_keep, *rest = local_call(
        functools.partial(feed_kernel, parts, depth),
        (meta, *norm2_pieces, *branch_pieces, *up_pieces, *down_pieces, vectors),
        [wide_like(rows, model)]
        + [low_like(rows, model)] * (parts - 1)
        + [low_like(group, hidden_part)] * 2
        + [low_like(group, model)] * 2
        + [low_like(hidden_part, model), wide_like(1, hidden_part)],
        [
            pltpu.VMEM((model, hidden_part), LOW),
            pltpu.VMEM((group, hidden_part), WIDE),
            pltpu.VMEM((group, hidden_part), WIDE),
        ],
        flops=6 * group * model * hidden_part,
    )
    norm2_sends = rest[: parts - 1]
    hidden, inner_grad, norm2_all, branch_all, down_matrix, up_bias = rest[parts - 1 :]
    norm2_arrived = send_pieces(norm2_sends, "dp")
    feed_grads = local_call(
        functools.partial(feed_grad_kernel, parts, depth),
        (meta, hidden, inner_grad, norm2_all, branch_all, down_matrix),
        [wide_like(hidden_shard, model)]
        + [low_like(hidden_shard, model)] * (depth - 1)
        + [wide_like(parts, shard, hidden_part)]
        + [low_like(parts, shard, hidden_part)] * (depth - 1)
        + [wide_like(rows, model)]
        + [low_like(rows, model)] * (parts - 1),
        [pltpu.VMEM((max(model, hidden_part), max(model, hidden_part)), WIDE)],
        flops=6 * group * model * hidden_part,
    )
    down_keep, down_sends, up_keep, up_sends, fed_keep, fed_sends = take(
        feed_grads, None, depth - 1, None, depth - 1, None, parts - 1
    )
    attn_grad, mixed_part, sums = local_call(
        functools.partial(second_norm_grad_kernel, parts),
        (meta, norm2_keep, *norm2_arrived, token_rows, attended, grad_rows, vectors),
        [low_like(rows, model), wide_like(rows, model), wide_like(8, model)],
    )
    attn_pieces = gather_pieces(attn_grad)
    down_arrived = send_pieces(down_sends, "fsdp")
    up_arrived = send_pieces(up_sends, "fsdp")
    fed_arrived = send_pieces(
        lax.optimization_barrier((*fed_sends, attn_pieces[-1]))[: parts - 1], "dp"
    )

    ctx_grad, attn_all, query_grad, kv_grad = local_call(
        functools.partial(context_grad_kernel, parts, heads),
        (meta, *attn_pieces, out_matrix, kvq, kv_earlier, context, stat),
        [
            low_like(group, width),
            low_like(group, model),
            wide_like(group, width),
            low_like(*kv_earlier.shape),
        ],
        [wide_square, wide_square, low_square, low_square],
        flops=5 * score_flops,
    )
    kv_arrived = jnp.stack(
        [shift(kv_grad[by - 1], "ctx", -by) for by in range(1, contexts)]
    )
    kvq_own, out_keep, *out_sends = local_call(
        functools.partial(own_grad_kernel, parts, depth, heads, rows),
        (meta, kvq, ctx_grad, context, stat, query_grad, context_low, attn_all),
        [wide_like(group, 3 * width), wide_like(shard, model)]
        + [low_like(shard, model)] * (depth - 1),
        [
            pltpu.VMEM((width, model), WIDE), wide_square, wide_square, low_square, low_square,
        ],
        flops=5 * score_flops,
    )
    out_arrived = send_pieces(out_sends, "fsdp")
    kvq_grad, norm1_keep, *rest = local_call(
        functools.partial(projection_back_kernel, parts),
        (meta, kvq_own, kv_arrived, kvq_matrix),
        [low_like(group, 3 * width), wide_like(rows, model)]
        + [low_like(rows, model)] * (parts - 1)
        + [wide_like(1, 3 * width)],
        flops=2 * group * model * 3 * width,
    )
    kvq_bias = rest[-1]
    norm1_arrived = send_pieces(rest[:-1], "dp")
    kvq_keep, *kvq_sends = local_call(
        functools.partial(projection_grad_kernel, parts, depth),
        (meta, norm1_all, kvq_grad),
        [wide_like(parts, shard, 3 * width)]
        + [low_like(parts, shard, 3 * width)] * (depth - 1),
        [pltpu.VMEM((model, 3 * width), WIDE)],
        flops=2 * group * model * 3 * width,
    )
    kvq_arrived = send_pieces(kvq_sends, "fsdp")
    input_part, sums = local_call(
        functools.partial(first_norm_grad_kernel, parts),
        (
            meta, norm1_keep, *norm1_arrived, token_rows, vectors, mixed_part, sums, kvq_bias,
            up_bias,
        ),
        [low_like(rows, model), wide_like(8, model)],
    )

    delta = sum_all(fed_keep, fed_arrived) + vectors[5:6] + attended
    delta = after(delta.astype(LOW), kvq_own)
    output = tokens[0] + transpose_homes(delta).astype(WIDE)
    input_grad = cotangent[0] + transpose_homes(input_part).astype(WIDE)

    def owner_sum(keep, pieces, *later):
        low = sum_all(keep, pieces).astype(LOW)
        return sum_replicas(after(low, *later) if later else low)

    down_total = owner_sum(down_keep, down_arrived, kv_arrived)
    up_total = owner_sum(up_keep, up_arrived, kv_arrived).astype(LOW)
    out_total = owner_sum(out_keep, out_arrived, kv_arrived)
    up_sends = [after(up_total[slot], norm1_arrived[-1]) for slot in range(1, parts)]
    (up_total,) = local_call(
        functools.partial(join_up_kernel, parts),
        (meta, up_total[0], *send_pieces(up_sends, "dp")),
        [wide_like(shard, parts * hidden_part)],
    )
    kvq_total = owner_sum(kvq_keep, kvq_arrived).astype(LOW)
    (qkv_total,) = local_call(
        functools.partial(join_qkv_kernel, parts, width),
        (meta, kvq_total[0], *send_pieces([kvq_total[s] for s in range(1, parts)], "dp")),
        [wide_like(shard, 3 * model)],
    )
    sums = sum_all(sums, gather_direct(sums, "fsdp")[1:])
    sums = sum_replicas(sums)
    everywhere = sum_all(sums, gather_direct(sums, "dp")[1:])
    owned = lax.dynamic_slice(everywhere, (0, (mine * depth + deep) * shard), (6, shard))
    value_bias = lax.dynamic_slice(sums, (6, width + deep * shard), (1, shard))[0]
    query_bias = lax.dynamic_slice(sums, (6, 2 * width + deep * shard), (1, shard))[0]
    inner_bias = lax.dynamic_slice(sums, (7, deep * hidden_shard), (1, hidden_shard))[0]

    return (
        output[None],
        input_grad[None],
        owned[0],
        owned[1],
        qkv_total,
        query_bias,
        value_bias,
        out_total,
        owned[4],
        owned[2],
        owned[3],
        up_total,
        inner_bias,
        down_total,
        owned[5],
    )


def solution(mesh):
    rows = P("dp", ("ctx", "fsdp"), None)
    vector = P(("dp", "fsdp"))
    matrix = P(("dp", "fsdp"), None)
    parameters = (
        vector, vector, matrix, vector, vector, matrix, vector, vector, vector, matrix, vector,
        matrix, vector,
    )
    return jax.shard_map(
        local,
        mesh=mesh,
        in_specs=(rows, rows) + parameters,
        out_specs=(rows, rows) + parameters,
        check_vma=False,
    )
```

time: 361 us -> 308 us (0.85)
  the two profiles are of different devices: /device:TPU:2 before, /device:TPU:0 now
where the time goes in v2:
time: 308 us
  waiting for transfers between devices  134 us (44%)
  starting transfers between devices  119 us (39%)
  Pallas kernels  37.9 us (12%)
  other arithmetic  9.28 us (3%)
  local copies, waits for them, and re-layouts  6.3 us (2%)
    ppermute x72, waiting for transfers between devices, swap(): return lax.ppermute(value, axis, [(at, at ^ bit) for at in range(count)])  124 us
    ppermute x72, starting transfers between devices, swap(): return lax.ppermute(value, axis, [(at, at ^ bit) for at in range(count)])  97.3 us
    pallas_call x16, Pallas kernels, local_call(): pl.pallas_call(kernel, out_shape=tuple(results), in_specs=[smem] + [vmem]...  37.9 us
    ppermute x7, starting transfers between devices, shift(): lax.ppermute(value, axis, [(at, (at + by) % count) for at in range(count)])  19.4 us
    ppermute x7, waiting for transfers between devices, shift(): lax.ppermute(value, axis, [(at, (at + by) % count) for at in range(count)])  9.47 us
  transfers between devices with their start and end apart: 83, of which 31 were waited for; matrix products, arithmetic and copies ran while one was open for 2% of the time, Pallas kernels for 10%

profile of v2, /device:TPU:0, one launch (start us, length us, event | category | flops | bytes accessed | tf_op | source)
XLA Modules:
  0.0 307.6 jit_solution(5174959416702038555)
XLA Ops:
  5.9 5.5 %collective-permute-start.3 = (f32[8,768]{1,0:T(8,128)S(1)}, f32[8,768]{1,0:T(8,128)S(1)}, u32[]{:S(2)}, u32[]{:S(2)}) collective-permute-start(f32[8,768]{1,0:T(8,128)S(1)} %dynamic_update_slice.15), channel_id=1, source_target_pairs={{0,3},{1,2},{2,1},{3,0},{4,7},{5,6},{6,5},{7,4},{8,11},{9,10},{10,... | collective-permute-start | bytes 73736 | tf_op jit(solution)/shard_map/ppermute | solution.py:23
  16.5 6.2 %collective-permute-start.12 = (bf16[48,576]{1,0:T(8,128)(2,1)S(1)}, bf16[48,576]{1,0:T(8,128)(2,1)S(1)}, u32[]{:S(2)}, u32[]{:S(2)}) collective-permute-start(bf16[48,576]{1,0:T(8,128)(2,1)S(1)} %get-tuple-element.103), channel_id=1, source_target_pairs={{0,24},{8,16},{16,8},{24,0},{1,25},{9,17},{17,9},{25,1},{2,26},{10... | collective-permute-start | bytes 165896 | tf_op jit(solution)/shard_map/ppermute | solution.py:23
  31.7 2.4 collective-permute-start.14
  36.8 6.8 %collective-permute-done.13.refs_5_ = bf16[4,48,576]{2,1,0:T(8,128)(2,1)S(1)} collective-permute-done((bf16[4,48,576]{2,1,0:T(8,128)(2,1)S(1)}, bf16[4,48,576]{2,1,0:T(8,128)(2,1)S(1)}, u32[]{:S(2)}, u32[]{:S(2)}) %collective-permute-start.13) | collective-permute-done | bytes 221216 | tf_op jit(solution)/shard_map/ppermute | solution.py:23
  43.7 8.3 %collective-permute-done.14.refs_6_ = bf16[4,48,576]{2,1,0:T(8,128)(2,1)S(1)} collective-permute-done((bf16[4,48,576]{2,1,0:T(8,128)(2,1)S(1)}, bf16[4,48,576]{2,1,0:T(8,128)(2,1)S(1)}, u32[]{:S(2)}, u32[]{:S(2)}) %collective-permute-start.14) | collective-permute-done | bytes 221216 | tf_op jit(solution)/shard_map/ppermute | solution.py:23
  56.4 3.7 %collective-permute-start.17 = (bf16[48,768]{1,0:T(8,128)(2,1)S(1)}, bf16[48,768]{1,0:T(8,128)(2,1)S(1)}, u32[]{:S(2)}, u32[]{:S(2)}) collective-permute-start(bf16[48,768]{1,0:T(8,128)(2,1)S(1)} %convert_element_type.154.refs_4_), channel_id=1, source_target_pairs={{0,1},{1,0},{2,3},{3,2},{4,5},{5,4},{6,7},{7,6},{8,9},{9,8},{10,11... | collective-permute-start | bytes 221192 | tf_op jit(solution)/shard_map/ppermute | solution.py:23
  60.9 4.5 %collective-permute-start.18 = (bf16[48,768]{1,0:T(8,128)(2,1)S(1)}, bf16[48,768]{1,0:T(8,128)(2,1)S(1)}, u32[]{:S(2)}, u32[]{:S(2)}) collective-permute-start(bf16[48,768]{1,0:T(8,128)(2,1)S(1)} %convert_element_type.154.refs_4_), channel_id=1, source_target_pairs={{0,2},{1,3},{2,0},{3,1},{4,6},{5,7},{6,4},{7,5},{8,10},{9,11},{10,... | collective-permute-start | bytes 221192 | tf_op jit(solution)/shard_map/ppermute | solution.py:23
  66.6 6.8 %shard_map.265 = (f32[512,192]{1,0:T(8,128)S(1)}, f32[512,128]{1,0:T(8,128)S(1)}) custom-call(s32[6]{0:T(128)S(1)} %stack.93.meta_ref.place_ref, bf16[512,576]{1,0:T(8,128)(2,1)S(1)} %get-tuple-element.104.kvq_ref.refs_0_.refs_5_), custom_call_target="tpu_custom_call" | custom-call | flops 201326592 | bytes 1245208 | tf_op jit(solution)/shard_map/pallas_call | solution.py:544
  73.4 6.7 %collective-permute-done.18.refs_6_ = bf16[48,768]{1,0:T(8,128)(2,1)S(1)} collective-permute-done((bf16[48,768]{1,0:T(8,128)(2,1)S(1)}, bf16[48,768]{1,0:T(8,128)(2,1)S(1)}, u32[]{:S(2)}, u32[]{:S(2)}) %collective-permute-start.18) | collective-permute-done | bytes 73760 | tf_op jit(solution)/shard_map/ppermute | solution.py:23
  84.4 3.4 %collective-permute-start.35 = (bf16[4,48,768]{2,1,0:T(8,128)(2,1)S(1)}, bf16[4,48,768]{2,1,0:T(8,128)(2,1)S(1)}, u32[]{:S(2)}, u32[]{:S(2)}) collective-permute-start(bf16[4,48,768]{2,1,0:T(8,128)(2,1)S(1)} %pad_maximum_fusion.refs_8_), channel_id=1, source_target_pairs={{0,3},{1,2},{2,1},{3,0},{4,7},{5,6},{6,5},{7,4},{8,11},{9,10},{10,... | collective-permute-start | bytes 884744 | tf_op jit(solution)/shard_map/ppermute | solution.py:23
  94.2 11.2 %collective-permute-done.34.refs_10_ = bf16[4,48,768]{2,1,0:T(8,128)(2,1)S(1)} collective-permute-done((bf16[4,48,768]{2,1,0:T(8,128)(2,1)S(1)}, bf16[4,48,768]{2,1,0:T(8,128)(2,1)S(1)}, u32[]{:S(2)}, u32[]{:S(2)}) %collective-permute-start.34) | collective-permute-done | bytes 294944 | tf_op jit(solution)/shard_map/ppermute | solution.py:23
  109.9 20.7 %collective-permute-done.37.refs_14_ = bf16[192,768]{1,0:T(8,128)(2,1)S(1)} collective-permute-done((bf16[192,768]{1,0:T(8,128)(2,1)S(1)}, bf16[192,768]{1,0:T(8,128)(2,1)S(1)}, u32[]{:S(2)}, u32[]{:S(2)}) %collective-permute-start.37) | collective-permute-done | bytes 294944 | tf_op jit(solution)/shard_map/ppermute | solution.py:23
  132.4 5.8 %shard_map.268 = (f32[128,768]{1,0:T(8,128)S(1)}, bf16[128,768]{1,0:T(8,128)(2,1)S(1)}, bf16[128,768]{1,0:T(8,128)(2,1)S(1)}, bf16[128,768]{1,0:T(8,128)(2,1)S(1...) custom-call(s32[6]{0:T(128)S(1)} %stack.93.meta_ref.place_ref, ...), custom_call_target="tpu_custom_call" | custom-call | flops 1811939328 | bytes 9268248 | tf_op jit(solution)/shard_map/pallas_call | solution.py:544
  139.6 4.1 %shard_map.269 = (f32[192,768]{1,0:T(8,128)S(1)}, bf16[192,768]{1,0:T(8,128)(2,1)S(1)}, bf16[192,768]{1,0:T(8,128)(2,1)S(1)}, bf16[192,768]{1,0:T(8,128)(2,1)S(1...) custom-call(s32[6]{0:T(128)S(1)} %stack.93.meta_ref.place_ref, ...), custom_call_target="tpu_custom_call" | custom-call | flops 1811939328 | bytes 8257560 | tf_op jit(solution)/shard_map/pallas_call | solution.py:544
  146.0 3.7 %collective-permute-start.73 = (bf16[4,48,768]{2,1,0:T(8,128)(2,1)S(1)}, bf16[4,48,768]{2,1,0:T(8,128)(2,1)S(1)}, u32[]{:S(2)}, u32[]{:S(2)}) collective-permute-start(bf16[4,48,768]{2,1,0:T(8,128)(2,1)S(1)} %get-tuple-element.174), channel_id=1, source_target_pairs={{0,2},{1,3},{2,0},{3,1},{4,6},{5,7},{6,4},{7,5},{8,10},{9,11},{10,... | collective-permute-start | bytes 884744 | tf_op jit(solution)/shard_map/ppermute | solution.py:23
  151.4 6.0 %collective-permute-done.40.refs_2_ = bf16[128,768]{1,0:T(8,128)(2,1)S(1)} collective-permute-done((bf16[128,768]{1,0:T(8,128)(2,1)S(1)}, bf16[128,768]{1,0:T(8,128)(2,1)S(1)}, u32[]{:S(2)}, u32[]{:S(2)}) %collective-permute-start.40) | collective-permute-done | bytes 196640 | tf_op jit(solution)/shard_map/ppermute | solution.py:23
  157.4 2.5 collective-permute-done.41.refs_3_
  164.2 4.6 %collective-permute-start.80 = (bf16[192,768]{1,0:T(8,128)(2,1)S(1)}, bf16[192,768]{1,0:T(8,128)(2,1)S(1)}, u32[]{:S(2)}, u32[]{:S(2)}) collective-permute-start(bf16[192,768]{1,0:T(8,128)(2,1)S(1)} %get-tuple-element.182), channel_id=1, source_target_pairs={{0,2},{1,3},{2,0},{3,1},{4,6},{5,7},{6,4},{7,5},{8,10},{9,11},{10,... | collective-permute-start | bytes 884744 | tf_op jit(solution)/shard_map/ppermute | solution.py:23
  168.9 17.5 %collective-permute-done.73 = bf16[4,48,768]{2,1,0:T(8,128)(2,1)S(1)} collective-permute-done((bf16[4,48,768]{2,1,0:T(8,128)(2,1)S(1)}, bf16[4,48,768]{2,1,0:T(8,128)(2,1)S(1)}, u32[]{:S(2)}, u32[]{:S(2)}) %collective-permute-start.73) | collective-permute-done | bytes 294944 | tf_op jit(solution)/shard_map/ppermute | solution.py:23
  190.2 8.9 %collective-permute-done.80 = bf16[192,768]{1,0:T(8,128)(2,1)S(1)} collective-permute-done((bf16[192,768]{1,0:T(8,128)(2,1)S(1)}, bf16[192,768]{1,0:T(8,128)(2,1)S(1)}, u32[]{:S(2)}, u32[]{:S(2)}) %collective-permute-start.80) | collective-permute-done | bytes 294944 | tf_op jit(solution)/shard_map/ppermute | solution.py:23
  199.1 2.5 collective-permute-done.79
  203.0 14.8 %collective-permute-start.49 = (bf16[512,384]{1,0:T(8,128)(2,1)S(1)}, bf16[512,384]{1,0:T(8,128)(2,1)S(1)}, u32[]{:S(2)}, u32[]{:S(2)}) collective-permute-start(bf16[512,384]{1,0:T(8,128)(2,1)S(1)} %bitcast.88), channel_id=1, source_target_pairs={{0,4},{4,0},{1,5},{5,1},{2,6},{6,2},{3,7},{7,3},{8,12},{12,8},{9,1... | collective-permute-start | bytes 1179656 | tf_op jit(solution)/shard_map/ppermute | solution.py:28
  217.9 6.9 %shard_map.272 = (f32[512,576]{1,0:T(8,128)S(1)}, f32[48,768]{1,0:T(8,128)S(1)}, bf16[48,768]{1,0:T(8,128)(2,1)S(1)}, bf16[48,768]{1,0:T(8,128)(2,1)S(1)}, bf16[48,768]{1,0:T(8,128)(2,1)S(1)}) custom-call(s32[6]{0:T(128)S(1)} %stack.93.meta_ref.place_ref, bf16[512,576]{1,0:T(8,128)(2,1)S(1)} %get-tuple-element.104.kvq_ref.refs_0_.refs_5_, ...), custom_call_target="tpu_custom_call" | custom-call | flops 503316480 | bytes 4366360 | tf_op jit(solution)/shard_map/pallas_call | solution.py:544
  224.7 2.3 collective-permute-start.70
  243.8 4.0 %collective-permute-done.52.refs_3_ = bf16[128,768]{1,0:T(8,128)(2,1)S(1)} collective-permute-done((bf16[128,768]{1,0:T(8,128)(2,1)S(1)}, bf16[128,768]{1,0:T(8,128)(2,1)S(1)}, u32[]{:S(2)}, u32[]{:S(2)}) %collective-permute-start.52) | collective-permute-done | bytes 196640 | tf_op jit(solution)/shard_map/ppermute | solution.py:23
  248.7 2.7 collective-permute-start.56
  254.5 11.1 %collective-permute-start.61 = (bf16[4,48,576]{2,1,0:T(8,128)(2,1)S(1)}, bf16[4,48,576]{2,1,0:T(8,128)(2,1)S(1)}, u32[]{:S(2)}, u32[]{:S(2)}) collective-permute-start(bf16[4,48,576]{2,1,0:T(8,128)(2,1)S(1)} %get-tuple-element.164), channel_id=1, source_target_pairs={{0,1},{1,0},{2,3},{3,2},{4,5},{5,4},{6,7},{7,6},{8,9},{9,8},{10,11... | collective-permute-start | bytes 663560 | tf_op jit(solution)/shard_map/ppermute | solution.py:23
  268.1 3.6 %collective-permute-done.61 = bf16[4,48,576]{2,1,0:T(8,128)(2,1)S(1)} collective-permute-done((bf16[4,48,576]{2,1,0:T(8,128)(2,1)S(1)}, bf16[4,48,576]{2,1,0:T(8,128)(2,1)S(1)}, u32[]{:S(2)}, u32[]{:S(2)}) %collective-permute-start.61) | collective-permute-done | bytes 221216 | tf_op jit(solution)/shard_map/ppermute | solution.py:23
  271.8 9.5 %collective-permute-done.57 = f32[8,768]{1,0:T(8,128)S(1)} collective-permute-done((f32[8,768]{1,0:T(8,128)S(1)}, f32[8,768]{1,0:T(8,128)S(1)}, u32[]{:S(2)}, u32[]{:S(2)}) %collective-permute-start.57) | collective-permute-done | bytes 24608 | tf_op jit(solution)/shard_map/ppermute | solution.py:28
  287.5 3.0 collective-permute-start.77
  291.4 5.0 %collective-permute-done.77.refs_2_ = bf16[48,768]{1,0:T(8,128)(2,1)S(1)} collective-permute-done((bf16[48,768]{1,0:T(8,128)(2,1)S(1)}, bf16[48,768]{1,0:T(8,128)(2,1)S(1)}, u32[]{:S(2)}, u32[]{:S(2)}) %collective-permute-start.77) | collective-permute-done | bytes 73760 | tf_op jit(solution)/shard_map/ppermute | solution.py:23
  299.6 2.5 collective-permute-start.66
  (207 shorter events, 99.1 us)
Async XLA Ops:
  5.9 16.9 %collective-permute-start.3 = (f32[8,768]{1,0:T(8,128)S(1)}, f32[8,768]{1,0:T(8,128)S(1)}, u32[]{:S(2)}, u32[]{:S(2)}) collective-permute-start(f32[8,768]{1,0:T(8,128)S(1)} %dynamic_update_slice.15), channel_id=1, source_target_pairs={{0,3},{1,2},{2,1},{3,0},{4,7},{5,6},{6,5},{7,4},{8,11},{9,10},{10,... | collective-permute-start | bytes 73736 | tf_op jit(solution)/shard_map/ppermute | solution.py:23
  31.7 20.4 %collective-permute-start.14 = (bf16[4,48,576]{2,1,0:T(8,128)(2,1)S(1)}, bf16[4,48,576]{2,1,0:T(8,128)(2,1)S(1)}, u32[]{:S(2)}, u32[]{:S(2)}) collective-permute-start(bf16[4,48,576]{2,1,0:T(8,128)(2,1)S(1)} %pad_maximum_fusion.1.refs_4_), channel_id=1, source_target_pairs={{0,2},{1,3},{2,0},{3,1},{4,6},{5,7},{6,4},{7,5},{8,10},{9,11},{10,... | collective-permute-start | bytes 663560 | tf_op jit(solution)/shard_map/ppermute | solution.py:23
  34.1 18.5 %collective-permute-start.15 = (bf16[4,48,576]{2,1,0:T(8,128)(2,1)S(1)}, bf16[4,48,576]{2,1,0:T(8,128)(2,1)S(1)}, u32[]{:S(2)}, u32[]{:S(2)}) collective-permute-start(bf16[4,48,576]{2,1,0:T(8,128)(2,1)S(1)} %pad_maximum_fusion.1.refs_4_), channel_id=1, source_target_pairs={{0,3},{1,2},{2,1},{3,0},{4,7},{5,6},{6,5},{7,4},{8,11},{9,10},{10,... | collective-permute-start | bytes 663560 | tf_op jit(solution)/shard_map/ppermute | solution.py:23
  36.0 16.5 %collective-permute-start.7 = (bf16[128,768]{1,0:T(8,128)(2,1)S(1)}, bf16[128,768]{1,0:T(8,128)(2,1)S(1)}, u32[]{:S(2)}, u32[]{:S(2)}) collective-permute-start(bf16[128,768]{1,0:T(8,128)(2,1)S(1)} %shard_map.262.refs_0_), channel_id=1, source_target_pairs={{0,8},{8,0},{16,24},{24,16},{1,9},{9,1},{17,25},{25,17},{2,10},{10... | collective-permute-start | bytes 589832 | tf_op jit(solution)/shard_map/ppermute | solution.py:23
  54.0 26.1 %collective-permute-start.16 = (bf16[512,384]{1,0:T(8,128)(2,1)S(1)}, bf16[512,384]{1,0:T(8,128)(2,1)S(1)}, u32[]{:S(2)}, u32[]{:S(2)}) collective-permute-start(bf16[512,384]{1,0:T(8,128)(2,1)S(1)} %get-tuple-element.105), channel_id=1, source_target_pairs={{0,4},{4,0},{1,5},{5,1},{2,6},{6,2},{3,7},{7,3},{8,12},{12,8},{9,1... | collective-permute-start | bytes 1179656 | tf_op jit(solution)/shard_map/ppermute | solution.py:28
  60.1 24.3 %collective-permute-start.33 = (bf16[4,48,768]{2,1,0:T(8,128)(2,1)S(1)}, bf16[4,48,768]{2,1,0:T(8,128)(2,1)S(1)}, u32[]{:S(2)}, u32[]{:S(2)}) collective-permute-start(bf16[4,48,768]{2,1,0:T(8,128)(2,1)S(1)} %pad_maximum_fusion.refs_8_), channel_id=1, source_target_pairs={{0,1},{1,0},{2,3},{3,2},{4,5},{5,4},{6,7},{7,6},{8,9},{9,8},{10,11... | collective-permute-start | bytes 884744 | tf_op jit(solution)/shard_map/ppermute | solution.py:23
  60.2 23.8 %collective-permute-start.26 = (bf16[128,768]{1,0:T(8,128)(2,1)S(1)}, bf16[128,768]{1,0:T(8,128)(2,1)S(1)}, u32[]{:S(2)}, u32[]{:S(2)}) collective-permute-start(bf16[128,768]{1,0:T(8,128)(2,1)S(1)} %bitcast_convert_fusion), channel_id=1, source_target_pairs={{0,0},{1,8},{2,16},{3,24},{8,1},{9,9},{10,17},{11,25},{16,2},{17,1... | collective-permute-start | bytes 589832 | tf_op jit(solution)/shard_map/ppermute | solution.py:34
  60.9 19.1 %collective-permute-start.18 = (bf16[48,768]{1,0:T(8,128)(2,1)S(1)}, bf16[48,768]{1,0:T(8,128)(2,1)S(1)}, u32[]{:S(2)}, u32[]{:S(2)}) collective-permute-start(bf16[48,768]{1,0:T(8,128)(2,1)S(1)} %convert_element_type.154.refs_4_), channel_id=1, source_target_pairs={{0,2},{1,3},{2,0},{3,1},{4,6},{5,7},{6,4},{7,5},{8,10},{9,11},{10,... | collective-permute-start | bytes 221192 | tf_op jit(solution)/shard_map/ppermute | solution.py:23
  81.9 23.5 %collective-permute-start.34 = (bf16[4,48,768]{2,1,0:T(8,128)(2,1)S(1)}, bf16[4,48,768]{2,1,0:T(8,128)(2,1)S(1)}, u32[]{:S(2)}, u32[]{:S(2)}) collective-permute-start(bf16[4,48,768]{2,1,0:T(8,128)(2,1)S(1)} %pad_maximum_fusion.refs_8_), channel_id=1, source_target_pairs={{0,2},{1,3},{2,0},{3,1},{4,6},{5,7},{6,4},{7,5},{8,10},{9,11},{10,... | collective-permute-start | bytes 884744 | tf_op jit(solution)/shard_map/ppermute | solution.py:23
  84.4 22.9 %collective-permute-start.35 = (bf16[4,48,768]{2,1,0:T(8,128)(2,1)S(1)}, bf16[4,48,768]{2,1,0:T(8,128)(2,1)S(1)}, u32[]{:S(2)}, u32[]{:S(2)}) collective-permute-start(bf16[4,48,768]{2,1,0:T(8,128)(2,1)S(1)} %pad_maximum_fusion.refs_8_), channel_id=1, source_target_pairs={{0,3},{1,2},{2,1},{3,0},{4,7},{5,6},{6,5},{7,4},{8,11},{9,10},{10,... | collective-permute-start | bytes 884744 | tf_op jit(solution)/shard_map/ppermute | solution.py:23
  87.9 21.5 %collective-permute-start.36 = (bf16[192,768]{1,0:T(8,128)(2,1)S(1)}, bf16[192,768]{1,0:T(8,128)(2,1)S(1)}, u32[]{:S(2)}, u32[]{:S(2)}) collective-permute-start(bf16[192,768]{1,0:T(8,128)(2,1)S(1)} %convert_element_type.156.refs_12_), channel_id=1, source_target_pairs={{0,1},{1,0},{2,3},{3,2},{4,5},{5,4},{6,7},{7,6},{8,9},{9,8},{10,11... | collective-permute-start | bytes 884744 | tf_op jit(solution)/shard_map/ppermute | solution.py:23
  89.6 41.1 %collective-permute-start.37 = (bf16[192,768]{1,0:T(8,128)(2,1)S(1)}, bf16[192,768]{1,0:T(8,128)(2,1)S(1)}, u32[]{:S(2)}, u32[]{:S(2)}) collective-permute-start(bf16[192,768]{1,0:T(8,128)(2,1)S(1)} %convert_element_type.156.refs_12_), channel_id=1, source_target_pairs={{0,2},{1,3},{2,0},{3,1},{4,6},{5,7},{6,4},{7,5},{8,10},{9,11},{10,... | collective-permute-start | bytes 884744 | tf_op jit(solution)/shard_map/ppermute | solution.py:23
  105.4 25.3 %collective-permute-start.24 = (bf16[128,768]{1,0:T(8,128)(2,1)S(1)}, bf16[128,768]{1,0:T(8,128)(2,1)S(1)}, u32[]{:S(2)}, u32[]{:S(2)}) collective-permute-start(bf16[128,768]{1,0:T(8,128)(2,1)S(1)} %get-tuple-element.113.refs_0_), channel_id=1, source_target_pairs={{0,16},{8,24},{16,0},{24,8},{1,17},{9,25},{17,1},{25,9},{2,18},{10... | collective-permute-start | bytes 589832 | tf_op jit(solution)/shard_map/ppermute | solution.py:23
  107.4 23.8 %collective-permute-start.38 = (bf16[192,768]{1,0:T(8,128)(2,1)S(1)}, bf16[192,768]{1,0:T(8,128)(2,1)S(1)}, u32[]{:S(2)}, u32[]{:S(2)}) collective-permute-start(bf16[192,768]{1,0:T(8,128)(2,1)S(1)} %convert_element_type.156.refs_12_), channel_id=1, source_target_pairs={{0,3},{1,2},{2,1},{3,0},{4,7},{5,6},{6,5},{7,4},{8,11},{9,10},{10,... | collective-permute-start | bytes 884744 | tf_op jit(solution)/shard_map/ppermute | solution.py:23
  109.4 21.8 %collective-permute-start.27 = (bf16[128,768]{1,0:T(8,128)(2,1)S(1)}, bf16[128,768]{1,0:T(8,128)(2,1)S(1)}, u32[]{:S(2)}, u32[]{:S(2)}) collective-permute-start(bf16[128,768]{1,0:T(8,128)(2,1)S(1)} %collective-permute-done.26.refs_4_.refs_6_), channel_id=1, source_target_pairs={{0,8},{8,0},{16,24},{24,16},{1,9},{9,1},{17,25},{25,17},{2,10},{10... | collective-permute-start | bytes 589832 | tf_op jit(solution)/shard_map/ppermute | solution.py:23
  109.4 21.8 %collective-permute-start.29 = (bf16[128,768]{1,0:T(8,128)(2,1)S(1)}, bf16[128,768]{1,0:T(8,128)(2,1)S(1)}, u32[]{:S(2)}, u32[]{:S(2)}) collective-permute-start(bf16[128,768]{1,0:T(8,128)(2,1)S(1)} %collective-permute-done.28.refs_6_), channel_id=1, source_target_pairs={{0,8},{8,0},{16,24},{24,16},{1,9},{9,1},{17,25},{25,17},{2,10},{10... | collective-permute-start | bytes 589832 | tf_op jit(solution)/shard_map/ppermute | solution.py:23
  143.7 20.5 %collective-permute-start.74 = (bf16[4,48,768]{2,1,0:T(8,128)(2,1)S(1)}, bf16[4,48,768]{2,1,0:T(8,128)(2,1)S(1)}, u32[]{:S(2)}, u32[]{:S(2)}) collective-permute-start(bf16[4,48,768]{2,1,0:T(8,128)(2,1)S(1)} %get-tuple-element.175), channel_id=1, source_target_pairs={{0,3},{1,2},{2,1},{3,0},{4,7},{5,6},{6,5},{7,4},{8,11},{9,10},{10,... | collective-permute-start | bytes 884744 | tf_op jit(solution)/shard_map/ppermute | solution.py:23
  146.0 40.4 %collective-permute-start.73 = (bf16[4,48,768]{2,1,0:T(8,128)(2,1)S(1)}, bf16[4,48,768]{2,1,0:T(8,128)(2,1)S(1)}, u32[]{:S(2)}, u32[]{:S(2)}) collective-permute-start(bf16[4,48,768]{2,1,0:T(8,128)(2,1)S(1)} %get-tuple-element.174), channel_id=1, source_target_pairs={{0,2},{1,3},{2,0},{3,1},{4,6},{5,7},{6,4},{7,5},{8,10},{9,11},{10,... | collective-permute-start | bytes 884744 | tf_op jit(solution)/shard_map/ppermute | solution.py:23
  151.4 35.0 %collective-permute-start.72 = (bf16[4,48,768]{2,1,0:T(8,128)(2,1)S(1)}, bf16[4,48,768]{2,1,0:T(8,128)(2,1)S(1)}, u32[]{:S(2)}, u32[]{:S(2)}) collective-permute-start(bf16[4,48,768]{2,1,0:T(8,128)(2,1)S(1)} %get-tuple-element.173), channel_id=1, source_target_pairs={{0,1},{1,0},{2,3},{3,2},{4,5},{5,4},{6,7},{7,6},{8,9},{9,8},{10,11... | collective-permute-start | bytes 884744 | tf_op jit(solution)/shard_map/ppermute | solution.py:23
  160.9 25.6 %collective-permute-start.42 = (bf16[128,768]{1,0:T(8,128)(2,1)S(1)}, bf16[128,768]{1,0:T(8,128)(2,1)S(1)}, u32[]{:S(2)}, u32[]{:S(2)}) collective-permute-start(bf16[128,768]{1,0:T(8,128)(2,1)S(1)} %get-tuple-element.136.refs_0_), channel_id=1, source_target_pairs={{0,16},{8,24},{16,0},{24,8},{1,17},{9,25},{17,1},{25,9},{2,18},{10... | collective-permute-start | bytes 589832 | tf_op jit(solution)/shard_map/ppermute | solution.py:23
  162.5 27.6 %collective-permute-start.81 = (bf16[192,768]{1,0:T(8,128)(2,1)S(1)}, bf16[192,768]{1,0:T(8,128)(2,1)S(1)}, u32[]{:S(2)}, u32[]{:S(2)}) collective-permute-start(bf16[192,768]{1,0:T(8,128)(2,1)S(1)} %get-tuple-element.183), channel_id=1, source_target_pairs={{0,3},{1,2},{2,1},{3,0},{4,7},{5,6},{6,5},{7,4},{8,11},{9,10},{10,... | collective-permute-start | bytes 884744 | tf_op jit(solution)/shard_map/ppermute | solution.py:23
  164.2 34.9 %collective-permute-start.80 = (bf16[192,768]{1,0:T(8,128)(2,1)S(1)}, bf16[192,768]{1,0:T(8,128)(2,1)S(1)}, u32[]{:S(2)}, u32[]{:S(2)}) collective-permute-start(bf16[192,768]{1,0:T(8,128)(2,1)S(1)} %get-tuple-element.182), channel_id=1, source_target_pairs={{0,2},{1,3},{2,0},{3,1},{4,6},{5,7},{6,4},{7,5},{8,10},{9,11},{10,... | collective-permute-start | bytes 884744 | tf_op jit(solution)/shard_map/ppermute | solution.py:23
  188.2 38.8 %collective-permute-start.46 = (bf16[128,768]{1,0:T(8,128)(2,1)S(1)}, bf16[128,768]{1,0:T(8,128)(2,1)S(1)}, u32[]{:S(2)}, u32[]{:S(2)}) collective-permute-start(bf16[128,768]{1,0:T(8,128)(2,1)S(1)} %get-tuple-element.139), channel_id=1, source_target_pairs={{0,24},{8,16},{16,8},{24,0},{1,25},{9,17},{17,9},{25,1},{2,26},{10... | collective-permute-start | bytes 589832 | tf_op jit(solution)/shard_map/ppermute | solution.py:23
  190.0 37.0 %collective-permute-start.45 = (bf16[128,768]{1,0:T(8,128)(2,1)S(1)}, bf16[128,768]{1,0:T(8,128)(2,1)S(1)}, u32[]{:S(2)}, u32[]{:S(2)}) collective-permute-start(bf16[128,768]{1,0:T(8,128)(2,1)S(1)} %get-tuple-element.138), channel_id=1, source_target_pairs={{0,16},{8,24},{16,0},{24,8},{1,17},{9,25},{17,1},{25,9},{2,18},{10... | collective-permute-start | bytes 589832 | tf_op jit(solution)/shard_map/ppermute | solution.py:23
  199.1 30.1 %collective-permute-start.44 = (bf16[128,768]{1,0:T(8,128)(2,1)S(1)}, bf16[128,768]{1,0:T(8,128)(2,1)S(1)}, u32[]{:S(2)}, u32[]{:S(2)}) collective-permute-start(bf16[128,768]{1,0:T(8,128)(2,1)S(1)} %get-tuple-element.137), channel_id=1, source_target_pairs={{0,8},{8,0},{16,24},{24,16},{1,9},{9,1},{17,25},{25,17},{2,10},{10... | collective-permute-start | bytes 589832 | tf_op jit(solution)/shard_map/ppermute | solution.py:23
  203.0 30.2 %collective-permute-start.49 = (bf16[512,384]{1,0:T(8,128)(2,1)S(1)}, bf16[512,384]{1,0:T(8,128)(2,1)S(1)}, u32[]{:S(2)}, u32[]{:S(2)}) collective-permute-start(bf16[512,384]{1,0:T(8,128)(2,1)S(1)} %bitcast.88), channel_id=1, source_target_pairs={{0,4},{4,0},{1,5},{5,1},{2,6},{6,2},{3,7},{7,3},{8,12},{12,8},{9,1... | collective-permute-start | bytes 1179656 | tf_op jit(solution)/shard_map/ppermute | solution.py:28
  238.1 29.6 %collective-permute-start.63 = (bf16[4,48,576]{2,1,0:T(8,128)(2,1)S(1)}, bf16[4,48,576]{2,1,0:T(8,128)(2,1)S(1)}, u32[]{:S(2)}, u32[]{:S(2)}) collective-permute-start(bf16[4,48,576]{2,1,0:T(8,128)(2,1)S(1)} %get-tuple-element.166), channel_id=1, source_target_pairs={{0,3},{1,2},{2,1},{3,0},{4,7},{5,6},{6,5},{7,4},{8,11},{9,10},{10,... | collective-permute-start | bytes 663560 | tf_op jit(solution)/shard_map/ppermute | solution.py:23
  241.1 26.9 %collective-permute-start.62 = (bf16[4,48,576]{2,1,0:T(8,128)(2,1)S(1)}, bf16[4,48,576]{2,1,0:T(8,128)(2,1)S(1)}, u32[]{:S(2)}, u32[]{:S(2)}) collective-permute-start(bf16[4,48,576]{2,1,0:T(8,128)(2,1)S(1)} %get-tuple-element.165), channel_id=1, source_target_pairs={{0,2},{1,3},{2,0},{3,1},{4,6},{5,7},{6,4},{7,5},{8,10},{9,11},{10,... | collective-permute-start | bytes 663560 | tf_op jit(solution)/shard_map/ppermute | solution.py:23
  254.5 17.2 %collective-permute-start.61 = (bf16[4,48,576]{2,1,0:T(8,128)(2,1)S(1)}, bf16[4,48,576]{2,1,0:T(8,128)(2,1)S(1)}, u32[]{:S(2)}, u32[]{:S(2)}) collective-permute-start(bf16[4,48,576]{2,1,0:T(8,128)(2,1)S(1)} %get-tuple-element.164), channel_id=1, source_target_pairs={{0,1},{1,0},{2,3},{3,2},{4,5},{5,4},{6,7},{7,6},{8,9},{9,8},{10,11... | collective-permute-start | bytes 663560 | tf_op jit(solution)/shard_map/ppermute | solution.py:23
  265.7 20.6 %collective-permute-start.75 = (bf16[4,48,768]{2,1,0:T(8,128)(2,1)S(1)}, bf16[4,48,768]{2,1,0:T(8,128)(2,1)S(1)}, u32[]{:S(2)}, u32[]{:S(2)}) collective-permute-start(bf16[4,48,768]{2,1,0:T(8,128)(2,1)S(1)} %add_convert_fusion.2), channel_id=1, source_target_pairs={{0,4},{4,0},{1,5},{5,1},{2,6},{6,2},{3,7},{7,3},{8,12},{12,8},{9,1... | collective-permute-start | bytes 884744 | tf_op jit(solution)/shard_map/ppermute | solution.py:28
  266.0 24.5 %collective-permute-start.82 = (bf16[192,768]{1,0:T(8,128)(2,1)S(1)}, bf16[192,768]{1,0:T(8,128)(2,1)S(1)}, u32[]{:S(2)}, u32[]{:S(2)}) collective-permute-start(bf16[192,768]{1,0:T(8,128)(2,1)S(1)} %add_convert_fusion), channel_id=1, source_target_pairs={{0,4},{4,0},{1,5},{5,1},{2,6},{6,2},{3,7},{7,3},{8,12},{12,8},{9,1... | collective-permute-start | bytes 884744 | tf_op jit(solution)/shard_map/ppermute | solution.py:28
  284.6 17.5 %collective-permute-start.53 = (bf16[128,768]{1,0:T(8,128)(2,1)S(1)}, bf16[128,768]{1,0:T(8,128)(2,1)S(1)}, u32[]{:S(2)}, u32[]{:S(2)}) collective-permute-start(bf16[128,768]{1,0:T(8,128)(2,1)S(1)} %get-tuple-element.159), channel_id=1, source_target_pairs={{0,0},{1,8},{2,16},{3,24},{8,1},{9,9},{10,17},{11,25},{16,2},{17,1... | collective-permute-start | bytes 589832 | tf_op jit(solution)/shard_map/ppermute | solution.py:34
  (58 other events, 527.0 us)

commit v3 on v2

--- a/solution.py
+++ b/solution.py
@@ -52,6 +52,14 @@
 
 def gather_direct(block, axis):
     return [block] + [swap(block, axis, slot) for slot in range(1, lax.axis_size(axis))]
+
+
+def sum_doubling(value, axis):
+    bit = 1
+    while bit < lax.axis_size(axis):
+        value = value + swap(value, axis, bit)
+        bit *= 2
+    return value
 
 
 def sum_all(kept, arrived):
@@ -283,13 +291,6 @@
             out_ref[pl.ds(start, rows), :] = pieces[deep][slot]
 
 
-def place_shards(meta_ref, parts, pieces, out_ref):
-    rows = pieces[0].shape[0]
-    for deep, piece in enumerate(pieces):
-        start = pl.multiple_of((meta_ref[parts + 1] ^ deep) * rows, 16)
-        out_ref[pl.ds(start, rows), :] = piece[...]
-
-
 def stack_rows(pieces, out_ref):
     rows = pieces[0].shape[0]
     for slot, piece in enumerate(pieces):
@@ -327,10 +328,37 @@
             keep_ref[...] = block
 
 
-def split_kernel(parts, width, meta_ref, qkv_ref, up_ref, *outs):
-    kvq_outs, up_outs = take(outs, parts, parts)
+def pack_sizes(parts, shard, hidden_shard):
+    main = max(parts * shard, hidden_shard)
+    extra = 16 * (-(-shard // 32))
+    return main, extra, main + extra
+
+
+def pack_kernel(parts, both, meta_ref, *refs):
+    up, out_weight, down_weight, packed = take(refs, parts, None, None, None)
+    shard = out_weight.shape[0]
+    hidden_shard = down_weight.shape[0]
+    main, extra, _ = pack_sizes(parts, shard, hidden_shard)
+    packed[...] = jnp.zeros_like(packed)
+
+    def fill(half, at):
+        if half == 0:
+            for slot in range(parts):
+                packed[at, slot * shard : (slot + 1) * shard, :] = up[slot][...]
+            packed[at, main : main + extra, :] = out_weight[:extra, :].astype(LOW)
+        else:
+            packed[at, :hidden_shard, :] = down_weight[...].astype(LOW)
+            packed[at, main : main + shard - extra, :] = out_weight[extra:, :].astype(LOW)
+
+    for half in range(2):
+        if both:
+            fill(half, half)
+        else:
+            pl.when(meta_ref[parts] == half)(functools.partial(fill, half, 0))
+
+
+def split_qkv_kernel(parts, width, meta_ref, qkv_ref, *outs):
     model = parts * width
-    part = up_ref.shape[1] // parts
     for case in range(parts):
 
         @pl.when(meta_ref[0] == case)
@@ -339,10 +367,16 @@
                 owner = case ^ slot
                 for at, first in enumerate((model, 2 * model, 0)):
                     start = first + owner * width
-                    kvq_outs[slot][:, at * width : (at + 1) * width] = qkv_ref[
+                    outs[slot][:, at * width : (at + 1) * width] = qkv_ref[
                         :, start : start + width
                     ].astype(LOW)
-                up_outs[slot][...] = up_ref[:, owner * part : (owner + 1) * part].astype(LOW)
+
+
+def split_up_kernel(parts, meta_ref, up_ref, *outs):
+    part = up_ref.shape[1] // parts
+    for slot in range(parts):
+        start = pl.multiple_of(meta_ref[slot] * part, 128)
+        outs[slot][...] = up_ref[:, pl.ds(start, part)].astype(LOW)
 
 
 def join_qkv_kernel(parts, width, meta_ref, *refs):
@@ -390,10 +424,15 @@
     (
         kvq, kv, acc_in, stat_in, weight, context, low, stat, matrix, keep, sends, score, prob, fade
     ) = take(
-        refs, None, None, None, None, depth, None, None, None, None, None, parts - 1, None, None,
+        refs, None, None, None, None, None, None, None, None, None, None, parts - 1, None, None,
         None,
     )
-    place_shards(meta_ref, parts, weight, matrix)
+    extra = weight.shape[2]
+    shard = matrix.shape[0] // depth
+    for deep in range(depth):
+        start = deep * shard
+        matrix[start : start + extra, :] = weight[0, deep]
+        matrix[start + extra : start + shard, :] = weight[1, deep, : shard - extra]
     earlier_forward(
         heads, parts, meta_ref, kvq, kv, acc_in, stat_in, context, low, stat, score, prob, fade
     )
@@ -412,14 +451,18 @@
 
 def feed_kernel(parts, depth, meta_ref, *refs):
     (
-        norm, branch, up, down, vectors, keep, sends, hidden, inner_grad, norm_all, branch_all,
+        norm, branch, weight, vectors, keep, sends, hidden, inner_grad, norm_all, branch_all,
         down_all, up_bias, up_all, inner, grad,
-    ) = take(
-        refs, parts, parts, depth, depth, None, None, parts - 1, None, None, None, None, None,
-        None, None, None, None,
-    )
-    place_blocks(meta_ref, parts, depth, up, up_all)
-    place_shards(meta_ref, parts, down, down_all)
+    ) = take(refs, parts, parts, None, None, None, parts - 1, *([None] * 9))
+    shard = up_all.shape[0] // (parts * depth)
+    hidden_shard = down_all.shape[0] // depth
+    for deep in range(depth):
+        for slot in range(parts):
+            start = pl.multiple_of((meta_ref[slot] * depth + deep) * shard, 16)
+            up_all[pl.ds(start, shard), :] = weight[0, deep, slot * shard : (slot + 1) * shard]
+        down_all[deep * hidden_shard : (deep + 1) * hidden_shard, :] = weight[
+            1, deep, :hidden_shard
+        ]
     stack_rows(norm, norm_all)
     stack_rows(branch, branch_all)
     inner[...] = matmul_nn(norm_all[...], up_all[...])
@@ -445,16 +488,24 @@
 
 
 def feed_grad_kernel(parts, depth, meta_ref, *refs):
-    (
-        hidden, inner_grad, norm_all, branch_all, down_all, down_keep, down_sends, up_keep,
-        up_sends, fed_keep, fed_sends, whole,
-    ) = take(
-        refs, None, None, None, None, None, None, depth - 1, None, depth - 1, None, parts - 1, None
-    )
+    hidden, inner_grad, norm_all, branch_all, down_all, grads, fed_keep, fed_sends, whole = take(
+        refs, None, None, None, None, None, None, None, parts - 1, None
+    )
+    hidden_shard = hidden.shape[1] // depth
+    shard = norm_all.shape[1] // (parts * depth)
+    grads[...] = jnp.zeros_like(grads)
     whole[...] = matmul_tn(hidden[...], branch_all[...])
-    emit_shards(meta_ref, parts, whole, down_keep, down_sends)
+    for deep in range(depth):
+        grads[1, deep, :hidden_shard] = whole[
+            deep * hidden_shard : (deep + 1) * hidden_shard, :
+        ].astype(LOW)
     whole[...] = matmul_tn(norm_all[...], inner_grad[...])
-    emit_blocks(meta_ref, parts, depth, whole, up_keep, up_sends)
+    for deep in range(depth):
+        for slot in range(parts):
+            start = pl.multiple_of((meta_ref[slot] * depth + deep) * shard, 16)
+            grads[0, deep, slot * shard : (slot + 1) * shard] = whole[
+                pl.ds(start, shard), :
+            ].astype(LOW)
     emit_rows(matmul_nn(hidden[...], down_all[...]), fed_keep, fed_sends)
 
 
@@ -537,14 +588,15 @@
     sums[7:8, :] = up_bias[...]
 
 
-def local_call(kernel, operands, results, scratch=(), flops=0):
+def local_call(kernel, operands, results, scratch=(), flops=0, specs={}):
     smem = pl.BlockSpec(memory_space=pltpu.SMEM)
     vmem = pl.BlockSpec(memory_space=pltpu.VMEM)
     moved = sum(each.size * each.dtype.itemsize for each in tuple(operands) + tuple(results))
     return pl.pallas_call(
         kernel,
         out_shape=tuple(results),
-        in_specs=[smem] + [vmem] * (len(operands) - 1),
+        grid=(1,),
+        in_specs=[smem] + [specs.get(at, vmem) for at in range(1, len(operands))],
         out_specs=tuple([vmem] * len(results)),
         scratch_shapes=list(scratch),
         compiler_params=pltpu.CompilerParams(vmem_limit_bytes=48 * 1024 * 1024),
@@ -581,38 +633,48 @@
         [mine ^ slot for slot in range(parts)] + [lax.axis_index("ctx"), deep]
     ).astype(jnp.int32)
 
-    token_rows = transpose_homes(tokens[0].astype(LOW))
-
-    split = local_call(
-        functools.partial(split_kernel, parts, width),
-        (meta, qkv_weight, fc1_weight),
-        [low_like(shard, 3 * width)] * parts + [low_like(shard, hidden_part)] * parts,
-    )
-    kvq_split, up_split = split[:parts], split[parts:]
+    kvq_split = local_call(
+        functools.partial(split_qkv_kernel, parts, width),
+        (meta, qkv_weight),
+        [low_like(shard, 3 * width)] * parts,
+    )
     kvq_rows = jnp.stack([kvq_split[0]] + send_pieces(kvq_split[1:], "dp"))
     kvq_pieces = gather_direct(kvq_rows, "fsdp")
 
-    low_vectors = [
-        each.astype(LOW).astype(WIDE)
-        for each in (ln1_gain, ln1_bias, ln2_gain, ln2_bias, out_bias, fc2_bias)
-    ]
+    token_rows = transpose_homes(after(tokens[0].astype(LOW), kvq_split[0]))
+
+    low_vectors = jnp.stack([ln1_gain, ln1_bias, ln2_gain, ln2_bias, out_bias, fc2_bias])
     vectors = jnp.zeros((8, model), WIDE)
     vectors = lax.dynamic_update_slice(
-        vectors, jnp.stack(low_vectors), (0, (mine * depth + deep) * shard)
+        vectors, low_vectors.astype(LOW).astype(WIDE), (0, (mine * depth + deep) * shard)
     )
     for row, first, part in (
         (6, width, v_bias), (6, 2 * width, q_bias), (7, 0, fc1_bias),
     ):
         part = part.astype(LOW).astype(WIDE)[None]
         vectors = lax.dynamic_update_slice(vectors, part, (row, first + deep * part.shape[1]))
-    vectors = sum_all(vectors, gather_direct(vectors, "fsdp")[1:])
-    everywhere = sum_all(vectors, gather_direct(vectors, "dp")[1:])
+    vectors = sum_doubling(after(vectors, kvq_split[0]), "fsdp")
+    everywhere = sum_doubling(vectors, "dp")
     vectors = jnp.where(jnp.arange(8)[:, None] < 6, everywhere, vectors)
 
-    up_rows = jnp.stack([up_split[0]] + send_pieces(up_split[1:], "dp"))
-    out_pieces = gather_direct(after(out_weight.astype(LOW), kvq_pieces[-1]), "fsdp")
-    up_pieces = gather_direct(after(up_rows, kvq_pieces[-1]), "fsdp")
-    down_pieces = gather_direct(after(fc2_weight.astype(LOW), kvq_pieces[-1]), "fsdp")
+    halves = contexts == 2
+    main, extra, half_rows = pack_sizes(parts, shard, hidden_shard)
+    up_split = local_call(
+        functools.partial(split_up_kernel, parts),
+        (meta, fc1_weight),
+        [low_like(shard, hidden_part)] * parts,
+    )
+    up_arrived = send_pieces(up_split[1:], "dp")
+    (packed,) = local_call(
+        functools.partial(pack_kernel, parts, not halves),
+        (meta, up_split[0], *up_arrived, out_weight, fc2_weight),
+        [low_like(1 if halves else 2, half_rows, model)],
+    )
+    if halves:
+        weights = lax.all_gather(packed, ("ctx", "fsdp"), axis=0, tiled=True)
+        weights = weights.reshape(2, depth, half_rows, model)
+    else:
+        weights = lax.all_gather(packed, "fsdp", axis=1)
 
     (norm1,) = local_call(
         first_norm_kernel, (meta, token_rows, vectors), [low_like(rows, model)]
@@ -646,7 +708,7 @@
     )
     context, context_low, stat, out_matrix, attended_keep, *attended_sends = local_call(
         functools.partial(context_kernel, parts, depth, heads),
-        (meta, kvq, kv_earlier, acc, stat, *out_pieces),
+        (meta, kvq, kv_earlier, acc, stat, weights),
         [
             wide_like(group, width),
             low_like(group, width),
@@ -657,6 +719,9 @@
         + [low_like(rows, model)] * (parts - 1),
         [wide_square, low_square, pltpu.VMEM((group, HEAD_DIM), WIDE)],
         flops=2 * score_flops,
+        specs={
+            5: pl.BlockSpec((2, depth, extra, model), lambda _: (0, 0, main // extra, 0))
+        },
     )
     arrived = send_pieces(attended_sends, "dp")
     norm2, attended = local_call(
@@ -668,7 +733,7 @@
     norm2_pieces = gather_pieces(norm2)
     norm2_keep, *rest = local_call(
         functools.partial(feed_kernel, parts, depth),
-        (meta, *norm2_pieces, *branch_pieces, *up_pieces, *down_pieces, vectors),
+        (meta, *norm2_pieces, *branch_pieces, weights, vectors),
         [wide_like(rows, model)]
         + [low_like(rows, model)] * (parts - 1)
         + [low_like(group, hidden_part)] * 2
@@ -684,29 +749,27 @@
     norm2_sends = rest[: parts - 1]
     hidden, inner_grad, norm2_all, branch_all, down_matrix, up_bias = rest[parts - 1 :]
     norm2_arrived = send_pieces(norm2_sends, "dp")
-    feed_grads = local_call(
+    feed_grads, fed_keep, *fed_sends = local_call(
         functools.partial(feed_grad_kernel, parts, depth),
         (meta, hidden, inner_grad, norm2_all, branch_all, down_matrix),
-        [wide_like(hidden_shard, model)]
-        + [low_like(hidden_shard, model)] * (depth - 1)
-        + [wide_like(parts, shard, hidden_part)]
-        + [low_like(parts, shard, hidden_part)] * (depth - 1)
-        + [wide_like(rows, model)]
+        [low_like(2, depth, main, model), wide_like(rows, model)]
         + [low_like(rows, model)] * (parts - 1),
         [pltpu.VMEM((max(model, hidden_part), max(model, hidden_part)), WIDE)],
         flops=6 * group * model * hidden_part,
     )
-    down_keep, down_sends, up_keep, up_sends, fed_keep, fed_sends = take(
-        feed_grads, None, depth - 1, None, depth - 1, None, parts - 1
-    )
+    if halves:
+        mine_half = lax.psum_scatter(
+            feed_grads.reshape(2 * depth, main, model), ("ctx", "fsdp"), tiled=True
+        )[0]
+    else:
+        feed_total = lax.psum_scatter(feed_grads, "fsdp", scatter_dimension=1)
+        feed_total = lax.psum(feed_total, "ctx")
     attn_grad, mixed_part, sums = local_call(
         functools.partial(second_norm_grad_kernel, parts),
         (meta, norm2_keep, *norm2_arrived, token_rows, attended, grad_rows, vectors),
         [low_like(rows, model), wide_like(rows, model), wide_like(8, model)],
     )
     attn_pieces = gather_pieces(attn_grad)
-    down_arrived = send_pieces(down_sends, "fsdp")
-    up_arrived = send_pieces(up_sends, "fsdp")
     fed_arrived = send_pieces(
         lax.optimization_barrier((*fed_sends, attn_pieces[-1]))[: parts - 1], "dp"
     )
@@ -774,9 +837,16 @@
         low = sum_all(keep, pieces).astype(LOW)
         return sum_replicas(after(low, *later) if later else low)
 
-    down_total = owner_sum(down_keep, down_arrived, kv_arrived)
-    up_total = owner_sum(up_keep, up_arrived, kv_arrived).astype(LOW)
     out_total = owner_sum(out_keep, out_arrived, kv_arrived)
+    if halves:
+        other_half = shift(after(mine_half, kv_arrived), "ctx", 1)
+        first = lax.axis_index("ctx") == 0
+        up_total = jnp.where(first, mine_half, other_half)
+        down_total = jnp.where(first, other_half, mine_half)
+    else:
+        up_total, down_total = feed_total
+    up_total = up_total[: parts * shard].reshape(parts, shard, hidden_part)
+    down_total = down_total[:hidden_shard].astype(WIDE)
     up_sends = [after(up_total[slot], norm1_arrived[-1]) for slot in range(1, parts)]
     (up_total,) = local_call(
         functools.partial(join_up_kernel, parts),
@@ -789,9 +859,8 @@
         (meta, kvq_total[0], *send_pieces([kvq_total[s] for s in range(1, parts)], "dp")),
         [wide_like(shard, 3 * model)],
     )
-    sums = sum_all(sums, gather_direct(sums, "fsdp")[1:])
-    sums = sum_replicas(sums)
-    everywhere = sum_all(sums, gather_direct(sums, "dp")[1:])
+    sums = sum_replicas(sum_doubling(sums, "fsdp"))
+    everywhere = sum_doubling(sums, "dp")
     owned = lax.dynamic_slice(everywhere, (0, (mine * depth + deep) * shard), (6, shard))
     value_bias = lax.dynamic_slice(sums, (6, width + deep * shard), (1, shard))[0]
     query_bias = lax.dynamic_slice(sums, (6, 2 * width + deep * shard), (1, shard))[0]

time: 308 us -> 299 us (0.971)
  starting transfers between devices: 119 us -> 98.1 us
  waiting for transfers between devices: 134 us -> 118 us
  local copies, waits for them, and re-layouts: 6.3 us -> 20.4 us
  between operations: 1.14 us -> 14.8 us
  other arithmetic: 9.28 us -> 4.77 us
  Pallas kernels: 37.9 us -> 42.1 us
    ppermute x72 -> x53, starting transfers between devices: 97.3 us -> 75.6 us  [swap(): return lax.ppermute(value, axis, [(at, at ^ bit) for at in range(count)])]
    ppermute x72 -> x53, waiting for transfers between devices: 124 us -> 110 us  [swap(): return lax.ppermute(value, axis, [(at, at ^ bit) for at in range(count)])]
    unnamed x14 -> x80, local copies, waits for them, and re-layouts: 3.23 us -> 17.1 us
    pallas_call x16 -> x18, Pallas kernels: 37.9 us -> 42.1 us  [local_call(): pl.pallas_call(kernel, out_shape=tuple(results), grid=(1,), in_specs=[sme...]
    ppermute x7 -> x6, waiting for transfers between devices: 9.47 us -> 7.93 us  [shift(): lax.ppermute(value, axis, [(at, (at + by) % count) for at in range(count)])]
    ppermute x7 -> x6, starting transfers between devices: 19.4 us -> 19 us  [shift(): lax.ppermute(value, axis, [(at, (at + by) % count) for at in range(count)])]
  transfers between devices with their start and end apart: 83 -> 65, of which waited for: 31 -> 26; matrix products, arithmetic and copies ran while one was open for 2% -> 3% of each run, Pallas kernels for 10% -> 10%
where the time goes in v3:
time: 299 us; the launch traced here: 298 us
  waiting for transfers between devices  118 us (39%)
  starting transfers between devices  98.1 us (33%)
  Pallas kernels  42.1 us (14%)
  local copies, waits for them, and re-layouts  20.4 us (7%)
  between operations  14.8 us (5%)
  other arithmetic  4.77 us (2%)
    ppermute x53, waiting for transfers between devices, swap(): return lax.ppermute(value, axis, [(at, at ^ bit) for at in range(count)])  110 us
    ppermute x53, starting transfers between devices, swap(): return lax.ppermute(value, axis, [(at, at ^ bit) for at in range(count)])  75.6 us
    pallas_call x18, Pallas kernels, local_call(): pl.pallas_call(kernel, out_shape=tuple(results), grid=(1,), in_specs=[sme...  42.1 us
    ppermute x6, starting transfers between devices, shift(): lax.ppermute(value, axis, [(at, (at + by) % count) for at in range(count)])  19 us
    unnamed x80, local copies, waits for them, and re-layouts  17.1 us
    ppermute x6, waiting for transfers between devices, shift(): lax.ppermute(value, axis, [(at, (at + by) % count) for at in range(count)])  7.93 us
  transfers between devices with their start and end apart: 65, of which 26 were waited for; matrix products, arithmetic and copies ran while one was open for 3% of the time, Pallas kernels for 10%

profile of v3, /device:TPU:0, one launch (start us, length us, event | category | flops | bytes accessed | tf_op | source)
XLA Modules:
  0.0 297.9 jit_solution(15171705146270156163)
XLA Ops:
  9.6 2.6 collective-permute-start.16
  12.2 2.8 collective-permute-done.16.refs_2_
  22.0 2.3 collective-permute-start.1
  26.1 2.9 collective-permute-start.2
  31.6 7.8 %collective-permute-start.10 = (bf16[48,576]{1,0:T(8,128)(2,1)S(1)}, bf16[48,576]{1,0:T(8,128)(2,1)S(1)}, u32[]{:S(2)}, u32[]{:S(2)}) collective-permute-start(bf16[48,576]{1,0:T(8,128)(2,1)S(1)} %get-tuple-element.96), channel_id=1, source_target_pairs={{0,24},{8,16},{16,8},{24,0},{1,25},{9,17},{17,9},{25,1},{2,26},{10... | collective-permute-start | bytes 165896 | tf_op jit(solution)/shard_map/ppermute | solution.py:23
  41.5 2.5 collective-permute-done.4
  44.9 10.4 %collective-permute-start.6 = (bf16[128,768]{1,0:T(8,128)(2,1)S(1)}, bf16[128,768]{1,0:T(8,128)(2,1)S(1)}, u32[]{:S(2)}, u32[]{:S(2)}) collective-permute-start(bf16[128,768]{1,0:T(8,128)(2,1)S(1)} %shard_map.263.refs_0_), channel_id=1, source_target_pairs={{0,16},{8,24},{16,0},{24,8},{1,17},{9,25},{17,1},{25,9},{2,18},{10... | collective-permute-start | bytes 589832 | tf_op jit(solution)/shard_map/ppermute | solution.py:23
  55.9 3.8 %collective-permute-start.13 = (bf16[4,48,576]{2,1,0:T(8,128)(2,1)S(1)}, bf16[4,48,576]{2,1,0:T(8,128)(2,1)S(1)}, u32[]{:S(2)}, u32[]{:S(2)}) collective-permute-start(bf16[4,48,576]{2,1,0:T(8,128)(2,1)S(1)} %pad_maximum_fusion.refs_4_), channel_id=1, source_target_pairs={{0,3},{1,2},{2,1},{3,0},{4,7},{5,6},{6,5},{7,4},{8,11},{9,10},{10,... | collective-permute-start | bytes 663560 | tf_op jit(solution)/shard_map/ppermute | solution.py:23
  60.3 11.2 %collective-permute-done.11.refs_5_ = bf16[4,48,576]{2,1,0:T(8,128)(2,1)S(1)} collective-permute-done((bf16[4,48,576]{2,1,0:T(8,128)(2,1)S(1)}, bf16[4,48,576]{2,1,0:T(8,128)(2,1)S(1)}, u32[]{:S(2)}, u32[]{:S(2)}) %collective-permute-start.11) | collective-permute-done | bytes 221216 | tf_op jit(solution)/shard_map/ppermute | solution.py:23
  71.5 18.7 %collective-permute-done.12.refs_6_ = bf16[4,48,576]{2,1,0:T(8,128)(2,1)S(1)} collective-permute-done((bf16[4,48,576]{2,1,0:T(8,128)(2,1)S(1)}, bf16[4,48,576]{2,1,0:T(8,128)(2,1)S(1)}, u32[]{:S(2)}, u32[]{:S(2)}) %collective-permute-start.12) | collective-permute-done | bytes 221216 | tf_op jit(solution)/shard_map/ppermute | solution.py:23
  95.4 6.8 %shard_map.265 = (f32[512,192]{1,0:T(8,128)S(1)}, f32[512,128]{1,0:T(8,128)S(1)}) custom-call(s32[6]{0:T(128)S(1)} %stack.76.meta_ref.place_ref, bf16[512,576]{1,0:T(8,128)(2,1)S(1)} %get-tuple-element.97.kvq_ref.refs_0_.refs_5_), custom_call_target="tpu_custom_call" | custom-call | flops 201326592 | bytes 1245208 | tf_op jit(solution)/shard_map/pallas_call | solution.py:595
  108.6 13.3 %collective-permute-start.18 = (bf16[128,768]{1,0:T(8,128)(2,1)S(1)}, bf16[128,768]{1,0:T(8,128)(2,1)S(1)}, u32[]{:S(2)}, u32[]{:S(2)}) collective-permute-start(bf16[128,768]{1,0:T(8,128)(2,1)S(1)} %get-tuple-element.106), channel_id=1, source_target_pairs={{0,8},{8,0},{16,24},{24,16},{1,9},{9,1},{17,25},{25,17},{2,10},{10... | collective-permute-start | bytes 589832 | tf_op jit(solution)/shard_map/ppermute | solution.py:23
  124.1 5.6 %collective-permute-done.19.refs_2_ = bf16[128,768]{1,0:T(8,128)(2,1)S(1)} collective-permute-done((bf16[128,768]{1,0:T(8,128)(2,1)S(1)}, bf16[128,768]{1,0:T(8,128)(2,1)S(1)}, u32[]{:S(2)}, u32[]{:S(2)}) %collective-permute-start.19) | collective-permute-done | bytes 196640 | tf_op jit(solution)/shard_map/ppermute | solution.py:23
  129.7 2.3 collective-permute-done.20.refs_3_
  134.7 2.4 collective-permute-done.26.refs_6_
  137.7 3.6 %collective-permute-done.22.refs_2_ = bf16[128,768]{1,0:T(8,128)(2,1)S(1)} collective-permute-done((bf16[128,768]{1,0:T(8,128)(2,1)S(1)}, bf16[128,768]{1,0:T(8,128)(2,1)S(1)}, u32[]{:S(2)}, u32[]{:S(2)}) %collective-permute-start.22) | collective-permute-done | bytes 196640 | tf_op jit(solution)/shard_map/ppermute | solution.py:23
  142.7 6.0 %shard_map.270 = (f32[128,768]{1,0:T(8,128)S(1)}, bf16[128,768]{1,0:T(8,128)(2,1)S(1)}, bf16[128,768]{1,0:T(8,128)(2,1)S(1)}, bf16[128,768]{1,0:T(8,128)(2,1)S(1...) custom-call(s32[6]{0:T(128)S(1)} %stack.76.meta_ref.place_ref, ...), custom_call_target="tpu_custom_call" | custom-call | flops 1811939328 | bytes 9661464 | tf_op jit(solution)/shard_map/pallas_call | solution.py:595
  152.1 3.8 %shard_map.271 = (bf16[2,4,192,768]{3,2,1,0:T(8,128)(2,1)}, f32[128,768]{1,0:T(8,128)S(1)}, bf16[128,768]{1,0:T(8,128)(2,1)S(1)}, bf16[128,768]{1,0:T(8,128)(2,1)S(1)}, bf16[128,768]{1,0:T(8,128)(2,1)S(1)}) custom-call(s32[6]{0:T(128)S(1)} %stack.76.meta_ref.place_ref, bf16[512,768]{1,0:T(8,128)(2,1)S(1)} %get-tuple-element.112.refs_0_, ...), custom_call_target="tpu_custom_call" | custom-call | flops 1811939328 | bytes 7667736 | tf_op jit(solution)/shard_map/pallas_call | solution.py:595
  160.7 6.2 %collective-permute-done.29.refs_2_ = bf16[128,768]{1,0:T(8,128)(2,1)S(1)} collective-permute-done((bf16[128,768]{1,0:T(8,128)(2,1)}, bf16[128,768]{1,0:T(8,128)(2,1)S(1)}, u32[]{:S(2)}, u32[]{:S(2)}) %collective-permute-start.29) | collective-permute-done | bytes 196640 | tf_op jit(solution)/shard_map/ppermute | solution.py:23
  166.9 3.1 %collective-permute-done.30.refs_3_ = bf16[128,768]{1,0:T(8,128)(2,1)S(1)} collective-permute-done((bf16[128,768]{1,0:T(8,128)(2,1)}, bf16[128,768]{1,0:T(8,128)(2,1)S(1)}, u32[]{:S(2)}, u32[]{:S(2)}) %collective-permute-start.30) | collective-permute-done | bytes 196640 | tf_op jit(solution)/shard_map/ppermute | solution.py:23
  174.9 6.6 %collective-permute-done.31.refs_2_ = bf16[128,768]{1,0:T(8,128)(2,1)} collective-permute-done((bf16[128,768]{1,0:T(8,128)(2,1)}, bf16[128,768]{1,0:T(8,128)(2,1)}, u32[]{:S(2)}, u32[]{:S(2)}) %collective-permute-start.31) | collective-permute-done | bytes 196640 | tf_op jit(solution)/shard_map/ppermute | solution.py:23
  188.0 14.8 %collective-permute-start.38 = (bf16[512,384]{1,0:T(8,128)(2,1)S(1)}, bf16[512,384]{1,0:T(8,128)(2,1)S(1)}, u32[]{:S(2)}, u32[]{:S(2)}) collective-permute-start(bf16[512,384]{1,0:T(8,128)(2,1)S(1)} %bitcast.80), channel_id=1, source_target_pairs={{0,4},{4,0},{1,5},{5,1},{2,6},{6,2},{3,7},{7,3},{8,12},{12,8},{9,1... | collective-permute-start | bytes 1179656 | tf_op jit(solution)/shard_map/ppermute | solution.py:28
  202.8 6.9 %shard_map.274 = (f32[512,576]{1,0:T(8,128)S(1)}, f32[48,768]{1,0:T(8,128)S(1)}, bf16[48,768]{1,0:T(8,128)(2,1)S(1)}, bf16[48,768]{1,0:T(8,128)(2,1)S(1)}, bf16[48,768]{1,0:T(8,128)(2,1)S(1)}) custom-call(s32[6]{0:T(128)S(1)} %stack.76.meta_ref.place_ref, bf16[512,576]{1,0:T(8,128)(2,1)S(1)} %get-tuple-element.97.kvq_ref.refs_0_.refs_5_, ...), custom_call_target="tpu_custom_call" | custom-call | flops 503316480 | bytes 4366360 | tf_op jit(solution)/shard_map/pallas_call | solution.py:595
  218.0 2.4 collective-permute-start.40
  222.0 2.8 collective-permute-start.50
  225.1 2.6 collective-permute-done.40.refs_2_
  227.7 4.3 %collective-permute-done.41.refs_3_ = bf16[128,768]{1,0:T(8,128)(2,1)S(1)} collective-permute-done((bf16[128,768]{1,0:T(8,128)(2,1)S(1)}, bf16[128,768]{1,0:T(8,128)(2,1)S(1)}, u32[]{:S(2)}, u32[]{:S(2)}) %collective-permute-start.41) | collective-permute-done | bytes 196640 | tf_op jit(solution)/shard_map/ppermute | solution.py:23
  234.4 13.5 %collective-permute-done.43 = f32[8,768]{1,0:T(8,128)S(1)} collective-permute-done((f32[8,768]{1,0:T(8,128)S(1)}, f32[8,768]{1,0:T(8,128)S(1)}, u32[]{:S(2)}, u32[]{:S(2)}) %collective-permute-start.43) | collective-permute-done | bytes 24608 | tf_op jit(solution)/shard_map/ppermute | solution.py:23
  247.9 3.4 %collective-permute-start.44 = (f32[8,768]{1,0:T(8,128)S(1)}, f32[8,768]{1,0:T(8,128)S(1)}, u32[]{:S(2)}, u32[]{:S(2)}) collective-permute-start(f32[8,768]{1,0:T(8,128)S(1)} %add.133), channel_id=1, source_target_pairs={{0,2},{1,3},{2,0},{3,1},{4,6},{5,7},{6,4},{7,5},{8,10},{9,11},{10,... | collective-permute-start | bytes 73736 | tf_op jit(solution)/shard_map/ppermute | solution.py:23
  252.7 11.3 %collective-permute-done.44 = f32[8,768]{1,0:T(8,128)S(1)} collective-permute-done((f32[8,768]{1,0:T(8,128)S(1)}, f32[8,768]{1,0:T(8,128)S(1)}, u32[]{:S(2)}, u32[]{:S(2)}) %collective-permute-start.44) | collective-permute-done | bytes 24608 | tf_op jit(solution)/shard_map/ppermute | solution.py:23
  270.0 3.2 %collective-permute-done.47 = f32[8,768]{1,0:T(8,128)S(1)} collective-permute-done((f32[8,768]{1,0:T(8,128)S(1)}, f32[8,768]{1,0:T(8,128)S(1)}, u32[]{:S(2)}, u32[]{:S(2)}) %collective-permute-start.47) | collective-permute-done | bytes 24608 | tf_op jit(solution)/shard_map/ppermute | solution.py:23
  275.9 6.1 %collective-permute-done.59 = bf16[192,768]{1,0:T(8,128)(2,1)S(1)} collective-permute-done((bf16[192,768]{1,0:T(8,128)(2,1)}, bf16[192,768]{1,0:T(8,128)(2,1)S(1)}, u32[]{:S(2)}, u32[]{:S(2)}) %collective-permute-start.59) | collective-permute-done | bytes 294944 | tf_op jit(solution)/shard_map/ppermute | solution.py:28
  (239 shorter events, 87.1 us)
Async XLA Ops:
  7.3 96.5 %all-gather.2.cloned.1.call-start = ((), (), s32[]{:S(2)}) async-start(), calls=%async_computation.1 | async-start | bytes 3096576 | tf_op jit(solution)/shard_map/all_gather | solution.py:674
  19.7 254.1 %reduce-scatter.2.cloned.1.call-start = ((), (), s32[]{:S(2)}) async-start(), calls=%async_computation.2 | async-start | bytes 2654208 | tf_op jit(solution)/shard_map/reduce_scatter | solution.py:761
  30.9 13.2 %collective-permute-start = (bf16[128,768]{1,0:T(8,128)(2,1)S(1)}, bf16[128,768]{1,0:T(8,128)(2,1)S(1)}, u32[]{:S(2)}, u32[]{:S(2)}) collective-permute-start(bf16[128,768]{1,0:T(8,128)(2,1)S(1)} %bitcast_convert_fusion.1), channel_id=1, source_target_pairs={{0,0},{1,8},{2,16},{3,24},{8,1},{9,9},{10,17},{11,25},{16,2},{17,1... | collective-permute-start | bytes 589832 | tf_op jit(solution)/shard_map/ppermute | solution.py:34
  31.6 23.7 %collective-permute-start.10 = (bf16[48,576]{1,0:T(8,128)(2,1)S(1)}, bf16[48,576]{1,0:T(8,128)(2,1)S(1)}, u32[]{:S(2)}, u32[]{:S(2)}) collective-permute-start(bf16[48,576]{1,0:T(8,128)(2,1)S(1)} %get-tuple-element.96), channel_id=1, source_target_pairs={{0,24},{8,16},{16,8},{24,0},{1,25},{9,17},{17,9},{25,1},{2,26},{10... | collective-permute-start | bytes 165896 | tf_op jit(solution)/shard_map/ppermute | solution.py:23
  39.4 15.9 %collective-permute-start.9 = (bf16[48,576]{1,0:T(8,128)(2,1)S(1)}, bf16[48,576]{1,0:T(8,128)(2,1)S(1)}, u32[]{:S(2)}, u32[]{:S(2)}) collective-permute-start(bf16[48,576]{1,0:T(8,128)(2,1)S(1)} %get-tuple-element.95), channel_id=1, source_target_pairs={{0,16},{8,24},{16,0},{24,8},{1,17},{9,25},{17,1},{25,9},{2,18},{10... | collective-permute-start | bytes 165896 | tf_op jit(solution)/shard_map/ppermute | solution.py:23
  39.4 15.9 %collective-permute-start.8 = (bf16[48,576]{1,0:T(8,128)(2,1)S(1)}, bf16[48,576]{1,0:T(8,128)(2,1)S(1)}, u32[]{:S(2)}, u32[]{:S(2)}) collective-permute-start(bf16[48,576]{1,0:T(8,128)(2,1)S(1)} %get-tuple-element.94), channel_id=1, source_target_pairs={{0,8},{8,0},{16,24},{24,16},{1,9},{9,1},{17,25},{25,17},{2,10},{10... | collective-permute-start | bytes 165896 | tf_op jit(solution)/shard_map/ppermute | solution.py:23
  44.9 14.9 %collective-permute-start.6 = (bf16[128,768]{1,0:T(8,128)(2,1)S(1)}, bf16[128,768]{1,0:T(8,128)(2,1)S(1)}, u32[]{:S(2)}, u32[]{:S(2)}) collective-permute-start(bf16[128,768]{1,0:T(8,128)(2,1)S(1)} %shard_map.263.refs_0_), channel_id=1, source_target_pairs={{0,16},{8,24},{16,0},{24,8},{1,17},{9,25},{17,1},{25,9},{2,18},{10... | collective-permute-start | bytes 589832 | tf_op jit(solution)/shard_map/ppermute | solution.py:23
  55.3 16.2 %collective-permute-start.11 = (bf16[4,48,576]{2,1,0:T(8,128)(2,1)S(1)}, bf16[4,48,576]{2,1,0:T(8,128)(2,1)S(1)}, u32[]{:S(2)}, u32[]{:S(2)}) collective-permute-start(bf16[4,48,576]{2,1,0:T(8,128)(2,1)S(1)} %pad_maximum_fusion.refs_4_), channel_id=1, source_target_pairs={{0,1},{1,0},{2,3},{3,2},{4,5},{5,4},{6,7},{7,6},{8,9},{9,8},{10,11... | collective-permute-start | bytes 663560 | tf_op jit(solution)/shard_map/ppermute | solution.py:23
  55.9 34.3 %collective-permute-start.12 = (bf16[4,48,576]{2,1,0:T(8,128)(2,1)S(1)}, bf16[4,48,576]{2,1,0:T(8,128)(2,1)S(1)}, u32[]{:S(2)}, u32[]{:S(2)}) collective-permute-start(bf16[4,48,576]{2,1,0:T(8,128)(2,1)S(1)} %pad_maximum_fusion.refs_4_), channel_id=1, source_target_pairs={{0,2},{1,3},{2,0},{3,1},{4,6},{5,7},{6,4},{7,5},{8,10},{9,11},{10,... | collective-permute-start | bytes 663560 | tf_op jit(solution)/shard_map/ppermute | solution.py:23
  55.9 34.3 %collective-permute-start.13 = (bf16[4,48,576]{2,1,0:T(8,128)(2,1)S(1)}, bf16[4,48,576]{2,1,0:T(8,128)(2,1)S(1)}, u32[]{:S(2)}, u32[]{:S(2)}) collective-permute-start(bf16[4,48,576]{2,1,0:T(8,128)(2,1)S(1)} %pad_maximum_fusion.refs_4_), channel_id=1, source_target_pairs={{0,3},{1,2},{2,1},{3,0},{4,7},{5,6},{6,5},{7,4},{8,11},{9,10},{10,... | collective-permute-start | bytes 663560 | tf_op jit(solution)/shard_map/ppermute | solution.py:23
  59.8 30.5 %collective-permute-start.5 = (bf16[128,768]{1,0:T(8,128)(2,1)S(1)}, bf16[128,768]{1,0:T(8,128)(2,1)S(1)}, u32[]{:S(2)}, u32[]{:S(2)}) collective-permute-start(bf16[128,768]{1,0:T(8,128)(2,1)S(1)} %shard_map.263.refs_0_), channel_id=1, source_target_pairs={{0,8},{8,0},{16,24},{24,16},{1,9},{9,1},{17,25},{25,17},{2,10},{10... | collective-permute-start | bytes 589832 | tf_op jit(solution)/shard_map/ppermute | solution.py:23
  59.8 30.5 %collective-permute-start.7 = (bf16[128,768]{1,0:T(8,128)(2,1)S(1)}, bf16[128,768]{1,0:T(8,128)(2,1)S(1)}, u32[]{:S(2)}, u32[]{:S(2)}) collective-permute-start(bf16[128,768]{1,0:T(8,128)(2,1)S(1)} %collective-permute-done.6.refs_2_), channel_id=1, source_target_pairs={{0,8},{8,0},{16,24},{24,16},{1,9},{9,1},{17,25},{25,17},{2,10},{10... | collective-permute-start | bytes 589832 | tf_op jit(solution)/shard_map/ppermute | solution.py:23
  92.6 11.2 %collective-permute-start.14 = (bf16[512,384]{1,0:T(8,128)(2,1)S(1)}, bf16[512,384]{1,0:T(8,128)(2,1)S(1)}, u32[]{:S(2)}, u32[]{:S(2)}) collective-permute-start(bf16[512,384]{1,0:T(8,128)(2,1)S(1)} %get-tuple-element.98), channel_id=1, source_target_pairs={{0,4},{4,0},{1,5},{5,1},{2,6},{6,2},{3,7},{7,3},{8,12},{12,8},{9,1... | collective-permute-start | bytes 1179656 | tf_op jit(solution)/shard_map/ppermute | solution.py:28
  94.1 29.2 %collective-permute-start.24 = (bf16[128,768]{1,0:T(8,128)(2,1)S(1)}, bf16[128,768]{1,0:T(8,128)(2,1)}, u32[]{:S(2)}, u32[]{:S(2)}) collective-permute-start(bf16[128,768]{1,0:T(8,128)(2,1)S(1)} %bitcast_convert_fusion), channel_id=1, source_target_pairs={{0,0},{1,8},{2,16},{3,24},{8,1},{9,9},{10,17},{11,25},{16,2},{17,1... | collective-permute-start | bytes 589832 | tf_op jit(solution)/shard_map/ppermute | solution.py:34
  108.6 15.5 %collective-permute-start.18 = (bf16[128,768]{1,0:T(8,128)(2,1)S(1)}, bf16[128,768]{1,0:T(8,128)(2,1)S(1)}, u32[]{:S(2)}, u32[]{:S(2)}) collective-permute-start(bf16[128,768]{1,0:T(8,128)(2,1)S(1)} %get-tuple-element.106), channel_id=1, source_target_pairs={{0,8},{8,0},{16,24},{24,16},{1,9},{9,1},{17,25},{25,17},{2,10},{10... | collective-permute-start | bytes 589832 | tf_op jit(solution)/shard_map/ppermute | solution.py:23
  123.3 13.9 %collective-permute-start.26 = (bf16[128,768]{1,0:T(8,128)(2,1)}, bf16[128,768]{1,0:T(8,128)(2,1)S(1)}, u32[]{:S(2)}, u32[]{:S(2)}) collective-permute-start(bf16[128,768]{1,0:T(8,128)(2,1)} %collective-permute-done.24.refs_4_.refs_6_), channel_id=1, source_target_pairs={{0,16},{8,24},{16,0},{24,8},{1,17},{9,25},{17,1},{25,9},{2,18},{10... | collective-permute-start | bytes 589832 | tf_op jit(solution)/shard_map/ppermute | solution.py:23
  183.2 27.5 %collective-permute-start.35 = (bf16[128,768]{1,0:T(8,128)(2,1)}, bf16[128,768]{1,0:T(8,128)(2,1)S(1)}, u32[]{:S(2)}, u32[]{:S(2)}) collective-permute-start(bf16[128,768]{1,0:T(8,128)(2,1)} %copy-done.22), channel_id=1, source_target_pairs={{0,24},{8,16},{16,8},{24,0},{1,25},{9,17},{17,9},{25,1},{2,26},{10... | collective-permute-start | bytes 589832 | tf_op jit(solution)/shard_map/ppermute | solution.py:23
  183.9 28.3 %collective-permute-start.34 = (bf16[128,768]{1,0:T(8,128)(2,1)}, bf16[128,768]{1,0:T(8,128)(2,1)S(1)}, u32[]{:S(2)}, u32[]{:S(2)}) collective-permute-start(bf16[128,768]{1,0:T(8,128)(2,1)} %copy-done.21), channel_id=1, source_target_pairs={{0,16},{8,24},{16,0},{24,8},{1,17},{9,25},{17,1},{25,9},{2,18},{10... | collective-permute-start | bytes 589832 | tf_op jit(solution)/shard_map/ppermute | solution.py:23
  185.0 29.2 %collective-permute-start.33 = (bf16[128,768]{1,0:T(8,128)(2,1)}, bf16[128,768]{1,0:T(8,128)(2,1)S(1)}, u32[]{:S(2)}, u32[]{:S(2)}) collective-permute-start(bf16[128,768]{1,0:T(8,128)(2,1)} %copy-done.20), channel_id=1, source_target_pairs={{0,8},{8,0},{16,24},{24,16},{1,9},{9,1},{17,25},{25,17},{2,10},{10... | collective-permute-start | bytes 589832 | tf_op jit(solution)/shard_map/ppermute | solution.py:23
  188.0 27.1 %collective-permute-start.38 = (bf16[512,384]{1,0:T(8,128)(2,1)S(1)}, bf16[512,384]{1,0:T(8,128)(2,1)S(1)}, u32[]{:S(2)}, u32[]{:S(2)}) collective-permute-start(bf16[512,384]{1,0:T(8,128)(2,1)S(1)} %bitcast.80), channel_id=1, source_target_pairs={{0,4},{4,0},{1,5},{5,1},{2,6},{6,2},{3,7},{7,3},{8,12},{12,8},{9,1... | collective-permute-start | bytes 1179656 | tf_op jit(solution)/shard_map/ppermute | solution.py:28
  214.3 19.2 %collective-permute-start.37 = (bf16[128,768]{1,0:T(8,128)(2,1)S(1)}, bf16[128,768]{1,0:T(8,128)(2,1)S(1)}, u32[]{:S(2)}, u32[]{:S(2)}) collective-permute-start(bf16[128,768]{1,0:T(8,128)(2,1)S(1)} %add_convert_fusion.2), channel_id=1, source_target_pairs={{0,0},{1,8},{2,16},{3,24},{8,1},{9,9},{10,17},{11,25},{16,2},{17,1... | collective-permute-start | bytes 589832 | tf_op jit(solution)/shard_map/ppermute | solution.py:34
  220.4 11.5 %collective-permute-start.41 = (bf16[128,768]{1,0:T(8,128)(2,1)S(1)}, bf16[128,768]{1,0:T(8,128)(2,1)S(1)}, u32[]{:S(2)}, u32[]{:S(2)}) collective-permute-start(bf16[128,768]{1,0:T(8,128)(2,1)S(1)} %get-tuple-element.144), channel_id=1, source_target_pairs={{0,24},{8,16},{16,8},{24,0},{1,25},{9,17},{17,9},{25,1},{2,26},{10... | collective-permute-start | bytes 589832 | tf_op jit(solution)/shard_map/ppermute | solution.py:23
  222.0 42.4 %collective-permute-start.50 = (bf16[4,48,576]{2,1,0:T(8,128)(2,1)S(1)}, bf16[4,48,576]{2,1,0:T(8,128)(2,1)S(1)}, u32[]{:S(2)}, u32[]{:S(2)}) collective-permute-start(bf16[4,48,576]{2,1,0:T(8,128)(2,1)S(1)} %get-tuple-element.156), channel_id=1, source_target_pairs={{0,3},{1,2},{2,1},{3,0},{4,7},{5,6},{6,5},{7,4},{8,11},{9,10},{10,... | collective-permute-start | bytes 663560 | tf_op jit(solution)/shard_map/ppermute | solution.py:23
  224.8 39.5 %collective-permute-start.49 = (bf16[4,48,576]{2,1,0:T(8,128)(2,1)S(1)}, bf16[4,48,576]{2,1,0:T(8,128)(2,1)S(1)}, u32[]{:S(2)}, u32[]{:S(2)}) collective-permute-start(bf16[4,48,576]{2,1,0:T(8,128)(2,1)S(1)} %get-tuple-element.155), channel_id=1, source_target_pairs={{0,2},{1,3},{2,0},{3,1},{4,6},{5,7},{6,4},{7,5},{8,10},{9,11},{10,... | collective-permute-start | bytes 663560 | tf_op jit(solution)/shard_map/ppermute | solution.py:23
  227.7 36.7 %collective-permute-start.48 = (bf16[4,48,576]{2,1,0:T(8,128)(2,1)S(1)}, bf16[4,48,576]{2,1,0:T(8,128)(2,1)S(1)}, u32[]{:S(2)}, u32[]{:S(2)}) collective-permute-start(bf16[4,48,576]{2,1,0:T(8,128)(2,1)S(1)} %get-tuple-element.154), channel_id=1, source_target_pairs={{0,1},{1,0},{2,3},{3,2},{4,5},{5,4},{6,7},{7,6},{8,9},{9,8},{10,11... | collective-permute-start | bytes 663560 | tf_op jit(solution)/shard_map/ppermute | solution.py:23
  232.0 19.4 %collective-permute-start.58 = (bf16[48,768]{1,0:T(8,128)(2,1)S(1)}, bf16[48,768]{1,0:T(8,128)(2,1)S(1)}, u32[]{:S(2)}, u32[]{:S(2)}) collective-permute-start(bf16[48,768]{1,0:T(8,128)(2,1)S(1)} %add_convert_fusion.3), channel_id=1, source_target_pairs={{0,4},{4,0},{1,5},{5,1},{2,6},{6,2},{3,7},{7,3},{8,12},{12,8},{9,1... | collective-permute-start | bytes 221192 | tf_op jit(solution)/shard_map/ppermute | solution.py:28
  233.5 14.4 %collective-permute-start.43 = (f32[8,768]{1,0:T(8,128)S(1)}, f32[8,768]{1,0:T(8,128)S(1)}, u32[]{:S(2)}, u32[]{:S(2)}) collective-permute-start(f32[8,768]{1,0:T(8,128)S(1)} %get-tuple-element.150), channel_id=1, source_target_pairs={{0,1},{1,0},{2,3},{3,2},{4,5},{5,4},{6,7},{7,6},{8,9},{9,8},{10,11... | collective-permute-start | bytes 73736 | tf_op jit(solution)/shard_map/ppermute | solution.py:23
  247.9 16.1 %collective-permute-start.44 = (f32[8,768]{1,0:T(8,128)S(1)}, f32[8,768]{1,0:T(8,128)S(1)}, u32[]{:S(2)}, u32[]{:S(2)}) collective-permute-start(f32[8,768]{1,0:T(8,128)S(1)} %add.133), channel_id=1, source_target_pairs={{0,2},{1,3},{2,0},{3,1},{4,6},{5,7},{6,4},{7,5},{8,10},{9,11},{10,... | collective-permute-start | bytes 73736 | tf_op jit(solution)/shard_map/ppermute | solution.py:23
  252.0 31.9 %collective-permute-start.42 = (bf16[128,768]{1,0:T(8,128)(2,1)S(1)}, bf16[128,768]{1,0:T(8,128)(2,1)S(1)}, u32[]{:S(2)}, u32[]{:S(2)}) collective-permute-start(bf16[128,768]{1,0:T(8,128)(2,1)S(1)} %get-tuple-element.149), channel_id=1, source_target_pairs={{0,0},{1,8},{2,16},{3,24},{8,1},{9,9},{10,17},{11,25},{16,2},{17,1... | collective-permute-start | bytes 589832 | tf_op jit(solution)/shard_map/ppermute | solution.py:34
  273.9 10.3 %collective-permute-start.52 = (bf16[48,576]{1,0:T(8,128)(2,1)S(1)}, bf16[48,576]{1,0:T(8,128)(2,1)S(1)}, u32[]{:S(2)}, u32[]{:S(2)}) collective-permute-start(bf16[48,576]{1,0:T(8,128)(2,1)S(1)} %get-tuple-element.175), channel_id=1, source_target_pairs={{0,8},{8,0},{16,24},{24,16},{1,9},{9,1},{17,25},{25,17},{2,10},{10... | collective-permute-start | bytes 165896 | tf_op jit(solution)/shard_map/ppermute | solution.py:23
  274.0 12.5 %collective-permute-start.53 = (bf16[48,576]{1,0:T(8,128)(2,1)S(1)}, bf16[48,576]{1,0:T(8,128)(2,1)S(1)}, u32[]{:S(2)}, u32[]{:S(2)}) collective-permute-start(bf16[48,576]{1,0:T(8,128)(2,1)S(1)} %get-tuple-element.174), channel_id=1, source_target_pairs={{0,16},{8,24},{16,0},{24,8},{1,17},{9,25},{17,1},{25,9},{2,18},{10... | collective-permute-start | bytes 165896 | tf_op jit(solution)/shard_map/ppermute | solution.py:23
  274.1 12.5 %collective-permute-start.54 = (bf16[48,576]{1,0:T(8,128)(2,1)S(1)}, bf16[48,576]{1,0:T(8,128)(2,1)S(1)}, u32[]{:S(2)}, u32[]{:S(2)}) collective-permute-start(bf16[48,576]{1,0:T(8,128)(2,1)S(1)} %get-tuple-element.173), channel_id=1, source_target_pairs={{0,24},{8,16},{16,8},{24,0},{1,25},{9,17},{17,9},{25,1},{2,26},{10... | collective-permute-start | bytes 165896 | tf_op jit(solution)/shard_map/ppermute | solution.py:23
  (73 other events, 576.4 us)
Sparse Core Ops, SparseCore 0:
  19.8 83.0 all-gather.1
  158.9 90.8 reduce-scatter.1

commit v4 on v2

--- a/solution.py
+++ b/solution.py
@@ -12,6 +12,7 @@
 SCALE = HEAD_DIM ** (-0.5)
 MASKED = -1e30
 CHUNK = 64
+VMEM_BYTES = 16 * 1024 * 1024
 GELU_SCALE = 0.7978845608
 GELU_CUBE = 0.044715
 LOW = jnp.bfloat16
@@ -52,6 +53,14 @@
 
 def gather_direct(block, axis):
     return [block] + [swap(block, axis, slot) for slot in range(1, lax.axis_size(axis))]
+
+
+def sum_doubling(value, axis):
+    bit = 1
+    while bit < lax.axis_size(axis):
+        value = value + swap(value, axis, bit)
+        bit *= 2
+    return value
 
 
 def sum_all(kept, arrived):
@@ -327,10 +336,22 @@
             keep_ref[...] = block
 
 
-def split_kernel(parts, width, meta_ref, qkv_ref, up_ref, *outs):
-    kvq_outs, up_outs = take(outs, parts, parts)
+def half_kernel(parts, meta_ref, *refs):
+    up, down_weight, out = take(refs, parts, None, None)
+    shard = up[0].shape[0]
+
+    @pl.when(meta_ref[parts] == 0)
+    def _up():
+        for slot in range(parts):
+            out[slot * shard : (slot + 1) * shard, :] = up[slot][...]
+
+    @pl.when(meta_ref[parts] != 0)
+    def _down():
+        out[...] = down_weight[...].astype(LOW)
+
+
+def split_qkv_kernel(parts, width, meta_ref, qkv_ref, *outs):
     model = parts * width
-    part = up_ref.shape[1] // parts
     for case in range(parts):
 
         @pl.when(meta_ref[0] == case)
@@ -339,10 +360,16 @@
                 owner = case ^ slot
                 for at, first in enumerate((model, 2 * model, 0)):
                     start = first + owner * width
-                    kvq_outs[slot][:, at * width : (at + 1) * width] = qkv_ref[
+                    outs[slot][:, at * width : (at + 1) * width] = qkv_ref[
                         :, start : start + width
                     ].astype(LOW)
-                up_outs[slot][...] = up_ref[:, owner * part : (owner + 1) * part].astype(LOW)
+
+
+def split_up_kernel(parts, meta_ref, up_ref, *outs):
+    part = up_ref.shape[1] // parts
+    for slot in range(parts):
+        start = pl.multiple_of(meta_ref[slot] * part, 128)
+        outs[slot][...] = up_ref[:, pl.ds(start, part)].astype(LOW)
 
 
 def join_qkv_kernel(parts, width, meta_ref, *refs):
@@ -410,16 +437,26 @@
     out[...] = (hat * vectors[2:3, :] + vectors[3:4, :]).astype(LOW)
 
 
-def feed_kernel(parts, depth, meta_ref, *refs):
+def feed_kernel(parts, depth, halves, meta_ref, *refs):
     (
-        norm, branch, up, down, vectors, keep, sends, hidden, inner_grad, norm_all, branch_all,
+        norm, branch, own, other, vectors, keep, sends, hidden, inner_grad, norm_all, branch_all,
         down_all, up_bias, up_all, inner, grad,
-    ) = take(
-        refs, parts, parts, depth, depth, None, None, parts - 1, None, None, None, None, None,
-        None, None, None, None,
-    )
-    place_blocks(meta_ref, parts, depth, up, up_all)
-    place_shards(meta_ref, parts, down, down_all)
+    ) = take(refs, parts, parts, depth, depth, None, None, parts - 1, *([None] * 9))
+
+    def place(up, down):
+        shard = up_all.shape[0] // (parts * depth)
+        for deep in range(depth):
+            member = meta_ref[parts + 1] ^ deep
+            for slot in range(parts):
+                start = pl.multiple_of((meta_ref[slot] * depth + member) * shard, 16)
+                up_all[pl.ds(start, shard), :] = up[deep][slot * shard : (slot + 1) * shard, :]
+        place_shards(meta_ref, parts, down, down_all)
+
+    if halves:
+        pl.when(meta_ref[parts] == 0)(lambda: place(own, other))
+        pl.when(meta_ref[parts] != 0)(lambda: place(other, own))
+    else:
+        place(own, other)
     stack_rows(norm, norm_all)
     stack_rows(branch, branch_all)
     inner[...] = matmul_nn(norm_all[...], up_all[...])
@@ -444,18 +481,43 @@
     emit_rows(matmul_nt(inner_grad[...], up_all[...]), keep, sends)
 
 
-def feed_grad_kernel(parts, depth, meta_ref, *refs):
-    (
-        hidden, inner_grad, norm_all, branch_all, down_all, down_keep, down_sends, up_keep,
-        up_sends, fed_keep, fed_sends, whole,
-    ) = take(
-        refs, None, None, None, None, None, None, depth - 1, None, depth - 1, None, parts - 1, None
-    )
-    whole[...] = matmul_tn(hidden[...], branch_all[...])
-    emit_shards(meta_ref, parts, whole, down_keep, down_sends)
-    whole[...] = matmul_tn(norm_all[...], inner_grad[...])
-    emit_blocks(meta_ref, parts, depth, whole, up_keep, up_sends)
+def feed_grad_kernel(parts, depth, halves, meta_ref, *refs):
+    hidden, inner_grad, norm_all, branch_all, down_all, kept, sent, fed_keep, fed_sends, whole = (
+        take(refs, *([None] * 8), parts - 1, None)
+    )
+    hidden_shard = hidden.shape[1] // depth
+    shard = norm_all.shape[1] // (parts * depth)
+
+    def emit(half, out):
+        for deep in range(depth):
+            member = meta_ref[parts + 1] ^ deep
+            if half:
+                start = pl.multiple_of(member * hidden_shard, 16)
+                out[deep] = whole[pl.ds(start, hidden_shard), :].astype(out.dtype)
+            else:
+                for slot in range(parts):
+                    start = pl.multiple_of((meta_ref[slot] * depth + member) * shard, 16)
+                    out[deep, slot * shard : (slot + 1) * shard] = whole[
+                        pl.ds(start, shard), :
+                    ].astype(out.dtype)
+
+    for half in range(2):
+        if half:
+            whole[...] = matmul_tn(hidden[...], branch_all[...])
+        else:
+            whole[...] = matmul_tn(norm_all[...], inner_grad[...])
+        if halves:
+            pl.when(meta_ref[parts] == half)(functools.partial(emit, half, kept))
+            pl.when(meta_ref[parts] != half)(functools.partial(emit, half, sent))
+        else:
+            emit(half, sent if half else kept)
     emit_rows(matmul_nn(hidden[...], down_all[...]), fed_keep, fed_sends)
+
+
+def fold_kernel(meta_ref, kept_ref, arrived_ref, keep_ref, *send_refs):
+    keep_ref[...] = kept_ref[0] + arrived_ref[0].astype(WIDE)
+    for deep, send in enumerate(send_refs, 1):
+        send[...] = (kept_ref[deep] + arrived_ref[deep].astype(WIDE)).astype(LOW)
 
 
 def second_norm_grad_kernel(parts, meta_ref, *refs):
@@ -547,7 +609,7 @@
         in_specs=[smem] + [vmem] * (len(operands) - 1),
         out_specs=tuple([vmem] * len(results)),
         scratch_shapes=list(scratch),
-        compiler_params=pltpu.CompilerParams(vmem_limit_bytes=48 * 1024 * 1024),
+        compiler_params=pltpu.CompilerParams(vmem_limit_bytes=VMEM_BYTES),
         cost_estimate=pl.CostEstimate(flops=flops, bytes_accessed=moved, transcendentals=0),
     )(*operands)
 
@@ -581,38 +643,50 @@
         [mine ^ slot for slot in range(parts)] + [lax.axis_index("ctx"), deep]
     ).astype(jnp.int32)
 
-    token_rows = transpose_homes(tokens[0].astype(LOW))
-
-    split = local_call(
-        functools.partial(split_kernel, parts, width),
-        (meta, qkv_weight, fc1_weight),
-        [low_like(shard, 3 * width)] * parts + [low_like(shard, hidden_part)] * parts,
-    )
-    kvq_split, up_split = split[:parts], split[parts:]
+    kvq_split = local_call(
+        functools.partial(split_qkv_kernel, parts, width),
+        (meta, qkv_weight),
+        [low_like(shard, 3 * width)] * parts,
+    )
     kvq_rows = jnp.stack([kvq_split[0]] + send_pieces(kvq_split[1:], "dp"))
     kvq_pieces = gather_direct(kvq_rows, "fsdp")
 
-    low_vectors = [
-        each.astype(LOW).astype(WIDE)
-        for each in (ln1_gain, ln1_bias, ln2_gain, ln2_bias, out_bias, fc2_bias)
-    ]
+    token_rows = transpose_homes(after(tokens[0].astype(LOW), kvq_split[0]))
+
+    low_vectors = jnp.stack([ln1_gain, ln1_bias, ln2_gain, ln2_bias, out_bias, fc2_bias])
     vectors = jnp.zeros((8, model), WIDE)
     vectors = lax.dynamic_update_slice(
-        vectors, jnp.stack(low_vectors), (0, (mine * depth + deep) * shard)
+        vectors, low_vectors.astype(LOW).astype(WIDE), (0, (mine * depth + deep) * shard)
     )
     for row, first, part in (
         (6, width, v_bias), (6, 2 * width, q_bias), (7, 0, fc1_bias),
     ):
         part = part.astype(LOW).astype(WIDE)[None]
         vectors = lax.dynamic_update_slice(vectors, part, (row, first + deep * part.shape[1]))
-    vectors = sum_all(vectors, gather_direct(vectors, "fsdp")[1:])
-    everywhere = sum_all(vectors, gather_direct(vectors, "dp")[1:])
+    vectors = sum_doubling(after(vectors, kvq_split[0]), "fsdp")
+    everywhere = sum_doubling(vectors, "dp")
     vectors = jnp.where(jnp.arange(8)[:, None] < 6, everywhere, vectors)
 
-    up_rows = jnp.stack([up_split[0]] + send_pieces(up_split[1:], "dp"))
+    halves = contexts == 2
+    up_split = local_call(
+        functools.partial(split_up_kernel, parts),
+        (meta, after(fc1_weight, kvq_rows)),
+        [low_like(shard, hidden_part)] * parts,
+    )
+    up_parts = [up_split[0]] + send_pieces(up_split[1:], "dp")
     out_pieces = gather_direct(after(out_weight.astype(LOW), kvq_pieces[-1]), "fsdp")
-    up_pieces = gather_direct(after(up_rows, kvq_pieces[-1]), "fsdp")
-    down_pieces = gather_direct(after(fc2_weight.astype(LOW), kvq_pieces[-1]), "fsdp")
+    grad_rows = transpose_homes(after(cotangent[0].astype(LOW), kvq_pieces[-1]))
+    if halves:
+        (half,) = local_call(
+            functools.partial(half_kernel, parts),
+            (meta, *up_parts, fc2_weight),
+            [low_like(hidden_shard, model)],
+        )
+        own_half = gather_direct(after(half, out_pieces[-1]), "fsdp")
+        other_half = [shift(piece, "ctx", 1) for piece in own_half]
+    else:
+        own_half = gather_direct(jnp.concatenate(up_parts), "fsdp")
+        other_half = gather_direct(fc2_weight.astype(LOW), "fsdp")
 
     (norm1,) = local_call(
         first_norm_kernel, (meta, token_rows, vectors), [low_like(rows, model)]
@@ -631,7 +705,6 @@
     )
     kv_earlier = jnp.stack([shift(kv, "ctx", by) for by in range(1, contexts)])
 
-    grad_rows = transpose_homes(after(cotangent[0].astype(LOW), token_rows))
     branch_pieces = gather_pieces(after(grad_rows, norm1_pieces[-1]))
 
     score_flops = 2 * group * group * width
@@ -667,8 +740,8 @@
 
     norm2_pieces = gather_pieces(norm2)
     norm2_keep, *rest = local_call(
-        functools.partial(feed_kernel, parts, depth),
-        (meta, *norm2_pieces, *branch_pieces, *up_pieces, *down_pieces, vectors),
+        functools.partial(feed_kernel, parts, depth, halves),
+        (meta, *norm2_pieces, *branch_pieces, *own_half, *other_half, vectors),
         [wide_like(rows, model)]
         + [low_like(rows, model)] * (parts - 1)
         + [low_like(group, hidden_part)] * 2
@@ -684,20 +757,17 @@
     norm2_sends = rest[: parts - 1]
     hidden, inner_grad, norm2_all, branch_all, down_matrix, up_bias = rest[parts - 1 :]
     norm2_arrived = send_pieces(norm2_sends, "dp")
-    feed_grads = local_call(
-        functools.partial(feed_grad_kernel, parts, depth),
+    kept_half, sent_half, fed_keep, *fed_sends = local_call(
+        functools.partial(feed_grad_kernel, parts, depth, halves),
         (meta, hidden, inner_grad, norm2_all, branch_all, down_matrix),
-        [wide_like(hidden_shard, model)]
-        + [low_like(hidden_shard, model)] * (depth - 1)
-        + [wide_like(parts, shard, hidden_part)]
-        + [low_like(parts, shard, hidden_part)] * (depth - 1)
-        + [wide_like(rows, model)]
+        [
+            wide_like(depth, hidden_shard, model),
+            low_like(depth, hidden_shard, model),
+            wide_like(rows, model),
+        ]
         + [low_like(rows, model)] * (parts - 1),
         [pltpu.VMEM((max(model, hidden_part), max(model, hidden_part)), WIDE)],
         flops=6 * group * model * hidden_part,
-    )
-    down_keep, down_sends, up_keep, up_sends, fed_keep, fed_sends = take(
-        feed_grads, None, depth - 1, None, depth - 1, None, parts - 1
     )
     attn_grad, mixed_part, sums = local_call(
         functools.partial(second_norm_grad_kernel, parts),
@@ -705,8 +775,14 @@
         [low_like(rows, model), wide_like(rows, model), wide_like(8, model)],
     )
     attn_pieces = gather_pieces(attn_grad)
-    down_arrived = send_pieces(down_sends, "fsdp")
-    up_arrived = send_pieces(up_sends, "fsdp")
+    if halves:
+        half_arrived = shift(sent_half, "ctx", 1)
+        half_keep, *half_sends = local_call(
+            fold_kernel,
+            (meta, kept_half, after(half_arrived, attn_pieces[-1])),
+            [wide_like(hidden_shard, model)] + [low_like(hidden_shard, model)] * (depth - 1),
+        )
+        half_pieces = send_pieces(half_sends, "fsdp")
     fed_arrived = send_pieces(
         lax.optimization_barrier((*fed_sends, attn_pieces[-1]))[: parts - 1], "dp"
     )
@@ -774,9 +850,20 @@
         low = sum_all(keep, pieces).astype(LOW)
         return sum_replicas(after(low, *later) if later else low)
 
-    down_total = owner_sum(down_keep, down_arrived, kv_arrived)
-    up_total = owner_sum(up_keep, up_arrived, kv_arrived).astype(LOW)
     out_total = owner_sum(out_keep, out_arrived, kv_arrived)
+    if halves:
+        mine_half = sum_all(half_keep, half_pieces).astype(LOW)
+        arrived_half = shift(after(mine_half, kv_arrived), "ctx", 1)
+        first = lax.axis_index("ctx") == 0
+        up_total = jnp.where(first, mine_half, arrived_half)
+        down_total = jnp.where(first, arrived_half, mine_half)
+    else:
+        up_total, down_total = [
+            owner_sum(half[0].astype(WIDE), send_pieces(list(half[1:].astype(LOW)), "fsdp"))
+            for half in (kept_half, sent_half)
+        ]
+    up_total = up_total.astype(LOW).reshape(parts, shard, hidden_part)
+    down_total = down_total.astype(WIDE)
     up_sends = [after(up_total[slot], norm1_arrived[-1]) for slot in range(1, parts)]
     (up_total,) = local_call(
         functools.partial(join_up_kernel, parts),
@@ -789,9 +876,8 @@
         (meta, kvq_total[0], *send_pieces([kvq_total[s] for s in range(1, parts)], "dp")),
         [wide_like(shard, 3 * model)],
     )
-    sums = sum_all(sums, gather_direct(sums, "fsdp")[1:])
-    sums = sum_replicas(sums)
-    everywhere = sum_all(sums, gather_direct(sums, "dp")[1:])
+    sums = sum_replicas(sum_doubling(sums, "fsdp"))
+    everywhere = sum_doubling(sums, "dp")
     owned = lax.dynamic_slice(everywhere, (0, (mine * depth + deep) * shard), (6, shard))
     value_bias = lax.dynamic_slice(sums, (6, width + deep * shard), (1, shard))[0]
     query_bias = lax.dynamic_slice(sums, (6, 2 * width + deep * shard), (1, shard))[0]

time: 308 us -> 302 us (0.981); the launches traced: 308 us -> 297 us
  waiting for transfers between devices: 134 us -> 120 us
  local copies, waits for them, and re-layouts: 6.3 us -> 16.7 us
  starting transfers between devices: 119 us -> 111 us
    ppermute x72 -> x62, waiting for transfers between devices: 124 us -> 80.7 us  [swap(): return lax.ppermute(value, axis, [(at, at ^ bit) for at in range(count)])]
    ppermute x7 -> x11, waiting for transfers between devices: 9.47 us -> 38.8 us  [shift(): lax.ppermute(value, axis, [(at, (at + by) % count) for at in range(count)])]
    ppermute x72 -> x62, starting transfers between devices: 97.3 us -> 77.8 us  [swap(): return lax.ppermute(value, axis, [(at, at ^ bit) for at in range(count)])]
    ppermute x7 -> x11, starting transfers between devices: 19.4 us -> 30.7 us  [shift(): lax.ppermute(value, axis, [(at, (at + by) % count) for at in range(count)])]
    unnamed x14 -> x50, local copies, waits for them, and re-layouts: 3.23 us -> 13.5 us
    pallas_call x16 -> x19, Pallas kernels: 37.9 us -> 39.7 us  [local_call(): pl.pallas_call(kernel, out_shape=tuple(results), in_specs=[smem] + [vmem]...]
  transfers between devices with their start and end apart: 83 -> 77, of which waited for: 31 -> 28; matrix products, arithmetic and copies ran while one was open for 2% -> 2% of each run, Pallas kernels for 10% -> 10%
where the time goes in v4:
time: 302 us; the launch traced here: 297 us
  waiting for transfers between devices  120 us (40%)
  starting transfers between devices  111 us (37%)
  Pallas kernels  39.7 us (13%)
  local copies, waits for them, and re-layouts  16.7 us (6%)
  other arithmetic  8.99 us (3%)
    ppermute x62, waiting for transfers between devices, swap(): return lax.ppermute(value, axis, [(at, at ^ bit) for at in range(count)])  80.7 us
    ppermute x62, starting transfers between devices, swap(): return lax.ppermute(value, axis, [(at, at ^ bit) for at in range(count)])  77.8 us
    pallas_call x19, Pallas kernels, local_call(): pl.pallas_call(kernel, out_shape=tuple(results), in_specs=[smem] + [vmem]...  39.7 us
    ppermute x11, waiting for transfers between devices, shift(): lax.ppermute(value, axis, [(at, (at + by) % count) for at in range(count)])  38.8 us
    ppermute x11, starting transfers between devices, shift(): lax.ppermute(value, axis, [(at, (at + by) % count) for at in range(count)])  30.7 us
    unnamed x50, local copies, waits for them, and re-layouts  13.5 us
  transfers between devices with their start and end apart: 77, of which 28 were waited for; matrix products, arithmetic and copies ran while one was open for 2% of the time, Pallas kernels for 10%

profile of v4, /device:TPU:0, one launch (start us, length us, event | category | flops | bytes accessed | tf_op | source)
XLA Modules:
  0.0 297.4 jit_solution(10931597334242589353)
XLA Ops:
  7.9 3.5 %collective-permute-start.1 = (f32[8,768]{1,0:T(8,128)S(1)}, f32[8,768]{1,0:T(8,128)S(1)}, u32[]{:S(2)}, u32[]{:S(2)}) collective-permute-start(f32[8,768]{1,0:T(8,128)S(1)} %dynamic_update_slice.15), channel_id=1, source_target_pairs={{0,1},{1,0},{2,3},{3,2},{4,5},{5,4},{6,7},{7,6},{8,9},{9,8},{10,11... | collective-permute-start | bytes 73736 | tf_op jit(solution)/shard_map/ppermute | solution.py:24
  19.8 3.4 %collective-permute-start.8 = (bf16[48,576]{1,0:T(8,128)(2,1)S(1)}, bf16[48,576]{1,0:T(8,128)(2,1)S(1)}, u32[]{:S(2)}, u32[]{:S(2)}) collective-permute-start(bf16[48,576]{1,0:T(8,128)(2,1)S(1)} %get-tuple-element.103), channel_id=1, source_target_pairs={{0,8},{8,0},{16,24},{24,16},{1,9},{9,1},{17,25},{25,17},{2,10},{10... | collective-permute-start | bytes 165896 | tf_op jit(solution)/shard_map/ppermute | solution.py:24
  23.2 3.5 %collective-permute-start.9 = (bf16[48,576]{1,0:T(8,128)(2,1)S(1)}, bf16[48,576]{1,0:T(8,128)(2,1)S(1)}, u32[]{:S(2)}, u32[]{:S(2)}) collective-permute-start(bf16[48,576]{1,0:T(8,128)(2,1)S(1)} %get-tuple-element.104), channel_id=1, source_target_pairs={{0,16},{8,24},{16,0},{24,8},{1,17},{9,25},{17,1},{25,9},{2,18},{10... | collective-permute-start | bytes 165896 | tf_op jit(solution)/shard_map/ppermute | solution.py:24
  28.2 4.9 %collective-permute-done.4 = f32[8,768]{1,0:T(8,128)S(1)} collective-permute-done((f32[8,768]{1,0:T(8,128)S(1)}, f32[8,768]{1,0:T(8,128)S(1)}, u32[]{:S(2)}, u32[]{:S(2)}) %collective-permute-start.4) | collective-permute-done | bytes 24608 | tf_op jit(solution)/shard_map/ppermute | solution.py:24
  34.0 3.1 %collective-permute-start.6 = (bf16[128,768]{1,0:T(8,128)(2,1)S(1)}, bf16[128,768]{1,0:T(8,128)(2,1)S(1)}, u32[]{:S(2)}, u32[]{:S(2)}) collective-permute-start(bf16[128,768]{1,0:T(8,128)(2,1)S(1)} %shard_map.263.refs_0_), channel_id=1, source_target_pairs={{0,16},{8,24},{16,0},{24,8},{1,17},{9,25},{17,1},{25,9},{2,18},{10... | collective-permute-start | bytes 589832 | tf_op jit(solution)/shard_map/ppermute | solution.py:24
  43.8 4.1 %collective-permute-done.13.refs_7_ = bf16[4,48,576]{2,1,0:T(8,128)(2,1)S(1)} collective-permute-done((bf16[4,48,576]{2,1,0:T(8,128)(2,1)S(1)}, bf16[4,48,576]{2,1,0:T(8,128)(2,1)S(1)}, u32[]{:S(2)}, u32[]{:S(2)}) %collective-permute-start.13) | collective-permute-done | bytes 221216 | tf_op jit(solution)/shard_map/ppermute | solution.py:24
  47.9 3.8 %collective-permute-done.30.refs_3_ = bf16[48,768]{1,0:T(8,128)(2,1)S(1)} collective-permute-done((bf16[48,768]{1,0:T(8,128)(2,1)S(1)}, bf16[48,768]{1,0:T(8,128)(2,1)S(1)}, u32[]{:S(2)}, u32[]{:S(2)}) %collective-permute-start.30) | collective-permute-done | bytes 73760 | tf_op jit(solution)/shard_map/ppermute | solution.py:24
  52.4 5.4 %collective-permute-done.17.refs_7_ = bf16[48,768]{1,0:T(8,128)(2,1)S(1)} collective-permute-done((bf16[48,768]{1,0:T(8,128)(2,1)S(1)}, bf16[48,768]{1,0:T(8,128)(2,1)S(1)}, u32[]{:S(2)}, u32[]{:S(2)}) %collective-permute-start.17) | collective-permute-done | bytes 73760 | tf_op jit(solution)/shard_map/ppermute | solution.py:24
  57.8 7.8 %collective-permute-start.31 = (bf16[192,768]{1,0:T(8,128)(2,1)S(1)}, bf16[192,768]{1,0:T(8,128)(2,1)S(1)}, u32[]{:S(2)}, u32[]{:S(2)}) collective-permute-start(bf16[192,768]{1,0:T(8,128)(2,1)S(1)} %shard_map.269.refs_8_), channel_id=1, source_target_pairs={{0,1},{1,0},{2,3},{3,2},{4,5},{5,4},{6,7},{7,6},{8,9},{9,8},{10,11... | collective-permute-start | bytes 884744 | tf_op jit(solution)/shard_map/ppermute | solution.py:24
  73.0 6.7 %collective-permute-done.15.refs_5_ = bf16[48,768]{1,0:T(8,128)(2,1)S(1)} collective-permute-done((bf16[48,768]{1,0:T(8,128)(2,1)S(1)}, bf16[48,768]{1,0:T(8,128)(2,1)S(1)}, u32[]{:S(2)}, u32[]{:S(2)}) %collective-permute-start.15) | collective-permute-done | bytes 73760 | tf_op jit(solution)/shard_map/ppermute | solution.py:24
  79.7 4.2 %collective-permute-start.16 = (bf16[48,768]{1,0:T(8,128)(2,1)S(1)}, bf16[48,768]{1,0:T(8,128)(2,1)S(1)}, u32[]{:S(2)}, u32[]{:S(2)}) collective-permute-start(bf16[48,768]{1,0:T(8,128)(2,1)S(1)} %convert_element_type.102.refs_4_), channel_id=1, source_target_pairs={{0,2},{1,3},{2,0},{3,1},{4,6},{5,7},{6,4},{7,5},{8,10},{9,11},{10,... | collective-permute-start | bytes 221192 | tf_op jit(solution)/shard_map/ppermute | solution.py:24
  83.9 6.8 %shard_map.265 = (f32[512,192]{1,0:T(8,128)S(1)}, f32[512,128]{1,0:T(8,128)S(1)}) custom-call(s32[6]{0:T(128)S(1)} %stack.76.meta_ref.place_ref, bf16[512,576]{1,0:T(8,128)(2,1)S(1)} %get-tuple-element.106.kvq_ref.refs_0_.refs_5_), custom_call_target="tpu_custom_call" | custom-call | flops 201326592 | bytes 1245208 | tf_op jit(solution)/shard_map/pallas_call | solution.py:606
  95.2 6.1 %collective-permute-start.33 = (bf16[192,768]{1,0:T(8,128)(2,1)S(1)}, bf16[192,768]{1,0:T(8,128)(2,1)S(1)}, u32[]{:S(2)}, u32[]{:S(2)}) collective-permute-start(bf16[192,768]{1,0:T(8,128)(2,1)S(1)} %shard_map.269.refs_8_), channel_id=1, source_target_pairs={{0,3},{1,2},{2,1},{3,0},{4,7},{5,6},{6,5},{7,4},{8,11},{9,10},{10,... | collective-permute-start | bytes 884744 | tf_op jit(solution)/shard_map/ppermute | solution.py:24
  101.3 8.8 %collective-permute-start.34 = (bf16[192,768]{1,0:T(8,128)(2,1)S(1)}, bf16[192,768]{1,0:T(8,128)(2,1)S(1)}, u32[]{:S(2)}, u32[]{:S(2)}) collective-permute-start(bf16[192,768]{1,0:T(8,128)(2,1)S(1)} %shard_map.269.refs_8_), channel_id=1, source_target_pairs={{0,4},{4,0},{1,5},{5,1},{2,6},{6,2},{3,7},{7,3},{8,12},{12,8},{9,1... | collective-permute-start | bytes 884744 | tf_op jit(solution)/shard_map/ppermute | solution.py:29
  113.1 4.7 %collective-permute-done.34.refs_12_ = bf16[192,768]{1,0:T(8,128)(2,1)S(1)} collective-permute-done((bf16[192,768]{1,0:T(8,128)(2,1)S(1)}, bf16[192,768]{1,0:T(8,128)(2,1)S(1)}, u32[]{:S(2)}, u32[]{:S(2)}) %collective-permute-start.34) | collective-permute-done | bytes 294944 | tf_op jit(solution)/shard_map/ppermute | solution.py:29
  124.7 5.8 %collective-permute-done.36.refs_14_ = bf16[192,768]{1,0:T(8,128)(2,1)S(1)} collective-permute-done((bf16[192,768]{1,0:T(8,128)(2,1)S(1)}, bf16[192,768]{1,0:T(8,128)(2,1)S(1)}, u32[]{:S(2)}, u32[]{:S(2)}) %collective-permute-start.36) | collective-permute-done | bytes 294944 | tf_op jit(solution)/shard_map/ppermute | solution.py:29
  130.5 5.8 %collective-permute-done.37.refs_15_ = bf16[192,768]{1,0:T(8,128)(2,1)S(1)} collective-permute-done((bf16[192,768]{1,0:T(8,128)(2,1)S(1)}, bf16[192,768]{1,0:T(8,128)(2,1)S(1)}, u32[]{:S(2)}, u32[]{:S(2)}) %collective-permute-start.37) | collective-permute-done | bytes 294944 | tf_op jit(solution)/shard_map/ppermute | solution.py:29
  136.3 5.0 %shard_map.270 = (f32[128,768]{1,0:T(8,128)S(1)}, bf16[128,768]{1,0:T(8,128)(2,1)S(1)}, bf16[128,768]{1,0:T(8,128)(2,1)S(1)}, bf16[128,768]{1,0:T(8,128)(2,1)S(1...) custom-call(s32[6]{0:T(128)S(1)} %stack.76.meta_ref.place_ref, ...), custom_call_target="tpu_custom_call" | custom-call | flops 1811939328 | bytes 9268248 | tf_op jit(solution)/shard_map/pallas_call | solution.py:606
  147.0 5.7 %collective-permute-done.39.refs_2_ = bf16[128,768]{1,0:T(8,128)(2,1)S(1)} collective-permute-done((bf16[128,768]{1,0:T(8,128)(2,1)S(1)}, bf16[128,768]{1,0:T(8,128)(2,1)S(1)}, u32[]{:S(2)}, u32[]{:S(2)}) %collective-permute-start.39) | collective-permute-done | bytes 196640 | tf_op jit(solution)/shard_map/ppermute | solution.py:24
  152.6 3.7 %collective-permute-done.40.refs_3_ = bf16[128,768]{1,0:T(8,128)(2,1)S(1)} collective-permute-done((bf16[128,768]{1,0:T(8,128)(2,1)S(1)}, bf16[128,768]{1,0:T(8,128)(2,1)S(1)}, u32[]{:S(2)}, u32[]{:S(2)}) %collective-permute-start.40) | collective-permute-done | bytes 196640 | tf_op jit(solution)/shard_map/ppermute | solution.py:24
  160.4 5.6 %collective-permute-done.41.refs_2_ = bf16[128,768]{1,0:T(8,128)(2,1)} collective-permute-done((bf16[128,768]{1,0:T(8,128)(2,1)}, bf16[128,768]{1,0:T(8,128)(2,1)}, u32[]{:S(2)}, u32[]{:S(2)}) %collective-permute-start.41) | collective-permute-done | bytes 196640 | tf_op jit(solution)/shard_map/ppermute | solution.py:24
  172.3 3.6 %shard_map.271 = (f32[4,192,768]{2,1,0:T(8,128)S(1)}, bf16[4,192,768]{2,1,0:T(8,128)(2,1)S(1)}, f32[128,768]{1,0:T(8,128)S(1)}, bf16[128,768]{1,0:T(8,128)(2,1)S...) custom-call(s32[6]{0:T(128)S(1)} %stack.76.meta_ref.place_ref, bf16[512,768]{1,0:T(8,128)(2,1)S(1)} %copy-done.14, ...), custom_call_target="tpu_custom_call" | custom-call | flops 1811939328 | bytes 8847384 | tf_op jit(solution)/shard_map/pallas_call | solution.py:606
  181.6 6.4 %collective-permute-start.48 = (bf16[512,384]{1,0:T(8,128)(2,1)S(1)}, bf16[512,384]{1,0:T(8,128)(2,1)S(1)}, u32[]{:S(2)}, u32[]{:S(2)}) collective-permute-start(bf16[512,384]{1,0:T(8,128)(2,1)S(1)} %bitcast.75), channel_id=1, source_target_pairs={{0,4},{4,0},{1,5},{5,1},{2,6},{6,2},{3,7},{7,3},{8,12},{12,8},{9,1... | collective-permute-start | bytes 1179656 | tf_op jit(solution)/shard_map/ppermute | solution.py:29
  188.0 6.9 %shard_map.274 = (f32[512,576]{1,0:T(8,128)S(1)}, f32[48,768]{1,0:T(8,128)S(1)}, bf16[48,768]{1,0:T(8,128)(2,1)S(1)}, bf16[48,768]{1,0:T(8,128)(2,1)S(1)}, bf16[48,768]{1,0:T(8,128)(2,1)S(1)}) custom-call(s32[6]{0:T(128)S(1)} %stack.76.meta_ref.place_ref, bf16[512,576]{1,0:T(8,128)(2,1)S(1)} %get-tuple-element.106.kvq_ref.refs_0_.refs_5_, ...), custom_call_target="tpu_custom_call" | custom-call | flops 503316480 | bytes 4366360 | tf_op jit(solution)/shard_map/pallas_call | solution.py:606
  195.6 3.8 %collective-permute-start.67 = (bf16[48,768]{1,0:T(8,128)(2,1)S(1)}, bf16[48,768]{1,0:T(8,128)(2,1)S(1)}, u32[]{:S(2)}, u32[]{:S(2)}) collective-permute-start(bf16[48,768]{1,0:T(8,128)(2,1)S(1)} %get-tuple-element.172), channel_id=1, source_target_pairs={{0,3},{1,2},{2,1},{3,0},{4,7},{5,6},{6,5},{7,4},{8,11},{9,10},{10,... | collective-permute-start | bytes 221192 | tf_op jit(solution)/shard_map/ppermute | solution.py:24
  199.5 12.9 %collective-permute-done.48 = bf16[512,384]{1,0:T(8,128)(2,1)S(1)} collective-permute-done((bf16[512,384]{1,0:T(8,128)(2,1)S(1)}, bf16[512,384]{1,0:T(8,128)(2,1)S(1)}, u32[]{:S(2)}, u32[]{:S(2)}) %collective-permute-start.48) | collective-permute-done | bytes 393248 | tf_op jit(solution)/shard_map/ppermute | solution.py:29
  219.2 7.3 %collective-permute-done.51.refs_3_ = bf16[128,768]{1,0:T(8,128)(2,1)S(1)} collective-permute-done((bf16[128,768]{1,0:T(8,128)(2,1)S(1)}, bf16[128,768]{1,0:T(8,128)(2,1)S(1)}, u32[]{:S(2)}, u32[]{:S(2)}) %collective-permute-start.51) | collective-permute-done | bytes 196640 | tf_op jit(solution)/shard_map/ppermute | solution.py:24
  234.5 5.3 %collective-permute-done.53 = f32[8,768]{1,0:T(8,128)S(1)} collective-permute-done((f32[8,768]{1,0:T(8,128)S(1)}, f32[8,768]{1,0:T(8,128)S(1)}, u32[]{:S(2)}, u32[]{:S(2)}) %collective-permute-start.53) | collective-permute-done | bytes 24608 | tf_op jit(solution)/shard_map/ppermute | solution.py:24
  245.9 9.5 %collective-permute-done.54 = f32[8,768]{1,0:T(8,128)S(1)} collective-permute-done((f32[8,768]{1,0:T(8,128)S(1)}, f32[8,768]{1,0:T(8,128)S(1)}, u32[]{:S(2)}, u32[]{:S(2)}) %collective-permute-start.54) | collective-permute-done | bytes 24608 | tf_op jit(solution)/shard_map/ppermute | solution.py:24
  271.8 7.5 %collective-permute-done.71 = bf16[192,768]{1,0:T(8,128)(2,1)S(1)} collective-permute-done((bf16[192,768]{1,0:T(8,128)(2,1)S(1)}, bf16[192,768]{1,0:T(8,128)(2,1)S(1)}, u32[]{:S(2)}, u32[]{:S(2)}) %collective-permute-start.71) | collective-permute-done | bytes 294944 | tf_op jit(solution)/shard_map/ppermute | solution.py:24
  279.5 3.1 %collective-permute-start.73 = (bf16[192,768]{1,0:T(8,128)(2,1)S(1)}, bf16[192,768]{1,0:T(8,128)(2,1)S(1)}, u32[]{:S(2)}, u32[]{:S(2)}) collective-permute-start(bf16[192,768]{1,0:T(8,128)(2,1)S(1)} %add_convert_fusion), channel_id=1, source_target_pairs={{0,4},{4,0},{1,5},{5,1},{2,6},{6,2},{3,7},{7,3},{8,12},{12,8},{9,1... | collective-permute-start | bytes 884744 | tf_op jit(solution)/shard_map/ppermute | solution.py:29
  284.6 5.0 %collective-permute-done.73 = bf16[192,768]{1,0:T(8,128)(2,1)S(1)} collective-permute-done((bf16[192,768]{1,0:T(8,128)(2,1)S(1)}, bf16[192,768]{1,0:T(8,128)(2,1)S(1)}, u32[]{:S(2)}, u32[]{:S(2)}) %collective-permute-start.73) | collective-permute-done | bytes 294944 | tf_op jit(solution)/shard_map/ppermute | solution.py:29
  (234 shorter events, 116.5 us)
Async XLA Ops:
  19.8 17.3 %collective-permute-start.8 = (bf16[48,576]{1,0:T(8,128)(2,1)S(1)}, bf16[48,576]{1,0:T(8,128)(2,1)S(1)}, u32[]{:S(2)}, u32[]{:S(2)}) collective-permute-start(bf16[48,576]{1,0:T(8,128)(2,1)S(1)} %get-tuple-element.103), channel_id=1, source_target_pairs={{0,8},{8,0},{16,24},{24,16},{1,9},{9,1},{17,25},{25,17},{2,10},{10... | collective-permute-start | bytes 165896 | tf_op jit(solution)/shard_map/ppermute | solution.py:24
  40.6 25.0 %collective-permute-start.11 = (bf16[4,48,576]{2,1,0:T(8,128)(2,1)S(1)}, bf16[4,48,576]{2,1,0:T(8,128)(2,1)S(1)}, u32[]{:S(2)}, u32[]{:S(2)}) collective-permute-start(bf16[4,48,576]{2,1,0:T(8,128)(2,1)S(1)} %pad_maximum_fusion.refs_4_), channel_id=1, source_target_pairs={{0,1},{1,0},{2,3},{3,2},{4,5},{5,4},{6,7},{7,6},{8,9},{9,8},{10,11... | collective-permute-start | bytes 663560 | tf_op jit(solution)/shard_map/ppermute | solution.py:24
  40.6 25.0 %collective-permute-start.12 = (bf16[4,48,576]{2,1,0:T(8,128)(2,1)S(1)}, bf16[4,48,576]{2,1,0:T(8,128)(2,1)S(1)}, u32[]{:S(2)}, u32[]{:S(2)}) collective-permute-start(bf16[4,48,576]{2,1,0:T(8,128)(2,1)S(1)} %pad_maximum_fusion.refs_4_), channel_id=1, source_target_pairs={{0,2},{1,3},{2,0},{3,1},{4,6},{5,7},{6,4},{7,5},{8,10},{9,11},{10,... | collective-permute-start | bytes 663560 | tf_op jit(solution)/shard_map/ppermute | solution.py:24
  43.3 22.4 %collective-permute-start.5 = (bf16[128,768]{1,0:T(8,128)(2,1)S(1)}, bf16[128,768]{1,0:T(8,128)(2,1)S(1)}, u32[]{:S(2)}, u32[]{:S(2)}) collective-permute-start(bf16[128,768]{1,0:T(8,128)(2,1)S(1)} %shard_map.263.refs_0_), channel_id=1, source_target_pairs={{0,8},{8,0},{16,24},{24,16},{1,9},{9,1},{17,25},{25,17},{2,10},{10... | collective-permute-start | bytes 589832 | tf_op jit(solution)/shard_map/ppermute | solution.py:24
  43.3 22.4 %collective-permute-start.7 = (bf16[128,768]{1,0:T(8,128)(2,1)S(1)}, bf16[128,768]{1,0:T(8,128)(2,1)S(1)}, u32[]{:S(2)}, u32[]{:S(2)}) collective-permute-start(bf16[128,768]{1,0:T(8,128)(2,1)S(1)} %collective-permute-done.6.refs_2_), channel_id=1, source_target_pairs={{0,8},{8,0},{16,24},{24,16},{1,9},{9,1},{17,25},{25,17},{2,10},{10... | collective-permute-start | bytes 589832 | tf_op jit(solution)/shard_map/ppermute | solution.py:24
  57.8 43.4 %collective-permute-start.31 = (bf16[192,768]{1,0:T(8,128)(2,1)S(1)}, bf16[192,768]{1,0:T(8,128)(2,1)S(1)}, u32[]{:S(2)}, u32[]{:S(2)}) collective-permute-start(bf16[192,768]{1,0:T(8,128)(2,1)S(1)} %shard_map.269.refs_8_), channel_id=1, source_target_pairs={{0,1},{1,0},{2,3},{3,2},{4,5},{5,4},{6,7},{7,6},{8,9},{9,8},{10,11... | collective-permute-start | bytes 884744 | tf_op jit(solution)/shard_map/ppermute | solution.py:24
  68.0 24.3 %collective-permute-start.14 = (bf16[512,384]{1,0:T(8,128)(2,1)S(1)}, bf16[512,384]{1,0:T(8,128)(2,1)S(1)}, u32[]{:S(2)}, u32[]{:S(2)}) collective-permute-start(bf16[512,384]{1,0:T(8,128)(2,1)S(1)} %get-tuple-element.107), channel_id=1, source_target_pairs={{0,4},{4,0},{1,5},{5,1},{2,6},{6,2},{3,7},{7,3},{8,12},{12,8},{9,1... | collective-permute-start | bytes 1179656 | tf_op jit(solution)/shard_map/ppermute | solution.py:29
  69.5 31.8 %collective-permute-start.32 = (bf16[192,768]{1,0:T(8,128)(2,1)S(1)}, bf16[192,768]{1,0:T(8,128)(2,1)S(1)}, u32[]{:S(2)}, u32[]{:S(2)}) collective-permute-start(bf16[192,768]{1,0:T(8,128)(2,1)S(1)} %shard_map.269.refs_8_), channel_id=1, source_target_pairs={{0,2},{1,3},{2,0},{3,1},{4,6},{5,7},{6,4},{7,5},{8,10},{9,11},{10,... | collective-permute-start | bytes 884744 | tf_op jit(solution)/shard_map/ppermute | solution.py:24
  69.6 25.6 %collective-permute-start.24 = (bf16[128,768]{1,0:T(8,128)(2,1)S(1)}, bf16[128,768]{1,0:T(8,128)(2,1)S(1)}, u32[]{:S(2)}, u32[]{:S(2)}) collective-permute-start(bf16[128,768]{1,0:T(8,128)(2,1)S(1)} %bitcast_convert_fusion), channel_id=1, source_target_pairs={{0,0},{1,8},{2,16},{3,24},{8,1},{9,9},{10,17},{11,25},{16,2},{17,1... | collective-permute-start | bytes 589832 | tf_op jit(solution)/shard_map/ppermute | solution.py:35
  95.2 14.9 %collective-permute-start.18 = (bf16[128,768]{1,0:T(8,128)(2,1)S(1)}, bf16[128,768]{1,0:T(8,128)(2,1)S(1)}, u32[]{:S(2)}, u32[]{:S(2)}) collective-permute-start(bf16[128,768]{1,0:T(8,128)(2,1)S(1)} %get-tuple-element.112), channel_id=1, source_target_pairs={{0,8},{8,0},{16,24},{24,16},{1,9},{9,1},{17,25},{25,17},{2,10},{10... | collective-permute-start | bytes 589832 | tf_op jit(solution)/shard_map/ppermute | solution.py:24
  95.2 16.4 %collective-permute-start.19 = (bf16[128,768]{1,0:T(8,128)(2,1)S(1)}, bf16[128,768]{1,0:T(8,128)(2,1)S(1)}, u32[]{:S(2)}, u32[]{:S(2)}) collective-permute-start(bf16[128,768]{1,0:T(8,128)(2,1)S(1)} %get-tuple-element.113), channel_id=1, source_target_pairs={{0,16},{8,24},{16,0},{24,8},{1,17},{9,25},{17,1},{25,9},{2,18},{10... | collective-permute-start | bytes 589832 | tf_op jit(solution)/shard_map/ppermute | solution.py:24
  95.2 17.3 %collective-permute-start.33 = (bf16[192,768]{1,0:T(8,128)(2,1)S(1)}, bf16[192,768]{1,0:T(8,128)(2,1)S(1)}, u32[]{:S(2)}, u32[]{:S(2)}) collective-permute-start(bf16[192,768]{1,0:T(8,128)(2,1)S(1)} %shard_map.269.refs_8_), channel_id=1, source_target_pairs={{0,3},{1,2},{2,1},{3,0},{4,7},{5,6},{6,5},{7,4},{8,11},{9,10},{10,... | collective-permute-start | bytes 884744 | tf_op jit(solution)/shard_map/ppermute | solution.py:24
  101.3 16.6 %collective-permute-start.34 = (bf16[192,768]{1,0:T(8,128)(2,1)S(1)}, bf16[192,768]{1,0:T(8,128)(2,1)S(1)}, u32[]{:S(2)}, u32[]{:S(2)}) collective-permute-start(bf16[192,768]{1,0:T(8,128)(2,1)S(1)} %shard_map.269.refs_8_), channel_id=1, source_target_pairs={{0,4},{4,0},{1,5},{5,1},{2,6},{6,2},{3,7},{7,3},{8,12},{12,8},{9,1... | collective-permute-start | bytes 884744 | tf_op jit(solution)/shard_map/ppermute | solution.py:29
  119.9 16.4 %collective-permute-start.37 = (bf16[192,768]{1,0:T(8,128)(2,1)S(1)}, bf16[192,768]{1,0:T(8,128)(2,1)S(1)}, u32[]{:S(2)}, u32[]{:S(2)}) collective-permute-start(bf16[192,768]{1,0:T(8,128)(2,1)S(1)} %collective-permute-done.33.refs_11_), channel_id=1, source_target_pairs={{0,4},{4,0},{1,5},{5,1},{2,6},{6,2},{3,7},{7,3},{8,12},{12,8},{9,1... | collective-permute-start | bytes 884744 | tf_op jit(solution)/shard_map/ppermute | solution.py:29
  121.5 14.8 %collective-permute-start.27 = (bf16[128,768]{1,0:T(8,128)(2,1)S(1)}, bf16[128,768]{1,0:T(8,128)(2,1)S(1)}, u32[]{:S(2)}, u32[]{:S(2)}) collective-permute-start(bf16[128,768]{1,0:T(8,128)(2,1)S(1)} %collective-permute-done.26.refs_6_), channel_id=1, source_target_pairs={{0,8},{8,0},{16,24},{24,16},{1,9},{9,1},{17,25},{25,17},{2,10},{10... | collective-permute-start | bytes 589832 | tf_op jit(solution)/shard_map/ppermute | solution.py:24
  176.0 68.6 %collective-permute-start.69 = (bf16[4,192,768]{2,1,0:T(8,128)(2,1)S(1)}, bf16[4,192,768]{2,1,0:T(8,128)(2,1)S(1)}, u32[]{:S(2)}, u32[]{:S(2)}) collective-permute-start(bf16[4,192,768]{2,1,0:T(8,128)(2,1)S(1)} %get-tuple-element.175), channel_id=1, source_target_pairs={{0,4},{4,0},{1,5},{5,1},{2,6},{6,2},{3,7},{7,3},{8,12},{12,8},{9,1... | collective-permute-start | bytes 3538952 | tf_op jit(solution)/shard_map/ppermute | solution.py:29
  177.8 17.1 %collective-permute-start.43 = (bf16[128,768]{1,0:T(8,128)(2,1)S(1)}, bf16[128,768]{1,0:T(8,128)(2,1)S(1)}, u32[]{:S(2)}, u32[]{:S(2)}) collective-permute-start(bf16[128,768]{1,0:T(8,128)(2,1)S(1)} %get-tuple-element.139), channel_id=1, source_target_pairs={{0,8},{8,0},{16,24},{24,16},{1,9},{9,1},{17,25},{25,17},{2,10},{10... | collective-permute-start | bytes 589832 | tf_op jit(solution)/shard_map/ppermute | solution.py:24
  177.8 17.2 %collective-permute-start.44 = (bf16[128,768]{1,0:T(8,128)(2,1)S(1)}, bf16[128,768]{1,0:T(8,128)(2,1)S(1)}, u32[]{:S(2)}, u32[]{:S(2)}) collective-permute-start(bf16[128,768]{1,0:T(8,128)(2,1)S(1)} %get-tuple-element.140), channel_id=1, source_target_pairs={{0,16},{8,24},{16,0},{24,8},{1,17},{9,25},{17,1},{25,9},{2,18},{10... | collective-permute-start | bytes 589832 | tf_op jit(solution)/shard_map/ppermute | solution.py:24
  179.5 16.1 %collective-permute-start.45 = (bf16[128,768]{1,0:T(8,128)(2,1)S(1)}, bf16[128,768]{1,0:T(8,128)(2,1)S(1)}, u32[]{:S(2)}, u32[]{:S(2)}) collective-permute-start(bf16[128,768]{1,0:T(8,128)(2,1)S(1)} %get-tuple-element.141), channel_id=1, source_target_pairs={{0,24},{8,16},{16,8},{24,0},{1,25},{9,17},{17,9},{25,1},{2,26},{10... | collective-permute-start | bytes 589832 | tf_op jit(solution)/shard_map/ppermute | solution.py:24
  181.6 30.8 %collective-permute-start.48 = (bf16[512,384]{1,0:T(8,128)(2,1)S(1)}, bf16[512,384]{1,0:T(8,128)(2,1)S(1)}, u32[]{:S(2)}, u32[]{:S(2)}) collective-permute-start(bf16[512,384]{1,0:T(8,128)(2,1)S(1)} %bitcast.75), channel_id=1, source_target_pairs={{0,4},{4,0},{1,5},{5,1},{2,6},{6,2},{3,7},{7,3},{8,12},{12,8},{9,1... | collective-permute-start | bytes 1179656 | tf_op jit(solution)/shard_map/ppermute | solution.py:29
  194.9 19.6 %collective-permute-start.65 = (bf16[48,768]{1,0:T(8,128)(2,1)S(1)}, bf16[48,768]{1,0:T(8,128)(2,1)S(1)}, u32[]{:S(2)}, u32[]{:S(2)}) collective-permute-start(bf16[48,768]{1,0:T(8,128)(2,1)S(1)} %get-tuple-element.170), channel_id=1, source_target_pairs={{0,1},{1,0},{2,3},{3,2},{4,5},{5,4},{6,7},{7,6},{8,9},{9,8},{10,11... | collective-permute-start | bytes 221192 | tf_op jit(solution)/shard_map/ppermute | solution.py:24
  195.0 22.0 %collective-permute-start.66 = (bf16[48,768]{1,0:T(8,128)(2,1)S(1)}, bf16[48,768]{1,0:T(8,128)(2,1)S(1)}, u32[]{:S(2)}, u32[]{:S(2)}) collective-permute-start(bf16[48,768]{1,0:T(8,128)(2,1)S(1)} %get-tuple-element.171), channel_id=1, source_target_pairs={{0,2},{1,3},{2,0},{3,1},{4,6},{5,7},{6,4},{7,5},{8,10},{9,11},{10,... | collective-permute-start | bytes 221192 | tf_op jit(solution)/shard_map/ppermute | solution.py:24
  195.6 22.0 %collective-permute-start.67 = (bf16[48,768]{1,0:T(8,128)(2,1)S(1)}, bf16[48,768]{1,0:T(8,128)(2,1)S(1)}, u32[]{:S(2)}, u32[]{:S(2)}) collective-permute-start(bf16[48,768]{1,0:T(8,128)(2,1)S(1)} %get-tuple-element.172), channel_id=1, source_target_pairs={{0,3},{1,2},{2,1},{3,0},{4,7},{5,6},{6,5},{7,4},{8,11},{9,10},{10,... | collective-permute-start | bytes 221192 | tf_op jit(solution)/shard_map/ppermute | solution.py:24
  212.3 19.5 %collective-permute-start.47 = (bf16[128,768]{1,0:T(8,128)(2,1)S(1)}, bf16[128,768]{1,0:T(8,128)(2,1)S(1)}, u32[]{:S(2)}, u32[]{:S(2)}) collective-permute-start(bf16[128,768]{1,0:T(8,128)(2,1)S(1)} %add_convert_fusion.3), channel_id=1, source_target_pairs={{0,0},{1,8},{2,16},{3,24},{8,1},{9,9},{10,17},{11,25},{16,2},{17,1... | collective-permute-start | bytes 589832 | tf_op jit(solution)/shard_map/ppermute | solution.py:35
  228.2 27.2 %collective-permute-start.58 = (bf16[4,48,576]{2,1,0:T(8,128)(2,1)S(1)}, bf16[4,48,576]{2,1,0:T(8,128)(2,1)S(1)}, u32[]{:S(2)}, u32[]{:S(2)}) collective-permute-start(bf16[4,48,576]{2,1,0:T(8,128)(2,1)S(1)} %get-tuple-element.166), channel_id=1, source_target_pairs={{0,1},{1,0},{2,3},{3,2},{4,5},{5,4},{6,7},{7,6},{8,9},{9,8},{10,11... | collective-permute-start | bytes 663560 | tf_op jit(solution)/shard_map/ppermute | solution.py:24
  230.7 26.5 %collective-permute-start.59 = (bf16[4,48,576]{2,1,0:T(8,128)(2,1)S(1)}, bf16[4,48,576]{2,1,0:T(8,128)(2,1)S(1)}, u32[]{:S(2)}, u32[]{:S(2)}) collective-permute-start(bf16[4,48,576]{2,1,0:T(8,128)(2,1)S(1)} %get-tuple-element.167), channel_id=1, source_target_pairs={{0,2},{1,3},{2,0},{3,1},{4,6},{5,7},{6,4},{7,5},{8,10},{9,11},{10,... | collective-permute-start | bytes 663560 | tf_op jit(solution)/shard_map/ppermute | solution.py:24
  239.9 17.9 %collective-permute-start.60 = (bf16[4,48,576]{2,1,0:T(8,128)(2,1)S(1)}, bf16[4,48,576]{2,1,0:T(8,128)(2,1)S(1)}, u32[]{:S(2)}, u32[]{:S(2)}) collective-permute-start(bf16[4,48,576]{2,1,0:T(8,128)(2,1)S(1)} %get-tuple-element.168), channel_id=1, source_target_pairs={{0,3},{1,2},{2,1},{3,0},{4,7},{5,6},{6,5},{7,4},{8,11},{9,10},{10,... | collective-permute-start | bytes 663560 | tf_op jit(solution)/shard_map/ppermute | solution.py:24
  240.9 14.5 %collective-permute-start.54 = (f32[8,768]{1,0:T(8,128)S(1)}, f32[8,768]{1,0:T(8,128)S(1)}, u32[]{:S(2)}, u32[]{:S(2)}) collective-permute-start(f32[8,768]{1,0:T(8,128)S(1)} %add.140), channel_id=1, source_target_pairs={{0,2},{1,3},{2,0},{3,1},{4,6},{5,7},{6,4},{7,5},{8,10},{9,11},{10,... | collective-permute-start | bytes 73736 | tf_op jit(solution)/shard_map/ppermute | solution.py:24
  245.4 26.4 %collective-permute-start.70 = (bf16[192,768]{1,0:T(8,128)(2,1)S(1)}, bf16[192,768]{1,0:T(8,128)(2,1)S(1)}, u32[]{:S(2)}, u32[]{:S(2)}) collective-permute-start(bf16[192,768]{1,0:T(8,128)(2,1)S(1)} %get-tuple-element.178), channel_id=1, source_target_pairs={{0,1},{1,0},{2,3},{3,2},{4,5},{5,4},{6,7},{7,6},{8,9},{9,8},{10,11... | collective-permute-start | bytes 884744 | tf_op jit(solution)/shard_map/ppermute | solution.py:24
  255.4 23.9 %collective-permute-start.71 = (bf16[192,768]{1,0:T(8,128)(2,1)S(1)}, bf16[192,768]{1,0:T(8,128)(2,1)S(1)}, u32[]{:S(2)}, u32[]{:S(2)}) collective-permute-start(bf16[192,768]{1,0:T(8,128)(2,1)S(1)} %get-tuple-element.179), channel_id=1, source_target_pairs={{0,2},{1,3},{2,0},{3,1},{4,6},{5,7},{6,4},{7,5},{8,10},{9,11},{10,... | collective-permute-start | bytes 884744 | tf_op jit(solution)/shard_map/ppermute | solution.py:24
  255.4 23.9 %collective-permute-start.72 = (bf16[192,768]{1,0:T(8,128)(2,1)S(1)}, bf16[192,768]{1,0:T(8,128)(2,1)S(1)}, u32[]{:S(2)}, u32[]{:S(2)}) collective-permute-start(bf16[192,768]{1,0:T(8,128)(2,1)S(1)} %get-tuple-element.180), channel_id=1, source_target_pairs={{0,3},{1,2},{2,1},{3,0},{4,7},{5,6},{6,5},{7,4},{8,11},{9,10},{10,... | collective-permute-start | bytes 884744 | tf_op jit(solution)/shard_map/ppermute | solution.py:24
  257.1 33.5 %collective-permute-start.52 = (bf16[128,768]{1,0:T(8,128)(2,1)S(1)}, bf16[128,768]{1,0:T(8,128)(2,1)S(1)}, u32[]{:S(2)}, u32[]{:S(2)}) collective-permute-start(bf16[128,768]{1,0:T(8,128)(2,1)S(1)} %get-tuple-element.161), channel_id=1, source_target_pairs={{0,0},{1,8},{2,16},{3,24},{8,1},{9,9},{10,17},{11,25},{16,2},{17,1... | collective-permute-start | bytes 589832 | tf_op jit(solution)/shard_map/ppermute | solution.py:35
  (70 other events, 610.0 us)

commit v5 on v4

--- a/solution.py
+++ b/solution.py
@@ -553,15 +553,14 @@
 
 def own_grad_kernel(parts, depth, heads, rows, meta_ref, *refs):
     (
-        kvq, ctx_grad, context, stat, query_grad, low, attn_all, kvq_grad, out_keep, out_sends,
-        whole, score, dots, prob, grad,
-    ) = take(refs, *([None] * 9), depth - 1, *([None] * 5))
+        kvq, ctx_grad, context, stat, query_grad, low, attn_all, kvq_grad, out_grad, score, dots,
+        prob, grad,
+    ) = refs
     own_backward(
         heads, rows, meta_ref, kvq, ctx_grad, context, stat, query_grad, kvq_grad, score, dots,
         prob, grad,
     )
-    whole[...] = matmul_tn(low[...], attn_all[...])
-    emit_shards(meta_ref, parts, whole, out_keep, out_sends)
+    out_grad[...] = matmul_tn(low[...], attn_all[...])
 
 
 def projection_back_kernel(parts, meta_ref, *refs):
@@ -578,10 +577,54 @@
     bias[...] = jnp.sum(kvq_grad[...].astype(WIDE), axis=0, keepdims=True)
 
 
-def projection_grad_kernel(parts, depth, meta_ref, *refs):
-    norm, kvq_grad, keep, sends, whole = take(refs, None, None, None, depth - 1, None)
+def projection_grad_kernel(parts, depth, halves, meta_ref, *refs):
+    norm, kvq_grad, out_grad, kept, sent, whole, folded = refs
+    columns = kvq_grad.shape[1]
+    model = norm.shape[1]
+    shard = model // (parts * depth)
+    rest = model - columns
+    slots = parts // 2
+    extra = kept.shape[1] - slots * shard
     whole[...] = matmul_tn(norm[...], kvq_grad[...])
-    emit_blocks(meta_ref, parts, depth, whole, keep, sends)
+
+    def emit(half, out):
+        for deep in range(depth):
+            member = meta_ref[parts + 1] ^ deep
+            for slot in range(slots):
+                row = (meta_ref[half * slots + slot] * depth + member) * shard
+                out[deep, slot * shard : (slot + 1) * shard] = whole[
+                    pl.ds(pl.multiple_of(row, 16), shard), :
+                ].astype(out.dtype)
+            start = pl.multiple_of(member * shard, 16)
+            folded[:shard, :] = out_grad[pl.ds(start, shard), :columns]
+            for at in range(columns // rest):
+                piece = out_grad[pl.ds(start + at * 16, 16), columns:]
+                folded[shard:, at * rest : (at + 1) * rest] = piece
+            out[deep, slots * shard :] = folded[half * extra : (half + 1) * extra, :].astype(
+                out.dtype
+            )
+
+    for half in range(2):
+        if halves:
+            pl.when(meta_ref[parts] == half)(functools.partial(emit, half, kept))
+            pl.when(meta_ref[parts] != half)(functools.partial(emit, half, sent))
+        else:
+            emit(half, sent if half else kept)
+
+
+def unfold_kernel(parts, meta_ref, first_ref, second_ref, *refs):
+    pieces, out_ref, folded = refs[:parts], refs[parts], refs[parts + 1]
+    shard, columns = pieces[0].shape
+    rest = out_ref.shape[1] - columns
+    slots = parts // 2
+    extra = folded.shape[0] // 2
+    for half, ref in enumerate((first_ref, second_ref)):
+        for slot in range(slots):
+            pieces[half * slots + slot][...] = ref[slot * shard : (slot + 1) * shard, :].astype(LOW)
+        folded[half * extra : (half + 1) * extra, :] = ref[slots * shard :, :].astype(WIDE)
+    out_ref[:, :columns] = folded[:shard, :]
+    for at in range(columns // rest):
+        out_ref[at * 16 : (at + 1) * 16, columns:] = folded[shard:, at * rest : (at + 1) * rest]
 
 
 def first_norm_grad_kernel(parts, meta_ref, *refs):
@@ -605,6 +648,7 @@
     moved = sum(each.size * each.dtype.itemsize for each in tuple(operands) + tuple(results))
     return pl.pallas_call(
         kernel,
+        name=getattr(kernel, "func", kernel).__name__,
         out_shape=tuple(results),
         in_specs=[smem] + [vmem] * (len(operands) - 1),
         out_specs=tuple([vmem] * len(results)),
@@ -648,7 +692,8 @@
         (meta, qkv_weight),
         [low_like(shard, 3 * width)] * parts,
     )
-    kvq_rows = jnp.stack([kvq_split[0]] + send_pieces(kvq_split[1:], "dp"))
+    kvq_arrived = send_pieces(kvq_split[1:], "dp")
+    kvq_rows = jnp.stack([kvq_split[0]] + kvq_arrived)
     kvq_pieces = gather_direct(kvq_rows, "fsdp")
 
     token_rows = transpose_homes(after(tokens[0].astype(LOW), kvq_split[0]))
@@ -663,7 +708,7 @@
     ):
         part = part.astype(LOW).astype(WIDE)[None]
         vectors = lax.dynamic_update_slice(vectors, part, (row, first + deep * part.shape[1]))
-    vectors = sum_doubling(after(vectors, kvq_split[0]), "fsdp")
+    vectors = sum_doubling(after(vectors, kvq_arrived[0]), "fsdp")
     everywhere = sum_doubling(vectors, "dp")
     vectors = jnp.where(jnp.arange(8)[:, None] < 6, everywhere, vectors)
 
@@ -676,18 +721,6 @@
     up_parts = [up_split[0]] + send_pieces(up_split[1:], "dp")
     out_pieces = gather_direct(after(out_weight.astype(LOW), kvq_pieces[-1]), "fsdp")
     grad_rows = transpose_homes(after(cotangent[0].astype(LOW), kvq_pieces[-1]))
-    if halves:
-        (half,) = local_call(
-            functools.partial(half_kernel, parts),
-            (meta, *up_parts, fc2_weight),
-            [low_like(hidden_shard, model)],
-        )
-        own_half = gather_direct(after(half, out_pieces[-1]), "fsdp")
-        other_half = [shift(piece, "ctx", 1) for piece in own_half]
-    else:
-        own_half = gather_direct(jnp.concatenate(up_parts), "fsdp")
-        other_half = gather_direct(fc2_weight.astype(LOW), "fsdp")
-
     (norm1,) = local_call(
         first_norm_kernel, (meta, token_rows, vectors), [low_like(rows, model)]
     )
@@ -705,7 +738,18 @@
     )
     kv_earlier = jnp.stack([shift(kv, "ctx", by) for by in range(1, contexts)])
 
-    branch_pieces = gather_pieces(after(grad_rows, norm1_pieces[-1]))
+    branch_pieces = gather_pieces(grad_rows)
+    if halves:
+        (half,) = local_call(
+            functools.partial(half_kernel, parts),
+            (meta, *up_parts, fc2_weight),
+            [low_like(hidden_shard, model)],
+        )
+        own_half = gather_direct(after(half, kv_earlier, *out_pieces[1:]), "fsdp")
+        other_half = [shift(piece, "ctx", 1) for piece in own_half]
+    else:
+        own_half = gather_direct(jnp.concatenate(up_parts), "fsdp")
+        other_half = gather_direct(fc2_weight.astype(LOW), "fsdp")
 
     score_flops = 2 * group * group * width
     wide_square = pltpu.VMEM((group, group), WIDE)
@@ -771,18 +815,38 @@
     )
     attn_grad, mixed_part, sums = local_call(
         functools.partial(second_norm_grad_kernel, parts),
-        (meta, norm2_keep, *norm2_arrived, token_rows, attended, grad_rows, vectors),
+        (
+            meta, after(norm2_keep, fed_keep), *norm2_arrived, token_rows, attended, grad_rows,
+            vectors,
+        ),
         [low_like(rows, model), wide_like(rows, model), wide_like(8, model)],
     )
     attn_pieces = gather_pieces(attn_grad)
-    if halves:
-        half_arrived = shift(sent_half, "ctx", 1)
-        half_keep, *half_sends = local_call(
-            fold_kernel,
-            (meta, kept_half, after(half_arrived, attn_pieces[-1])),
-            [wide_like(hidden_shard, model)] + [low_like(hidden_shard, model)] * (depth - 1),
+
+    def fold(kept, sent, *later):
+        arrived = after(shift(sent, "ctx", 1), *later)
+        shape = kept.shape[1:]
+        keep, *sends = local_call(
+            fold_kernel, (meta, kept, arrived), [wide_like(*shape)] + [low_like(*shape)] * (depth - 1)
         )
-        half_pieces = send_pieces(half_sends, "fsdp")
+        return keep, sends
+
+    def direct_totals(*grads):
+        return [
+            owner_sum(grad[0].astype(WIDE), send_pieces(list(grad[1:].astype(LOW)), "fsdp"))
+            for grad in grads
+        ]
+
+    def both_halves(mine_half, *later):
+        arrived_half = shift(after(mine_half, *later) if later else mine_half, "ctx", 1)
+        first = lax.axis_index("ctx") == 0
+        return (
+            jnp.where(first, mine_half, arrived_half), jnp.where(first, arrived_half, mine_half)
+        )
+
+    def owner_sum(keep, pieces):
+        return sum_replicas(sum_all(keep, pieces).astype(LOW))
+
     fed_arrived = send_pieces(
         lax.optimization_barrier((*fed_sends, attn_pieces[-1]))[: parts - 1], "dp"
     )
@@ -799,20 +863,20 @@
         [wide_square, wide_square, low_square, low_square],
         flops=5 * score_flops,
     )
+    if halves:
+        half_keep, half_sends = fold(kept_half, sent_half, query_grad)
+        half_pieces = send_pieces(half_sends, "fsdp")
+        query_grad = after(query_grad, half_keep)
     kv_arrived = jnp.stack(
         [shift(kv_grad[by - 1], "ctx", -by) for by in range(1, contexts)]
     )
-    kvq_own, out_keep, *out_sends = local_call(
+    kvq_own, out_grad = local_call(
         functools.partial(own_grad_kernel, parts, depth, heads, rows),
         (meta, kvq, ctx_grad, context, stat, query_grad, context_low, attn_all),
-        [wide_like(group, 3 * width), wide_like(shard, model)]
-        + [low_like(shard, model)] * (depth - 1),
-        [
-            pltpu.VMEM((width, model), WIDE), wide_square, wide_square, low_square, low_square,
-        ],
+        [wide_like(group, 3 * width), wide_like(width, model)],
+        [wide_square, wide_square, low_square, low_square],
         flops=5 * score_flops,
     )
-    out_arrived = send_pieces(out_sends, "fsdp")
     kvq_grad, norm1_keep, *rest = local_call(
         functools.partial(projection_back_kernel, parts),
         (meta, kvq_own, kv_arrived, kvq_matrix),
@@ -823,57 +887,56 @@
     )
     kvq_bias = rest[-1]
     norm1_arrived = send_pieces(rest[:-1], "dp")
-    kvq_keep, *kvq_sends = local_call(
-        functools.partial(projection_grad_kernel, parts, depth),
-        (meta, norm1_all, kvq_grad),
-        [wide_like(parts, shard, 3 * width)]
-        + [low_like(parts, shard, 3 * width)] * (depth - 1),
-        [pltpu.VMEM((model, 3 * width), WIDE)],
+    share_rows = (parts * shard + shard * model // (3 * width)) // 2
+    kept_share, sent_share = local_call(
+        functools.partial(projection_grad_kernel, parts, depth, halves),
+        (meta, norm1_all, kvq_grad, out_grad),
+        [wide_like(depth, share_rows, 3 * width), low_like(depth, share_rows, 3 * width)],
+        [
+            pltpu.VMEM((model, 3 * width), WIDE),
+            pltpu.VMEM((shard * model // (3 * width), 3 * width), WIDE),
+        ],
         flops=2 * group * model * 3 * width,
     )
-    kvq_arrived = send_pieces(kvq_sends, "fsdp")
     input_part, sums = local_call(
         functools.partial(first_norm_grad_kernel, parts),
         (
-            meta, norm1_keep, *norm1_arrived, token_rows, vectors, mixed_part, sums, kvq_bias,
-            up_bias,
+            meta, after(norm1_keep, kept_share), *norm1_arrived, token_rows, vectors, mixed_part,
+            sums, kvq_bias, up_bias,
         ),
         [low_like(rows, model), wide_like(8, model)],
     )
 
+    input_rows = transpose_homes(input_part)
+    input_grad = cotangent[0] + input_rows.astype(WIDE)
     delta = sum_all(fed_keep, fed_arrived) + vectors[5:6] + attended
-    delta = after(delta.astype(LOW), kvq_own)
+    delta = after(delta.astype(LOW), input_rows)
     output = tokens[0] + transpose_homes(delta).astype(WIDE)
-    input_grad = cotangent[0] + transpose_homes(input_part).astype(WIDE)
-
-    def owner_sum(keep, pieces, *later):
-        low = sum_all(keep, pieces).astype(LOW)
-        return sum_replicas(after(low, *later) if later else low)
-
-    out_total = owner_sum(out_keep, out_arrived, kv_arrived)
+
     if halves:
-        mine_half = sum_all(half_keep, half_pieces).astype(LOW)
-        arrived_half = shift(after(mine_half, kv_arrived), "ctx", 1)
-        first = lax.axis_index("ctx") == 0
-        up_total = jnp.where(first, mine_half, arrived_half)
-        down_total = jnp.where(first, arrived_half, mine_half)
+        share_keep, share_sends = fold(kept_share, sent_share, input_part)
+        share_pieces = send_pieces(share_sends, "fsdp")
+        up_total, down_total = both_halves(sum_all(half_keep, half_pieces).astype(LOW))
+        first_share, second_share = both_halves(sum_all(share_keep, share_pieces).astype(LOW))
     else:
-        up_total, down_total = [
-            owner_sum(half[0].astype(WIDE), send_pieces(list(half[1:].astype(LOW)), "fsdp"))
-            for half in (kept_half, sent_half)
-        ]
+        up_total, down_total = direct_totals(kept_half, sent_half)
+        first_share, second_share = direct_totals(kept_share, sent_share)
     up_total = up_total.astype(LOW).reshape(parts, shard, hidden_part)
     down_total = down_total.astype(WIDE)
-    up_sends = [after(up_total[slot], norm1_arrived[-1]) for slot in range(1, parts)]
     (up_total,) = local_call(
         functools.partial(join_up_kernel, parts),
-        (meta, up_total[0], *send_pieces(up_sends, "dp")),
+        (meta, up_total[0], *send_pieces([up_total[s] for s in range(1, parts)], "dp")),
         [wide_like(shard, parts * hidden_part)],
     )
-    kvq_total = owner_sum(kvq_keep, kvq_arrived).astype(LOW)
+    *kvq_total, out_total = local_call(
+        functools.partial(unfold_kernel, parts),
+        (meta, first_share, second_share),
+        [low_like(shard, 3 * width)] * parts + [wide_like(shard, model)],
+        [pltpu.VMEM((shard * model // (3 * width), 3 * width), WIDE)],
+    )
     (qkv_total,) = local_call(
         functools.partial(join_qkv_kernel, parts, width),
-        (meta, kvq_total[0], *send_pieces([kvq_total[s] for s in range(1, parts)], "dp")),
+        (meta, kvq_total[0], *send_pieces(kvq_total[1:], "dp")),
         [wide_like(shard, 3 * model)],
     )
     sums = sum_replicas(sum_doubling(sums, "fsdp"))

time: 302 us -> 290 us (0.960); the launches traced: 297 us -> 290 us
  local copies, waits for them, and re-layouts: 16.7 us -> 7.36 us
  waiting for transfers between devices: 120 us -> 115 us
    ppermute x11, waiting for transfers between devices: 38.8 us -> 12.2 us  [shift(): lax.ppermute(value, axis, [(at, (at + by) % count) for at in range(count)])]
    ppermute x62 -> x59, waiting for transfers between devices: 80.7 us -> 103 us  [swap(): return lax.ppermute(value, axis, [(at, at ^ bit) for at in range(count)])]
    unnamed x50 -> x22, local copies, waits for them, and re-layouts: 13.5 us -> 1.73 us
    ppermute x11, starting transfers between devices: 30.7 us -> 38.2 us  [shift(): lax.ppermute(value, axis, [(at, (at + by) % count) for at in range(count)])]
    ppermute x62 -> x59, starting transfers between devices: 77.8 us -> 70.9 us  [swap(): return lax.ppermute(value, axis, [(at, at ^ bit) for at in range(count)])]
    pallas_call x19 -> x21, Pallas kernels: 39.7 us -> 41.1 us  [local_call(): pl.pallas_call(kernel, name=getattr(kernel, 'func', kernel).__name__, out...]
  transfers between devices with their start and end apart: 77 -> 74, of which waited for: 28 -> 30; matrix products, arithmetic and copies ran while one was open for 2% -> 6% of each run, Pallas kernels for 10% -> 9%
where the time goes in v5:
time: 290 us
  waiting for transfers between devices  115 us (40%)
  starting transfers between devices  114 us (39%)
  Pallas kernels  41.1 us (14%)
  other arithmetic  11.1 us (4%)
  local copies, waits for them, and re-layouts  7.36 us (3%)
    ppermute x59, waiting for transfers between devices, swap(): return lax.ppermute(value, axis, [(at, at ^ bit) for at in range(count)])  103 us
    ppermute x59, starting transfers between devices, swap(): return lax.ppermute(value, axis, [(at, at ^ bit) for at in range(count)])  70.9 us
    pallas_call x21, Pallas kernels, local_call(): pl.pallas_call(kernel, name=getattr(kernel, 'func', kernel).__name__, out...  41.1 us
    ppermute x11, starting transfers between devices, shift(): lax.ppermute(value, axis, [(at, (at + by) % count) for at in range(count)])  38.2 us
    ppermute x11, waiting for transfers between devices, shift(): lax.ppermute(value, axis, [(at, (at + by) % count) for at in range(count)])  12.2 us
  transfers between devices with their start and end apart: 74, of which 30 were waited for; matrix products, arithmetic and copies ran while one was open for 6% of the time, Pallas kernels for 9%

profile of v5, /device:TPU:0, one launch (start us, length us, event | category | flops | bytes accessed | tf_op | source)
XLA Modules:
  0.0 289.8 jit_solution(9476976285089716443)
XLA Ops:
  8.3 3.0 %collective-permute-start.2 = (f32[8,768]{1,0:T(8,128)S(1)}, f32[8,768]{1,0:T(8,128)S(1)}, u32[]{:S(2)}, u32[]{:S(2)}) collective-permute-start(f32[8,768]{1,0:T(8,128)S(1)} %dynamic_update_slice.15), channel_id=1, source_target_pairs={{0,1},{1,0},{2,3},{3,2},{4,5},{5,4},{6,7},{7,6},{8,9},{9,8},{10,11... | collective-permute-start | bytes 73736 | tf_op jit(solution)/shard_map/ppermute | solution.py:24
  13.3 2.8 collective-permute-start.3
  19.7 6.4 %collective-permute-start.10 = (bf16[48,576]{1,0:T(8,128)(2,1)S(1)}, bf16[48,576]{1,0:T(8,128)(2,1)S(1)}, u32[]{:S(2)}, u32[]{:S(2)}) collective-permute-start(bf16[48,576]{1,0:T(8,128)(2,1)S(1)} %get-tuple-element.107), channel_id=1, source_target_pairs={{0,24},{8,16},{16,8},{24,0},{1,25},{9,17},{17,9},{25,1},{2,26},{10... | collective-permute-start | bytes 165896 | tf_op jit(solution)/shard_map/ppermute | solution.py:24
  28.3 3.7 %collective-permute-done.5 = f32[8,768]{1,0:T(8,128)S(1)} collective-permute-done((f32[8,768]{1,0:T(8,128)S(1)}, f32[8,768]{1,0:T(8,128)S(1)}, u32[]{:S(2)}, u32[]{:S(2)}) %collective-permute-start.5) | collective-permute-done | bytes 24608 | tf_op jit(solution)/shard_map/ppermute | solution.py:24
  32.8 4.1 %collective-permute-start.7 = (bf16[128,768]{1,0:T(8,128)(2,1)S(1)}, bf16[128,768]{1,0:T(8,128)(2,1)S(1)}, u32[]{:S(2)}, u32[]{:S(2)}) collective-permute-start(bf16[128,768]{1,0:T(8,128)(2,1)S(1)} %first_norm_kernel.1.refs_0_), channel_id=1, source_target_pairs={{0,16},{8,24},{16,0},{24,8},{1,17},{9,25},{17,1},{25,9},{2,18},{10... | collective-permute-start | bytes 589832 | tf_op jit(solution)/shard_map/ppermute | solution.py:24
  37.6 3.9 %collective-permute-start.13 = (bf16[4,48,576]{2,1,0:T(8,128)(2,1)S(1)}, bf16[4,48,576]{2,1,0:T(8,128)(2,1)S(1)}, u32[]{:S(2)}, u32[]{:S(2)}) collective-permute-start(bf16[4,48,576]{2,1,0:T(8,128)(2,1)S(1)} %pad_maximum_fusion.refs_4_), channel_id=1, source_target_pairs={{0,3},{1,2},{2,1},{3,0},{4,7},{5,6},{6,5},{7,4},{8,11},{9,10},{10,... | collective-permute-start | bytes 663560 | tf_op jit(solution)/shard_map/ppermute | solution.py:24
  42.0 3.9 %collective-permute-done.11.refs_5_ = bf16[4,48,576]{2,1,0:T(8,128)(2,1)S(1)} collective-permute-done((bf16[4,48,576]{2,1,0:T(8,128)(2,1)S(1)}, bf16[4,48,576]{2,1,0:T(8,128)(2,1)S(1)}, u32[]{:S(2)}, u32[]{:S(2)}) %collective-permute-start.11) | collective-permute-done | bytes 221216 | tf_op jit(solution)/shard_map/ppermute | solution.py:24
  45.9 12.0 %collective-permute-done.12.refs_6_ = bf16[4,48,576]{2,1,0:T(8,128)(2,1)S(1)} collective-permute-done((bf16[4,48,576]{2,1,0:T(8,128)(2,1)S(1)}, bf16[4,48,576]{2,1,0:T(8,128)(2,1)S(1)}, u32[]{:S(2)}, u32[]{:S(2)}) %collective-permute-start.12) | collective-permute-done | bytes 221216 | tf_op jit(solution)/shard_map/ppermute | solution.py:24
  61.7 4.7 %collective-permute-start.15 = (bf16[48,768]{1,0:T(8,128)(2,1)S(1)}, bf16[48,768]{1,0:T(8,128)(2,1)S(1)}, u32[]{:S(2)}, u32[]{:S(2)}) collective-permute-start(bf16[48,768]{1,0:T(8,128)(2,1)S(1)} %convert_element_type.75.refs_4_), channel_id=1, source_target_pairs={{0,1},{1,0},{2,3},{3,2},{4,5},{5,4},{6,7},{7,6},{8,9},{9,8},{10,11... | collective-permute-start | bytes 221192 | tf_op jit(solution)/shard_map/ppermute | solution.py:24
  69.4 3.2 %collective-permute-done.15.refs_5_ = bf16[48,768]{1,0:T(8,128)(2,1)S(1)} collective-permute-done((bf16[48,768]{1,0:T(8,128)(2,1)S(1)}, bf16[48,768]{1,0:T(8,128)(2,1)S(1)}, u32[]{:S(2)}, u32[]{:S(2)}) %collective-permute-start.15) | collective-permute-done | bytes 73760 | tf_op jit(solution)/shard_map/ppermute | solution.py:24
  72.6 6.4 %collective-permute-done.16.refs_6_ = bf16[48,768]{1,0:T(8,128)(2,1)S(1)} collective-permute-done((bf16[48,768]{1,0:T(8,128)(2,1)S(1)}, bf16[48,768]{1,0:T(8,128)(2,1)S(1)}, u32[]{:S(2)}, u32[]{:S(2)}) %collective-permute-start.16) | collective-permute-done | bytes 73760 | tf_op jit(solution)/shard_map/ppermute | solution.py:24
  79.0 6.8 %own_forward.1 = (f32[512,192]{1,0:T(8,128)S(1)}, f32[512,128]{1,0:T(8,128)S(1)}) custom-call(s32[6]{0:T(128)S(1)} %stack.76.meta_ref.place_ref, bf16[512,576]{1,0:T(8,128)(2,1)S(1)} %get-tuple-element.108.kvq_ref.refs_0_.refs_5_), custom_call_target="tpu_custom_call" | custom-call | flops 201326592 | bytes 1245208 | tf_op jit(solution)/shard_map/own_forward/pallas_call | solution.py:649
  92.5 7.1 %collective-permute-done.30.refs_3_ = bf16[48,768]{1,0:T(8,128)(2,1)S(1)} collective-permute-done((bf16[48,768]{1,0:T(8,128)(2,1)S(1)}, bf16[48,768]{1,0:T(8,128)(2,1)S(1)}, u32[]{:S(2)}, u32[]{:S(2)}) %collective-permute-start.30) | collective-permute-done | bytes 73760 | tf_op jit(solution)/shard_map/ppermute | solution.py:24
  106.5 8.2 %collective-permute-start.34 = (bf16[192,768]{1,0:T(8,128)(2,1)S(1)}, bf16[192,768]{1,0:T(8,128)(2,1)S(1)}, u32[]{:S(2)}, u32[]{:S(2)}) collective-permute-start(bf16[192,768]{1,0:T(8,128)(2,1)S(1)} %half_kernel.1.refs_8_), channel_id=1, source_target_pairs={{0,4},{4,0},{1,5},{5,1},{2,6},{6,2},{3,7},{7,3},{8,12},{12,8},{9,1... | collective-permute-start | bytes 884744 | tf_op jit(solution)/shard_map/ppermute | solution.py:29
  116.8 7.2 %collective-permute-start.35 = (bf16[192,768]{1,0:T(8,128)(2,1)S(1)}, bf16[192,768]{1,0:T(8,128)(2,1)S(1)}, u32[]{:S(2)}, u32[]{:S(2)}) collective-permute-start(bf16[192,768]{1,0:T(8,128)(2,1)S(1)} %collective-permute-done.31.refs_9_), channel_id=1, source_target_pairs={{0,4},{4,0},{1,5},{5,1},{2,6},{6,2},{3,7},{7,3},{8,12},{12,8},{9,1... | collective-permute-start | bytes 884744 | tf_op jit(solution)/shard_map/ppermute | solution.py:29
  125.4 7.4 %collective-permute-start.36 = (bf16[192,768]{1,0:T(8,128)(2,1)S(1)}, bf16[192,768]{1,0:T(8,128)(2,1)S(1)}, u32[]{:S(2)}, u32[]{:S(2)}) collective-permute-start(bf16[192,768]{1,0:T(8,128)(2,1)S(1)} %collective-permute-done.32.refs_10_), channel_id=1, source_target_pairs={{0,4},{4,0},{1,5},{5,1},{2,6},{6,2},{3,7},{7,3},{8,12},{12,8},{9,1... | collective-permute-start | bytes 884744 | tf_op jit(solution)/shard_map/ppermute | solution.py:29
  134.6 5.5 %collective-permute-done.36.refs_14_ = bf16[192,768]{1,0:T(8,128)(2,1)S(1)} collective-permute-done((bf16[192,768]{1,0:T(8,128)(2,1)S(1)}, bf16[192,768]{1,0:T(8,128)(2,1)S(1)}, u32[]{:S(2)}, u32[]{:S(2)}) %collective-permute-start.36) | collective-permute-done | bytes 294944 | tf_op jit(solution)/shard_map/ppermute | solution.py:29
  140.1 3.2 %collective-permute-done.37.refs_15_ = bf16[192,768]{1,0:T(8,128)(2,1)S(1)} collective-permute-done((bf16[192,768]{1,0:T(8,128)(2,1)S(1)}, bf16[192,768]{1,0:T(8,128)(2,1)S(1)}, u32[]{:S(2)}, u32[]{:S(2)}) %collective-permute-start.37) | collective-permute-done | bytes 294944 | tf_op jit(solution)/shard_map/ppermute | solution.py:29
  143.3 4.9 %feed_kernel.1 = (f32[128,768]{1,0:T(8,128)S(1)}, bf16[128,768]{1,0:T(8,128)(2,1)S(1)}, bf16[128,768]{1,0:T(8,128)(2,1)S(1)}, bf16[128,768]{1,0:T(8,128)(2,1)S(1...) custom-call(s32[6]{0:T(128)S(1)} %stack.76.meta_ref.place_ref, ...), custom_call_target="tpu_custom_call" | custom-call | flops 1811939328 | bytes 9268248 | tf_op jit(solution)/shard_map/feed_kernel/pallas_call | solution.py:649
  148.2 4.4 %feed_grad_kernel.1 = (f32[4,192,768]{2,1,0:T(8,128)S(1)}, bf16[4,192,768]{2,1,0:T(8,128)(2,1)S(1)}, f32[128,768]{1,0:T(8,128)S(1)}, bf16[128,768]{1,0:T(8,128)(...) custom-call(s32[6]{0:T(128)S(1)} %stack.76.meta_ref.place_ref, ...), custom_call_target="tpu_custom_call" | custom-call | flops 1811939328 | bytes 8847384 | tf_op jit(solution)/shard_map/feed_grad_kernel/pallas_call | solution.py:649
  154.4 3.2 %collective-permute-start.39 = (bf16[128,768]{1,0:T(8,128)(2,1)S(1)}, bf16[128,768]{1,0:T(8,128)(2,1)S(1)}, u32[]{:S(2)}, u32[]{:S(2)}) collective-permute-start(bf16[128,768]{1,0:T(8,128)(2,1)S(1)} %get-tuple-element.137), channel_id=1, source_target_pairs={{0,16},{8,24},{16,0},{24,8},{1,17},{9,25},{17,1},{25,9},{2,18},{10... | collective-permute-start | bytes 589832 | tf_op jit(solution)/shard_map/ppermute | solution.py:24
  157.7 5.6 %collective-permute-done.39.refs_2_ = bf16[128,768]{1,0:T(8,128)(2,1)S(1)} collective-permute-done((bf16[128,768]{1,0:T(8,128)(2,1)S(1)}, bf16[128,768]{1,0:T(8,128)(2,1)S(1)}, u32[]{:S(2)}, u32[]{:S(2)}) %collective-permute-start.39) | collective-permute-done | bytes 196640 | tf_op jit(solution)/shard_map/ppermute | solution.py:24
  163.3 3.8 %collective-permute-done.40.refs_3_ = bf16[128,768]{1,0:T(8,128)(2,1)S(1)} collective-permute-done((bf16[128,768]{1,0:T(8,128)(2,1)S(1)}, bf16[128,768]{1,0:T(8,128)(2,1)S(1)}, u32[]{:S(2)}, u32[]{:S(2)}) %collective-permute-start.40) | collective-permute-done | bytes 196640 | tf_op jit(solution)/shard_map/ppermute | solution.py:24
  170.0 5.3 %collective-permute-done.41.refs_2_ = bf16[128,768]{1,0:T(8,128)(2,1)S(1)} collective-permute-done((bf16[128,768]{1,0:T(8,128)(2,1)S(1)}, bf16[128,768]{1,0:T(8,128)(2,1)S(1)}, u32[]{:S(2)}, u32[]{:S(2)}) %collective-permute-start.41) | collective-permute-done | bytes 196640 | tf_op jit(solution)/shard_map/ppermute | solution.py:24
  177.9 6.4 %collective-permute-start.48 = (bf16[512,384]{1,0:T(8,128)(2,1)S(1)}, bf16[512,384]{1,0:T(8,128)(2,1)S(1)}, u32[]{:S(2)}, u32[]{:S(2)}) collective-permute-start(bf16[512,384]{1,0:T(8,128)(2,1)S(1)} %bitcast.67), channel_id=1, source_target_pairs={{0,4},{4,0},{1,5},{5,1},{2,6},{6,2},{3,7},{7,3},{8,12},{12,8},{9,1... | collective-permute-start | bytes 1179656 | tf_op jit(solution)/shard_map/ppermute | solution.py:29
  185.1 6.8 %own_grad_kernel.1 = (f32[512,576]{1,0:T(8,128)S(1)}, f32[192,768]{1,0:T(8,128)S(1)}) custom-call(s32[6]{0:T(128)S(1)} %stack.76.meta_ref.place_ref, bf16[512,576]{1,0:T(8,128)(2,1)S(1)} %get-tuple-element.108.kvq_ref.refs_0_.refs_5_, bf16[512,192]{1,0:T(8,128)(2,1)S(1)} %get-tuple-element.147.refs_1_, f32[512,192]{1,0:T(8,128)S(1)} %get-tuple-element.145.refs_7_.refs_2_, ...), custom_call_target="tpu_custom_call" | custom-call | flops 503316480 | bytes 4587544 | tf_op jit(solution)/shard_map/own_grad_kernel/pallas_call | solution.py:649
  203.1 3.5 %collective-permute-done.51.refs_3_ = bf16[128,768]{1,0:T(8,128)(2,1)S(1)} collective-permute-done((bf16[128,768]{1,0:T(8,128)(2,1)S(1)}, bf16[128,768]{1,0:T(8,128)(2,1)S(1)}, u32[]{:S(2)}, u32[]{:S(2)}) %collective-permute-start.51) | collective-permute-done | bytes 196640 | tf_op jit(solution)/shard_map/ppermute | solution.py:24
  209.2 3.1 %collective-permute-done.54 = f32[8,768]{1,0:T(8,128)S(1)} collective-permute-done((f32[8,768]{1,0:T(8,128)S(1)}, f32[8,768]{1,0:T(8,128)S(1)}, u32[]{:S(2)}, u32[]{:S(2)}) %collective-permute-start.54) | collective-permute-done | bytes 24608 | tf_op jit(solution)/shard_map/ppermute | solution.py:24
  230.7 17.7 %collective-permute-done.68 = bf16[192,768]{1,0:T(8,128)(2,1)} collective-permute-done((bf16[192,768]{1,0:T(8,128)(2,1)}, bf16[192,768]{1,0:T(8,128)(2,1)}, u32[]{:S(2)}, u32[]{:S(2)}) %collective-permute-start.68) | collective-permute-done | bytes 294944 | tf_op jit(solution)/shard_map/ppermute | solution.py:24
  256.6 3.7 %collective-permute-start.61 = (bf16[128,576]{1,0:T(8,128)(2,1)S(1)}, bf16[128,576]{1,0:T(8,128)(2,1)S(1)}, u32[]{:S(2)}, u32[]{:S(2)}) collective-permute-start(bf16[128,576]{1,0:T(8,128)(2,1)S(1)} %get-tuple-element.179), channel_id=1, source_target_pairs={{0,2},{1,3},{2,0},{3,1},{4,6},{5,7},{6,4},{7,5},{8,10},{9,11},{10,... | collective-permute-start | bytes 442376 | tf_op jit(solution)/shard_map/ppermute | solution.py:24
  261.9 3.6 %collective-permute-done.62 = bf16[128,576]{1,0:T(8,128)(2,1)S(1)} collective-permute-done((bf16[128,576]{1,0:T(8,128)(2,1)S(1)}, bf16[128,576]{1,0:T(8,128)(2,1)S(1)}, u32[]{:S(2)}, u32[]{:S(2)}) %collective-permute-start.62) | collective-permute-done | bytes 147488 | tf_op jit(solution)/shard_map/ppermute | solution.py:24
  265.5 10.5 %collective-permute-done.61 = bf16[128,576]{1,0:T(8,128)(2,1)S(1)} collective-permute-done((bf16[128,576]{1,0:T(8,128)(2,1)S(1)}, bf16[128,576]{1,0:T(8,128)(2,1)S(1)}, u32[]{:S(2)}, u32[]{:S(2)}) %collective-permute-start.61) | collective-permute-done | bytes 147488 | tf_op jit(solution)/shard_map/ppermute | solution.py:24
  (201 shorter events, 106.4 us)
Async XLA Ops:
  19.7 17.2 %collective-permute-start.10 = (bf16[48,576]{1,0:T(8,128)(2,1)S(1)}, bf16[48,576]{1,0:T(8,128)(2,1)S(1)}, u32[]{:S(2)}, u32[]{:S(2)}) collective-permute-start(bf16[48,576]{1,0:T(8,128)(2,1)S(1)} %get-tuple-element.107), channel_id=1, source_target_pairs={{0,24},{8,16},{16,8},{24,0},{1,25},{9,17},{17,9},{25,1},{2,26},{10... | collective-permute-start | bytes 165896 | tf_op jit(solution)/shard_map/ppermute | solution.py:24
  37.6 20.3 %collective-permute-start.12 = (bf16[4,48,576]{2,1,0:T(8,128)(2,1)S(1)}, bf16[4,48,576]{2,1,0:T(8,128)(2,1)S(1)}, u32[]{:S(2)}, u32[]{:S(2)}) collective-permute-start(bf16[4,48,576]{2,1,0:T(8,128)(2,1)S(1)} %pad_maximum_fusion.refs_4_), channel_id=1, source_target_pairs={{0,2},{1,3},{2,0},{3,1},{4,6},{5,7},{6,4},{7,5},{8,10},{9,11},{10,... | collective-permute-start | bytes 663560 | tf_op jit(solution)/shard_map/ppermute | solution.py:24
  37.6 20.3 %collective-permute-start.13 = (bf16[4,48,576]{2,1,0:T(8,128)(2,1)S(1)}, bf16[4,48,576]{2,1,0:T(8,128)(2,1)S(1)}, u32[]{:S(2)}, u32[]{:S(2)}) collective-permute-start(bf16[4,48,576]{2,1,0:T(8,128)(2,1)S(1)} %pad_maximum_fusion.refs_4_), channel_id=1, source_target_pairs={{0,3},{1,2},{2,1},{3,0},{4,7},{5,6},{6,5},{7,4},{8,11},{9,10},{10,... | collective-permute-start | bytes 663560 | tf_op jit(solution)/shard_map/ppermute | solution.py:24
  41.5 16.4 %collective-permute-start.6 = (bf16[128,768]{1,0:T(8,128)(2,1)S(1)}, bf16[128,768]{1,0:T(8,128)(2,1)S(1)}, u32[]{:S(2)}, u32[]{:S(2)}) collective-permute-start(bf16[128,768]{1,0:T(8,128)(2,1)S(1)} %first_norm_kernel.1.refs_0_), channel_id=1, source_target_pairs={{0,8},{8,0},{16,24},{24,16},{1,9},{9,1},{17,25},{25,17},{2,10},{10... | collective-permute-start | bytes 589832 | tf_op jit(solution)/shard_map/ppermute | solution.py:24
  41.5 16.4 %collective-permute-start.8 = (bf16[128,768]{1,0:T(8,128)(2,1)S(1)}, bf16[128,768]{1,0:T(8,128)(2,1)S(1)}, u32[]{:S(2)}, u32[]{:S(2)}) collective-permute-start(bf16[128,768]{1,0:T(8,128)(2,1)S(1)} %collective-permute-done.7.refs_2_), channel_id=1, source_target_pairs={{0,8},{8,0},{16,24},{24,16},{1,9},{9,1},{17,25},{25,17},{2,10},{10... | collective-permute-start | bytes 589832 | tf_op jit(solution)/shard_map/ppermute | solution.py:24
  59.3 29.8 %collective-permute-start.14 = (bf16[512,384]{1,0:T(8,128)(2,1)S(1)}, bf16[512,384]{1,0:T(8,128)(2,1)S(1)}, u32[]{:S(2)}, u32[]{:S(2)}) collective-permute-start(bf16[512,384]{1,0:T(8,128)(2,1)S(1)} %get-tuple-element.109), channel_id=1, source_target_pairs={{0,4},{4,0},{1,5},{5,1},{2,6},{6,2},{3,7},{7,3},{8,12},{12,8},{9,1... | collective-permute-start | bytes 1179656 | tf_op jit(solution)/shard_map/ppermute | solution.py:29
  61.0 24.9 %collective-permute-start.24 = (bf16[128,768]{1,0:T(8,128)(2,1)S(1)}, bf16[128,768]{1,0:T(8,128)(2,1)S(1)}, u32[]{:S(2)}, u32[]{:S(2)}) collective-permute-start(bf16[128,768]{1,0:T(8,128)(2,1)S(1)} %bitcast_convert_fusion), channel_id=1, source_target_pairs={{0,0},{1,8},{2,16},{3,24},{8,1},{9,9},{10,17},{11,25},{16,2},{17,1... | collective-permute-start | bytes 589832 | tf_op jit(solution)/shard_map/ppermute | solution.py:35
  67.4 19.9 %collective-permute-start.17 = (bf16[48,768]{1,0:T(8,128)(2,1)S(1)}, bf16[48,768]{1,0:T(8,128)(2,1)S(1)}, u32[]{:S(2)}, u32[]{:S(2)}) collective-permute-start(bf16[48,768]{1,0:T(8,128)(2,1)S(1)} %convert_element_type.75.refs_4_), channel_id=1, source_target_pairs={{0,3},{1,2},{2,1},{3,0},{4,7},{5,6},{6,5},{7,4},{8,11},{9,10},{10,... | collective-permute-start | bytes 221192 | tf_op jit(solution)/shard_map/ppermute | solution.py:24
  72.6 18.0 %collective-permute-start.28 = (bf16[48,768]{1,0:T(8,128)(2,1)S(1)}, bf16[48,768]{1,0:T(8,128)(2,1)S(1)}, u32[]{:S(2)}, u32[]{:S(2)}) collective-permute-start(bf16[48,768]{1,0:T(8,128)(2,1)S(1)} %get-tuple-element.121), channel_id=1, source_target_pairs={{0,8},{8,0},{16,24},{24,16},{1,9},{9,1},{17,25},{25,17},{2,10},{10... | collective-permute-start | bytes 221192 | tf_op jit(solution)/shard_map/ppermute | solution.py:24
  85.9 16.0 %collective-permute-start.25 = (bf16[128,768]{1,0:T(8,128)(2,1)S(1)}, bf16[128,768]{1,0:T(8,128)(2,1)S(1)}, u32[]{:S(2)}, u32[]{:S(2)}) collective-permute-start(bf16[128,768]{1,0:T(8,128)(2,1)S(1)} %collective-permute-done.24.refs_4_.refs_6_), channel_id=1, source_target_pairs={{0,8},{8,0},{16,24},{24,16},{1,9},{9,1},{17,25},{25,17},{2,10},{10... | collective-permute-start | bytes 589832 | tf_op jit(solution)/shard_map/ppermute | solution.py:24
  87.4 14.4 %collective-permute-start.26 = (bf16[128,768]{1,0:T(8,128)(2,1)S(1)}, bf16[128,768]{1,0:T(8,128)(2,1)S(1)}, u32[]{:S(2)}, u32[]{:S(2)}) collective-permute-start(bf16[128,768]{1,0:T(8,128)(2,1)S(1)} %collective-permute-done.24.refs_4_.refs_6_), channel_id=1, source_target_pairs={{0,16},{8,24},{16,0},{24,8},{1,17},{9,25},{17,1},{25,9},{2,18},{10... | collective-permute-start | bytes 589832 | tf_op jit(solution)/shard_map/ppermute | solution.py:24
  101.9 14.9 %collective-permute-start.31 = (bf16[192,768]{1,0:T(8,128)(2,1)S(1)}, bf16[192,768]{1,0:T(8,128)(2,1)S(1)}, u32[]{:S(2)}, u32[]{:S(2)}) collective-permute-start(bf16[192,768]{1,0:T(8,128)(2,1)S(1)} %half_kernel.1.refs_8_), channel_id=1, source_target_pairs={{0,1},{1,0},{2,3},{3,2},{4,5},{5,4},{6,7},{7,6},{8,9},{9,8},{10,11... | collective-permute-start | bytes 884744 | tf_op jit(solution)/shard_map/ppermute | solution.py:24
  102.0 23.5 %collective-permute-start.32 = (bf16[192,768]{1,0:T(8,128)(2,1)S(1)}, bf16[192,768]{1,0:T(8,128)(2,1)S(1)}, u32[]{:S(2)}, u32[]{:S(2)}) collective-permute-start(bf16[192,768]{1,0:T(8,128)(2,1)S(1)} %half_kernel.1.refs_8_), channel_id=1, source_target_pairs={{0,2},{1,3},{2,0},{3,1},{4,6},{5,7},{6,4},{7,5},{8,10},{9,11},{10,... | collective-permute-start | bytes 884744 | tf_op jit(solution)/shard_map/ppermute | solution.py:24
  104.7 28.1 %collective-permute-start.33 = (bf16[192,768]{1,0:T(8,128)(2,1)S(1)}, bf16[192,768]{1,0:T(8,128)(2,1)S(1)}, u32[]{:S(2)}, u32[]{:S(2)}) collective-permute-start(bf16[192,768]{1,0:T(8,128)(2,1)S(1)} %half_kernel.1.refs_8_), channel_id=1, source_target_pairs={{0,3},{1,2},{2,1},{3,0},{4,7},{5,6},{6,5},{7,4},{8,11},{9,10},{10,... | collective-permute-start | bytes 884744 | tf_op jit(solution)/shard_map/ppermute | solution.py:24
  106.5 26.4 %collective-permute-start.34 = (bf16[192,768]{1,0:T(8,128)(2,1)S(1)}, bf16[192,768]{1,0:T(8,128)(2,1)S(1)}, u32[]{:S(2)}, u32[]{:S(2)}) collective-permute-start(bf16[192,768]{1,0:T(8,128)(2,1)S(1)} %half_kernel.1.refs_8_), channel_id=1, source_target_pairs={{0,4},{4,0},{1,5},{5,1},{2,6},{6,2},{3,7},{7,3},{8,12},{12,8},{9,1... | collective-permute-start | bytes 884744 | tf_op jit(solution)/shard_map/ppermute | solution.py:29
  115.5 17.5 %collective-permute-start.22 = (bf16[128,768]{1,0:T(8,128)(2,1)S(1)}, bf16[128,768]{1,0:T(8,128)(2,1)S(1)}, u32[]{:S(2)}, u32[]{:S(2)}) collective-permute-start(bf16[128,768]{1,0:T(8,128)(2,1)S(1)} %get-tuple-element.117.refs_0_), channel_id=1, source_target_pairs={{0,16},{8,24},{16,0},{24,8},{1,17},{9,25},{17,1},{25,9},{2,18},{10... | collective-permute-start | bytes 589832 | tf_op jit(solution)/shard_map/ppermute | solution.py:24
  116.8 17.8 %collective-permute-start.35 = (bf16[192,768]{1,0:T(8,128)(2,1)S(1)}, bf16[192,768]{1,0:T(8,128)(2,1)S(1)}, u32[]{:S(2)}, u32[]{:S(2)}) collective-permute-start(bf16[192,768]{1,0:T(8,128)(2,1)S(1)} %collective-permute-done.31.refs_9_), channel_id=1, source_target_pairs={{0,4},{4,0},{1,5},{5,1},{2,6},{6,2},{3,7},{7,3},{8,12},{12,8},{9,1... | collective-permute-start | bytes 884744 | tf_op jit(solution)/shard_map/ppermute | solution.py:29
  125.4 14.7 %collective-permute-start.36 = (bf16[192,768]{1,0:T(8,128)(2,1)S(1)}, bf16[192,768]{1,0:T(8,128)(2,1)S(1)}, u32[]{:S(2)}, u32[]{:S(2)}) collective-permute-start(bf16[192,768]{1,0:T(8,128)(2,1)S(1)} %collective-permute-done.32.refs_10_), channel_id=1, source_target_pairs={{0,4},{4,0},{1,5},{5,1},{2,6},{6,2},{3,7},{7,3},{8,12},{12,8},{9,1... | collective-permute-start | bytes 884744 | tf_op jit(solution)/shard_map/ppermute | solution.py:29
  152.6 31.8 %collective-permute-start.47 = (bf16[4,192,768]{2,1,0:T(8,128)(2,1)S(1)}, bf16[4,192,768]{2,1,0:T(8,128)(2,1)S(1)}, u32[]{:S(2)}, u32[]{:S(2)}) collective-permute-start(bf16[4,192,768]{2,1,0:T(8,128)(2,1)S(1)} %get-tuple-element.150), channel_id=1, source_target_pairs={{0,4},{4,0},{1,5},{5,1},{2,6},{6,2},{3,7},{7,3},{8,12},{12,8},{9,1... | collective-permute-start | bytes 3538952 | tf_op jit(solution)/shard_map/ppermute | solution.py:29
  177.9 15.8 %collective-permute-start.48 = (bf16[512,384]{1,0:T(8,128)(2,1)S(1)}, bf16[512,384]{1,0:T(8,128)(2,1)S(1)}, u32[]{:S(2)}, u32[]{:S(2)}) collective-permute-start(bf16[512,384]{1,0:T(8,128)(2,1)S(1)} %bitcast.67), channel_id=1, source_target_pairs={{0,4},{4,0},{1,5},{5,1},{2,6},{6,2},{3,7},{7,3},{8,12},{12,8},{9,1... | collective-permute-start | bytes 1179656 | tf_op jit(solution)/shard_map/ppermute | solution.py:29
  197.2 21.7 %collective-permute-start.45 = (bf16[128,768]{1,0:T(8,128)(2,1)}, bf16[128,768]{1,0:T(8,128)(2,1)}, u32[]{:S(2)}, u32[]{:S(2)}) collective-permute-start(bf16[128,768]{1,0:T(8,128)(2,1)} %get-tuple-element.143), channel_id=1, source_target_pairs={{0,24},{8,16},{16,8},{24,0},{1,25},{9,17},{17,9},{25,1},{2,26},{10... | collective-permute-start | bytes 589832 | tf_op jit(solution)/shard_map/ppermute | solution.py:24
  198.8 22.1 %collective-permute-start.44 = (bf16[128,768]{1,0:T(8,128)(2,1)}, bf16[128,768]{1,0:T(8,128)(2,1)}, u32[]{:S(2)}, u32[]{:S(2)}) collective-permute-start(bf16[128,768]{1,0:T(8,128)(2,1)} %get-tuple-element.142), channel_id=1, source_target_pairs={{0,16},{8,24},{16,0},{24,8},{1,17},{9,25},{17,1},{25,9},{2,18},{10... | collective-permute-start | bytes 589832 | tf_op jit(solution)/shard_map/ppermute | solution.py:24
  199.1 23.5 %collective-permute-start.43 = (bf16[128,768]{1,0:T(8,128)(2,1)}, bf16[128,768]{1,0:T(8,128)(2,1)}, u32[]{:S(2)}, u32[]{:S(2)}) collective-permute-start(bf16[128,768]{1,0:T(8,128)(2,1)} %get-tuple-element.141), channel_id=1, source_target_pairs={{0,8},{8,0},{16,24},{24,16},{1,9},{9,1},{17,25},{25,17},{2,10},{10... | collective-permute-start | bytes 589832 | tf_op jit(solution)/shard_map/ppermute | solution.py:24
  214.1 14.7 %collective-permute-start.69 = (bf16[192,768]{1,0:T(8,128)(2,1)}, bf16[192,768]{1,0:T(8,128)(2,1)}, u32[]{:S(2)}, u32[]{:S(2)}) collective-permute-start(bf16[192,768]{1,0:T(8,128)(2,1)} %copy-done.5), channel_id=1, source_target_pairs={{0,3},{1,2},{2,1},{3,0},{4,7},{5,6},{6,5},{7,4},{8,11},{9,10},{10,... | collective-permute-start | bytes 884744 | tf_op jit(solution)/shard_map/ppermute | solution.py:24
  217.0 31.4 %collective-permute-start.68 = (bf16[192,768]{1,0:T(8,128)(2,1)}, bf16[192,768]{1,0:T(8,128)(2,1)}, u32[]{:S(2)}, u32[]{:S(2)}) collective-permute-start(bf16[192,768]{1,0:T(8,128)(2,1)} %copy-done.4), channel_id=1, source_target_pairs={{0,2},{1,3},{2,0},{3,1},{4,6},{5,7},{6,4},{7,5},{8,10},{9,11},{10,... | collective-permute-start | bytes 884744 | tf_op jit(solution)/shard_map/ppermute | solution.py:24
  218.8 29.6 %collective-permute-start.67 = (bf16[192,768]{1,0:T(8,128)(2,1)}, bf16[192,768]{1,0:T(8,128)(2,1)}, u32[]{:S(2)}, u32[]{:S(2)}) collective-permute-start(bf16[192,768]{1,0:T(8,128)(2,1)} %copy-done.3), channel_id=1, source_target_pairs={{0,1},{1,0},{2,3},{3,2},{4,5},{5,4},{6,7},{7,6},{8,9},{9,8},{10,11... | collective-permute-start | bytes 884744 | tf_op jit(solution)/shard_map/ppermute | solution.py:24
  225.6 28.9 %collective-permute-start.59 = (bf16[4,128,576]{1,2,0:T(8,128)(2,1)}, bf16[4,128,576]{1,2,0:T(8,128)(2,1)}, u32[]{:S(2)}, u32[]{:S(2)}) collective-permute-start(bf16[4,128,576]{1,2,0:T(8,128)(2,1)} %copy.30), channel_id=1, source_target_pairs={{0,4},{4,0},{1,5},{5,1},{2,6},{6,2},{3,7},{7,3},{8,12},{12,8},{9,1... | collective-permute-start | bytes 1769480 | tf_op jit(solution)/shard_map/ppermute | solution.py:29
  227.2 24.9 %collective-permute-start.52 = (bf16[128,768]{1,0:T(8,128)(2,1)}, bf16[128,768]{1,0:T(8,128)(2,1)S(1)}, u32[]{:S(2)}, u32[]{:S(2)}) collective-permute-start(bf16[128,768]{1,0:T(8,128)(2,1)} %copy-done.6), channel_id=1, source_target_pairs={{0,0},{1,8},{2,16},{3,24},{8,1},{9,9},{10,17},{11,25},{16,2},{17,1... | collective-permute-start | bytes 589832 | tf_op jit(solution)/shard_map/ppermute | solution.py:35
  228.8 22.7 %collective-permute-start.58 = (f32[8,768]{1,0:T(8,128)S(1)}, f32[8,768]{1,0:T(8,128)S(1)}, u32[]{:S(2)}, u32[]{:S(2)}) collective-permute-start(f32[8,768]{1,0:T(8,128)S(1)} %add.128), channel_id=1, source_target_pairs={{0,16},{8,24},{16,0},{24,8},{1,17},{9,25},{17,1},{25,9},{2,18},{10... | collective-permute-start | bytes 73736 | tf_op jit(solution)/shard_map/ppermute | solution.py:24
  252.1 30.8 %collective-permute-start.53 = (bf16[128,768]{1,0:T(8,128)(2,1)}, bf16[128,768]{1,0:T(8,128)(2,1)S(1)}, u32[]{:S(2)}, u32[]{:S(2)}) collective-permute-start(bf16[128,768]{1,0:T(8,128)(2,1)} %add_convert_fusion.1), channel_id=1, source_target_pairs={{0,0},{1,8},{2,16},{3,24},{8,1},{9,9},{10,17},{11,25},{16,2},{17,1... | collective-permute-start | bytes 589832 | tf_op jit(solution)/shard_map/ppermute | solution.py:35
  256.6 19.4 %collective-permute-start.61 = (bf16[128,576]{1,0:T(8,128)(2,1)S(1)}, bf16[128,576]{1,0:T(8,128)(2,1)S(1)}, u32[]{:S(2)}, u32[]{:S(2)}) collective-permute-start(bf16[128,576]{1,0:T(8,128)(2,1)S(1)} %get-tuple-element.179), channel_id=1, source_target_pairs={{0,2},{1,3},{2,0},{3,1},{4,6},{5,7},{6,4},{7,5},{8,10},{9,11},{10,... | collective-permute-start | bytes 442376 | tf_op jit(solution)/shard_map/ppermute | solution.py:24
  260.4 15.7 %collective-permute-start.60 = (bf16[128,576]{1,0:T(8,128)(2,1)S(1)}, bf16[128,576]{1,0:T(8,128)(2,1)S(1)}, u32[]{:S(2)}, u32[]{:S(2)}) collective-permute-start(bf16[128,576]{1,0:T(8,128)(2,1)S(1)} %get-tuple-element.178), channel_id=1, source_target_pairs={{0,1},{1,0},{2,3},{3,2},{4,5},{5,4},{6,7},{7,6},{8,9},{9,8},{10,11... | collective-permute-start | bytes 442376 | tf_op jit(solution)/shard_map/ppermute | solution.py:24
  (53 other events, 488.9 us)

commit v6 on v5

--- a/solution.py
+++ b/solution.py
@@ -12,6 +12,7 @@
 SCALE = HEAD_DIM ** (-0.5)
 MASKED = -1e30
 CHUNK = 64
+HURRY = 20
 VMEM_BYTES = 16 * 1024 * 1024
 GELU_SCALE = 0.7978845608
 GELU_CUBE = 0.044715
@@ -336,22 +337,61 @@
             keep_ref[...] = block
 
 
-def half_kernel(parts, meta_ref, *refs):
-    up, down_weight, out = take(refs, parts, None, None)
-    shard = up[0].shape[0]
-
-    @pl.when(meta_ref[parts] == 0)
-    def _up():
+def stack_kernel(parts, depth, halves, meta_ref, *refs):
+    split, down_weight, kvq_rows, vectors, feeds = take(
+        refs, parts, None, None, None, 1 if halves else 2
+    )
+    columns = kvq_rows.shape[2]
+    shard = kvq_rows.shape[1]
+    model = vectors.shape[1]
+    width = columns // 3
+    hidden_shard = down_weight.shape[0]
+    member = meta_ref[parts + 1]
+
+    def placed(slot, start):
+        rows = split[slot][:, columns : -feeds[0].shape[1]]
+        row = lax.broadcasted_iota(jnp.int32, (rows.shape[1], model), 0)
+        column = lax.broadcasted_iota(jnp.int32, (rows.shape[1], model), 1)
+        chosen = jnp.where((column == start + row) & (row < shard), 1.0, 0.0)
+        return matmul_nn(rows, chosen.astype(LOW))
+
+    whole = sum(placed(slot, (meta_ref[slot] * depth + member) * shard) for slot in range(parts))
+    vectors[0:6, :] = whole[0:6]
+    vectors[6:7, :] = (
+        placed(0, width + member * shard)[7:8] + placed(0, 2 * width + member * shard)[6:7]
+    )
+    vectors[7:8, :] = sum(
+        placed(0, member * hidden_shard + at * shard)[8 + at : 9 + at]
+        for at in range(hidden_shard // shard)
+    )
+    for slot in range(parts):
+        kvq_rows[slot] = split[slot][:, :columns]
+
+    def up(out):
         for slot in range(parts):
-            out[slot * shard : (slot + 1) * shard, :] = up[slot][...]
-
-    @pl.when(meta_ref[parts] != 0)
-    def _down():
+            out[slot * shard : (slot + 1) * shard, :] = split[slot][:, -out.shape[1] :]
+
+    def down(out):
         out[...] = down_weight[...].astype(LOW)
 
-
-def split_qkv_kernel(parts, width, meta_ref, qkv_ref, *outs):
+    if halves:
+        pl.when(meta_ref[parts] == 0)(lambda: up(feeds[0]))
+        pl.when(meta_ref[parts] != 0)(lambda: down(feeds[0]))
+    else:
+        up(feeds[0])
+        down(feeds[1])
+
+
+def split_kernel(parts, width, meta_ref, qkv_ref, up_ref, *refs):
+    vectors, outs, packed = take(refs, 9, parts, None)
     model = parts * width
+    shard = qkv_ref.shape[0]
+    packed[...] = jnp.zeros_like(packed)
+    for row, vector in enumerate(vectors):
+        values = vector[...].reshape(1, vector.shape[0])
+        for at in range(vector.shape[0] // shard):
+            packed[row + at : row + at + 1, :shard] = values[:, at * shard : (at + 1) * shard]
+    part = up_ref.shape[1] // parts
     for case in range(parts):
 
         @pl.when(meta_ref[0] == case)
@@ -363,13 +403,8 @@
                     outs[slot][:, at * width : (at + 1) * width] = qkv_ref[
                         :, start : start + width
                     ].astype(LOW)
-
-
-def split_up_kernel(parts, meta_ref, up_ref, *outs):
-    part = up_ref.shape[1] // parts
-    for slot in range(parts):
-        start = pl.multiple_of(meta_ref[slot] * part, 128)
-        outs[slot][...] = up_ref[:, pl.ds(start, part)].astype(LOW)
+                outs[slot][:, 3 * width : -part] = packed[...].astype(LOW)
+                outs[slot][:, -part:] = up_ref[:, owner * part : (owner + 1) * part].astype(LOW)
 
 
 def join_qkv_kernel(parts, width, meta_ref, *refs):
@@ -396,18 +431,24 @@
         out_ref[:, pl.ds(start, part)] = pieces[slot][...].astype(WIDE)
 
 
-def first_norm_kernel(meta_ref, tokens_ref, vectors_ref, out_ref):
-    hat, _ = normalize(tokens_ref[...].astype(WIDE))
-    out_ref[...] = (hat * vectors_ref[0:1, :] + vectors_ref[1:2, :]).astype(LOW)
-
-
 def project_kernel(parts, depth, meta_ref, *refs):
-    norm, weight, vectors_ref, kvq_ref, kv_ref, matrix_ref, norm_ref = take(
+    tokens, weight, vectors_ref, kvq_ref, kv_ref, matrix_ref, norm_ref = take(
         refs, parts, depth, None, None, None, None, None
     )
     columns = kvq_ref.shape[1]
+    rows = tokens[0].shape[0]
     place_blocks(meta_ref, parts, depth, weight, matrix_ref)
-    stack_rows(norm, norm_ref)
+    for slot, piece in enumerate(tokens):
+
+        def chunk(step, carry, slot=slot, piece=piece):
+            here = pl.multiple_of(step * CHUNK, CHUNK)
+            hat, _ = normalize(piece[pl.ds(here, CHUNK), :].astype(WIDE))
+            norm_ref[pl.ds(slot * rows + here, CHUNK), :] = (
+                hat * vectors_ref[0:1, :] + vectors_ref[1:2, :]
+            ).astype(LOW)
+            return carry
+
+        lax.fori_loop(0, rows // CHUNK, chunk, 0)
     low = (matmul_nn(norm_ref[...], matrix_ref[...]) + vectors_ref[6:7, :columns]).astype(LOW)
     kvq_ref[...] = low
     kv_ref[...] = low[:, : kv_ref.shape[1]]
@@ -654,7 +695,9 @@
         out_specs=tuple([vmem] * len(results)),
         scratch_shapes=list(scratch),
         compiler_params=pltpu.CompilerParams(vmem_limit_bytes=VMEM_BYTES),
-        cost_estimate=pl.CostEstimate(flops=flops, bytes_accessed=moved, transcendentals=0),
+        cost_estimate=pl.CostEstimate(
+            flops=flops // HURRY, bytes_accessed=moved // HURRY, transcendentals=0
+        ),
     )(*operands)
 
 
@@ -687,47 +730,37 @@
         [mine ^ slot for slot in range(parts)] + [lax.axis_index("ctx"), deep]
     ).astype(jnp.int32)
 
-    kvq_split = local_call(
-        functools.partial(split_qkv_kernel, parts, width),
-        (meta, qkv_weight),
-        [low_like(shard, 3 * width)] * parts,
-    )
-    kvq_arrived = send_pieces(kvq_split[1:], "dp")
-    kvq_rows = jnp.stack([kvq_split[0]] + kvq_arrived)
+    halves = contexts == 2
+    padded = -(-3 * width // 128) * 128
+    split = local_call(
+        functools.partial(split_kernel, parts, width),
+        (
+            meta, qkv_weight, fc1_weight, ln1_gain, ln1_bias, ln2_gain, ln2_bias, out_bias,
+            fc2_bias, q_bias, v_bias, fc1_bias,
+        ),
+        [low_like(shard, padded + hidden_part)] * parts,
+        [pltpu.VMEM((shard, padded - 3 * width), WIDE)],
+    )
+    split_arrived = send_pieces(split[1:], "dp")
+    kvq_rows, vectors, *feeds = local_call(
+        functools.partial(stack_kernel, parts, depth, halves),
+        (meta, split[0], *split_arrived, fc2_weight),
+        [low_like(parts, shard, 3 * width), wide_like(8, model)]
+        + [low_like(hidden_shard, model)] * (1 if halves else 2),
+    )
     kvq_pieces = gather_direct(kvq_rows, "fsdp")
 
-    token_rows = transpose_homes(after(tokens[0].astype(LOW), kvq_split[0]))
-
-    low_vectors = jnp.stack([ln1_gain, ln1_bias, ln2_gain, ln2_bias, out_bias, fc2_bias])
-    vectors = jnp.zeros((8, model), WIDE)
-    vectors = lax.dynamic_update_slice(
-        vectors, low_vectors.astype(LOW).astype(WIDE), (0, (mine * depth + deep) * shard)
-    )
-    for row, first, part in (
-        (6, width, v_bias), (6, 2 * width, q_bias), (7, 0, fc1_bias),
-    ):
-        part = part.astype(LOW).astype(WIDE)[None]
-        vectors = lax.dynamic_update_slice(vectors, part, (row, first + deep * part.shape[1]))
-    vectors = sum_doubling(after(vectors, kvq_arrived[0]), "fsdp")
-    everywhere = sum_doubling(vectors, "dp")
-    vectors = jnp.where(jnp.arange(8)[:, None] < 6, everywhere, vectors)
-
-    halves = contexts == 2
-    up_split = local_call(
-        functools.partial(split_up_kernel, parts),
-        (meta, after(fc1_weight, kvq_rows)),
-        [low_like(shard, hidden_part)] * parts,
-    )
-    up_parts = [up_split[0]] + send_pieces(up_split[1:], "dp")
-    out_pieces = gather_direct(after(out_weight.astype(LOW), kvq_pieces[-1]), "fsdp")
-    grad_rows = transpose_homes(after(cotangent[0].astype(LOW), kvq_pieces[-1]))
-    (norm1,) = local_call(
-        first_norm_kernel, (meta, token_rows, vectors), [low_like(rows, model)]
-    )
-    norm1_pieces = gather_pieces(norm1)
+    token_rows = transpose_homes(after(tokens[0].astype(LOW), split[0]))
+    token_pieces = gather_pieces(after(token_rows, *split_arrived))
+
+    vectors = sum_doubling(vectors, "fsdp")
+
+    out_pieces = gather_direct(after(out_weight.astype(LOW), *kvq_pieces[1:]), "fsdp")
+    grad_rows = transpose_homes(after(cotangent[0].astype(LOW), *kvq_pieces[1:]))
+
     kvq, kv, kvq_matrix, norm1_all = local_call(
         functools.partial(project_kernel, parts, depth),
-        (meta, *norm1_pieces, *kvq_pieces, vectors),
+        (meta, *token_pieces, *kvq_pieces, vectors),
         [
             low_like(group, 3 * width),
             low_like(group, 2 * width),
@@ -737,19 +770,6 @@
         flops=2 * group * model * 3 * width,
     )
     kv_earlier = jnp.stack([shift(kv, "ctx", by) for by in range(1, contexts)])
-
-    branch_pieces = gather_pieces(grad_rows)
-    if halves:
-        (half,) = local_call(
-            functools.partial(half_kernel, parts),
-            (meta, *up_parts, fc2_weight),
-            [low_like(hidden_shard, model)],
-        )
-        own_half = gather_direct(after(half, kv_earlier, *out_pieces[1:]), "fsdp")
-        other_half = [shift(piece, "ctx", 1) for piece in own_half]
-    else:
-        own_half = gather_direct(jnp.concatenate(up_parts), "fsdp")
-        other_half = gather_direct(fc2_weight.astype(LOW), "fsdp")
 
     score_flops = 2 * group * group * width
     wide_square = pltpu.VMEM((group, group), WIDE)
@@ -761,6 +781,15 @@
         [wide_square, low_square],
         flops=2 * score_flops,
     )
+    branch_pieces = gather_pieces(after(grad_rows, acc))
+    if halves:
+        own_half = gather_direct(after(feeds[0], acc, *out_pieces[1:]), "fsdp")
+        other_half = [shift(after(feeds[0], kv_earlier), "ctx", 1)]
+        other_half += [shift(piece, "ctx", 1) for piece in own_half[1:]]
+    else:
+        own_half = gather_direct(feeds[0], "fsdp")
+        other_half = gather_direct(feeds[1], "fsdp")
+
     context, context_low, stat, out_matrix, attended_keep, *attended_sends = local_call(
         functools.partial(context_kernel, parts, depth, heads),
         (meta, kvq, kv_earlier, acc, stat, *out_pieces),
@@ -866,6 +895,9 @@
     if halves:
         half_keep, half_sends = fold(kept_half, sent_half, query_grad)
         half_pieces = send_pieces(half_sends, "fsdp")
+    else:
+        half_pieces = []
+    if halves:
         query_grad = after(query_grad, half_keep)
     kv_arrived = jnp.stack(
         [shift(kv_grad[by - 1], "ctx", -by) for by in range(1, contexts)]
@@ -879,7 +911,7 @@
     )
     kvq_grad, norm1_keep, *rest = local_call(
         functools.partial(projection_back_kernel, parts),
-        (meta, kvq_own, kv_arrived, kvq_matrix),
+        (meta, after(kvq_own, *fed_arrived), kv_arrived, kvq_matrix),
         [low_like(group, 3 * width), wide_like(rows, model)]
         + [low_like(rows, model)] * (parts - 1)
         + [wide_like(1, 3 * width)],
@@ -901,7 +933,7 @@
     input_part, sums = local_call(
         functools.partial(first_norm_grad_kernel, parts),
         (
-            meta, after(norm1_keep, kept_share), *norm1_arrived, token_rows, vectors, mixed_part,
+            meta, after(norm1_keep, kept_share, *half_pieces), *norm1_arrived, token_rows, vectors, mixed_part,
             sums, kvq_bias, up_bias,
         ),
         [low_like(rows, model), wide_like(8, model)],
@@ -939,7 +971,7 @@
         (meta, kvq_total[0], *send_pieces(kvq_total[1:], "dp")),
         [wide_like(shard, 3 * model)],
     )
-    sums = sum_replicas(sum_doubling(sums, "fsdp"))
+    sums = sum_replicas(sum_doubling(after(sums, share_keep) if halves else sums, "fsdp"))
     everywhere = sum_doubling(sums, "dp")
     owned = lax.dynamic_slice(everywhere, (0, (mine * depth + deep) * shard), (6, shard))
     value_bias = lax.dynamic_slice(sums, (6, width + deep * shard), (1, shard))[0]

time: 290 us -> 277 us (0.955)
  starting transfers between devices: 114 us -> 97.7 us
  local copies, waits for them, and re-layouts: 7.36 us -> 21.1 us
  waiting for transfers between devices: 115 us -> 104 us
  Pallas kernels: 41.1 us -> 44.3 us
  other arithmetic: 11.1 us -> 7.91 us
    ppermute x59 -> x54, waiting for transfers between devices: 103 us -> 77.2 us  [swap(): return lax.ppermute(value, axis, [(at, at ^ bit) for at in range(count)])]
    unnamed x22 -> x82, local copies, waits for them, and re-layouts: 1.73 us -> 16.8 us
    ppermute x11, waiting for transfers between devices: 12.2 us -> 26.5 us  [shift(): lax.ppermute(value, axis, [(at, (at + by) % count) for at in range(count)])]
    ppermute x11, starting transfers between devices: 38.2 us -> 31 us  [shift(): lax.ppermute(value, axis, [(at, (at + by) % count) for at in range(count)])]
    ppermute x59 -> x54, starting transfers between devices: 70.9 us -> 64 us  [swap(): return lax.ppermute(value, axis, [(at, at ^ bit) for at in range(count)])]
    pallas_call x21 -> x19, Pallas kernels: 41.1 us -> 44.3 us  [local_call(): pl.pallas_call(kernel, name=getattr(kernel, 'func', kernel).__name__, out...]
  transfers between devices with their start and end apart: 74 -> 69, of which waited for: 30 -> 29; matrix products, arithmetic and copies ran while one was open for 6% -> 4% of each run, Pallas kernels for 9% -> 10%
where the time goes in v6:
time: 277 us; the launch traced here: 276 us
  waiting for transfers between devices  104 us (38%)
  starting transfers between devices  97.7 us (35%)
  Pallas kernels  44.3 us (16%)
  local copies, waits for them, and re-layouts  21.1 us (8%)
  other arithmetic  7.91 us (3%)
    ppermute x54, waiting for transfers between devices, swap(): return lax.ppermute(value, axis, [(at, at ^ bit) for at in range(count)])  77.2 us
    ppermute x54, starting transfers between devices, swap(): return lax.ppermute(value, axis, [(at, at ^ bit) for at in range(count)])  64 us
    pallas_call x19, Pallas kernels, local_call(): pl.pallas_call(kernel, name=getattr(kernel, 'func', kernel).__name__, out...  44.3 us
    ppermute x11, starting transfers between devices, shift(): lax.ppermute(value, axis, [(at, (at + by) % count) for at in range(count)])  31 us
    ppermute x11, waiting for transfers between devices, shift(): lax.ppermute(value, axis, [(at, (at + by) % count) for at in range(count)])  26.5 us
    unnamed x82, local copies, waits for them, and re-layouts  16.8 us
  transfers between devices with their start and end apart: 69, of which 29 were waited for; matrix products, arithmetic and copies ran while one was open for 4% of the time, Pallas kernels for 10%

profile of v6, /device:TPU:0, one launch (start us, length us, event | category | flops | bytes accessed | tf_op | source)
XLA Modules:
  0.0 276.0 jit_solution(2538596004619792257)
XLA Ops:
  11.3 4.4 %collective-permute-start.1 = (bf16[48,1408]{1,0:T(8,128)(2,1)S(1)}, bf16[48,1408]{1,0:T(8,128)(2,1)S(1)}, u32[]{:S(2)}, u32[]{:S(2)}) collective-permute-start(bf16[48,1408]{1,0:T(8,128)(2,1)S(1)} %get-tuple-element.106), channel_id=1, source_target_pairs={{0,8},{8,0},{16,24},{24,16},{1,9},{9,1},{17,25},{25,17},{2,10},{10... | collective-permute-start | bytes 405512 | tf_op jit(solution)/shard_map/ppermute | solution.py:25
  15.7 3.5 %collective-permute-start.2 = (bf16[48,1408]{1,0:T(8,128)(2,1)S(1)}, bf16[48,1408]{1,0:T(8,128)(2,1)S(1)}, u32[]{:S(2)}, u32[]{:S(2)}) collective-permute-start(bf16[48,1408]{1,0:T(8,128)(2,1)S(1)} %get-tuple-element.107), channel_id=1, source_target_pairs={{0,16},{8,24},{16,0},{24,8},{1,17},{9,25},{17,1},{25,9},{2,18},{10... | collective-permute-start | bytes 405512 | tf_op jit(solution)/shard_map/ppermute | solution.py:25
  19.2 6.8 %collective-permute-done.2.refs_2_ = bf16[48,1408]{1,0:T(8,128)(2,1)S(1)} collective-permute-done((bf16[48,1408]{1,0:T(8,128)(2,1)S(1)}, bf16[48,1408]{1,0:T(8,128)(2,1)S(1)}, u32[]{:S(2)}, u32[]{:S(2)}) %collective-permute-start.2) | collective-permute-done | bytes 135200 | tf_op jit(solution)/shard_map/ppermute | solution.py:25
  26.0 3.0 %collective-permute-done.3.refs_3_ = bf16[48,1408]{1,0:T(8,128)(2,1)S(1)} collective-permute-done((bf16[48,1408]{1,0:T(8,128)(2,1)S(1)}, bf16[48,1408]{1,0:T(8,128)(2,1)S(1)}, u32[]{:S(2)}, u32[]{:S(2)}) %collective-permute-start.3) | collective-permute-done | bytes 135200 | tf_op jit(solution)/shard_map/ppermute | solution.py:25
  38.3 17.2 %collective-permute-done.11 = f32[8,768]{1,0:T(8,128)S(1)} collective-permute-done((f32[8,768]{1,0:T(8,128)S(1)}, f32[8,768]{1,0:T(8,128)S(1)}, u32[]{:S(2)}, u32[]{:S(2)}) %collective-permute-start.11) | collective-permute-done | bytes 24608 | tf_op jit(solution)/shard_map/ppermute | solution.py:25
  57.3 3.0 %project_kernel.1 = (bf16[512,576]{1,0:T(8,128)(2,1)S(1)}, bf16[512,384]{1,0:T(8,128)(2,1)S(1)}, bf16[768,576]{1,0:T(8,128)(2,1)S(1)}, bf16[512,768]{1,0:T(8,128)(2,1)S(1)}) custom-call(s32[6]{0:T(128)S(1)} %stack.33.meta_ref.place_ref, bf16[128,768]{1,0:T(8,128)(2,1)S(1)} %collective-permute-done.refs_0_.refs_4_, ...), custom_call_target="tpu_custom_call" | custom-call | flops 22649240 | bytes 217498 | tf_op jit(solution)/shard_map/project_kernel/pallas_call | solution.py:690
  62.6 3.9 %collective-permute-start.13 = (bf16[48,768]{1,0:T(8,128)(2,1)S(1)}, bf16[48,768]{1,0:T(8,128)(2,1)S(1)}, u32[]{:S(2)}, u32[]{:S(2)}) collective-permute-start(bf16[48,768]{1,0:T(8,128)(2,1)S(1)} %convert_element_type.55.refs_4_), channel_id=1, source_target_pairs={{0,1},{1,0},{2,3},{3,2},{4,5},{5,4},{6,7},{7,6},{8,9},{9,8},{10,11... | collective-permute-start | bytes 221192 | tf_op jit(solution)/shard_map/ppermute | solution.py:25
  68.9 6.8 %own_forward.1 = (f32[512,192]{1,0:T(8,128)S(1)}, f32[512,128]{1,0:T(8,128)S(1)}) custom-call(s32[6]{0:T(128)S(1)} %stack.33.meta_ref.place_ref, bf16[512,576]{1,0:T(8,128)(2,1)S(1)} %get-tuple-element.112.kvq_ref.refs_0_.refs_5_), custom_call_target="tpu_custom_call" | custom-call | flops 10066329 | bytes 62260 | tf_op jit(solution)/shard_map/own_forward/pallas_call | solution.py:690
  75.8 4.9 %collective-permute-done.14.refs_6_ = bf16[48,768]{1,0:T(8,128)(2,1)S(1)} collective-permute-done((bf16[48,768]{1,0:T(8,128)(2,1)S(1)}, bf16[48,768]{1,0:T(8,128)(2,1)S(1)}, u32[]{:S(2)}, u32[]{:S(2)}) %collective-permute-start.14) | collective-permute-done | bytes 73760 | tf_op jit(solution)/shard_map/ppermute | solution.py:25
  87.2 3.3 %collective-permute-done.24.refs_6_ = bf16[128,768]{1,0:T(8,128)(2,1)S(1)} collective-permute-done((bf16[128,768]{1,0:T(8,128)(2,1)S(1)}, bf16[128,768]{1,0:T(8,128)(2,1)S(1)}, u32[]{:S(2)}, u32[]{:S(2)}) %collective-permute-start.24) | collective-permute-done | bytes 196640 | tf_op jit(solution)/shard_map/ppermute | solution.py:25
  90.5 2.5 collective-permute-start.28
  96.9 8.4 %collective-permute-start.30 = (bf16[192,768]{1,0:T(8,128)(2,1)S(1)}, bf16[192,768]{1,0:T(8,128)(2,1)S(1)}, u32[]{:S(2)}, u32[]{:S(2)}) collective-permute-start(bf16[192,768]{1,0:T(8,128)(2,1)S(1)} %collective-permute-done.26.refs_9_), channel_id=1, source_target_pairs={{0,4},{4,0},{1,5},{5,1},{2,6},{6,2},{3,7},{7,3},{8,12},{12,8},{9,1... | collective-permute-start | bytes 884744 | tf_op jit(solution)/shard_map/ppermute | solution.py:30
  107.8 3.2 %collective-permute-done.27.refs_10_ = bf16[192,768]{1,0:T(8,128)(2,1)S(1)} collective-permute-done((bf16[192,768]{1,0:T(8,128)(2,1)S(1)}, bf16[192,768]{1,0:T(8,128)(2,1)S(1)}, u32[]{:S(2)}, u32[]{:S(2)}) %collective-permute-start.27) | collective-permute-done | bytes 294944 | tf_op jit(solution)/shard_map/ppermute | solution.py:25
  111.0 7.0 %collective-permute-start.31 = (bf16[192,768]{1,0:T(8,128)(2,1)S(1)}, bf16[192,768]{1,0:T(8,128)(2,1)S(1)}, u32[]{:S(2)}, u32[]{:S(2)}) collective-permute-start(bf16[192,768]{1,0:T(8,128)(2,1)S(1)} %collective-permute-done.27.refs_10_), channel_id=1, source_target_pairs={{0,4},{4,0},{1,5},{5,1},{2,6},{6,2},{3,7},{7,3},{8,12},{12,8},{9,1... | collective-permute-start | bytes 884744 | tf_op jit(solution)/shard_map/ppermute | solution.py:30
  120.6 5.3 %collective-permute-done.31.refs_14_ = bf16[192,768]{1,0:T(8,128)(2,1)S(1)} collective-permute-done((bf16[192,768]{1,0:T(8,128)(2,1)S(1)}, bf16[192,768]{1,0:T(8,128)(2,1)S(1)}, u32[]{:S(2)}, u32[]{:S(2)}) %collective-permute-start.31) | collective-permute-done | bytes 294944 | tf_op jit(solution)/shard_map/ppermute | solution.py:30
  125.9 6.3 %collective-permute-done.32.refs_15_ = bf16[192,768]{1,0:T(8,128)(2,1)S(1)} collective-permute-done((bf16[192,768]{1,0:T(8,128)(2,1)S(1)}, bf16[192,768]{1,0:T(8,128)(2,1)S(1)}, u32[]{:S(2)}, u32[]{:S(2)}) %collective-permute-start.32) | collective-permute-done | bytes 294944 | tf_op jit(solution)/shard_map/ppermute | solution.py:30
  132.2 5.6 %collective-permute-done.29.refs_12_ = bf16[192,768]{1,0:T(8,128)(2,1)S(1)} collective-permute-done((bf16[192,768]{1,0:T(8,128)(2,1)S(1)}, bf16[192,768]{1,0:T(8,128)(2,1)S(1)}, u32[]{:S(2)}, u32[]{:S(2)}) %collective-permute-start.29) | collective-permute-done | bytes 294944 | tf_op jit(solution)/shard_map/ppermute | solution.py:30
  137.8 4.9 %feed_kernel.1 = (f32[128,768]{1,0:T(8,128)S(1)}, bf16[128,768]{1,0:T(8,128)(2,1)S(1)}, bf16[128,768]{1,0:T(8,128)(2,1)S(1)}, bf16[128,768]{1,0:T(8,128)(2,1)S(1...) custom-call(s32[6]{0:T(128)S(1)} %stack.33.meta_ref.place_ref, ...), custom_call_target="tpu_custom_call" | custom-call | flops 90596968 | bytes 463412 | tf_op jit(solution)/shard_map/feed_kernel/pallas_call | solution.py:690
  142.8 4.2 %feed_grad_kernel.1 = (f32[4,192,768]{2,1,0:T(8,128)S(1)}, bf16[4,192,768]{2,1,0:T(8,128)(2,1)S(1)}, f32[128,768]{1,0:T(8,128)S(1)}, bf16[128,768]{1,0:T(8,128)(...) custom-call(s32[6]{0:T(128)S(1)} %stack.33.meta_ref.place_ref, ...), custom_call_target="tpu_custom_call" | custom-call | flops 90596968 | bytes 442369 | tf_op jit(solution)/shard_map/feed_grad_kernel/pallas_call | solution.py:690
  150.8 5.7 %collective-permute-done.34.refs_2_ = bf16[128,768]{1,0:T(8,128)(2,1)S(1)} collective-permute-done((bf16[128,768]{1,0:T(8,128)(2,1)S(1)}, bf16[128,768]{1,0:T(8,128)(2,1)S(1)}, u32[]{:S(2)}, u32[]{:S(2)}) %collective-permute-start.34) | collective-permute-done | bytes 196640 | tf_op jit(solution)/shard_map/ppermute | solution.py:25
  156.5 3.6 %collective-permute-done.35.refs_3_ = bf16[128,768]{1,0:T(8,128)(2,1)S(1)} collective-permute-done((bf16[128,768]{1,0:T(8,128)(2,1)S(1)}, bf16[128,768]{1,0:T(8,128)(2,1)S(1)}, u32[]{:S(2)}, u32[]{:S(2)}) %collective-permute-start.35) | collective-permute-done | bytes 196640 | tf_op jit(solution)/shard_map/ppermute | solution.py:25
  163.5 5.6 %collective-permute-done.36.refs_2_ = bf16[128,768]{1,0:T(8,128)(2,1)S(1)} collective-permute-done((bf16[128,768]{1,0:T(8,128)(2,1)S(1)}, bf16[128,768]{1,0:T(8,128)(2,1)S(1)}, u32[]{:S(2)}, u32[]{:S(2)}) %collective-permute-start.36) | collective-permute-done | bytes 196640 | tf_op jit(solution)/shard_map/ppermute | solution.py:25
  175.9 6.3 %collective-permute-start.43 = (bf16[512,384]{1,0:T(8,128)(2,1)}, bf16[512,384]{1,0:T(8,128)(2,1)S(1)}, u32[]{:S(2)}, u32[]{:S(2)}) collective-permute-start(bf16[512,384]{1,0:T(8,128)(2,1)} %bitcast.9), channel_id=1, source_target_pairs={{0,4},{4,0},{1,5},{5,1},{2,6},{6,2},{3,7},{7,3},{8,12},{12,8},{9,1... | collective-permute-start | bytes 1179656 | tf_op jit(solution)/shard_map/ppermute | solution.py:30
  186.2 2.9 %collective-permute-start.46 = (bf16[192,768]{1,0:T(8,128)(2,1)}, bf16[192,768]{1,0:T(8,128)(2,1)}, u32[]{:S(2)}, u32[]{:S(2)}) collective-permute-start(bf16[192,768]{1,0:T(8,128)(2,1)} %get-tuple-element.169), channel_id=1, source_target_pairs={{0,3},{1,2},{2,1},{3,0},{4,7},{5,6},{6,5},{7,4},{8,11},{9,10},{10,... | collective-permute-start | bytes 884744 | tf_op jit(solution)/shard_map/ppermute | solution.py:25
  193.8 6.8 %own_grad_kernel.1 = (f32[512,576]{1,0:T(8,128)S(1)}, f32[192,768]{1,0:T(8,128)S(1)}) custom-call(s32[6]{0:T(128)S(1)} %stack.33.meta_ref.place_ref, bf16[512,576]{1,0:T(8,128)(2,1)S(1)} %get-tuple-element.112.kvq_ref.refs_0_.refs_5_, bf16[512,192]{1,0:T(8,128)(2,1)S(1)} %copy-done.20, f32[512,192]{1,0:T(8,128)S(1)} %get-tuple-element.147.refs_7_.refs_2_, ...), custom_call_target="tpu_custom_call" | custom-call | flops 25165824 | bytes 229377 | tf_op jit(solution)/shard_map/own_grad_kernel/pallas_call | solution.py:690
  219.2 6.4 %collective-permute-done.52 = bf16[4,128,576]{1,2,0:T(8,128)(2,1)} collective-permute-done((bf16[4,128,576]{1,2,0:T(8,128)(2,1)}, bf16[4,128,576]{1,2,0:T(8,128)(2,1)}, u32[]{:S(2)}, u32[]{:S(2)}) %collective-permute-start.52) | collective-permute-done | bytes 589856 | tf_op jit(solution)/shard_map/ppermute | solution.py:30
  227.7 2.4 collective-permute-start.53
  232.9 9.9 %collective-permute-start.54 = (f32[8,768]{1,0:T(8,128)S(1)}, f32[8,768]{1,0:T(8,128)S(1)}, u32[]{:S(2)}, u32[]{:S(2)}) collective-permute-start(f32[8,768]{1,0:T(8,128)S(1)} %add.100), channel_id=1, source_target_pairs={{0,2},{1,3},{2,0},{3,1},{4,6},{5,7},{6,4},{7,5},{8,10},{9,11},{10,... | collective-permute-start | bytes 73736 | tf_op jit(solution)/shard_map/ppermute | solution.py:25
  245.7 2.4 collective-permute-start.60
  254.7 7.7 %collective-permute-done.59 = bf16[128,576]{1,0:T(8,128)(2,1)S(1)} collective-permute-done((bf16[128,576]{1,0:T(8,128)(2,1)S(1)}, bf16[128,576]{1,0:T(8,128)(2,1)S(1)}, u32[]{:S(2)}, u32[]{:S(2)}) %collective-permute-start.59) | collective-permute-done | bytes 147488 | tf_op jit(solution)/shard_map/ppermute | solution.py:25
  265.1 2.7 collective-permute-done.61
  271.6 2.4 collective-permute-done.63.refs_2_
  (232 shorter events, 105.6 us)
Async XLA Ops:
  10.6 18.4 %collective-permute-start = (bf16[128,768]{1,0:T(8,128)(2,1)S(1)}, bf16[128,768]{1,0:T(8,128)(2,1)S(1)}, u32[]{:S(2)}, u32[]{:S(2)}) collective-permute-start(bf16[128,768]{1,0:T(8,128)(2,1)S(1)} %bitcast_convert_fusion.1), channel_id=1, source_target_pairs={{0,0},{1,8},{2,16},{3,24},{8,1},{9,9},{10,17},{11,25},{16,2},{17,1... | collective-permute-start | bytes 589832 | tf_op jit(solution)/shard_map/ppermute | solution.py:36
  29.0 26.5 %collective-permute-start.5 = (bf16[128,768]{1,0:T(8,128)(2,1)S(1)}, bf16[128,768]{1,0:T(8,128)(2,1)S(1)}, u32[]{:S(2)}, u32[]{:S(2)}) collective-permute-start(bf16[128,768]{1,0:T(8,128)(2,1)S(1)} %collective-permute-done.refs_0_.refs_4_), channel_id=1, source_target_pairs={{0,16},{8,24},{16,0},{24,8},{1,17},{9,25},{17,1},{25,9},{2,18},{10... | collective-permute-start | bytes 589832 | tf_op jit(solution)/shard_map/ppermute | solution.py:25
  32.1 23.9 %collective-permute-start.7 = (bf16[4,48,576]{2,1,0:T(8,128)(2,1)S(1)}, bf16[4,48,576]{2,1,0:T(8,128)(2,1)S(1)}, u32[]{:S(2)}, u32[]{:S(2)}) collective-permute-start(bf16[4,48,576]{2,1,0:T(8,128)(2,1)S(1)} %get-tuple-element.110.refs_4_), channel_id=1, source_target_pairs={{0,1},{1,0},{2,3},{3,2},{4,5},{5,4},{6,7},{7,6},{8,9},{9,8},{10,11... | collective-permute-start | bytes 663560 | tf_op jit(solution)/shard_map/ppermute | solution.py:25
  34.2 21.9 %collective-permute-start.8 = (bf16[4,48,576]{2,1,0:T(8,128)(2,1)S(1)}, bf16[4,48,576]{2,1,0:T(8,128)(2,1)S(1)}, u32[]{:S(2)}, u32[]{:S(2)}) collective-permute-start(bf16[4,48,576]{2,1,0:T(8,128)(2,1)S(1)} %get-tuple-element.110.refs_4_), channel_id=1, source_target_pairs={{0,2},{1,3},{2,0},{3,1},{4,6},{5,7},{6,4},{7,5},{8,10},{9,11},{10,... | collective-permute-start | bytes 663560 | tf_op jit(solution)/shard_map/ppermute | solution.py:25
  36.2 19.3 %collective-permute-start.11 = (f32[8,768]{1,0:T(8,128)S(1)}, f32[8,768]{1,0:T(8,128)S(1)}, u32[]{:S(2)}, u32[]{:S(2)}) collective-permute-start(f32[8,768]{1,0:T(8,128)S(1)} %add.89), channel_id=1, source_target_pairs={{0,2},{1,3},{2,0},{3,1},{4,6},{5,7},{6,4},{7,5},{8,10},{9,11},{10,... | collective-permute-start | bytes 73736 | tf_op jit(solution)/shard_map/ppermute | solution.py:25
  37.2 18.9 %collective-permute-start.9 = (bf16[4,48,576]{2,1,0:T(8,128)(2,1)S(1)}, bf16[4,48,576]{2,1,0:T(8,128)(2,1)S(1)}, u32[]{:S(2)}, u32[]{:S(2)}) collective-permute-start(bf16[4,48,576]{2,1,0:T(8,128)(2,1)S(1)} %get-tuple-element.110.refs_4_), channel_id=1, source_target_pairs={{0,3},{1,2},{2,1},{3,0},{4,7},{5,6},{6,5},{7,4},{8,11},{9,10},{10,... | collective-permute-start | bytes 663560 | tf_op jit(solution)/shard_map/ppermute | solution.py:25
  60.3 22.6 %collective-permute-start.12 = (bf16[512,384]{1,0:T(8,128)(2,1)S(1)}, bf16[512,384]{1,0:T(8,128)(2,1)S(1)}, u32[]{:S(2)}, u32[]{:S(2)}) collective-permute-start(bf16[512,384]{1,0:T(8,128)(2,1)S(1)} %get-tuple-element.113), channel_id=1, source_target_pairs={{0,4},{4,0},{1,5},{5,1},{2,6},{6,2},{3,7},{7,3},{8,12},{12,8},{9,1... | collective-permute-start | bytes 1179656 | tf_op jit(solution)/shard_map/ppermute | solution.py:30
  61.9 20.9 %collective-permute-start.22 = (bf16[128,768]{1,0:T(8,128)(2,1)S(1)}, bf16[128,768]{1,0:T(8,128)(2,1)S(1)}, u32[]{:S(2)}, u32[]{:S(2)}) collective-permute-start(bf16[128,768]{1,0:T(8,128)(2,1)S(1)} %bitcast_convert_fusion), channel_id=1, source_target_pairs={{0,0},{1,8},{2,16},{3,24},{8,1},{9,9},{10,17},{11,25},{16,2},{17,1... | collective-permute-start | bytes 589832 | tf_op jit(solution)/shard_map/ppermute | solution.py:36
  66.5 14.2 %collective-permute-start.14 = (bf16[48,768]{1,0:T(8,128)(2,1)S(1)}, bf16[48,768]{1,0:T(8,128)(2,1)S(1)}, u32[]{:S(2)}, u32[]{:S(2)}) collective-permute-start(bf16[48,768]{1,0:T(8,128)(2,1)S(1)} %convert_element_type.55.refs_4_), channel_id=1, source_target_pairs={{0,2},{1,3},{2,0},{3,1},{4,6},{5,7},{6,4},{7,5},{8,10},{9,11},{10,... | collective-permute-start | bytes 221192 | tf_op jit(solution)/shard_map/ppermute | solution.py:25
  67.3 13.4 %collective-permute-start.15 = (bf16[48,768]{1,0:T(8,128)(2,1)S(1)}, bf16[48,768]{1,0:T(8,128)(2,1)S(1)}, u32[]{:S(2)}, u32[]{:S(2)}) collective-permute-start(bf16[48,768]{1,0:T(8,128)(2,1)S(1)} %convert_element_type.55.refs_4_), channel_id=1, source_target_pairs={{0,3},{1,2},{2,1},{3,0},{4,7},{5,6},{6,5},{7,4},{8,11},{9,10},{10,... | collective-permute-start | bytes 221192 | tf_op jit(solution)/shard_map/ppermute | solution.py:25
  90.5 20.6 %collective-permute-start.27 = (bf16[192,768]{1,0:T(8,128)(2,1)S(1)}, bf16[192,768]{1,0:T(8,128)(2,1)S(1)}, u32[]{:S(2)}, u32[]{:S(2)}) collective-permute-start(bf16[192,768]{1,0:T(8,128)(2,1)S(1)} %get-tuple-element.126.refs_8_), channel_id=1, source_target_pairs={{0,2},{1,3},{2,0},{3,1},{4,6},{5,7},{6,4},{7,5},{8,10},{9,11},{10,... | collective-permute-start | bytes 884744 | tf_op jit(solution)/shard_map/ppermute | solution.py:25
  90.5 27.5 %collective-permute-start.28 = (bf16[192,768]{1,0:T(8,128)(2,1)S(1)}, bf16[192,768]{1,0:T(8,128)(2,1)S(1)}, u32[]{:S(2)}, u32[]{:S(2)}) collective-permute-start(bf16[192,768]{1,0:T(8,128)(2,1)S(1)} %get-tuple-element.126.refs_8_), channel_id=1, source_target_pairs={{0,3},{1,2},{2,1},{3,0},{4,7},{5,6},{6,5},{7,4},{8,11},{9,10},{10,... | collective-permute-start | bytes 884744 | tf_op jit(solution)/shard_map/ppermute | solution.py:25
  94.7 23.4 %collective-permute-start.25 = (bf16[128,768]{1,0:T(8,128)(2,1)S(1)}, bf16[128,768]{1,0:T(8,128)(2,1)S(1)}, u32[]{:S(2)}, u32[]{:S(2)}) collective-permute-start(bf16[128,768]{1,0:T(8,128)(2,1)S(1)} %collective-permute-done.24.refs_6_), channel_id=1, source_target_pairs={{0,8},{8,0},{16,24},{24,16},{1,9},{9,1},{17,25},{25,17},{2,10},{10... | collective-permute-start | bytes 589832 | tf_op jit(solution)/shard_map/ppermute | solution.py:25
  96.9 23.2 %collective-permute-start.30 = (bf16[192,768]{1,0:T(8,128)(2,1)S(1)}, bf16[192,768]{1,0:T(8,128)(2,1)S(1)}, u32[]{:S(2)}, u32[]{:S(2)}) collective-permute-start(bf16[192,768]{1,0:T(8,128)(2,1)S(1)} %collective-permute-done.26.refs_9_), channel_id=1, source_target_pairs={{0,4},{4,0},{1,5},{5,1},{2,6},{6,2},{3,7},{7,3},{8,12},{12,8},{9,1... | collective-permute-start | bytes 884744 | tf_op jit(solution)/shard_map/ppermute | solution.py:30
  106.2 13.9 %collective-permute-start.20 = (bf16[128,768]{1,0:T(8,128)(2,1)S(1)}, bf16[128,768]{1,0:T(8,128)(2,1)S(1)}, u32[]{:S(2)}, u32[]{:S(2)}) collective-permute-start(bf16[128,768]{1,0:T(8,128)(2,1)S(1)} %get-tuple-element.121.refs_0_), channel_id=1, source_target_pairs={{0,16},{8,24},{16,0},{24,8},{1,17},{9,25},{17,1},{25,9},{2,18},{10... | collective-permute-start | bytes 589832 | tf_op jit(solution)/shard_map/ppermute | solution.py:25
  111.0 14.8 %collective-permute-start.31 = (bf16[192,768]{1,0:T(8,128)(2,1)S(1)}, bf16[192,768]{1,0:T(8,128)(2,1)S(1)}, u32[]{:S(2)}, u32[]{:S(2)}) collective-permute-start(bf16[192,768]{1,0:T(8,128)(2,1)S(1)} %collective-permute-done.27.refs_10_), channel_id=1, source_target_pairs={{0,4},{4,0},{1,5},{5,1},{2,6},{6,2},{3,7},{7,3},{8,12},{12,8},{9,1... | collective-permute-start | bytes 884744 | tf_op jit(solution)/shard_map/ppermute | solution.py:30
  118.0 14.1 %collective-permute-start.32 = (bf16[192,768]{1,0:T(8,128)(2,1)S(1)}, bf16[192,768]{1,0:T(8,128)(2,1)S(1)}, u32[]{:S(2)}, u32[]{:S(2)}) collective-permute-start(bf16[192,768]{1,0:T(8,128)(2,1)S(1)} %collective-permute-done.28.refs_11_), channel_id=1, source_target_pairs={{0,4},{4,0},{1,5},{5,1},{2,6},{6,2},{3,7},{7,3},{8,12},{12,8},{9,1... | collective-permute-start | bytes 884744 | tf_op jit(solution)/shard_map/ppermute | solution.py:30
  118.1 19.7 %collective-permute-start.29 = (bf16[192,768]{1,0:T(8,128)(2,1)S(1)}, bf16[192,768]{1,0:T(8,128)(2,1)S(1)}, u32[]{:S(2)}, u32[]{:S(2)}) collective-permute-start(bf16[192,768]{1,0:T(8,128)(2,1)S(1)} %get-tuple-element.126.refs_8_), channel_id=1, source_target_pairs={{0,4},{4,0},{1,5},{5,1},{2,6},{6,2},{3,7},{7,3},{8,12},{12,8},{9,1... | collective-permute-start | bytes 884744 | tf_op jit(solution)/shard_map/ppermute | solution.py:30
  120.1 17.7 %collective-permute-start.19 = (bf16[128,768]{1,0:T(8,128)(2,1)S(1)}, bf16[128,768]{1,0:T(8,128)(2,1)S(1)}, u32[]{:S(2)}, u32[]{:S(2)}) collective-permute-start(bf16[128,768]{1,0:T(8,128)(2,1)S(1)} %get-tuple-element.121.refs_0_), channel_id=1, source_target_pairs={{0,8},{8,0},{16,24},{24,16},{1,9},{9,1},{17,25},{25,17},{2,10},{10... | collective-permute-start | bytes 589832 | tf_op jit(solution)/shard_map/ppermute | solution.py:25
  120.1 17.7 %collective-permute-start.21 = (bf16[128,768]{1,0:T(8,128)(2,1)S(1)}, bf16[128,768]{1,0:T(8,128)(2,1)S(1)}, u32[]{:S(2)}, u32[]{:S(2)}) collective-permute-start(bf16[128,768]{1,0:T(8,128)(2,1)S(1)} %collective-permute-done.20.refs_2_), channel_id=1, source_target_pairs={{0,8},{8,0},{16,24},{24,16},{1,9},{9,1},{17,25},{25,17},{2,10},{10... | collective-permute-start | bytes 589832 | tf_op jit(solution)/shard_map/ppermute | solution.py:25
  147.0 35.3 %collective-permute-start.42 = (bf16[4,192,768]{2,1,0:T(8,128)(2,1)S(1)}, bf16[4,192,768]{2,1,0:T(8,128)(2,1)S(1)}, u32[]{:S(2)}, u32[]{:S(2)}) collective-permute-start(bf16[4,192,768]{2,1,0:T(8,128)(2,1)S(1)} %get-tuple-element.152), channel_id=1, source_target_pairs={{0,4},{4,0},{1,5},{5,1},{2,6},{6,2},{3,7},{7,3},{8,12},{12,8},{9,1... | collective-permute-start | bytes 3538952 | tf_op jit(solution)/shard_map/ppermute | solution.py:30
  170.5 15.6 %collective-permute-start.40 = (bf16[128,768]{1,0:T(8,128)(2,1)S(1)}, bf16[128,768]{1,0:T(8,128)(2,1)S(1)}, u32[]{:S(2)}, u32[]{:S(2)}) collective-permute-start(bf16[128,768]{1,0:T(8,128)(2,1)S(1)} %get-tuple-element.145), channel_id=1, source_target_pairs={{0,24},{8,16},{16,8},{24,0},{1,25},{9,17},{17,9},{25,1},{2,26},{10... | collective-permute-start | bytes 589832 | tf_op jit(solution)/shard_map/ppermute | solution.py:25
  172.0 17.0 %collective-permute-start.39 = (bf16[128,768]{1,0:T(8,128)(2,1)S(1)}, bf16[128,768]{1,0:T(8,128)(2,1)S(1)}, u32[]{:S(2)}, u32[]{:S(2)}) collective-permute-start(bf16[128,768]{1,0:T(8,128)(2,1)S(1)} %get-tuple-element.144), channel_id=1, source_target_pairs={{0,16},{8,24},{16,0},{24,8},{1,17},{9,25},{17,1},{25,9},{2,18},{10... | collective-permute-start | bytes 589832 | tf_op jit(solution)/shard_map/ppermute | solution.py:25
  175.9 24.7 %collective-permute-start.43 = (bf16[512,384]{1,0:T(8,128)(2,1)}, bf16[512,384]{1,0:T(8,128)(2,1)S(1)}, u32[]{:S(2)}, u32[]{:S(2)}) collective-permute-start(bf16[512,384]{1,0:T(8,128)(2,1)} %bitcast.9), channel_id=1, source_target_pairs={{0,4},{4,0},{1,5},{5,1},{2,6},{6,2},{3,7},{7,3},{8,12},{12,8},{9,1... | collective-permute-start | bytes 1179656 | tf_op jit(solution)/shard_map/ppermute | solution.py:30
  184.7 23.2 %collective-permute-start.44 = (bf16[192,768]{1,0:T(8,128)(2,1)}, bf16[192,768]{1,0:T(8,128)(2,1)}, u32[]{:S(2)}, u32[]{:S(2)}) collective-permute-start(bf16[192,768]{1,0:T(8,128)(2,1)} %get-tuple-element.167), channel_id=1, source_target_pairs={{0,1},{1,0},{2,3},{3,2},{4,5},{5,4},{6,7},{7,6},{8,9},{9,8},{10,11... | collective-permute-start | bytes 884744 | tf_op jit(solution)/shard_map/ppermute | solution.py:25
  185.2 23.8 %collective-permute-start.45 = (bf16[192,768]{1,0:T(8,128)(2,1)}, bf16[192,768]{1,0:T(8,128)(2,1)}, u32[]{:S(2)}, u32[]{:S(2)}) collective-permute-start(bf16[192,768]{1,0:T(8,128)(2,1)} %get-tuple-element.168), channel_id=1, source_target_pairs={{0,2},{1,3},{2,0},{3,1},{4,6},{5,7},{6,4},{7,5},{8,10},{9,11},{10,... | collective-permute-start | bytes 884744 | tf_op jit(solution)/shard_map/ppermute | solution.py:25
  186.2 22.8 %collective-permute-start.46 = (bf16[192,768]{1,0:T(8,128)(2,1)}, bf16[192,768]{1,0:T(8,128)(2,1)}, u32[]{:S(2)}, u32[]{:S(2)}) collective-permute-start(bf16[192,768]{1,0:T(8,128)(2,1)} %get-tuple-element.169), channel_id=1, source_target_pairs={{0,3},{1,2},{2,1},{3,0},{4,7},{5,6},{6,5},{7,4},{8,11},{9,10},{10,... | collective-permute-start | bytes 884744 | tf_op jit(solution)/shard_map/ppermute | solution.py:25
  209.0 16.6 %collective-permute-start.52 = (bf16[4,128,576]{1,2,0:T(8,128)(2,1)}, bf16[4,128,576]{1,2,0:T(8,128)(2,1)}, u32[]{:S(2)}, u32[]{:S(2)}) collective-permute-start(bf16[4,128,576]{1,2,0:T(8,128)(2,1)} %copy.30), channel_id=1, source_target_pairs={{0,4},{4,0},{1,5},{5,1},{2,6},{6,2},{3,7},{7,3},{8,12},{12,8},{9,1... | collective-permute-start | bytes 1769480 | tf_op jit(solution)/shard_map/ppermute | solution.py:30
  211.0 19.1 %collective-permute-start.65 = (bf16[192,768]{1,0:T(8,128)(2,1)}, bf16[192,768]{1,0:T(8,128)(2,1)}, u32[]{:S(2)}, u32[]{:S(2)}) collective-permute-start(bf16[192,768]{1,0:T(8,128)(2,1)} %add_convert_fusion), channel_id=1, source_target_pairs={{0,4},{4,0},{1,5},{5,1},{2,6},{6,2},{3,7},{7,3},{8,12},{12,8},{9,1... | collective-permute-start | bytes 884744 | tf_op jit(solution)/shard_map/ppermute | solution.py:30
  218.5 45.8 %collective-permute-start.51 = (bf16[128,768]{1,0:T(8,128)(2,1)S(1)}, bf16[128,768]{1,0:T(8,128)(2,1)S(1)}, u32[]{:S(2)}, u32[]{:S(2)}) collective-permute-start(bf16[128,768]{1,0:T(8,128)(2,1)S(1)} %add_convert_fusion.1), channel_id=1, source_target_pairs={{0,0},{1,8},{2,16},{3,24},{8,1},{9,9},{10,17},{11,25},{16,2},{17,1... | collective-permute-start | bytes 589832 | tf_op jit(solution)/shard_map/ppermute | solution.py:36
  248.1 14.3 %collective-permute-start.59 = (bf16[128,576]{1,0:T(8,128)(2,1)S(1)}, bf16[128,576]{1,0:T(8,128)(2,1)S(1)}, u32[]{:S(2)}, u32[]{:S(2)}) collective-permute-start(bf16[128,576]{1,0:T(8,128)(2,1)S(1)} %get-tuple-element.186), channel_id=1, source_target_pairs={{0,2},{1,3},{2,0},{3,1},{4,6},{5,7},{6,4},{7,5},{8,10},{9,11},{10,... | collective-permute-start | bytes 442376 | tf_op jit(solution)/shard_map/ppermute | solution.py:25
  248.7 13.6 %collective-permute-start.58 = (bf16[128,576]{1,0:T(8,128)(2,1)S(1)}, bf16[128,576]{1,0:T(8,128)(2,1)S(1)}, u32[]{:S(2)}, u32[]{:S(2)}) collective-permute-start(bf16[128,576]{1,0:T(8,128)(2,1)S(1)} %get-tuple-element.185), channel_id=1, source_target_pairs={{0,1},{1,0},{2,3},{3,2},{4,5},{5,4},{6,7},{7,6},{8,9},{9,8},{10,11... | collective-permute-start | bytes 442376 | tf_op jit(solution)/shard_map/ppermute | solution.py:25
  (78 other events, 549.7 us)

commit v7 on v6

--- a/solution.py
+++ b/solution.py
@@ -284,15 +284,6 @@
     return groups
 
 
-def place_blocks(meta_ref, parts, depth, pieces, out_ref):
-    rows = pieces[0].shape[1]
-    for deep in range(depth):
-        member = meta_ref[parts + 1] ^ deep
-        for slot in range(parts):
-            start = pl.multiple_of((meta_ref[slot] * depth + member) * rows, 16)
-            out_ref[pl.ds(start, rows), :] = pieces[deep][slot]
-
-
 def place_shards(meta_ref, parts, pieces, out_ref):
     rows = pieces[0].shape[0]
     for deep, piece in enumerate(pieces):
@@ -338,11 +329,11 @@
 
 
 def stack_kernel(parts, depth, halves, meta_ref, *refs):
-    split, down_weight, kvq_rows, vectors, feeds = take(
-        refs, parts, None, None, None, 1 if halves else 2
-    )
-    columns = kvq_rows.shape[2]
-    shard = kvq_rows.shape[1]
+    split, down_weight, kvq_rows, feeds, vectors = take(
+        refs, parts, None, None, 1 if halves else 2, None
+    )
+    columns = kvq_rows.shape[1]
+    shard = split[0].shape[0]
     model = vectors.shape[1]
     width = columns // 3
     hidden_shard = down_weight.shape[0]
@@ -356,6 +347,7 @@
         return matmul_nn(rows, chosen.astype(LOW))
 
     whole = sum(placed(slot, (meta_ref[slot] * depth + member) * shard) for slot in range(parts))
+    vectors[...] = jnp.zeros_like(vectors)
     vectors[0:6, :] = whole[0:6]
     vectors[6:7, :] = (
         placed(0, width + member * shard)[7:8] + placed(0, 2 * width + member * shard)[6:7]
@@ -365,7 +357,9 @@
         for at in range(hidden_shard // shard)
     )
     for slot in range(parts):
-        kvq_rows[slot] = split[slot][:, :columns]
+        kvq_rows[slot * shard : (slot + 1) * shard, :] = split[slot][:, :columns]
+    vectors[8:16, : model - columns] = vectors[0:8, columns:]
+    kvq_rows[parts * shard :, :] = vectors[:, :columns].astype(LOW)
 
     def up(out):
         for slot in range(parts):
@@ -383,14 +377,13 @@
 
 
 def split_kernel(parts, width, meta_ref, qkv_ref, up_ref, *refs):
-    vectors, outs, packed = take(refs, 9, parts, None)
+    vectors, outs, packed = take(refs, None, parts, None)
     model = parts * width
     shard = qkv_ref.shape[0]
     packed[...] = jnp.zeros_like(packed)
-    for row, vector in enumerate(vectors):
-        values = vector[...].reshape(1, vector.shape[0])
-        for at in range(vector.shape[0] // shard):
-            packed[row + at : row + at + 1, :shard] = values[:, at * shard : (at + 1) * shard]
+    values = vectors[...].reshape(1, vectors.shape[0])
+    for row in range(vectors.shape[0] // shard):
+        packed[row : row + 1, :shard] = values[:, row * shard : (row + 1) * shard]
     part = up_ref.shape[1] // parts
     for case in range(parts):
 
@@ -432,12 +425,20 @@
 
 
 def project_kernel(parts, depth, meta_ref, *refs):
-    tokens, weight, vectors_ref, kvq_ref, kv_ref, matrix_ref, norm_ref = take(
+    tokens, weight, kvq_ref, kv_ref, matrix_ref, norm_ref, vectors_ref = take(
         refs, parts, depth, None, None, None, None, None
     )
     columns = kvq_ref.shape[1]
     rows = tokens[0].shape[0]
-    place_blocks(meta_ref, parts, depth, weight, matrix_ref)
+    shard = matrix_ref.shape[0] // (parts * depth)
+    for deep in range(depth):
+        member = meta_ref[parts + 1] ^ deep
+        for slot in range(parts):
+            start = pl.multiple_of((meta_ref[slot] * depth + member) * shard, 16)
+            matrix_ref[pl.ds(start, shard), :] = weight[deep][slot * shard : (slot + 1) * shard, :]
+    folded = sum(piece[parts * shard :, :].astype(WIDE) for piece in weight)
+    vectors_ref[:, :columns] = folded[:8]
+    vectors_ref[:, columns:] = folded[8:, : vectors_ref.shape[1] - columns]
     for slot, piece in enumerate(tokens):
 
         def chunk(step, carry, slot=slot, piece=piece):
@@ -454,17 +455,9 @@
     kv_ref[...] = low[:, : kv_ref.shape[1]]
 
 
-def context_kernel(parts, depth, heads, meta_ref, *refs):
-    (
-        kvq, kv, acc_in, stat_in, weight, context, low, stat, matrix, keep, sends, score, prob, fade
-    ) = take(
-        refs, None, None, None, None, depth, None, None, None, None, None, parts - 1, None, None,
-        None,
-    )
+def mix_kernel(parts, depth, meta_ref, *refs):
+    low, weight, matrix, keep, sends = take(refs, None, depth, None, None, parts - 1)
     place_shards(meta_ref, parts, weight, matrix)
-    earlier_forward(
-        heads, parts, meta_ref, kvq, kv, acc_in, stat_in, context, low, stat, score, prob, fade
-    )
     emit_rows(matmul_nn(low[...], matrix[...]), keep, sends)
 
 
@@ -735,37 +728,39 @@
     split = local_call(
         functools.partial(split_kernel, parts, width),
         (
-            meta, qkv_weight, fc1_weight, ln1_gain, ln1_bias, ln2_gain, ln2_bias, out_bias,
-            fc2_bias, q_bias, v_bias, fc1_bias,
+            meta, qkv_weight, fc1_weight,
+            jnp.concatenate(
+                [
+                    ln1_gain, ln1_bias, ln2_gain, ln2_bias, out_bias, fc2_bias, q_bias, v_bias,
+                    fc1_bias,
+                ]
+            ),
         ),
         [low_like(shard, padded + hidden_part)] * parts,
         [pltpu.VMEM((shard, padded - 3 * width), WIDE)],
     )
     split_arrived = send_pieces(split[1:], "dp")
-    kvq_rows, vectors, *feeds = local_call(
+    kvq_rows, *feeds = local_call(
         functools.partial(stack_kernel, parts, depth, halves),
         (meta, split[0], *split_arrived, fc2_weight),
-        [low_like(parts, shard, 3 * width), wide_like(8, model)]
+        [low_like(parts * shard + 16, 3 * width)]
         + [low_like(hidden_shard, model)] * (1 if halves else 2),
+        [pltpu.VMEM((16, model), WIDE)],
     )
     kvq_pieces = gather_direct(kvq_rows, "fsdp")
 
-    token_rows = transpose_homes(after(tokens[0].astype(LOW), split[0]))
-    token_pieces = gather_pieces(after(token_rows, *split_arrived))
-
-    vectors = sum_doubling(vectors, "fsdp")
-
-    out_pieces = gather_direct(after(out_weight.astype(LOW), *kvq_pieces[1:]), "fsdp")
-    grad_rows = transpose_homes(after(cotangent[0].astype(LOW), *kvq_pieces[1:]))
-
-    kvq, kv, kvq_matrix, norm1_all = local_call(
+    token_rows = transpose_homes(after(tokens[0].astype(LOW), split_arrived[0]))
+    pieces = gather_pieces(after(token_rows, *split_arrived))
+
+    kvq, kv, kvq_matrix, norm1_all, vectors = local_call(
         functools.partial(project_kernel, parts, depth),
-        (meta, *token_pieces, *kvq_pieces, vectors),
+        (meta, *pieces, *kvq_pieces),
         [
             low_like(group, 3 * width),
             low_like(group, 2 * width),
             low_like(model, 3 * width),
             low_like(group, model),
+            wide_like(8, model),
         ],
         flops=2 * group * model * 3 * width,
     )
@@ -781,29 +776,31 @@
         [wide_square, low_square],
         flops=2 * score_flops,
     )
-    branch_pieces = gather_pieces(after(grad_rows, acc))
+    out_pieces = gather_direct(after(out_weight.astype(LOW), acc, kv_earlier), "fsdp")
+    grad_rows = transpose_homes(after(cotangent[0].astype(LOW), acc, kv_earlier))
+    context, context_low, stat = local_call(
+        functools.partial(earlier_forward, heads, parts),
+        (meta, kvq, kv_earlier, acc, stat),
+        [wide_like(group, width), low_like(group, width), wide_like(group, 128)],
+        [wide_square, low_square, pltpu.VMEM((group, HEAD_DIM), WIDE)],
+        flops=2 * score_flops,
+    )
+    out_matrix, attended_keep, *attended_sends = local_call(
+        functools.partial(mix_kernel, parts, depth),
+        (meta, context_low, *out_pieces),
+        [low_like(width, model), wide_like(rows, model)] + [low_like(rows, model)] * (parts - 1),
+        flops=2 * group * width * model,
+    )
+    branch_pieces = gather_pieces(after(grad_rows, context_low))
     if halves:
-        own_half = gather_direct(after(feeds[0], acc, *out_pieces[1:]), "fsdp")
+        own_half = gather_direct(after(feeds[0], context_low), "fsdp")
         other_half = [shift(after(feeds[0], kv_earlier), "ctx", 1)]
-        other_half += [shift(piece, "ctx", 1) for piece in own_half[1:]]
+        for piece in own_half[1:]:
+            other_half.append(shift(piece, "ctx", 1))
     else:
         own_half = gather_direct(feeds[0], "fsdp")
         other_half = gather_direct(feeds[1], "fsdp")
 
-    context, context_low, stat, out_matrix, attended_keep, *attended_sends = local_call(
-        functools.partial(context_kernel, parts, depth, heads),
-        (meta, kvq, kv_earlier, acc, stat, *out_pieces),
-        [
-            wide_like(group, width),
-            low_like(group, width),
-            wide_like(group, 128),
-            low_like(width, model),
-            wide_like(rows, model),
-        ]
-        + [low_like(rows, model)] * (parts - 1),
-        [wide_square, low_square, pltpu.VMEM((group, HEAD_DIM), WIDE)],
-        flops=2 * score_flops,
-    )
     arrived = send_pieces(attended_sends, "dp")
     norm2, attended = local_call(
         functools.partial(second_norm_kernel, parts),
@@ -939,21 +936,17 @@
         [low_like(rows, model), wide_like(8, model)],
     )
 
-    input_rows = transpose_homes(input_part)
-    input_grad = cotangent[0] + input_rows.astype(WIDE)
-    delta = sum_all(fed_keep, fed_arrived) + vectors[5:6] + attended
-    delta = after(delta.astype(LOW), input_rows)
-    output = tokens[0] + transpose_homes(delta).astype(WIDE)
-
     if halves:
         share_keep, share_sends = fold(kept_share, sent_share, input_part)
         share_pieces = send_pieces(share_sends, "fsdp")
         up_total, down_total = both_halves(sum_all(half_keep, half_pieces).astype(LOW))
         first_share, second_share = both_halves(sum_all(share_keep, share_pieces).astype(LOW))
+        sums = after(sums, share_pieces[0])
     else:
+        share_pieces = []
         up_total, down_total = direct_totals(kept_half, sent_half)
         first_share, second_share = direct_totals(kept_share, sent_share)
-    up_total = up_total.astype(LOW).reshape(parts, shard, hidden_part)
+    up_total = after(up_total.astype(LOW), *share_pieces).reshape(parts, shard, hidden_part)
     down_total = down_total.astype(WIDE)
     (up_total,) = local_call(
         functools.partial(join_up_kernel, parts),
@@ -971,7 +964,13 @@
         (meta, kvq_total[0], *send_pieces(kvq_total[1:], "dp")),
         [wide_like(shard, 3 * model)],
     )
-    sums = sum_replicas(sum_doubling(after(sums, share_keep) if halves else sums, "fsdp"))
+    delta = sum_all(fed_keep, fed_arrived) + vectors[5:6] + attended
+    delta = after(delta.astype(LOW), *share_pieces)
+    output = tokens[0] + transpose_homes(delta).astype(WIDE)
+    input_rows = after(transpose_homes(input_part), *share_pieces)
+    input_grad = cotangent[0] + input_rows.astype(WIDE)
+
+    sums = sum_replicas(after(sum_doubling(sums, "fsdp"), *share_pieces))
     everywhere = sum_doubling(sums, "dp")
     owned = lax.dynamic_slice(everywhere, (0, (mine * depth + deep) * shard), (6, shard))
     value_bias = lax.dynamic_slice(sums, (6, width + deep * shard), (1, shard))[0]

time: 277 us -> 282 us (1.018)
  waiting for transfers between devices: 104 us -> 119 us
  local copies, waits for them, and re-layouts: 21.1 us -> 14.4 us
  starting transfers between devices: 97.7 us -> 94.1 us
    ppermute x54 -> x52, waiting for transfers between devices: 77.2 us -> 101 us  [swap(): return lax.ppermute(value, axis, [(at, at ^ bit) for at in range(count)])]
    ppermute x11, waiting for transfers between devices: 26.5 us -> 17.6 us  [shift(): lax.ppermute(value, axis, [(at, (at + by) % count) for at in range(count)])]
    ppermute x11, starting transfers between devices: 31 us -> 22.9 us  [shift(): lax.ppermute(value, axis, [(at, (at + by) % count) for at in range(count)])]
    unnamed x82 -> x64, local copies, waits for them, and re-layouts: 16.8 us -> 9.2 us
    ppermute x54 -> x52, starting transfers between devices: 64 us -> 68.5 us  [swap(): return lax.ppermute(value, axis, [(at, at ^ bit) for at in range(count)])]
    pallas_call x19 -> x20, Pallas kernels: 44.3 us -> 44.3 us  [local_call(): pl.pallas_call(kernel, name=getattr(kernel, 'func', kernel).__name__, out...]
  transfers between devices with their start and end apart: 69 -> 67, of which waited for: 29 -> 30; matrix products, arithmetic and copies ran while one was open for 4% -> 5% of each run, Pallas kernels for 10% -> 11%
where the time goes in v7:
time: 282 us; the launch traced here: 281 us
  waiting for transfers between devices  119 us (42%)
  starting transfers between devices  94.1 us (33%)
  Pallas kernels  44.3 us (16%)
  local copies, waits for them, and re-layouts  14.4 us (5%)
  other arithmetic  8.56 us (3%)
    ppermute x52, waiting for transfers between devices, swap(): return lax.ppermute(value, axis, [(at, at ^ bit) for at in range(count)])  101 us
    ppermute x52, starting transfers between devices, swap(): return lax.ppermute(value, axis, [(at, at ^ bit) for at in range(count)])  68.5 us
    pallas_call x20, Pallas kernels, local_call(): pl.pallas_call(kernel, name=getattr(kernel, 'func', kernel).__name__, out...  44.3 us
    ppermute x11, starting transfers between devices, shift(): lax.ppermute(value, axis, [(at, (at + by) % count) for at in range(count)])  22.9 us
    ppermute x11, waiting for transfers between devices, shift(): lax.ppermute(value, axis, [(at, (at + by) % count) for at in range(count)])  17.6 us
    unnamed x64, local copies, waits for them, and re-layouts  9.2 us
  transfers between devices with their start and end apart: 67, of which 30 were waited for; matrix products, arithmetic and copies ran while one was open for 5% of the time, Pallas kernels for 11%

profile of v7, /device:TPU:0, one launch (start us, length us, event | category | flops | bytes accessed | tf_op | source)
XLA Modules:
  0.0 281.1 jit_solution(8801180567586960484)
XLA Ops:
  6.7 6.7 %collective-permute-start.2 = (bf16[48,1408]{1,0:T(8,128)(2,1)S(1)}, bf16[48,1408]{1,0:T(8,128)(2,1)S(1)}, u32[]{:S(2)}, u32[]{:S(2)}) collective-permute-start(bf16[48,1408]{1,0:T(8,128)(2,1)S(1)} %get-tuple-element.109), channel_id=1, source_target_pairs={{0,16},{8,24},{16,0},{24,8},{1,17},{9,25},{17,1},{25,9},{2,18},{10... | collective-permute-start | bytes 405512 | tf_op jit(solution)/shard_map/ppermute | solution.py:25
  14.2 5.8 %collective-permute-done.2.refs_2_ = bf16[48,1408]{1,0:T(8,128)(2,1)S(1)} collective-permute-done((bf16[48,1408]{1,0:T(8,128)(2,1)S(1)}, bf16[48,1408]{1,0:T(8,128)(2,1)S(1)}, u32[]{:S(2)}, u32[]{:S(2)}) %collective-permute-start.2) | collective-permute-done | bytes 135200 | tf_op jit(solution)/shard_map/ppermute | solution.py:25
  20.0 4.1 %collective-permute-done.3.refs_3_ = bf16[48,1408]{1,0:T(8,128)(2,1)S(1)} collective-permute-done((bf16[48,1408]{1,0:T(8,128)(2,1)S(1)}, bf16[48,1408]{1,0:T(8,128)(2,1)S(1)}, u32[]{:S(2)}, u32[]{:S(2)}) %collective-permute-start.3) | collective-permute-done | bytes 135200 | tf_op jit(solution)/shard_map/ppermute | solution.py:25
  27.9 4.3 %collective-permute-start.9 = (bf16[208,576]{1,0:T(8,128)(2,1)S(1)}, bf16[208,576]{1,0:T(8,128)(2,1)S(1)}, u32[]{:S(2)}, u32[]{:S(2)}) collective-permute-start(bf16[208,576]{1,0:T(8,128)(2,1)S(1)} %get-tuple-element.113.refs_4_), channel_id=1, source_target_pairs={{0,3},{1,2},{2,1},{3,0},{4,7},{5,6},{6,5},{7,4},{8,11},{9,10},{10,... | collective-permute-start | bytes 718856 | tf_op jit(solution)/shard_map/ppermute | solution.py:25
  32.7 6.8 %collective-permute-done.7.refs_5_ = bf16[208,576]{1,0:T(8,128)(2,1)S(1)} collective-permute-done((bf16[208,576]{1,0:T(8,128)(2,1)S(1)}, bf16[208,576]{1,0:T(8,128)(2,1)S(1)}, u32[]{:S(2)}, u32[]{:S(2)}) %collective-permute-start.7) | collective-permute-done | bytes 239648 | tf_op jit(solution)/shard_map/ppermute | solution.py:25
  39.4 10.0 %collective-permute-done.8.refs_6_ = bf16[208,576]{1,0:T(8,128)(2,1)S(1)} collective-permute-done((bf16[208,576]{1,0:T(8,128)(2,1)S(1)}, bf16[208,576]{1,0:T(8,128)(2,1)S(1)}, u32[]{:S(2)}, u32[]{:S(2)}) %collective-permute-start.8) | collective-permute-done | bytes 239648 | tf_op jit(solution)/shard_map/ppermute | solution.py:25
  54.1 6.8 %own_forward.1 = (f32[512,192]{1,0:T(8,128)S(1)}, f32[512,128]{1,0:T(8,128)S(1)}) custom-call(s32[6]{0:T(128)S(1)} %stack.33.meta_ref.place_ref, bf16[512,576]{1,0:T(8,128)(2,1)S(1)} %get-tuple-element.114.kvq_ref.refs_5_.refs_0_), custom_call_target="tpu_custom_call" | custom-call | flops 10066329 | bytes 62260 | tf_op jit(solution)/shard_map/own_forward/pallas_call | solution.py:683
  61.3 6.3 %collective-permute-start.11 = (bf16[48,768]{1,0:T(8,128)(2,1)S(1)}, bf16[48,768]{1,0:T(8,128)(2,1)S(1)}, u32[]{:S(2)}, u32[]{:S(2)}) collective-permute-start(bf16[48,768]{1,0:T(8,128)(2,1)S(1)} %convert_element_type.55.refs_1_), channel_id=1, source_target_pairs={{0,1},{1,0},{2,3},{3,2},{4,5},{5,4},{6,7},{7,6},{8,9},{9,8},{10,11... | collective-permute-start | bytes 221192 | tf_op jit(solution)/shard_map/ppermute | solution.py:25
  71.8 6.7 %collective-permute-done.12.refs_3_ = bf16[48,768]{1,0:T(8,128)(2,1)S(1)} collective-permute-done((bf16[48,768]{1,0:T(8,128)(2,1)S(1)}, bf16[48,768]{1,0:T(8,128)(2,1)S(1)}, u32[]{:S(2)}, u32[]{:S(2)}) %collective-permute-start.12) | collective-permute-done | bytes 73760 | tf_op jit(solution)/shard_map/ppermute | solution.py:25
  87.4 5.5 %collective-permute-start.27 = (bf16[192,768]{1,0:T(8,128)(2,1)S(1)}, bf16[192,768]{1,0:T(8,128)(2,1)S(1)}, u32[]{:S(2)}, u32[]{:S(2)}) collective-permute-start(bf16[192,768]{1,0:T(8,128)(2,1)S(1)} %get-tuple-element.130.refs_8_), channel_id=1, source_target_pairs={{0,4},{4,0},{1,5},{5,1},{2,6},{6,2},{3,7},{7,3},{8,12},{12,8},{9,1... | collective-permute-start | bytes 884744 | tf_op jit(solution)/shard_map/ppermute | solution.py:30
  96.2 9.1 %collective-permute-done.25.refs_10_ = bf16[192,768]{1,0:T(8,128)(2,1)S(1)} collective-permute-done((bf16[192,768]{1,0:T(8,128)(2,1)S(1)}, bf16[192,768]{1,0:T(8,128)(2,1)S(1)}, u32[]{:S(2)}, u32[]{:S(2)}) %collective-permute-start.25) | collective-permute-done | bytes 294944 | tf_op jit(solution)/shard_map/ppermute | solution.py:25
  107.3 3.4 %collective-permute-start.28 = (bf16[192,768]{1,0:T(8,128)(2,1)S(1)}, bf16[192,768]{1,0:T(8,128)(2,1)S(1)}, u32[]{:S(2)}, u32[]{:S(2)}) collective-permute-start(bf16[192,768]{1,0:T(8,128)(2,1)S(1)} %collective-permute-done.24.refs_9_), channel_id=1, source_target_pairs={{0,4},{4,0},{1,5},{5,1},{2,6},{6,2},{3,7},{7,3},{8,12},{12,8},{9,1... | collective-permute-start | bytes 884744 | tf_op jit(solution)/shard_map/ppermute | solution.py:30
  114.1 4.3 %collective-permute-done.28.refs_13_ = bf16[192,768]{1,0:T(8,128)(2,1)S(1)} collective-permute-done((bf16[192,768]{1,0:T(8,128)(2,1)S(1)}, bf16[192,768]{1,0:T(8,128)(2,1)S(1)}, u32[]{:S(2)}, u32[]{:S(2)}) %collective-permute-start.28) | collective-permute-done | bytes 294944 | tf_op jit(solution)/shard_map/ppermute | solution.py:30
  118.4 6.3 %collective-permute-done.29.refs_14_ = bf16[192,768]{1,0:T(8,128)(2,1)S(1)} collective-permute-done((bf16[192,768]{1,0:T(8,128)(2,1)S(1)}, bf16[192,768]{1,0:T(8,128)(2,1)S(1)}, u32[]{:S(2)}, u32[]{:S(2)}) %collective-permute-start.29) | collective-permute-done | bytes 294944 | tf_op jit(solution)/shard_map/ppermute | solution.py:30
  124.7 6.1 %collective-permute-done.30.refs_15_ = bf16[192,768]{1,0:T(8,128)(2,1)S(1)} collective-permute-done((bf16[192,768]{1,0:T(8,128)(2,1)S(1)}, bf16[192,768]{1,0:T(8,128)(2,1)S(1)}, u32[]{:S(2)}, u32[]{:S(2)}) %collective-permute-start.30) | collective-permute-done | bytes 294944 | tf_op jit(solution)/shard_map/ppermute | solution.py:30
  130.8 4.8 %feed_kernel.1 = (f32[128,768]{1,0:T(8,128)S(1)}, bf16[128,768]{1,0:T(8,128)(2,1)S(1)}, bf16[128,768]{1,0:T(8,128)(2,1)S(1)}, bf16[128,768]{1,0:T(8,128)(2,1)S(1...) custom-call(s32[6]{0:T(128)S(1)} %stack.33.meta_ref.place_ref, ...), custom_call_target="tpu_custom_call" | custom-call | flops 90596968 | bytes 463412 | tf_op jit(solution)/shard_map/feed_kernel/pallas_call | solution.py:683
  135.5 4.4 %feed_grad_kernel.1 = (f32[4,192,768]{2,1,0:T(8,128)S(1)}, bf16[4,192,768]{2,1,0:T(8,128)(2,1)S(1)}, f32[128,768]{1,0:T(8,128)S(1)}, bf16[128,768]{1,0:T(8,128)(...) custom-call(s32[6]{0:T(128)S(1)} %stack.33.meta_ref.place_ref, ...), custom_call_target="tpu_custom_call" | custom-call | flops 90596968 | bytes 442369 | tf_op jit(solution)/shard_map/feed_grad_kernel/pallas_call | solution.py:683
  143.5 5.8 %collective-permute-done.32.refs_2_ = bf16[128,768]{1,0:T(8,128)(2,1)S(1)} collective-permute-done((bf16[128,768]{1,0:T(8,128)(2,1)S(1)}, bf16[128,768]{1,0:T(8,128)(2,1)S(1)}, u32[]{:S(2)}, u32[]{:S(2)}) %collective-permute-start.32) | collective-permute-done | bytes 196640 | tf_op jit(solution)/shard_map/ppermute | solution.py:25
  149.4 3.4 %collective-permute-done.33.refs_3_ = bf16[128,768]{1,0:T(8,128)(2,1)S(1)} collective-permute-done((bf16[128,768]{1,0:T(8,128)(2,1)S(1)}, bf16[128,768]{1,0:T(8,128)(2,1)S(1)}, u32[]{:S(2)}, u32[]{:S(2)}) %collective-permute-start.33) | collective-permute-done | bytes 196640 | tf_op jit(solution)/shard_map/ppermute | solution.py:25
  156.3 5.6 %collective-permute-done.34.refs_2_ = bf16[128,768]{1,0:T(8,128)(2,1)S(1)} collective-permute-done((bf16[128,768]{1,0:T(8,128)(2,1)S(1)}, bf16[128,768]{1,0:T(8,128)(2,1)S(1)}, u32[]{:S(2)}, u32[]{:S(2)}) %collective-permute-start.34) | collective-permute-done | bytes 196640 | tf_op jit(solution)/shard_map/ppermute | solution.py:25
  168.5 6.3 %collective-permute-start.41 = (bf16[512,384]{1,0:T(8,128)(2,1)}, bf16[512,384]{1,0:T(8,128)(2,1)}, u32[]{:S(2)}, u32[]{:S(2)}) collective-permute-start(bf16[512,384]{1,0:T(8,128)(2,1)} %bitcast.9), channel_id=1, source_target_pairs={{0,4},{4,0},{1,5},{5,1},{2,6},{6,2},{3,7},{7,3},{8,12},{12,8},{9,1... | collective-permute-start | bytes 1179656 | tf_op jit(solution)/shard_map/ppermute | solution.py:30
  177.2 4.5 %collective-permute-start.43 = (bf16[192,768]{1,0:T(8,128)(2,1)}, bf16[192,768]{1,0:T(8,128)(2,1)}, u32[]{:S(2)}, u32[]{:S(2)}) collective-permute-start(bf16[192,768]{1,0:T(8,128)(2,1)} %get-tuple-element.171), channel_id=1, source_target_pairs={{0,1},{1,0},{2,3},{3,2},{4,5},{5,4},{6,7},{7,6},{8,9},{9,8},{10,11... | collective-permute-start | bytes 884744 | tf_op jit(solution)/shard_map/ppermute | solution.py:25
  187.9 6.8 %own_grad_kernel.1 = (f32[512,576]{1,0:T(8,128)S(1)}, f32[192,768]{1,0:T(8,128)S(1)}) custom-call(s32[6]{0:T(128)S(1)} %stack.33.meta_ref.place_ref, bf16[512,576]{1,0:T(8,128)(2,1)S(1)} %get-tuple-element.114.kvq_ref.refs_5_.refs_0_, bf16[512,192]{1,0:T(8,128)(2,1)S(1)} %copy-done.18, f32[512,192]{1,0:T(8,128)S(1)} %get-tuple-element.152.refs_7_.refs_2_, ...), custom_call_target="tpu_custom_call" | custom-call | flops 25165824 | bytes 229377 | tf_op jit(solution)/shard_map/own_grad_kernel/pallas_call | solution.py:683
  200.5 4.9 %collective-permute-done.44 = bf16[192,768]{1,0:T(8,128)(2,1)} collective-permute-done((bf16[192,768]{1,0:T(8,128)(2,1)}, bf16[192,768]{1,0:T(8,128)(2,1)}, u32[]{:S(2)}, u32[]{:S(2)}) %collective-permute-start.44) | collective-permute-done | bytes 294944 | tf_op jit(solution)/shard_map/ppermute | solution.py:25
  211.3 4.1 %collective-permute-done.47.refs_2_ = bf16[128,768]{1,0:T(8,128)(2,1)S(1)} collective-permute-done((bf16[128,768]{1,0:T(8,128)(2,1)S(1)}, bf16[128,768]{1,0:T(8,128)(2,1)S(1)}, u32[]{:S(2)}, u32[]{:S(2)}) %collective-permute-start.47) | collective-permute-done | bytes 196640 | tf_op jit(solution)/shard_map/ppermute | solution.py:25
  215.4 3.3 %collective-permute-done.48.refs_3_ = bf16[128,768]{1,0:T(8,128)(2,1)S(1)} collective-permute-done((bf16[128,768]{1,0:T(8,128)(2,1)S(1)}, bf16[128,768]{1,0:T(8,128)(2,1)S(1)}, u32[]{:S(2)}, u32[]{:S(2)}) %collective-permute-start.48) | collective-permute-done | bytes 196640 | tf_op jit(solution)/shard_map/ppermute | solution.py:25
  222.3 7.0 %collective-permute-start.49 = (bf16[128,576]{1,0:T(8,128)(2,1)S(1)}, bf16[128,576]{1,0:T(8,128)(2,1)S(1)}, u32[]{:S(2)}, u32[]{:S(2)}) collective-permute-start(bf16[128,576]{1,0:T(8,128)(2,1)S(1)} %get-tuple-element.184), channel_id=1, source_target_pairs={{0,1},{1,0},{2,3},{3,2},{4,5},{5,4},{6,7},{7,6},{8,9},{9,8},{10,11... | collective-permute-start | bytes 442376 | tf_op jit(solution)/shard_map/ppermute | solution.py:25
  234.3 4.3 %collective-permute-done.49 = bf16[128,576]{1,0:T(8,128)(2,1)S(1)} collective-permute-done((bf16[128,576]{1,0:T(8,128)(2,1)S(1)}, bf16[128,576]{1,0:T(8,128)(2,1)S(1)}, u32[]{:S(2)}, u32[]{:S(2)}) %collective-permute-start.49) | collective-permute-done | bytes 147488 | tf_op jit(solution)/shard_map/ppermute | solution.py:25
  238.6 8.4 %collective-permute-done.50 = bf16[128,576]{1,0:T(8,128)(2,1)S(1)} collective-permute-done((bf16[128,576]{1,0:T(8,128)(2,1)S(1)}, bf16[128,576]{1,0:T(8,128)(2,1)S(1)}, u32[]{:S(2)}, u32[]{:S(2)}) %collective-permute-start.50) | collective-permute-done | bytes 147488 | tf_op jit(solution)/shard_map/ppermute | solution.py:25
  247.7 5.4 %collective-permute-start.54 = (f32[8,768]{1,0:T(8,128)S(1)}, f32[8,768]{1,0:T(8,128)S(1)}, u32[]{:S(2)}, u32[]{:S(2)}) collective-permute-start(f32[8,768]{1,0:T(8,128)S(1)} %get-tuple-element.190), channel_id=1, source_target_pairs={{0,1},{1,0},{2,3},{3,2},{4,5},{5,4},{6,7},{7,6},{8,9},{9,8},{10,11... | collective-permute-start | bytes 73736 | tf_op jit(solution)/shard_map/ppermute | solution.py:25
  253.8 4.5 %collective-permute-done.54 = f32[8,768]{1,0:T(8,128)S(1)} collective-permute-done((f32[8,768]{1,0:T(8,128)S(1)}, f32[8,768]{1,0:T(8,128)S(1)}, u32[]{:S(2)}, u32[]{:S(2)}) %collective-permute-start.54) | collective-permute-done | bytes 24608 | tf_op jit(solution)/shard_map/ppermute | solution.py:25
  269.2 3.2 %collective-permute-done.58 = f32[8,768]{1,0:T(8,128)S(1)} collective-permute-done((f32[8,768]{1,0:T(8,128)S(1)}, f32[8,768]{1,0:T(8,128)S(1)}, u32[]{:S(2)}, u32[]{:S(2)}) %collective-permute-start.58) | collective-permute-done | bytes 24608 | tf_op jit(solution)/shard_map/ppermute | solution.py:25
  (210 shorter events, 101.0 us)
Async XLA Ops:
  6.0 18.1 %collective-permute-start.1 = (bf16[128,768]{1,0:T(8,128)(2,1)S(1)}, bf16[128,768]{1,0:T(8,128)(2,1)S(1)}, u32[]{:S(2)}, u32[]{:S(2)}) collective-permute-start(bf16[128,768]{1,0:T(8,128)(2,1)S(1)} %bitcast_convert_fusion.1), channel_id=1, source_target_pairs={{0,0},{1,8},{2,16},{3,24},{8,1},{9,9},{10,17},{11,25},{16,2},{17,1... | collective-permute-start | bytes 589832 | tf_op jit(solution)/shard_map/ppermute | solution.py:36
  6.7 13.3 %collective-permute-start.2 = (bf16[48,1408]{1,0:T(8,128)(2,1)S(1)}, bf16[48,1408]{1,0:T(8,128)(2,1)S(1)}, u32[]{:S(2)}, u32[]{:S(2)}) collective-permute-start(bf16[48,1408]{1,0:T(8,128)(2,1)S(1)} %get-tuple-element.109), channel_id=1, source_target_pairs={{0,16},{8,24},{16,0},{24,8},{1,17},{9,25},{17,1},{25,9},{2,18},{10... | collective-permute-start | bytes 405512 | tf_op jit(solution)/shard_map/ppermute | solution.py:25
  27.7 11.7 %collective-permute-start.7 = (bf16[208,576]{1,0:T(8,128)(2,1)S(1)}, bf16[208,576]{1,0:T(8,128)(2,1)S(1)}, u32[]{:S(2)}, u32[]{:S(2)}) collective-permute-start(bf16[208,576]{1,0:T(8,128)(2,1)S(1)} %get-tuple-element.113.refs_4_), channel_id=1, source_target_pairs={{0,1},{1,0},{2,3},{3,2},{4,5},{5,4},{6,7},{7,6},{8,9},{9,8},{10,11... | collective-permute-start | bytes 718856 | tf_op jit(solution)/shard_map/ppermute | solution.py:25
  27.8 21.7 %collective-permute-start.8 = (bf16[208,576]{1,0:T(8,128)(2,1)S(1)}, bf16[208,576]{1,0:T(8,128)(2,1)S(1)}, u32[]{:S(2)}, u32[]{:S(2)}) collective-permute-start(bf16[208,576]{1,0:T(8,128)(2,1)S(1)} %get-tuple-element.113.refs_4_), channel_id=1, source_target_pairs={{0,2},{1,3},{2,0},{3,1},{4,6},{5,7},{6,4},{7,5},{8,10},{9,11},{10,... | collective-permute-start | bytes 718856 | tf_op jit(solution)/shard_map/ppermute | solution.py:25
  27.9 21.6 %collective-permute-start.9 = (bf16[208,576]{1,0:T(8,128)(2,1)S(1)}, bf16[208,576]{1,0:T(8,128)(2,1)S(1)}, u32[]{:S(2)}, u32[]{:S(2)}) collective-permute-start(bf16[208,576]{1,0:T(8,128)(2,1)S(1)} %get-tuple-element.113.refs_4_), channel_id=1, source_target_pairs={{0,3},{1,2},{2,1},{3,0},{4,7},{5,6},{6,5},{7,4},{8,11},{9,10},{10,... | collective-permute-start | bytes 718856 | tf_op jit(solution)/shard_map/ppermute | solution.py:25
  32.1 17.3 %collective-permute-start.4 = (bf16[128,768]{1,0:T(8,128)(2,1)S(1)}, bf16[128,768]{1,0:T(8,128)(2,1)S(1)}, u32[]{:S(2)}, u32[]{:S(2)}) collective-permute-start(bf16[128,768]{1,0:T(8,128)(2,1)S(1)} %collective-permute-done.1.refs_0_.refs_4_), channel_id=1, source_target_pairs={{0,8},{8,0},{16,24},{24,16},{1,9},{9,1},{17,25},{25,17},{2,10},{10... | collective-permute-start | bytes 589832 | tf_op jit(solution)/shard_map/ppermute | solution.py:25
  32.2 17.3 %collective-permute-start.6 = (bf16[128,768]{1,0:T(8,128)(2,1)S(1)}, bf16[128,768]{1,0:T(8,128)(2,1)S(1)}, u32[]{:S(2)}, u32[]{:S(2)}) collective-permute-start(bf16[128,768]{1,0:T(8,128)(2,1)S(1)} %collective-permute-done.5.refs_2_), channel_id=1, source_target_pairs={{0,8},{8,0},{16,24},{24,16},{1,9},{9,1},{17,25},{25,17},{2,10},{10... | collective-permute-start | bytes 589832 | tf_op jit(solution)/shard_map/ppermute | solution.py:25
  70.0 11.9 %collective-permute-start.20 = (bf16[128,768]{1,0:T(8,128)(2,1)S(1)}, bf16[128,768]{1,0:T(8,128)(2,1)S(1)}, u32[]{:S(2)}, u32[]{:S(2)}) collective-permute-start(bf16[128,768]{1,0:T(8,128)(2,1)S(1)} %bitcast_convert_fusion), channel_id=1, source_target_pairs={{0,0},{1,8},{2,16},{3,24},{8,1},{9,9},{10,17},{11,25},{16,2},{17,1... | collective-permute-start | bytes 589832 | tf_op jit(solution)/shard_map/ppermute | solution.py:36
  79.7 14.2 %collective-permute-start.24 = (bf16[192,768]{1,0:T(8,128)(2,1)S(1)}, bf16[192,768]{1,0:T(8,128)(2,1)S(1)}, u32[]{:S(2)}, u32[]{:S(2)}) collective-permute-start(bf16[192,768]{1,0:T(8,128)(2,1)S(1)} %get-tuple-element.130.refs_8_), channel_id=1, source_target_pairs={{0,1},{1,0},{2,3},{3,2},{4,5},{5,4},{6,7},{7,6},{8,9},{9,8},{10,11... | collective-permute-start | bytes 884744 | tf_op jit(solution)/shard_map/ppermute | solution.py:25
  81.9 23.4 %collective-permute-start.25 = (bf16[192,768]{1,0:T(8,128)(2,1)S(1)}, bf16[192,768]{1,0:T(8,128)(2,1)S(1)}, u32[]{:S(2)}, u32[]{:S(2)}) collective-permute-start(bf16[192,768]{1,0:T(8,128)(2,1)S(1)} %get-tuple-element.130.refs_8_), channel_id=1, source_target_pairs={{0,2},{1,3},{2,0},{3,1},{4,6},{5,7},{6,4},{7,5},{8,10},{9,11},{10,... | collective-permute-start | bytes 884744 | tf_op jit(solution)/shard_map/ppermute | solution.py:25
  83.3 22.0 %collective-permute-start.26 = (bf16[192,768]{1,0:T(8,128)(2,1)S(1)}, bf16[192,768]{1,0:T(8,128)(2,1)S(1)}, u32[]{:S(2)}, u32[]{:S(2)}) collective-permute-start(bf16[192,768]{1,0:T(8,128)(2,1)S(1)} %get-tuple-element.130.refs_8_), channel_id=1, source_target_pairs={{0,3},{1,2},{2,1},{3,0},{4,7},{5,6},{6,5},{7,4},{8,11},{9,10},{10,... | collective-permute-start | bytes 884744 | tf_op jit(solution)/shard_map/ppermute | solution.py:25
  87.4 19.9 %collective-permute-start.27 = (bf16[192,768]{1,0:T(8,128)(2,1)S(1)}, bf16[192,768]{1,0:T(8,128)(2,1)S(1)}, u32[]{:S(2)}, u32[]{:S(2)}) collective-permute-start(bf16[192,768]{1,0:T(8,128)(2,1)S(1)} %get-tuple-element.130.refs_8_), channel_id=1, source_target_pairs={{0,4},{4,0},{1,5},{5,1},{2,6},{6,2},{3,7},{7,3},{8,12},{12,8},{9,1... | collective-permute-start | bytes 884744 | tf_op jit(solution)/shard_map/ppermute | solution.py:30
  92.9 17.8 %collective-permute-start.21 = (bf16[128,768]{1,0:T(8,128)(2,1)S(1)}, bf16[128,768]{1,0:T(8,128)(2,1)S(1)}, u32[]{:S(2)}, u32[]{:S(2)}) collective-permute-start(bf16[128,768]{1,0:T(8,128)(2,1)S(1)} %collective-permute-done.20.refs_4_.refs_6_), channel_id=1, source_target_pairs={{0,8},{8,0},{16,24},{24,16},{1,9},{9,1},{17,25},{25,17},{2,10},{10... | collective-permute-start | bytes 589832 | tf_op jit(solution)/shard_map/ppermute | solution.py:25
  93.9 16.8 %collective-permute-start.22 = (bf16[128,768]{1,0:T(8,128)(2,1)S(1)}, bf16[128,768]{1,0:T(8,128)(2,1)S(1)}, u32[]{:S(2)}, u32[]{:S(2)}) collective-permute-start(bf16[128,768]{1,0:T(8,128)(2,1)S(1)} %collective-permute-done.20.refs_4_.refs_6_), channel_id=1, source_target_pairs={{0,16},{8,24},{16,0},{24,8},{1,17},{9,25},{17,1},{25,9},{2,18},{10... | collective-permute-start | bytes 589832 | tf_op jit(solution)/shard_map/ppermute | solution.py:25
  107.3 11.1 %collective-permute-start.28 = (bf16[192,768]{1,0:T(8,128)(2,1)S(1)}, bf16[192,768]{1,0:T(8,128)(2,1)S(1)}, u32[]{:S(2)}, u32[]{:S(2)}) collective-permute-start(bf16[192,768]{1,0:T(8,128)(2,1)S(1)} %collective-permute-done.24.refs_9_), channel_id=1, source_target_pairs={{0,4},{4,0},{1,5},{5,1},{2,6},{6,2},{3,7},{7,3},{8,12},{12,8},{9,1... | collective-permute-start | bytes 884744 | tf_op jit(solution)/shard_map/ppermute | solution.py:30
  110.6 14.1 %collective-permute-start.29 = (bf16[192,768]{1,0:T(8,128)(2,1)S(1)}, bf16[192,768]{1,0:T(8,128)(2,1)S(1)}, u32[]{:S(2)}, u32[]{:S(2)}) collective-permute-start(bf16[192,768]{1,0:T(8,128)(2,1)S(1)} %collective-permute-done.25.refs_10_), channel_id=1, source_target_pairs={{0,4},{4,0},{1,5},{5,1},{2,6},{6,2},{3,7},{7,3},{8,12},{12,8},{9,1... | collective-permute-start | bytes 884744 | tf_op jit(solution)/shard_map/ppermute | solution.py:30
  110.7 20.1 %collective-permute-start.30 = (bf16[192,768]{1,0:T(8,128)(2,1)S(1)}, bf16[192,768]{1,0:T(8,128)(2,1)S(1)}, u32[]{:S(2)}, u32[]{:S(2)}) collective-permute-start(bf16[192,768]{1,0:T(8,128)(2,1)S(1)} %collective-permute-done.26.refs_11_), channel_id=1, source_target_pairs={{0,4},{4,0},{1,5},{5,1},{2,6},{6,2},{3,7},{7,3},{8,12},{12,8},{9,1... | collective-permute-start | bytes 884744 | tf_op jit(solution)/shard_map/ppermute | solution.py:30
  112.8 17.9 %collective-permute-start.19 = (bf16[128,768]{1,0:T(8,128)(2,1)S(1)}, bf16[128,768]{1,0:T(8,128)(2,1)S(1)}, u32[]{:S(2)}, u32[]{:S(2)}) collective-permute-start(bf16[128,768]{1,0:T(8,128)(2,1)S(1)} %collective-permute-done.18.refs_2_), channel_id=1, source_target_pairs={{0,8},{8,0},{16,24},{24,16},{1,9},{9,1},{17,25},{25,17},{2,10},{10... | collective-permute-start | bytes 589832 | tf_op jit(solution)/shard_map/ppermute | solution.py:25
  139.9 34.9 %collective-permute-start.40 = (bf16[4,192,768]{2,1,0:T(8,128)(2,1)S(1)}, bf16[4,192,768]{2,1,0:T(8,128)(2,1)S(1)}, u32[]{:S(2)}, u32[]{:S(2)}) collective-permute-start(bf16[4,192,768]{2,1,0:T(8,128)(2,1)S(1)} %get-tuple-element.157), channel_id=1, source_target_pairs={{0,4},{4,0},{1,5},{5,1},{2,6},{6,2},{3,7},{7,3},{8,12},{12,8},{9,1... | collective-permute-start | bytes 3538952 | tf_op jit(solution)/shard_map/ppermute | solution.py:30
  163.3 19.9 %collective-permute-start.38 = (bf16[128,768]{1,0:T(8,128)(2,1)S(1)}, bf16[128,768]{1,0:T(8,128)(2,1)S(1)}, u32[]{:S(2)}, u32[]{:S(2)}) collective-permute-start(bf16[128,768]{1,0:T(8,128)(2,1)S(1)} %get-tuple-element.149), channel_id=1, source_target_pairs={{0,24},{8,16},{16,8},{24,0},{1,25},{9,17},{17,9},{25,1},{2,26},{10... | collective-permute-start | bytes 589832 | tf_op jit(solution)/shard_map/ppermute | solution.py:25
  164.8 20.0 %collective-permute-start.37 = (bf16[128,768]{1,0:T(8,128)(2,1)S(1)}, bf16[128,768]{1,0:T(8,128)(2,1)}, u32[]{:S(2)}, u32[]{:S(2)}) collective-permute-start(bf16[128,768]{1,0:T(8,128)(2,1)S(1)} %get-tuple-element.148), channel_id=1, source_target_pairs={{0,16},{8,24},{16,0},{24,8},{1,17},{9,25},{17,1},{25,9},{2,18},{10... | collective-permute-start | bytes 589832 | tf_op jit(solution)/shard_map/ppermute | solution.py:25
  168.5 26.2 %collective-permute-start.41 = (bf16[512,384]{1,0:T(8,128)(2,1)}, bf16[512,384]{1,0:T(8,128)(2,1)}, u32[]{:S(2)}, u32[]{:S(2)}) collective-permute-start(bf16[512,384]{1,0:T(8,128)(2,1)} %bitcast.9), channel_id=1, source_target_pairs={{0,4},{4,0},{1,5},{5,1},{2,6},{6,2},{3,7},{7,3},{8,12},{12,8},{9,1... | collective-permute-start | bytes 1179656 | tf_op jit(solution)/shard_map/ppermute | solution.py:30
  177.2 23.3 %collective-permute-start.43 = (bf16[192,768]{1,0:T(8,128)(2,1)}, bf16[192,768]{1,0:T(8,128)(2,1)}, u32[]{:S(2)}, u32[]{:S(2)}) collective-permute-start(bf16[192,768]{1,0:T(8,128)(2,1)} %get-tuple-element.171), channel_id=1, source_target_pairs={{0,1},{1,0},{2,3},{3,2},{4,5},{5,4},{6,7},{7,6},{8,9},{9,8},{10,11... | collective-permute-start | bytes 884744 | tf_op jit(solution)/shard_map/ppermute | solution.py:25
  181.7 23.8 %collective-permute-start.44 = (bf16[192,768]{1,0:T(8,128)(2,1)}, bf16[192,768]{1,0:T(8,128)(2,1)}, u32[]{:S(2)}, u32[]{:S(2)}) collective-permute-start(bf16[192,768]{1,0:T(8,128)(2,1)} %get-tuple-element.172), channel_id=1, source_target_pairs={{0,2},{1,3},{2,0},{3,1},{4,6},{5,7},{6,4},{7,5},{8,10},{9,11},{10,... | collective-permute-start | bytes 884744 | tf_op jit(solution)/shard_map/ppermute | solution.py:25
  183.2 22.2 %collective-permute-start.45 = (bf16[192,768]{1,0:T(8,128)(2,1)}, bf16[192,768]{1,0:T(8,128)(2,1)}, u32[]{:S(2)}, u32[]{:S(2)}) collective-permute-start(bf16[192,768]{1,0:T(8,128)(2,1)} %get-tuple-element.173), channel_id=1, source_target_pairs={{0,3},{1,2},{2,1},{3,0},{4,7},{5,6},{6,5},{7,4},{8,11},{9,10},{10,... | collective-permute-start | bytes 884744 | tf_op jit(solution)/shard_map/ppermute | solution.py:25
  200.4 19.9 %collective-permute-start.42 = (bf16[4,128,576]{1,2,0:T(8,128)(2,1)}, bf16[4,128,576]{1,2,0:T(8,128)(2,1)}, u32[]{:S(2)}, u32[]{:S(2)}) collective-permute-start(bf16[4,128,576]{1,2,0:T(8,128)(2,1)} %copy.30), channel_id=1, source_target_pairs={{0,4},{4,0},{1,5},{5,1},{2,6},{6,2},{3,7},{7,3},{8,12},{12,8},{9,1... | collective-permute-start | bytes 1769480 | tf_op jit(solution)/shard_map/ppermute | solution.py:30
  207.5 24.9 %collective-permute-start.63 = (bf16[192,768]{1,0:T(8,128)(2,1)}, bf16[192,768]{1,0:T(8,128)(2,1)}, u32[]{:S(2)}, u32[]{:S(2)}) collective-permute-start(bf16[192,768]{1,0:T(8,128)(2,1)} %add_convert_fusion), channel_id=1, source_target_pairs={{0,4},{4,0},{1,5},{5,1},{2,6},{6,2},{3,7},{7,3},{8,12},{12,8},{9,1... | collective-permute-start | bytes 884744 | tf_op jit(solution)/shard_map/ppermute | solution.py:30
  219.6 28.1 %collective-permute-start.53 = (bf16[128,768]{1,0:T(8,128)(2,1)S(1)}, bf16[128,768]{1,0:T(8,128)(2,1)S(1)}, u32[]{:S(2)}, u32[]{:S(2)}) collective-permute-start(bf16[128,768]{1,0:T(8,128)(2,1)S(1)} %get-tuple-element.182), channel_id=1, source_target_pairs={{0,0},{1,8},{2,16},{3,24},{8,1},{9,9},{10,17},{11,25},{16,2},{17,1... | collective-permute-start | bytes 589832 | tf_op jit(solution)/shard_map/ppermute | solution.py:36
  222.3 16.2 %collective-permute-start.49 = (bf16[128,576]{1,0:T(8,128)(2,1)S(1)}, bf16[128,576]{1,0:T(8,128)(2,1)S(1)}, u32[]{:S(2)}, u32[]{:S(2)}) collective-permute-start(bf16[128,576]{1,0:T(8,128)(2,1)S(1)} %get-tuple-element.184), channel_id=1, source_target_pairs={{0,1},{1,0},{2,3},{3,2},{4,5},{5,4},{6,7},{7,6},{8,9},{9,8},{10,11... | collective-permute-start | bytes 442376 | tf_op jit(solution)/shard_map/ppermute | solution.py:25
  229.4 17.6 %collective-permute-start.50 = (bf16[128,576]{1,0:T(8,128)(2,1)S(1)}, bf16[128,576]{1,0:T(8,128)(2,1)S(1)}, u32[]{:S(2)}, u32[]{:S(2)}) collective-permute-start(bf16[128,576]{1,0:T(8,128)(2,1)S(1)} %get-tuple-element.185), channel_id=1, source_target_pairs={{0,2},{1,3},{2,0},{3,1},{4,6},{5,7},{6,4},{7,5},{8,10},{9,11},{10,... | collective-permute-start | bytes 442376 | tf_op jit(solution)/shard_map/ppermute | solution.py:25
  231.0 16.0 %collective-permute-start.51 = (bf16[128,576]{1,0:T(8,128)(2,1)S(1)}, bf16[128,576]{1,0:T(8,128)(2,1)S(1)}, u32[]{:S(2)}, u32[]{:S(2)}) collective-permute-start(bf16[128,576]{1,0:T(8,128)(2,1)S(1)} %get-tuple-element.186), channel_id=1, source_target_pairs={{0,3},{1,2},{2,1},{3,0},{4,7},{5,6},{6,5},{7,4},{8,11},{9,10},{10,... | collective-permute-start | bytes 442376 | tf_op jit(solution)/shard_map/ppermute | solution.py:25
  247.0 29.2 %collective-permute-start.52 = (bf16[128,768]{1,0:T(8,128)(2,1)S(1)}, bf16[128,768]{1,0:T(8,128)(2,1)S(1)}, u32[]{:S(2)}, u32[]{:S(2)}) collective-permute-start(bf16[128,768]{1,0:T(8,128)(2,1)S(1)} %copy-done.28), channel_id=1, source_target_pairs={{0,0},{1,8},{2,16},{3,24},{8,1},{9,9},{10,17},{11,25},{16,2},{17,1... | collective-permute-start | bytes 589832 | tf_op jit(solution)/shard_map/ppermute | solution.py:36
  (67 other events, 545.1 us)

commit v8 on v7

--- a/solution.py
+++ b/solution.py
@@ -50,6 +50,14 @@
 
 def send_pieces(sends, axis):
     return [swap(send, axis, slot) for slot, send in enumerate(sends, 1)]
+
+
+def sum_rows(keep, send):
+    assert lax.axis_size("dp") == 4
+    near = swap(send, "dp", 1)
+    rows = keep.shape[0] // 2
+    far = swap((keep[rows:] + near[rows:].astype(WIDE)).astype(LOW), "dp", 2)
+    return keep, near, far
 
 
 def gather_direct(block, axis):
@@ -297,11 +305,17 @@
         out_ref[slot * rows : (slot + 1) * rows, :] = piece[...]
 
 
-def emit_rows(partial, keep_ref, send_refs):
-    rows = keep_ref.shape[0]
-    keep_ref[...] = partial[:rows]
-    for slot, send in enumerate(send_refs, 1):
-        send[...] = partial[slot * rows : (slot + 1) * rows].astype(LOW)
+def emit_rows(partial, keep_ref, send_ref):
+    rows = keep_ref.shape[0] // 2
+    for pair in range(2):
+        here = slice(pair * rows, (pair + 1) * rows)
+        keep_ref[here, :] = partial[2 * pair * rows : (2 * pair + 1) * rows]
+        send_ref[here, :] = partial[(2 * pair + 1) * rows : (2 * pair + 2) * rows].astype(LOW)
+
+
+def row_sum(keep, near, far):
+    rows = far.shape[0]
+    return keep[:rows, :] + near[:rows, :].astype(WIDE) + far[...].astype(WIDE)
 
 
 def emit_blocks(meta_ref, parts, depth, whole_ref, keep_ref, send_refs):
@@ -329,8 +343,8 @@
 
 
 def stack_kernel(parts, depth, halves, meta_ref, *refs):
-    split, down_weight, kvq_rows, feeds, vectors = take(
-        refs, parts, None, None, 1 if halves else 2, None
+    split, down_weight, out_weight, kvq_rows, feeds, vectors = take(
+        refs, parts, None, None, None, 1 if halves else 2, None
     )
     columns = kvq_rows.shape[1]
     shard = split[0].shape[0]
@@ -359,7 +373,14 @@
     for slot in range(parts):
         kvq_rows[slot * shard : (slot + 1) * shard, :] = split[slot][:, :columns]
     vectors[8:16, : model - columns] = vectors[0:8, columns:]
-    kvq_rows[parts * shard :, :] = vectors[:, :columns].astype(LOW)
+    first = parts * shard + 16
+    kvq_rows[parts * shard : first, :] = vectors[:, :columns].astype(LOW)
+    kvq_rows[first : first + shard, :] = out_weight[:, :columns].astype(LOW)
+    rest = model - columns
+    for at in range(columns // rest):
+        kvq_rows[first + shard :, at * rest : (at + 1) * rest] = out_weight[
+            at * 16 : (at + 1) * 16, columns:
+        ].astype(LOW)
 
     def up(out):
         for slot in range(parts):
@@ -436,7 +457,7 @@
         for slot in range(parts):
             start = pl.multiple_of((meta_ref[slot] * depth + member) * shard, 16)
             matrix_ref[pl.ds(start, shard), :] = weight[deep][slot * shard : (slot + 1) * shard, :]
-    folded = sum(piece[parts * shard :, :].astype(WIDE) for piece in weight)
+    folded = sum(piece[parts * shard : parts * shard + 16, :].astype(WIDE) for piece in weight)
     vectors_ref[:, :columns] = folded[:8]
     vectors_ref[:, columns:] = folded[8:, : vectors_ref.shape[1] - columns]
     for slot, piece in enumerate(tokens):
@@ -456,16 +477,24 @@
 
 
 def mix_kernel(parts, depth, meta_ref, *refs):
-    low, weight, matrix, keep, sends = take(refs, None, depth, None, None, parts - 1)
-    place_shards(meta_ref, parts, weight, matrix)
-    emit_rows(matmul_nn(low[...], matrix[...]), keep, sends)
+    low, weight, matrix, keep, send = take(refs, None, depth, None, None, None)
+    shard = matrix.shape[0] // depth
+    columns = weight[0].shape[1]
+    rest = matrix.shape[1] - columns
+    first = parts * shard + 16
+    for deep in range(depth):
+        start = pl.multiple_of((meta_ref[parts + 1] ^ deep) * shard, 16)
+        matrix[pl.ds(start, shard), :columns] = weight[deep][first : first + shard, :]
+        for at in range(columns // rest):
+            matrix[pl.ds(start + at * 16, 16), columns:] = weight[deep][
+                first + shard :, at * rest : (at + 1) * rest
+            ]
+    emit_rows(matmul_nn(low[...], matrix[...]), keep, send)
 
 
 def second_norm_kernel(parts, meta_ref, *refs):
-    keep, arrived, tokens, vectors, out, attended_ref = take(
-        refs, None, parts - 1, None, None, None, None
-    )
-    attended = sum_all(keep[...], [piece[...] for piece in arrived]) + vectors[4:5, :]
+    keep, near, far, tokens, vectors, out, attended_ref = refs
+    attended = row_sum(keep, near, far) + vectors[4:5, :]
     attended_ref[...] = attended
     hat, _ = normalize(tokens[...].astype(WIDE) + attended)
     out[...] = (hat * vectors[2:3, :] + vectors[3:4, :]).astype(LOW)
@@ -473,9 +502,9 @@
 
 def feed_kernel(parts, depth, halves, meta_ref, *refs):
     (
-        norm, branch, own, other, vectors, keep, sends, hidden, inner_grad, norm_all, branch_all,
+        norm, branch, own, other, vectors, keep, send, hidden, inner_grad, norm_all, branch_all,
         down_all, up_bias, up_all, inner, grad,
-    ) = take(refs, parts, parts, depth, depth, None, None, parts - 1, *([None] * 9))
+    ) = take(refs, parts, parts, depth, depth, *([None] * 12))
 
     def place(up, down):
         shard = up_all.shape[0] // (parts * depth)
@@ -512,26 +541,25 @@
         return carry
 
     lax.fori_loop(0, inner.shape[0] // CHUNK, chunk, 0)
-    emit_rows(matmul_nt(inner_grad[...], up_all[...]), keep, sends)
+    emit_rows(matmul_nt(inner_grad[...], up_all[...]), keep, send)
 
 
 def feed_grad_kernel(parts, depth, halves, meta_ref, *refs):
-    hidden, inner_grad, norm_all, branch_all, down_all, kept, sent, fed_keep, fed_sends, whole = (
-        take(refs, *([None] * 8), parts - 1, None)
-    )
+    hidden, inner_grad, norm_all, branch_all, down_all, kept, *sent, fed_keep, fed_send, whole = refs
     hidden_shard = hidden.shape[1] // depth
     shard = norm_all.shape[1] // (parts * depth)
 
-    def emit(half, out):
+    def emit(half, outs):
         for deep in range(depth):
+            out = outs[deep * len(outs) // depth].at[deep % (depth // len(outs))]
             member = meta_ref[parts + 1] ^ deep
             if half:
                 start = pl.multiple_of(member * hidden_shard, 16)
-                out[deep] = whole[pl.ds(start, hidden_shard), :].astype(out.dtype)
+                out[...] = whole[pl.ds(start, hidden_shard), :].astype(out.dtype)
             else:
                 for slot in range(parts):
                     start = pl.multiple_of((meta_ref[slot] * depth + member) * shard, 16)
-                    out[deep, slot * shard : (slot + 1) * shard] = whole[
+                    out[slot * shard : (slot + 1) * shard, :] = whole[
                         pl.ds(start, shard), :
                     ].astype(out.dtype)
 
@@ -541,24 +569,27 @@
         else:
             whole[...] = matmul_tn(norm_all[...], inner_grad[...])
         if halves:
-            pl.when(meta_ref[parts] == half)(functools.partial(emit, half, kept))
+            pl.when(meta_ref[parts] == half)(functools.partial(emit, half, [kept]))
             pl.when(meta_ref[parts] != half)(functools.partial(emit, half, sent))
         else:
-            emit(half, sent if half else kept)
-    emit_rows(matmul_nn(hidden[...], down_all[...]), fed_keep, fed_sends)
-
-
-def fold_kernel(meta_ref, kept_ref, arrived_ref, keep_ref, *send_refs):
-    keep_ref[...] = kept_ref[0] + arrived_ref[0].astype(WIDE)
-    for deep, send in enumerate(send_refs, 1):
-        send[...] = (kept_ref[deep] + arrived_ref[deep].astype(WIDE)).astype(LOW)
+            emit(half, sent if half else [kept])
+    emit_rows(matmul_nn(hidden[...], down_all[...]), fed_keep, fed_send)
+
+
+def fold_kernel(count, meta_ref, kept_ref, *refs):
+    arrived, keep_ref, send_refs = refs[:count], refs[count], refs[count + 1 :]
+    depth = kept_ref.shape[0]
+    for deep in range(depth):
+        piece = arrived[deep * count // depth][deep % (depth // count)].astype(WIDE)
+        if deep:
+            send_refs[deep - 1][...] = (kept_ref[deep] + piece).astype(LOW)
+        else:
+            keep_ref[...] = kept_ref[deep] + piece
 
 
 def second_norm_grad_kernel(parts, meta_ref, *refs):
-    keep, arrived, tokens, attended, branch, vectors, attn_grad, mixed_part, sums = take(
-        refs, None, parts - 1, None, None, None, None, None, None, None
-    )
-    grad = sum_all(keep[...], [piece[...] for piece in arrived])
+    keep, near, far, tokens, attended, branch, vectors, attn_grad, mixed_part, sums = refs
+    grad = row_sum(keep, near, far)
     hat, inverse = normalize(tokens[...].astype(WIDE) + attended[...])
     part, gain_grad, bias_grad = normalize_back(grad, vectors[2:3, :], hat, inverse)
     mixed_part[...] = part
@@ -598,16 +629,14 @@
 
 
 def projection_back_kernel(parts, meta_ref, *refs):
-    own, arrived, matrix, kvq_grad, keep, sends, bias = take(
-        refs, None, None, None, None, None, parts - 1, None
-    )
+    own, arrived, matrix, kvq_grad, keep, send, bias = refs
     kv_width = arrived.shape[2]
     total = own[:, :kv_width]
     for piece in range(arrived.shape[0]):
         total = total + arrived[piece].astype(WIDE)
     kvq_grad[:, :kv_width] = total.astype(LOW)
     kvq_grad[:, kv_width:] = own[:, kv_width:].astype(LOW)
-    emit_rows(matmul_nt(kvq_grad[...], matrix[...]), keep, sends)
+    emit_rows(matmul_nt(kvq_grad[...], matrix[...]), keep, send)
     bias[...] = jnp.sum(kvq_grad[...].astype(WIDE), axis=0, keepdims=True)
 
 
@@ -662,10 +691,8 @@
 
 
 def first_norm_grad_kernel(parts, meta_ref, *refs):
-    keep, arrived, tokens, vectors, mixed_part, sums_in, kvq_bias, up_bias, out, sums = take(
-        refs, None, parts - 1, *([None] * 8)
-    )
-    grad = sum_all(keep[...], [piece[...] for piece in arrived])
+    keep, near, far, tokens, vectors, mixed_part, sums_in, kvq_bias, up_bias, out, sums = refs
+    grad = row_sum(keep, near, far)
     hat, inverse = normalize(tokens[...].astype(WIDE))
     part, gain_grad, bias_grad = normalize_back(grad, vectors[0:1, :], hat, inverse)
     out[...] = (mixed_part[...] + part).astype(LOW)
@@ -742,14 +769,14 @@
     split_arrived = send_pieces(split[1:], "dp")
     kvq_rows, *feeds = local_call(
         functools.partial(stack_kernel, parts, depth, halves),
-        (meta, split[0], *split_arrived, fc2_weight),
-        [low_like(parts * shard + 16, 3 * width)]
+        (meta, split[0], *split_arrived, fc2_weight, out_weight),
+        [low_like(parts * shard + 16 + shard * model // (3 * width), 3 * width)]
         + [low_like(hidden_shard, model)] * (1 if halves else 2),
         [pltpu.VMEM((16, model), WIDE)],
     )
     kvq_pieces = gather_direct(kvq_rows, "fsdp")
 
-    token_rows = transpose_homes(after(tokens[0].astype(LOW), split_arrived[0]))
+    token_rows = transpose_homes(after(tokens[0].astype(LOW), split_arrived[1]))
     pieces = gather_pieces(after(token_rows, *split_arrived))
 
     kvq, kv, kvq_matrix, norm1_all, vectors = local_call(
@@ -766,6 +793,17 @@
     )
     kv_earlier = jnp.stack([shift(kv, "ctx", by) for by in range(1, contexts)])
 
+    if halves:
+        own_half = gather_direct(after(feeds[0], *kvq_pieces[1:]), "fsdp")
+        other_half = [shift(after(feeds[0], kv_earlier), "ctx", 1)]
+        for piece in own_half[1:]:
+            other_half.append(shift(piece, "ctx", 1))
+    else:
+        own_half = gather_direct(feeds[0], "fsdp")
+        other_half = gather_direct(feeds[1], "fsdp")
+    grad_rows = transpose_homes(after(cotangent[0].astype(LOW), own_half[1]))
+    branch_pieces = gather_pieces(grad_rows)
+
     score_flops = 2 * group * group * width
     wide_square = pltpu.VMEM((group, group), WIDE)
     low_square = pltpu.VMEM((group, group), LOW)
@@ -776,44 +814,31 @@
         [wide_square, low_square],
         flops=2 * score_flops,
     )
-    out_pieces = gather_direct(after(out_weight.astype(LOW), acc, kv_earlier), "fsdp")
-    grad_rows = transpose_homes(after(cotangent[0].astype(LOW), acc, kv_earlier))
     context, context_low, stat = local_call(
         functools.partial(earlier_forward, heads, parts),
-        (meta, kvq, kv_earlier, acc, stat),
+        (meta, kvq, kv_earlier, after(acc, own_half[1]), stat),
         [wide_like(group, width), low_like(group, width), wide_like(group, 128)],
         [wide_square, low_square, pltpu.VMEM((group, HEAD_DIM), WIDE)],
         flops=2 * score_flops,
     )
-    out_matrix, attended_keep, *attended_sends = local_call(
+    out_matrix, attended_keep, attended_send = local_call(
         functools.partial(mix_kernel, parts, depth),
-        (meta, context_low, *out_pieces),
-        [low_like(width, model), wide_like(rows, model)] + [low_like(rows, model)] * (parts - 1),
+        (meta, after(context_low, *own_half[2:]), *kvq_pieces),
+        [low_like(width, model), wide_like(2 * rows, model), low_like(2 * rows, model)],
         flops=2 * group * width * model,
     )
-    branch_pieces = gather_pieces(after(grad_rows, context_low))
-    if halves:
-        own_half = gather_direct(after(feeds[0], context_low), "fsdp")
-        other_half = [shift(after(feeds[0], kv_earlier), "ctx", 1)]
-        for piece in own_half[1:]:
-            other_half.append(shift(piece, "ctx", 1))
-    else:
-        own_half = gather_direct(feeds[0], "fsdp")
-        other_half = gather_direct(feeds[1], "fsdp")
-
-    arrived = send_pieces(attended_sends, "dp")
+    attended_sum = sum_rows(attended_keep, attended_send)
     norm2, attended = local_call(
         functools.partial(second_norm_kernel, parts),
-        (meta, attended_keep, *arrived, token_rows, vectors),
+        (meta, *attended_sum, token_rows, vectors),
         [low_like(rows, model), wide_like(rows, model)],
     )
 
     norm2_pieces = gather_pieces(norm2)
-    norm2_keep, *rest = local_call(
+    norm2_keep, norm2_send, *rest = local_call(
         functools.partial(feed_kernel, parts, depth, halves),
         (meta, *norm2_pieces, *branch_pieces, *own_half, *other_half, vectors),
-        [wide_like(rows, model)]
-        + [low_like(rows, model)] * (parts - 1)
+        [wide_like(2 * rows, model), low_like(2 * rows, model)]
         + [low_like(group, hidden_part)] * 2
         + [low_like(group, model)] * 2
         + [low_like(hidden_part, model), wide_like(1, hidden_part)],
@@ -824,25 +849,25 @@
         ],
         flops=6 * group * model * hidden_part,
     )
-    norm2_sends = rest[: parts - 1]
-    hidden, inner_grad, norm2_all, branch_all, down_matrix, up_bias = rest[parts - 1 :]
-    norm2_arrived = send_pieces(norm2_sends, "dp")
-    kept_half, sent_half, fed_keep, *fed_sends = local_call(
+    hidden, inner_grad, norm2_all, branch_all, down_matrix, up_bias = rest
+    norm2_sum = sum_rows(norm2_keep, norm2_send)
+    kept_half, *sent_half, fed_keep, fed_send = local_call(
         functools.partial(feed_grad_kernel, parts, depth, halves),
         (meta, hidden, inner_grad, norm2_all, branch_all, down_matrix),
         [
             wide_like(depth, hidden_shard, model),
-            low_like(depth, hidden_shard, model),
-            wide_like(rows, model),
-        ]
-        + [low_like(rows, model)] * (parts - 1),
+            low_like(depth // 2, hidden_shard, model),
+            low_like(depth // 2, hidden_shard, model),
+            wide_like(2 * rows, model),
+            low_like(2 * rows, model),
+        ],
         [pltpu.VMEM((max(model, hidden_part), max(model, hidden_part)), WIDE)],
         flops=6 * group * model * hidden_part,
     )
     attn_grad, mixed_part, sums = local_call(
         functools.partial(second_norm_grad_kernel, parts),
         (
-            meta, after(norm2_keep, fed_keep), *norm2_arrived, token_rows, attended, grad_rows,
+            meta, after(norm2_sum[0], fed_keep), *norm2_sum[1:], token_rows, attended, grad_rows,
             vectors,
         ),
         [low_like(rows, model), wide_like(rows, model), wide_like(8, model)],
@@ -850,10 +875,14 @@
     attn_pieces = gather_pieces(attn_grad)
 
     def fold(kept, sent, *later):
-        arrived = after(shift(sent, "ctx", 1), *later)
+        arrived = [shift(sent[0], "ctx", 1)]
+        for piece in sent[1:]:
+            arrived.append(shift(after(piece, arrived[-1]), "ctx", 1))
         shape = kept.shape[1:]
         keep, *sends = local_call(
-            fold_kernel, (meta, kept, arrived), [wide_like(*shape)] + [low_like(*shape)] * (depth - 1)
+            functools.partial(fold_kernel, len(sent)),
+            (meta, after(kept, *later), *arrived),
+            [wide_like(*shape)] + [low_like(*shape)] * (depth - 1),
         )
         return keep, sends
 
@@ -873,9 +902,7 @@
     def owner_sum(keep, pieces):
         return sum_replicas(sum_all(keep, pieces).astype(LOW))
 
-    fed_arrived = send_pieces(
-        lax.optimization_barrier((*fed_sends, attn_pieces[-1]))[: parts - 1], "dp"
-    )
+    fed_sum = sum_rows(fed_keep, after(fed_send, attn_pieces[-1]))
 
     ctx_grad, attn_all, query_grad, kv_grad = local_call(
         functools.partial(context_grad_kernel, parts, heads),
@@ -891,7 +918,9 @@
     )
     if halves:
         half_keep, half_sends = fold(kept_half, sent_half, query_grad)
-        half_pieces = send_pieces(half_sends, "fsdp")
+        farthest = swap(half_sends[-1], "fsdp", depth - 1)
+        nearer = [after(send, farthest) for send in half_sends[:-1]]
+        half_pieces = send_pieces(nearer, "fsdp") + [farthest]
     else:
         half_pieces = []
     if halves:
@@ -906,16 +935,18 @@
         [wide_square, wide_square, low_square, low_square],
         flops=5 * score_flops,
     )
-    kvq_grad, norm1_keep, *rest = local_call(
+    kvq_grad, norm1_keep, norm1_send, kvq_bias = local_call(
         functools.partial(projection_back_kernel, parts),
-        (meta, after(kvq_own, *fed_arrived), kv_arrived, kvq_matrix),
-        [low_like(group, 3 * width), wide_like(rows, model)]
-        + [low_like(rows, model)] * (parts - 1)
-        + [wide_like(1, 3 * width)],
+        (meta, after(kvq_own, fed_sum[2], *half_pieces[-1:]), kv_arrived, kvq_matrix),
+        [
+            low_like(group, 3 * width),
+            wide_like(2 * rows, model),
+            low_like(2 * rows, model),
+            wide_like(1, 3 * width),
+        ],
         flops=2 * group * model * 3 * width,
     )
-    kvq_bias = rest[-1]
-    norm1_arrived = send_pieces(rest[:-1], "dp")
+    norm1_sum = sum_rows(norm1_keep, norm1_send)
     share_rows = (parts * shard + shard * model // (3 * width)) // 2
     kept_share, sent_share = local_call(
         functools.partial(projection_grad_kernel, parts, depth, halves),
@@ -930,21 +961,23 @@
     input_part, sums = local_call(
         functools.partial(first_norm_grad_kernel, parts),
         (
-            meta, after(norm1_keep, kept_share, *half_pieces), *norm1_arrived, token_rows, vectors, mixed_part,
+            meta, after(norm1_sum[0], kept_share), *norm1_sum[1:], token_rows, vectors, mixed_part,
             sums, kvq_bias, up_bias,
         ),
         [low_like(rows, model), wide_like(8, model)],
     )
 
     if halves:
-        share_keep, share_sends = fold(kept_share, sent_share, input_part)
+        share_keep, share_sends = fold(kept_share, [sent_share], input_part)
         share_pieces = send_pieces(share_sends, "fsdp")
-        up_total, down_total = both_halves(sum_all(half_keep, half_pieces).astype(LOW))
+        up_total, down_total = both_halves(
+            sum_all(after(half_keep, input_part), half_pieces).astype(LOW)
+        )
         first_share, second_share = both_halves(sum_all(share_keep, share_pieces).astype(LOW))
         sums = after(sums, share_pieces[0])
     else:
         share_pieces = []
-        up_total, down_total = direct_totals(kept_half, sent_half)
+        up_total, down_total = direct_totals(kept_half, jnp.concatenate(sent_half))
         first_share, second_share = direct_totals(kept_share, sent_share)
     up_total = after(up_total.astype(LOW), *share_pieces).reshape(parts, shard, hidden_part)
     down_total = down_total.astype(WIDE)
@@ -964,8 +997,8 @@
         (meta, kvq_total[0], *send_pieces(kvq_total[1:], "dp")),
         [wide_like(shard, 3 * model)],
     )
-    delta = sum_all(fed_keep, fed_arrived) + vectors[5:6] + attended
-    delta = after(delta.astype(LOW), *share_pieces)
+    delta = row_sum(*fed_sum) + vectors[5:6] + attended
+    delta = after(delta.astype(LOW), *share_pieces[:1])
     output = tokens[0] + transpose_homes(delta).astype(WIDE)
     input_rows = after(transpose_homes(input_part), *share_pieces)
     input_grad = cotangent[0] + input_rows.astype(WIDE)

time: 282 us -> 270 us (0.957)
  waiting for transfers between devices: 119 us -> 115 us
    ppermute x52 -> x45, waiting for transfers between devices: 101 us -> 82.4 us  [swap(): return lax.ppermute(value, axis, [(at, at ^ bit) for at in range(count)])]
    ppermute x11 -> x12, waiting for transfers between devices: 17.6 us -> 32.4 us  [shift(): lax.ppermute(value, axis, [(at, (at + by) % count) for at in range(count)])]
    unnamed x64 -> x48, local copies, waits for them, and re-layouts: 9.2 us -> 5.73 us
    ppermute x11 -> x12, starting transfers between devices: 22.9 us -> 19.6 us  [shift(): lax.ppermute(value, axis, [(at, (at + by) % count) for at in range(count)])]
    ppermute x52 -> x45, starting transfers between devices: 68.5 us -> 70.3 us  [swap(): return lax.ppermute(value, axis, [(at, at ^ bit) for at in range(count)])]
  transfers between devices with their start and end apart: 67 -> 61, of which waited for: 30 -> 24; matrix products, arithmetic and copies ran while one was open for 5% -> 4% of each run, Pallas kernels for 11% -> 11%
where the time goes in v8:
time: 270 us; the launch traced here: 269 us
  waiting for transfers between devices  115 us (43%)
  starting transfers between devices  92.6 us (34%)
  Pallas kernels  42.8 us (16%)
  local copies, waits for them, and re-layouts  12 us (4%)
  other arithmetic  5.91 us (2%)
    ppermute x45, waiting for transfers between devices, swap(): return lax.ppermute(value, axis, [(at, at ^ bit) for at in range(count)])  82.4 us
    ppermute x45, starting transfers between devices, swap(): return lax.ppermute(value, axis, [(at, at ^ bit) for at in range(count)])  70.3 us
    pallas_call x20, Pallas kernels, local_call(): pl.pallas_call(kernel, name=getattr(kernel, 'func', kernel).__name__, out...  42.8 us
    ppermute x12, waiting for transfers between devices, shift(): lax.ppermute(value, axis, [(at, (at + by) % count) for at in range(count)])  32.4 us
    ppermute x12, starting transfers between devices, shift(): lax.ppermute(value, axis, [(at, (at + by) % count) for at in range(count)])  19.6 us
    unnamed x48, local copies, waits for them, and re-layouts  5.73 us
  transfers between devices with their start and end apart: 61, of which 24 were waited for; matrix products, arithmetic and copies ran while one was open for 4% of the time, Pallas kernels for 11%

profile of v8, /device:TPU:0, one launch (start us, length us, event | category | flops | bytes accessed | tf_op | source)
XLA Modules:
  0.0 269.3 jit_solution(14060655213041660416)
XLA Ops:
  4.5 3.0 %collective-permute-start = (bf16[48,1408]{1,0:T(8,128)(2,1)S(1)}, bf16[48,1408]{1,0:T(8,128)(2,1)S(1)}, u32[]{:S(2)}, u32[]{:S(2)}) collective-permute-start(bf16[48,1408]{1,0:T(8,128)(2,1)S(1)} %get-tuple-element.102), channel_id=1, source_target_pairs={{0,16},{8,24},{16,0},{24,8},{1,17},{9,25},{17,1},{25,9},{2,18},{10... | collective-permute-start | bytes 405512 | tf_op jit(solution)/shard_map/ppermute | solution.py:25
  8.5 2.6 collective-permute-done.refs_2_
  11.7 3.3 %collective-permute-start.2 = (bf16[48,1408]{1,0:T(8,128)(2,1)S(1)}, bf16[48,1408]{1,0:T(8,128)(2,1)S(1)}, u32[]{:S(2)}, u32[]{:S(2)}) collective-permute-start(bf16[48,1408]{1,0:T(8,128)(2,1)S(1)} %get-tuple-element.104), channel_id=1, source_target_pairs={{0,8},{8,0},{16,24},{24,16},{1,9},{9,1},{17,25},{25,17},{2,10},{10... | collective-permute-start | bytes 405512 | tf_op jit(solution)/shard_map/ppermute | solution.py:25
  15.0 3.2 %collective-permute-start.3 = (bf16[48,1408]{1,0:T(8,128)(2,1)S(1)}, bf16[48,1408]{1,0:T(8,128)(2,1)S(1)}, u32[]{:S(2)}, u32[]{:S(2)}) collective-permute-start(bf16[48,1408]{1,0:T(8,128)(2,1)S(1)} %get-tuple-element.105), channel_id=1, source_target_pairs={{0,24},{8,16},{16,8},{24,0},{1,25},{9,17},{17,9},{25,1},{2,26},{10... | collective-permute-start | bytes 405512 | tf_op jit(solution)/shard_map/ppermute | solution.py:25
  18.2 7.1 %collective-permute-done.3.refs_3_ = bf16[48,1408]{1,0:T(8,128)(2,1)S(1)} collective-permute-done((bf16[48,1408]{1,0:T(8,128)(2,1)S(1)}, bf16[48,1408]{1,0:T(8,128)(2,1)S(1)}, u32[]{:S(2)}, u32[]{:S(2)}) %collective-permute-start.3) | collective-permute-done | bytes 135200 | tf_op jit(solution)/shard_map/ppermute | solution.py:25
  29.1 4.0 %collective-permute-start.9 = (bf16[272,576]{1,0:T(8,128)(2,1)S(1)}, bf16[272,576]{1,0:T(8,128)(2,1)S(1)}, u32[]{:S(2)}, u32[]{:S(2)}) collective-permute-start(bf16[272,576]{1,0:T(8,128)(2,1)S(1)} %get-tuple-element.108.refs_4_.refs_1_), channel_id=1, source_target_pairs={{0,3},{1,2},{2,1},{3,0},{4,7},{5,6},{6,5},{7,4},{8,11},{9,10},{10,... | collective-permute-start | bytes 940040 | tf_op jit(solution)/shard_map/ppermute | solution.py:25
  33.6 10.2 %collective-permute-done.7.refs_5_.refs_2_ = bf16[272,576]{1,0:T(8,128)(2,1)S(1)} collective-permute-done((bf16[272,576]{1,0:T(8,128)(2,1)S(1)}, bf16[272,576]{1,0:T(8,128)(2,1)S(1)}, u32[]{:S(2)}, u32[]{:S(2)}) %collective-permute-start.7) | collective-permute-done | bytes 313376 | tf_op jit(solution)/shard_map/ppermute | solution.py:25
  43.8 12.2 %collective-permute-done.8.refs_6_.refs_3_ = bf16[272,576]{1,0:T(8,128)(2,1)S(1)} collective-permute-done((bf16[272,576]{1,0:T(8,128)(2,1)S(1)}, bf16[272,576]{1,0:T(8,128)(2,1)S(1)}, u32[]{:S(2)}, u32[]{:S(2)}) %collective-permute-start.8) | collective-permute-done | bytes 313376 | tf_op jit(solution)/shard_map/ppermute | solution.py:25
  56.0 3.0 %project_kernel.1 = (bf16[512,576]{1,0:T(8,128)(2,1)S(1)}, bf16[512,384]{1,0:T(8,128)(2,1)S(1)}, bf16[768,576]{1,0:T(8,128)(2,1)S(1)}, bf16[512,768]{1,0:T(8,128)(2,1)S(1)}, f32[8,768]{1,0:T(8,128)S(1)}) custom-call(s32[6]{0:T(128)S(1)} %stack.33.meta_ref.place_ref, bf16[128,768]{1,0:T(8,128)(2,1)S(1)} %collective-permute-done.1.refs_0_.refs_3_, ...), custom_call_target="tpu_custom_call" | custom-call | flops 22649240 | bytes 235930 | tf_op jit(solution)/shard_map/project_kernel/pallas_call | solution.py:710
  60.6 6.6 %collective-permute-start.11 = (bf16[192,768]{1,0:T(8,128)(2,1)S(1)}, bf16[192,768]{1,0:T(8,128)(2,1)S(1)}, u32[]{:S(2)}, u32[]{:S(2)}) collective-permute-start(bf16[192,768]{1,0:T(8,128)(2,1)S(1)} %get-tuple-element.123.refs_8_), channel_id=1, source_target_pairs={{0,1},{1,0},{2,3},{3,2},{4,5},{5,4},{6,7},{7,6},{8,9},{9,8},{10,11... | collective-permute-start | bytes 884744 | tf_op jit(solution)/shard_map/ppermute | solution.py:25
  69.6 6.8 %own_forward.1 = (f32[512,192]{1,0:T(8,128)S(1)}, f32[512,128]{1,0:T(8,128)S(1)}) custom-call(s32[6]{0:T(128)S(1)} %stack.33.meta_ref.place_ref, bf16[512,576]{1,0:T(8,128)(2,1)S(1)} %get-tuple-element.109.kvq_ref.refs_5_.refs_0_), custom_call_target="tpu_custom_call" | custom-call | flops 10066329 | bytes 62260 | tf_op jit(solution)/shard_map/own_forward/pallas_call | solution.py:710
  78.4 12.3 %collective-permute-done.12.refs_10_ = bf16[192,768]{1,0:T(8,128)(2,1)S(1)} collective-permute-done((bf16[192,768]{1,0:T(8,128)(2,1)S(1)}, bf16[192,768]{1,0:T(8,128)(2,1)S(1)}, u32[]{:S(2)}, u32[]{:S(2)}) %collective-permute-start.12) | collective-permute-done | bytes 294944 | tf_op jit(solution)/shard_map/ppermute | solution.py:25
  93.5 6.0 %collective-permute-start.15 = (bf16[128,768]{1,0:T(8,128)(2,1)S(1)}, bf16[128,768]{1,0:T(8,128)(2,1)S(1)}, u32[]{:S(2)}, u32[]{:S(2)}) collective-permute-start(bf16[128,768]{1,0:T(8,128)(2,1)S(1)} %add_convert_fusion.5), channel_id=1, source_target_pairs={{0,16},{8,24},{16,0},{24,8},{1,17},{9,25},{17,1},{25,9},{2,18},{10... | collective-permute-start | bytes 589832 | tf_op jit(solution)/shard_map/ppermute | solution.py:25
  102.1 6.7 %collective-permute-start.21 = (bf16[128,768]{1,0:T(8,128)(2,1)S(1)}, bf16[128,768]{1,0:T(8,128)(2,1)S(1)}, u32[]{:S(2)}, u32[]{:S(2)}) collective-permute-start(bf16[128,768]{1,0:T(8,128)(2,1)S(1)} %collective-permute-done.19.refs_4_.refs_5_), channel_id=1, source_target_pairs={{0,16},{8,24},{16,0},{24,8},{1,17},{9,25},{17,1},{25,9},{2,18},{10... | collective-permute-start | bytes 589832 | tf_op jit(solution)/shard_map/ppermute | solution.py:25
  110.8 5.1 %collective-permute-done.25.refs_14_ = bf16[192,768]{1,0:T(8,128)(2,1)S(1)} collective-permute-done((bf16[192,768]{1,0:T(8,128)(2,1)S(1)}, bf16[192,768]{1,0:T(8,128)(2,1)S(1)}, u32[]{:S(2)}, u32[]{:S(2)}) %collective-permute-start.25) | collective-permute-done | bytes 294944 | tf_op jit(solution)/shard_map/ppermute | solution.py:30
  116.4 5.8 %collective-permute-done.26.refs_15_ = bf16[192,768]{1,0:T(8,128)(2,1)S(1)} collective-permute-done((bf16[192,768]{1,0:T(8,128)(2,1)S(1)}, bf16[192,768]{1,0:T(8,128)(2,1)S(1)}, u32[]{:S(2)}, u32[]{:S(2)}) %collective-permute-start.26) | collective-permute-done | bytes 294944 | tf_op jit(solution)/shard_map/ppermute | solution.py:30
  122.7 3.3 %collective-permute-done.23.refs_12_ = bf16[192,768]{1,0:T(8,128)(2,1)S(1)} collective-permute-done((bf16[192,768]{1,0:T(8,128)(2,1)S(1)}, bf16[192,768]{1,0:T(8,128)(2,1)S(1)}, u32[]{:S(2)}, u32[]{:S(2)}) %collective-permute-start.23) | collective-permute-done | bytes 294944 | tf_op jit(solution)/shard_map/ppermute | solution.py:30
  126.0 4.8 %feed_kernel.1 = (f32[256,768]{1,0:T(8,128)S(1)}, bf16[256,768]{1,0:T(8,128)(2,1)S(1)}, bf16[512,768]{1,0:T(8,128)(2,1)S(1)}, bf16[512,768]{1,0:T(8,128)(2,1)S(1...) custom-call(s32[6]{0:T(128)S(1)} %stack.33.meta_ref.place_ref, ...), custom_call_target="tpu_custom_call" | custom-call | flops 90596968 | bytes 473242 | tf_op jit(solution)/shard_map/feed_kernel/pallas_call | solution.py:710
  130.8 3.8 %feed_grad_kernel.1 = (f32[4,192,768]{2,1,0:T(8,128)S(1)}, bf16[2,192,768]{2,1,0:T(8,128)(2,1)S(1)}, bf16[2,192,768]{2,1,0:T(8,128)(2,1)S(1)}, f32[256,768]{1,0:T(8,128)S(1)}, bf16[256,768]{1,0:T(8,128)(2,1)S(1)}) custom-call(s32[6]{0:T(128)S(1)} %stack.33.meta_ref.place_ref, bf16[512,768]{1,0:T(8,128)(2,1)S(1)} %get-tuple-element.124.refs_0_, ...), custom_call_target="tpu_custom_call" | custom-call | flops 90596968 | bytes 452199 | tf_op jit(solution)/shard_map/feed_grad_kernel/pallas_call | solution.py:710
  137.0 5.4 %collective-permute-done.28.refs_2_ = bf16[128,768]{1,0:T(8,128)(2,1)S(1)} collective-permute-done((bf16[128,768]{1,0:T(8,128)(2,1)S(1)}, bf16[128,768]{1,0:T(8,128)(2,1)S(1)}, u32[]{:S(2)}, u32[]{:S(2)}) %collective-permute-start.28) | collective-permute-done | bytes 196640 | tf_op jit(solution)/shard_map/ppermute | solution.py:25
  145.7 4.7 %collective-permute-done.34.refs_0_ = bf16[2,192,768]{2,1,0:T(8,128)(2,1)S(1)} collective-permute-done((bf16[2,192,768]{2,1,0:T(8,128)(2,1)S(1)}, bf16[2,192,768]{2,1,0:T(8,128)(2,1)S(1)}, u32[]{:S(2)}, u32[]{:S(2)}) %collective-permute-start.34) | collective-permute-done | bytes 589856 | tf_op jit(solution)/shard_map/ppermute | solution.py:30
  154.8 7.5 %collective-permute-start.37 = (bf16[512,384]{1,0:T(8,128)(2,1)S(1)}, bf16[512,384]{1,0:T(8,128)(2,1)S(1)}, u32[]{:S(2)}, u32[]{:S(2)}) collective-permute-start(bf16[512,384]{1,0:T(8,128)(2,1)S(1)} %bitcast.43), channel_id=1, source_target_pairs={{0,4},{4,0},{1,5},{5,1},{2,6},{6,2},{3,7},{7,3},{8,12},{12,8},{9,1... | collective-permute-start | bytes 1179656 | tf_op jit(solution)/shard_map/ppermute | solution.py:30
  162.4 4.2 %collective-permute-done.35.refs_1_ = bf16[2,192,768]{2,1,0:T(8,128)(2,1)S(1)} collective-permute-done((bf16[2,192,768]{2,1,0:T(8,128)(2,1)S(1)}, bf16[2,192,768]{2,1,0:T(8,128)(2,1)S(1)}, u32[]{:S(2)}, u32[]{:S(2)}) %collective-permute-start.35) | collective-permute-done | bytes 589856 | tf_op jit(solution)/shard_map/ppermute | solution.py:30
  167.3 2.6 collective-permute-start.36
  171.7 6.8 %own_grad_kernel.1 = (f32[512,576]{1,0:T(8,128)S(1)}, f32[192,768]{1,0:T(8,128)S(1)}) custom-call(s32[6]{0:T(128)S(1)} %stack.33.meta_ref.place_ref, bf16[512,576]{1,0:T(8,128)(2,1)S(1)} %get-tuple-element.109.kvq_ref.refs_5_.refs_0_, bf16[512,192]{1,0:T(8,128)(2,1)S(1)} %get-tuple-element.141.refs_1_, f32[512,192]{1,0:T(8,128)S(1)} %get-tuple-element.139.refs_7_.refs_2_, ...), custom_call_target="tpu_custom_call" | custom-call | flops 25165824 | bytes 229377 | tf_op jit(solution)/shard_map/own_grad_kernel/pallas_call | solution.py:710
  188.5 5.6 %collective-permute-start.56 = (bf16[192,768]{1,0:T(8,128)(2,1)}, bf16[192,768]{1,0:T(8,128)(2,1)}, u32[]{:S(2)}, u32[]{:S(2)}) collective-permute-start(bf16[192,768]{1,0:T(8,128)(2,1)} %copy-done.14), channel_id=1, source_target_pairs={{0,2},{1,3},{2,0},{3,1},{4,6},{5,7},{6,4},{7,5},{8,10},{9,11},{10,... | collective-permute-start | bytes 884744 | tf_op jit(solution)/shard_map/ppermute | solution.py:25
  194.1 7.7 %collective-permute-done.40 = bf16[4,128,576]{1,2,0:T(8,128)(2,1)} collective-permute-done((bf16[4,128,576]{1,2,0:T(8,128)(2,1)}, bf16[4,128,576]{1,2,0:T(8,128)(2,1)}, u32[]{:S(2)}, u32[]{:S(2)}) %collective-permute-start.40) | collective-permute-done | bytes 589856 | tf_op jit(solution)/shard_map/ppermute | solution.py:30
  207.2 4.2 %collective-permute-start.41 = (bf16[128,576]{1,0:T(8,128)(2,1)S(1)}, bf16[128,576]{1,0:T(8,128)(2,1)S(1)}, u32[]{:S(2)}, u32[]{:S(2)}) collective-permute-start(bf16[128,576]{1,0:T(8,128)(2,1)S(1)} %get-tuple-element.169), channel_id=1, source_target_pairs={{0,1},{1,0},{2,3},{3,2},{4,5},{5,4},{6,7},{7,6},{8,9},{9,8},{10,11... | collective-permute-start | bytes 442376 | tf_op jit(solution)/shard_map/ppermute | solution.py:25
  212.2 4.6 %collective-permute-start.44 = (bf16[128,576]{1,0:T(8,128)(2,1)S(1)}, bf16[128,576]{1,0:T(8,128)(2,1)S(1)}, u32[]{:S(2)}, u32[]{:S(2)}) collective-permute-start(bf16[128,576]{1,0:T(8,128)(2,1)S(1)} %get-tuple-element.171), channel_id=1, source_target_pairs={{0,2},{1,3},{2,0},{3,1},{4,6},{5,7},{6,4},{7,5},{8,10},{9,11},{10,... | collective-permute-start | bytes 442376 | tf_op jit(solution)/shard_map/ppermute | solution.py:25
  225.2 16.3 %collective-permute-done.44 = bf16[128,576]{1,0:T(8,128)(2,1)S(1)} collective-permute-done((bf16[128,576]{1,0:T(8,128)(2,1)S(1)}, bf16[128,576]{1,0:T(8,128)(2,1)S(1)}, u32[]{:S(2)}, u32[]{:S(2)}) %collective-permute-start.44) | collective-permute-done | bytes 147488 | tf_op jit(solution)/shard_map/ppermute | solution.py:25
  242.9 5.8 %collective-permute-done.47 = f32[8,768]{1,0:T(8,128)S(1)} collective-permute-done((f32[8,768]{1,0:T(8,128)S(1)}, f32[8,768]{1,0:T(8,128)S(1)}, u32[]{:S(2)}, u32[]{:S(2)}) %collective-permute-start.47) | collective-permute-done | bytes 24608 | tf_op jit(solution)/shard_map/ppermute | solution.py:25
  254.4 3.2 %collective-permute-done.50 = f32[8,768]{1,0:T(8,128)S(1)} collective-permute-done((f32[8,768]{1,0:T(8,128)S(1)}, f32[8,768]{1,0:T(8,128)S(1)}, u32[]{:S(2)}, u32[]{:S(2)}) %collective-permute-start.50) | collective-permute-done | bytes 24608 | tf_op jit(solution)/shard_map/ppermute | solution.py:25
  (185 shorter events, 79.8 us)
Async XLA Ops:
  11.1 14.3 %collective-permute-start.1 = (bf16[128,768]{1,0:T(8,128)(2,1)S(1)}, bf16[128,768]{1,0:T(8,128)(2,1)S(1)}, u32[]{:S(2)}, u32[]{:S(2)}) collective-permute-start(bf16[128,768]{1,0:T(8,128)(2,1)S(1)} %bitcast_convert_fusion.1), channel_id=1, source_target_pairs={{0,0},{1,8},{2,16},{3,24},{8,1},{9,9},{10,17},{11,25},{16,2},{17,1... | collective-permute-start | bytes 589832 | tf_op jit(solution)/shard_map/ppermute | solution.py:36
  28.6 15.1 %collective-permute-start.7 = (bf16[272,576]{1,0:T(8,128)(2,1)S(1)}, bf16[272,576]{1,0:T(8,128)(2,1)S(1)}, u32[]{:S(2)}, u32[]{:S(2)}) collective-permute-start(bf16[272,576]{1,0:T(8,128)(2,1)S(1)} %get-tuple-element.108.refs_4_.refs_1_), channel_id=1, source_target_pairs={{0,1},{1,0},{2,3},{3,2},{4,5},{5,4},{6,7},{7,6},{8,9},{9,8},{10,11... | collective-permute-start | bytes 940040 | tf_op jit(solution)/shard_map/ppermute | solution.py:25
  29.1 26.9 %collective-permute-start.8 = (bf16[272,576]{1,0:T(8,128)(2,1)S(1)}, bf16[272,576]{1,0:T(8,128)(2,1)S(1)}, u32[]{:S(2)}, u32[]{:S(2)}) collective-permute-start(bf16[272,576]{1,0:T(8,128)(2,1)S(1)} %get-tuple-element.108.refs_4_.refs_1_), channel_id=1, source_target_pairs={{0,2},{1,3},{2,0},{3,1},{4,6},{5,7},{6,4},{7,5},{8,10},{9,11},{10,... | collective-permute-start | bytes 940040 | tf_op jit(solution)/shard_map/ppermute | solution.py:25
  29.1 26.9 %collective-permute-start.9 = (bf16[272,576]{1,0:T(8,128)(2,1)S(1)}, bf16[272,576]{1,0:T(8,128)(2,1)S(1)}, u32[]{:S(2)}, u32[]{:S(2)}) collective-permute-start(bf16[272,576]{1,0:T(8,128)(2,1)S(1)} %get-tuple-element.108.refs_4_.refs_1_), channel_id=1, source_target_pairs={{0,3},{1,2},{2,1},{3,0},{4,7},{5,6},{6,5},{7,4},{8,11},{9,10},{10,... | collective-permute-start | bytes 940040 | tf_op jit(solution)/shard_map/ppermute | solution.py:25
  33.1 22.9 %collective-permute-start.4 = (bf16[128,768]{1,0:T(8,128)(2,1)S(1)}, bf16[128,768]{1,0:T(8,128)(2,1)S(1)}, u32[]{:S(2)}, u32[]{:S(2)}) collective-permute-start(bf16[128,768]{1,0:T(8,128)(2,1)S(1)} %collective-permute-done.1.refs_0_.refs_3_), channel_id=1, source_target_pairs={{0,8},{8,0},{16,24},{24,16},{1,9},{9,1},{17,25},{25,17},{2,10},{10... | collective-permute-start | bytes 589832 | tf_op jit(solution)/shard_map/ppermute | solution.py:25
  33.1 22.9 %collective-permute-start.6 = (bf16[128,768]{1,0:T(8,128)(2,1)S(1)}, bf16[128,768]{1,0:T(8,128)(2,1)S(1)}, u32[]{:S(2)}, u32[]{:S(2)}) collective-permute-start(bf16[128,768]{1,0:T(8,128)(2,1)S(1)} %collective-permute-done.5.refs_2_), channel_id=1, source_target_pairs={{0,8},{8,0},{16,24},{24,16},{1,9},{9,1},{17,25},{25,17},{2,10},{10... | collective-permute-start | bytes 589832 | tf_op jit(solution)/shard_map/ppermute | solution.py:25
  59.0 18.2 %collective-permute-start.10 = (bf16[512,384]{1,0:T(8,128)(2,1)S(1)}, bf16[512,384]{1,0:T(8,128)(2,1)S(1)}, u32[]{:S(2)}, u32[]{:S(2)}) collective-permute-start(bf16[512,384]{1,0:T(8,128)(2,1)S(1)} %get-tuple-element.110), channel_id=1, source_target_pairs={{0,4},{4,0},{1,5},{5,1},{2,6},{6,2},{3,7},{7,3},{8,12},{12,8},{9,1... | collective-permute-start | bytes 1179656 | tf_op jit(solution)/shard_map/ppermute | solution.py:30
  60.6 16.6 %collective-permute-start.11 = (bf16[192,768]{1,0:T(8,128)(2,1)S(1)}, bf16[192,768]{1,0:T(8,128)(2,1)S(1)}, u32[]{:S(2)}, u32[]{:S(2)}) collective-permute-start(bf16[192,768]{1,0:T(8,128)(2,1)S(1)} %get-tuple-element.123.refs_8_), channel_id=1, source_target_pairs={{0,1},{1,0},{2,3},{3,2},{4,5},{5,4},{6,7},{7,6},{8,9},{9,8},{10,11... | collective-permute-start | bytes 884744 | tf_op jit(solution)/shard_map/ppermute | solution.py:25
  67.2 23.5 %collective-permute-start.12 = (bf16[192,768]{1,0:T(8,128)(2,1)S(1)}, bf16[192,768]{1,0:T(8,128)(2,1)S(1)}, u32[]{:S(2)}, u32[]{:S(2)}) collective-permute-start(bf16[192,768]{1,0:T(8,128)(2,1)S(1)} %get-tuple-element.123.refs_8_), channel_id=1, source_target_pairs={{0,2},{1,3},{2,0},{3,1},{4,6},{5,7},{6,4},{7,5},{8,10},{9,11},{10,... | collective-permute-start | bytes 884744 | tf_op jit(solution)/shard_map/ppermute | solution.py:25
  67.2 23.5 %collective-permute-start.13 = (bf16[192,768]{1,0:T(8,128)(2,1)S(1)}, bf16[192,768]{1,0:T(8,128)(2,1)S(1)}, u32[]{:S(2)}, u32[]{:S(2)}) collective-permute-start(bf16[192,768]{1,0:T(8,128)(2,1)S(1)} %get-tuple-element.123.refs_8_), channel_id=1, source_target_pairs={{0,3},{1,2},{2,1},{3,0},{4,7},{5,6},{6,5},{7,4},{8,11},{9,10},{10,... | collective-permute-start | bytes 884744 | tf_op jit(solution)/shard_map/ppermute | solution.py:25
  93.5 15.3 %collective-permute-start.15 = (bf16[128,768]{1,0:T(8,128)(2,1)S(1)}, bf16[128,768]{1,0:T(8,128)(2,1)S(1)}, u32[]{:S(2)}, u32[]{:S(2)}) collective-permute-start(bf16[128,768]{1,0:T(8,128)(2,1)S(1)} %add_convert_fusion.5), channel_id=1, source_target_pairs={{0,16},{8,24},{16,0},{24,8},{1,17},{9,25},{17,1},{25,9},{2,18},{10... | collective-permute-start | bytes 589832 | tf_op jit(solution)/shard_map/ppermute | solution.py:25
  99.6 10.7 %collective-permute-start.24 = (bf16[192,768]{1,0:T(8,128)(2,1)S(1)}, bf16[192,768]{1,0:T(8,128)(2,1)S(1)}, u32[]{:S(2)}, u32[]{:S(2)}) collective-permute-start(bf16[192,768]{1,0:T(8,128)(2,1)S(1)} %collective-permute-done.11.refs_9_), channel_id=1, source_target_pairs={{0,4},{4,0},{1,5},{5,1},{2,6},{6,2},{3,7},{7,3},{8,12},{12,8},{9,1... | collective-permute-start | bytes 884744 | tf_op jit(solution)/shard_map/ppermute | solution.py:30
  100.1 15.8 %collective-permute-start.25 = (bf16[192,768]{1,0:T(8,128)(2,1)S(1)}, bf16[192,768]{1,0:T(8,128)(2,1)S(1)}, u32[]{:S(2)}, u32[]{:S(2)}) collective-permute-start(bf16[192,768]{1,0:T(8,128)(2,1)S(1)} %collective-permute-done.12.refs_10_), channel_id=1, source_target_pairs={{0,4},{4,0},{1,5},{5,1},{2,6},{6,2},{3,7},{7,3},{8,12},{12,8},{9,1... | collective-permute-start | bytes 884744 | tf_op jit(solution)/shard_map/ppermute | solution.py:30
  101.6 20.6 %collective-permute-start.26 = (bf16[192,768]{1,0:T(8,128)(2,1)S(1)}, bf16[192,768]{1,0:T(8,128)(2,1)S(1)}, u32[]{:S(2)}, u32[]{:S(2)}) collective-permute-start(bf16[192,768]{1,0:T(8,128)(2,1)S(1)} %collective-permute-done.13.refs_11_), channel_id=1, source_target_pairs={{0,4},{4,0},{1,5},{5,1},{2,6},{6,2},{3,7},{7,3},{8,12},{12,8},{9,1... | collective-permute-start | bytes 884744 | tf_op jit(solution)/shard_map/ppermute | solution.py:30
  102.1 13.8 %collective-permute-start.21 = (bf16[128,768]{1,0:T(8,128)(2,1)S(1)}, bf16[128,768]{1,0:T(8,128)(2,1)S(1)}, u32[]{:S(2)}, u32[]{:S(2)}) collective-permute-start(bf16[128,768]{1,0:T(8,128)(2,1)S(1)} %collective-permute-done.19.refs_4_.refs_5_), channel_id=1, source_target_pairs={{0,16},{8,24},{16,0},{24,8},{1,17},{9,25},{17,1},{25,9},{2,18},{10... | collective-permute-start | bytes 589832 | tf_op jit(solution)/shard_map/ppermute | solution.py:25
  109.6 12.6 %collective-permute-start.17 = (bf16[128,768]{1,0:T(8,128)(2,1)S(1)}, bf16[128,768]{1,0:T(8,128)(2,1)S(1)}, u32[]{:S(2)}, u32[]{:S(2)}) collective-permute-start(bf16[128,768]{1,0:T(8,128)(2,1)S(1)} %get-tuple-element.121.refs_0_), channel_id=1, source_target_pairs={{0,16},{8,24},{16,0},{24,8},{1,17},{9,25},{17,1},{25,9},{2,18},{10... | collective-permute-start | bytes 589832 | tf_op jit(solution)/shard_map/ppermute | solution.py:25
  110.3 15.7 %collective-permute-start.23 = (bf16[192,768]{1,0:T(8,128)(2,1)S(1)}, bf16[192,768]{1,0:T(8,128)(2,1)S(1)}, u32[]{:S(2)}, u32[]{:S(2)}) collective-permute-start(bf16[192,768]{1,0:T(8,128)(2,1)S(1)} %get-tuple-element.123.refs_8_), channel_id=1, source_target_pairs={{0,4},{4,0},{1,5},{5,1},{2,6},{6,2},{3,7},{7,3},{8,12},{12,8},{9,1... | collective-permute-start | bytes 884744 | tf_op jit(solution)/shard_map/ppermute | solution.py:30
  134.6 15.8 %collective-permute-start.34 = (bf16[2,192,768]{2,1,0:T(8,128)(2,1)S(1)}, bf16[2,192,768]{2,1,0:T(8,128)(2,1)S(1)}, u32[]{:S(2)}, u32[]{:S(2)}) collective-permute-start(bf16[2,192,768]{2,1,0:T(8,128)(2,1)S(1)} %get-tuple-element.145), channel_id=1, source_target_pairs={{0,4},{4,0},{1,5},{5,1},{2,6},{6,2},{3,7},{7,3},{8,12},{12,8},{9,1... | collective-permute-start | bytes 1769480 | tf_op jit(solution)/shard_map/ppermute | solution.py:30
  150.4 16.1 %collective-permute-start.35 = (bf16[2,192,768]{2,1,0:T(8,128)(2,1)S(1)}, bf16[2,192,768]{2,1,0:T(8,128)(2,1)S(1)}, u32[]{:S(2)}, u32[]{:S(2)}) collective-permute-start(bf16[2,192,768]{2,1,0:T(8,128)(2,1)S(1)} %get-tuple-element.147), channel_id=1, source_target_pairs={{0,4},{4,0},{1,5},{5,1},{2,6},{6,2},{3,7},{7,3},{8,12},{12,8},{9,1... | collective-permute-start | bytes 1769480 | tf_op jit(solution)/shard_map/ppermute | solution.py:30
  151.9 18.1 %collective-permute-start.31 = (bf16[256,768]{1,0:T(8,128)(2,1)S(1)}, bf16[256,768]{1,0:T(8,128)(2,1)S(1)}, u32[]{:S(2)}, u32[]{:S(2)}) collective-permute-start(bf16[256,768]{1,0:T(8,128)(2,1)S(1)} %get-tuple-element.136), channel_id=1, source_target_pairs={{0,8},{8,0},{16,24},{24,16},{1,9},{9,1},{17,25},{25,17},{2,10},{10... | collective-permute-start | bytes 1179656 | tf_op jit(solution)/shard_map/ppermute | solution.py:25
  154.8 23.8 %collective-permute-start.37 = (bf16[512,384]{1,0:T(8,128)(2,1)S(1)}, bf16[512,384]{1,0:T(8,128)(2,1)S(1)}, u32[]{:S(2)}, u32[]{:S(2)}) collective-permute-start(bf16[512,384]{1,0:T(8,128)(2,1)S(1)} %bitcast.43), channel_id=1, source_target_pairs={{0,4},{4,0},{1,5},{5,1},{2,6},{6,2},{3,7},{7,3},{8,12},{12,8},{9,1... | collective-permute-start | bytes 1179656 | tf_op jit(solution)/shard_map/ppermute | solution.py:30
  167.3 11.3 %collective-permute-start.36 = (bf16[192,768]{1,0:T(8,128)(2,1)S(1)}, bf16[192,768]{1,0:T(8,128)(2,1)S(1)}, u32[]{:S(2)}, u32[]{:S(2)}) collective-permute-start(bf16[192,768]{1,0:T(8,128)(2,1)S(1)} %get-tuple-element.152), channel_id=1, source_target_pairs={{0,3},{1,2},{2,1},{3,0},{4,7},{5,6},{6,5},{7,4},{8,11},{9,10},{10,... | collective-permute-start | bytes 884744 | tf_op jit(solution)/shard_map/ppermute | solution.py:25
  185.7 16.1 %collective-permute-start.40 = (bf16[4,128,576]{1,2,0:T(8,128)(2,1)}, bf16[4,128,576]{1,2,0:T(8,128)(2,1)}, u32[]{:S(2)}, u32[]{:S(2)}) collective-permute-start(bf16[4,128,576]{1,2,0:T(8,128)(2,1)} %copy.30), channel_id=1, source_target_pairs={{0,4},{4,0},{1,5},{5,1},{2,6},{6,2},{3,7},{7,3},{8,12},{12,8},{9,1... | collective-permute-start | bytes 1769480 | tf_op jit(solution)/shard_map/ppermute | solution.py:30
  187.9 15.3 %collective-permute-start.39 = (bf16[128,768]{1,0:T(8,128)(2,1)}, bf16[128,768]{1,0:T(8,128)(2,1)}, u32[]{:S(2)}, u32[]{:S(2)}) collective-permute-start(bf16[128,768]{1,0:T(8,128)(2,1)} %add_convert_fusion.1), channel_id=1, source_target_pairs={{0,16},{8,24},{16,0},{24,8},{1,17},{9,25},{17,1},{25,9},{2,18},{10... | collective-permute-start | bytes 589832 | tf_op jit(solution)/shard_map/ppermute | solution.py:25
  188.5 29.8 %collective-permute-start.56 = (bf16[192,768]{1,0:T(8,128)(2,1)}, bf16[192,768]{1,0:T(8,128)(2,1)}, u32[]{:S(2)}, u32[]{:S(2)}) collective-permute-start(bf16[192,768]{1,0:T(8,128)(2,1)} %copy-done.14), channel_id=1, source_target_pairs={{0,2},{1,3},{2,0},{3,1},{4,6},{5,7},{6,4},{7,5},{8,10},{9,11},{10,... | collective-permute-start | bytes 884744 | tf_op jit(solution)/shard_map/ppermute | solution.py:25
  194.1 25.8 %collective-permute-start.55 = (bf16[192,768]{1,0:T(8,128)(2,1)}, bf16[192,768]{1,0:T(8,128)(2,1)}, u32[]{:S(2)}, u32[]{:S(2)}) collective-permute-start(bf16[192,768]{1,0:T(8,128)(2,1)} %copy-done.13), channel_id=1, source_target_pairs={{0,1},{1,0},{2,3},{3,2},{4,5},{5,4},{6,7},{7,6},{8,9},{9,8},{10,11... | collective-permute-start | bytes 884744 | tf_op jit(solution)/shard_map/ppermute | solution.py:25
  211.5 31.4 %collective-permute-start.43 = (bf16[128,768]{1,0:T(8,128)(2,1)S(1)}, bf16[128,768]{1,0:T(8,128)(2,1)S(1)}, u32[]{:S(2)}, u32[]{:S(2)}) collective-permute-start(bf16[128,768]{1,0:T(8,128)(2,1)S(1)} %get-tuple-element.166), channel_id=1, source_target_pairs={{0,0},{1,8},{2,16},{3,24},{8,1},{9,9},{10,17},{11,25},{16,2},{17,1... | collective-permute-start | bytes 589832 | tf_op jit(solution)/shard_map/ppermute | solution.py:36
  212.2 29.2 %collective-permute-start.44 = (bf16[128,576]{1,0:T(8,128)(2,1)S(1)}, bf16[128,576]{1,0:T(8,128)(2,1)S(1)}, u32[]{:S(2)}, u32[]{:S(2)}) collective-permute-start(bf16[128,576]{1,0:T(8,128)(2,1)S(1)} %get-tuple-element.171), channel_id=1, source_target_pairs={{0,2},{1,3},{2,0},{3,1},{4,6},{5,7},{6,4},{7,5},{8,10},{9,11},{10,... | collective-permute-start | bytes 442376 | tf_op jit(solution)/shard_map/ppermute | solution.py:25
  216.8 24.6 %collective-permute-start.45 = (bf16[128,576]{1,0:T(8,128)(2,1)S(1)}, bf16[128,576]{1,0:T(8,128)(2,1)S(1)}, u32[]{:S(2)}, u32[]{:S(2)}) collective-permute-start(bf16[128,576]{1,0:T(8,128)(2,1)S(1)} %get-tuple-element.172), channel_id=1, source_target_pairs={{0,3},{1,2},{2,1},{3,0},{4,7},{5,6},{6,5},{7,4},{8,11},{9,10},{10,... | collective-permute-start | bytes 442376 | tf_op jit(solution)/shard_map/ppermute | solution.py:25
  221.1 40.3 %collective-permute-start.57 = (bf16[192,768]{1,0:T(8,128)(2,1)S(1)}, bf16[192,768]{1,0:T(8,128)(2,1)S(1)}, u32[]{:S(2)}, u32[]{:S(2)}) collective-permute-start(bf16[192,768]{1,0:T(8,128)(2,1)S(1)} %add_convert_fusion), channel_id=1, source_target_pairs={{0,4},{4,0},{1,5},{5,1},{2,6},{6,2},{3,7},{7,3},{8,12},{12,8},{9,1... | collective-permute-start | bytes 884744 | tf_op jit(solution)/shard_map/ppermute | solution.py:30
  224.5 38.2 %collective-permute-start.42 = (bf16[128,768]{1,0:T(8,128)(2,1)S(1)}, bf16[128,768]{1,0:T(8,128)(2,1)S(1)}, u32[]{:S(2)}, u32[]{:S(2)}) collective-permute-start(bf16[128,768]{1,0:T(8,128)(2,1)S(1)} %add_convert_fusion.2), channel_id=1, source_target_pairs={{0,0},{1,8},{2,16},{3,24},{8,1},{9,9},{10,17},{11,25},{16,2},{17,1... | collective-permute-start | bytes 589832 | tf_op jit(solution)/shard_map/ppermute | solution.py:36
  241.6 16.7 %collective-permute-start.51 = (bf16[128,576]{1,0:T(8,128)(2,1)S(1)}, bf16[128,576]{1,0:T(8,128)(2,1)S(1)}, u32[]{:S(2)}, u32[]{:S(2)}) collective-permute-start(bf16[128,576]{1,0:T(8,128)(2,1)S(1)} %add_convert_fusion.6), channel_id=1, source_target_pairs={{0,4},{4,0},{1,5},{5,1},{2,6},{6,2},{3,7},{7,3},{8,12},{12,8},{9,1... | collective-permute-start | bytes 442376 | tf_op jit(solution)/shard_map/ppermute | solution.py:30
  (53 other events, 397.8 us)

commit v9 on v8

--- a/solution.py
+++ b/solution.py
@@ -40,11 +40,15 @@
     return lax.optimization_barrier((value,) + others)[0]
 
 
-def gather_pieces(block):
+def gather_pieces(block, *before_last):
     pieces = [block]
-    for slot in range(1, lax.axis_size("dp")):
+    count = lax.axis_size("dp")
+    for slot in range(1, count):
         low_bit = slot & -slot
-        pieces.append(swap(pieces[slot ^ low_bit], "dp", low_bit))
+        source = pieces[slot ^ low_bit]
+        if before_last and slot == count - 1:
+            source = after(source, *before_last)
+        pieces.append(swap(source, "dp", low_bit))
     return pieces
 
 
@@ -421,9 +425,11 @@
                 outs[slot][:, -part:] = up_ref[:, owner * part : (owner + 1) * part].astype(LOW)
 
 
-def join_qkv_kernel(parts, width, meta_ref, *refs):
-    pieces, out_ref = refs[:parts], refs[parts]
+def join_kernel(parts, width, meta_ref, *refs):
+    pieces, out_ref, up_ref, vectors = take(refs, parts, None, None, None)
     model = parts * width
+    shard = out_ref.shape[0]
+    hidden = up_ref.shape[1] // parts
     for case in range(parts):
 
         @pl.when(meta_ref[0] == case)
@@ -433,16 +439,13 @@
                 for at, first in enumerate((model, 2 * model, 0)):
                     start = first + owner * width
                     out_ref[:, start : start + width] = pieces[slot][
-                        :, at * width : (at + 1) * width
+                        :shard, at * width : (at + 1) * width
                     ].astype(WIDE)
-
-
-def join_up_kernel(parts, meta_ref, *refs):
-    pieces, out_ref = refs[:parts], refs[parts]
-    part = pieces[0].shape[1]
-    for slot in range(parts):
-        start = pl.multiple_of(meta_ref[slot] * part, 128)
-        out_ref[:, pl.ds(start, part)] = pieces[slot][...].astype(WIDE)
+                up_ref[:, owner * hidden : (owner + 1) * hidden] = pieces[slot][
+                    :shard, -hidden:
+                ].astype(WIDE)
+
+    vectors[...] = sum(piece[shard:, : vectors.shape[1]].astype(WIDE) for piece in pieces)
 
 
 def project_kernel(parts, depth, meta_ref, *refs):
@@ -675,16 +678,67 @@
             emit(half, sent if half else kept)
 
 
-def unfold_kernel(parts, meta_ref, first_ref, second_ref, *refs):
-    pieces, out_ref, folded = refs[:parts], refs[parts], refs[parts + 1]
-    shard, columns = pieces[0].shape
+def fold_vectors(sums, folded):
+    rest = sums.shape[1] - folded.shape[1]
+    folded[...] = jnp.zeros_like(folded)
+    folded[0:8, :] = sums[:, : folded.shape[1]]
+    folded[8:16, :rest] = sums[:, folded.shape[1] :]
+
+
+def fold_share_kernel(meta_ref, kept, arrived, sums, keep, *refs):
+    sends, folded = refs[:-1], refs[-1]
+    rows = kept.shape[1]
+    fold_vectors(sums, folded)
+    keep[:rows, :] = kept[0] + arrived[0].astype(WIDE)
+    keep[rows:, :] = folded[...]
+    for deep, send in enumerate(sends, 1):
+        send[:rows, :] = (kept[deep] + arrived[deep].astype(WIDE)).astype(LOW)
+        send[rows:, :] = folded[...].astype(LOW)
+
+
+def unfold_kernel(parts, halves, meta_ref, mine, arrived, *refs):
+    sums, mine_feed, other_feed, pieces, out_ref, down_ref, vectors, folded = take(
+        refs, 0 if halves else 1, None, None, parts, None, None, None, None
+    )
+    shard, columns = pieces[0].shape[0] - 16, vectors.shape[1]
+    hidden = mine_feed.shape[1]
     rest = out_ref.shape[1] - columns
     slots = parts // 2
     extra = folded.shape[0] // 2
-    for half, ref in enumerate((first_ref, second_ref)):
+
+    def unfold(half, ref):
         for slot in range(slots):
-            pieces[half * slots + slot][...] = ref[slot * shard : (slot + 1) * shard, :].astype(LOW)
-        folded[half * extra : (half + 1) * extra, :] = ref[slots * shard :, :].astype(WIDE)
+            pieces[half * slots + slot][:shard, :columns] = ref[
+                slot * shard : (slot + 1) * shard, :
+            ].astype(LOW)
+        start = slots * shard
+        folded[half * extra : (half + 1) * extra, :] = ref[start : start + extra, :].astype(WIDE)
+
+    def feeds(up, down):
+        for slot in range(parts):
+            pieces[slot][:shard, -hidden:] = up[slot * shard : (slot + 1) * shard, :].astype(LOW)
+        down_ref[...] = down[...].astype(WIDE)
+
+    if halves:
+        first = meta_ref[parts] == 0
+        pl.when(first)(lambda: feeds(mine_feed, other_feed))
+        pl.when(jnp.logical_not(first))(lambda: feeds(other_feed, mine_feed))
+        for half in range(2):
+            pl.when(first)(functools.partial(unfold, half, arrived if half else mine))
+            pl.when(jnp.logical_not(first))(
+                functools.partial(unfold, half, mine if half else arrived)
+            )
+        start = slots * shard + extra
+        vectors[...] = mine[start:, :].astype(WIDE) + arrived[start:, :].astype(WIDE)
+    else:
+        feeds(mine_feed, other_feed)
+        unfold(0, mine)
+        unfold(1, arrived)
+        fold_vectors(sums[0], vectors)
+    for piece in pieces:
+        piece[shard:, :columns] = vectors[...].astype(LOW)
+        piece[shard:, columns:] = jnp.zeros_like(piece[shard:, columns:])
+        piece[:shard, columns:-hidden] = jnp.zeros_like(piece[:shard, columns:-hidden])
     out_ref[:, :columns] = folded[:shard, :]
     for at in range(columns // rest):
         out_ref[at * 16 : (at + 1) * 16, columns:] = folded[shard:, at * rest : (at + 1) * rest]
@@ -776,8 +830,8 @@
     )
     kvq_pieces = gather_direct(kvq_rows, "fsdp")
 
-    token_rows = transpose_homes(after(tokens[0].astype(LOW), split_arrived[1]))
-    pieces = gather_pieces(after(token_rows, *split_arrived))
+    token_rows = transpose_homes(after(tokens[0].astype(LOW), *split_arrived))
+    pieces = gather_pieces(after(token_rows, kvq_pieces[1]), *kvq_pieces[2:])
 
     kvq, kv, kvq_matrix, norm1_all, vectors = local_call(
         functools.partial(project_kernel, parts, depth),
@@ -795,9 +849,6 @@
 
     if halves:
         own_half = gather_direct(after(feeds[0], *kvq_pieces[1:]), "fsdp")
-        other_half = [shift(after(feeds[0], kv_earlier), "ctx", 1)]
-        for piece in own_half[1:]:
-            other_half.append(shift(piece, "ctx", 1))
     else:
         own_half = gather_direct(feeds[0], "fsdp")
         other_half = gather_direct(feeds[1], "fsdp")
@@ -814,6 +865,10 @@
         [wide_square, low_square],
         flops=2 * score_flops,
     )
+    if halves:
+        other_half = [shift(after(feeds[0], kv_earlier, acc), "ctx", 1)]
+        other_half.append(shift(after(own_half[1], acc), "ctx", 1))
+        other_half += [shift(piece, "ctx", 1) for piece in own_half[2:]]
     context, context_low, stat = local_call(
         functools.partial(earlier_forward, heads, parts),
         (meta, kvq, kv_earlier, after(acc, own_half[1]), stat),
@@ -823,7 +878,7 @@
     )
     out_matrix, attended_keep, attended_send = local_call(
         functools.partial(mix_kernel, parts, depth),
-        (meta, after(context_low, *own_half[2:]), *kvq_pieces),
+        (meta, after(context_low, *own_half[2:], *other_half[:2]), *kvq_pieces),
         [low_like(width, model), wide_like(2 * rows, model), low_like(2 * rows, model)],
         flops=2 * group * width * model,
     )
@@ -856,8 +911,7 @@
         (meta, hidden, inner_grad, norm2_all, branch_all, down_matrix),
         [
             wide_like(depth, hidden_shard, model),
-            low_like(depth // 2, hidden_shard, model),
-            low_like(depth // 2, hidden_shard, model),
+            low_like(depth, hidden_shard, model),
             wide_like(2 * rows, model),
             low_like(2 * rows, model),
         ],
@@ -892,13 +946,6 @@
             for grad in grads
         ]
 
-    def both_halves(mine_half, *later):
-        arrived_half = shift(after(mine_half, *later) if later else mine_half, "ctx", 1)
-        first = lax.axis_index("ctx") == 0
-        return (
-            jnp.where(first, mine_half, arrived_half), jnp.where(first, arrived_half, mine_half)
-        )
-
     def owner_sum(keep, pieces):
         return sum_replicas(sum_all(keep, pieces).astype(LOW))
 
@@ -950,7 +997,7 @@
     share_rows = (parts * shard + shard * model // (3 * width)) // 2
     kept_share, sent_share = local_call(
         functools.partial(projection_grad_kernel, parts, depth, halves),
-        (meta, norm1_all, kvq_grad, out_grad),
+        (meta, norm1_all, after(kvq_grad, norm1_sum[1]), out_grad),
         [wide_like(depth, share_rows, 3 * width), low_like(depth, share_rows, 3 * width)],
         [
             pltpu.VMEM((model, 3 * width), WIDE),
@@ -967,48 +1014,57 @@
         [low_like(rows, model), wide_like(8, model)],
     )
 
+    input_rows = transpose_homes(input_part)
     if halves:
-        share_keep, share_sends = fold(kept_share, [sent_share], input_part)
+        shape = (share_rows + 16, 3 * width)
+        share_keep, *share_sends = local_call(
+            fold_share_kernel,
+            (meta, after(kept_share, *half_pieces[:-1]), shift(sent_share, "ctx", 1), sums),
+            [wide_like(*shape)] + [low_like(*shape)] * (depth - 1),
+            [pltpu.VMEM((16, 3 * width), WIDE)],
+        )
         share_pieces = send_pieces(share_sends, "fsdp")
-        up_total, down_total = both_halves(
-            sum_all(after(half_keep, input_part), half_pieces).astype(LOW)
-        )
-        first_share, second_share = both_halves(sum_all(share_keep, share_pieces).astype(LOW))
-        sums = after(sums, share_pieces[0])
+        mine_half = sum_all(after(half_keep, share_pieces[0]), half_pieces).astype(LOW)
+        feed_totals = (mine_half, shift(mine_half, "ctx", 1))
+        mine_share = sum_all(share_keep, share_pieces).astype(LOW)
+        shares = (mine_share, shift(after(mine_share, input_rows), "ctx", 1))
     else:
         share_pieces = []
-        up_total, down_total = direct_totals(kept_half, jnp.concatenate(sent_half))
-        first_share, second_share = direct_totals(kept_share, sent_share)
-    up_total = after(up_total.astype(LOW), *share_pieces).reshape(parts, shard, hidden_part)
-    down_total = down_total.astype(WIDE)
-    (up_total,) = local_call(
-        functools.partial(join_up_kernel, parts),
-        (meta, up_total[0], *send_pieces([up_total[s] for s in range(1, parts)], "dp")),
-        [wide_like(shard, parts * hidden_part)],
-    )
-    *kvq_total, out_total = local_call(
-        functools.partial(unfold_kernel, parts),
-        (meta, first_share, second_share),
-        [low_like(shard, 3 * width)] * parts + [wide_like(shard, model)],
+        feed_totals = direct_totals(kept_half, sent_half[0])
+        shares = (
+            *direct_totals(kept_share, sent_share), sum_replicas(sum_doubling(sums, "fsdp"))
+        )
+    *totals, out_total, down_total, vector_part = local_call(
+        functools.partial(unfold_kernel, parts, halves),
+        (meta, *shares, *feed_totals),
+        [low_like(shard + 16, padded + hidden_part)] * parts
+        + [wide_like(shard, model), wide_like(hidden_shard, model), wide_like(16, 3 * width)],
         [pltpu.VMEM((shard * model // (3 * width), 3 * width), WIDE)],
     )
-    (qkv_total,) = local_call(
-        functools.partial(join_qkv_kernel, parts, width),
-        (meta, kvq_total[0], *send_pieces(kvq_total[1:], "dp")),
-        [wide_like(shard, 3 * model)],
+    qkv_total, up_total, vector_total = local_call(
+        functools.partial(join_kernel, parts, width),
+        (meta, totals[0], *send_pieces(totals[1:], "dp")),
+        [
+            wide_like(shard, 3 * model),
+            wide_like(shard, parts * hidden_part),
+            wide_like(16, 3 * width),
+        ],
     )
     delta = row_sum(*fed_sum) + vectors[5:6] + attended
-    delta = after(delta.astype(LOW), *share_pieces[:1])
+    delta = after(delta.astype(LOW), shares[1])
     output = tokens[0] + transpose_homes(delta).astype(WIDE)
-    input_rows = after(transpose_homes(input_part), *share_pieces)
     input_grad = cotangent[0] + input_rows.astype(WIDE)
 
-    sums = sum_replicas(after(sum_doubling(sums, "fsdp"), *share_pieces))
-    everywhere = sum_doubling(sums, "dp")
-    owned = lax.dynamic_slice(everywhere, (0, (mine * depth + deep) * shard), (6, shard))
-    value_bias = lax.dynamic_slice(sums, (6, width + deep * shard), (1, shard))[0]
-    query_bias = lax.dynamic_slice(sums, (6, 2 * width + deep * shard), (1, shard))[0]
-    inner_bias = lax.dynamic_slice(sums, (7, deep * hidden_shard), (1, hidden_shard))[0]
+    def vector_at(source, row, start, size):
+        late = start >= 3 * width
+        count = 8 if row == 0 else 1
+        at = (row + jnp.where(late, 8, 0), start - jnp.where(late, 3 * width, 0))
+        return lax.dynamic_slice(source, at, (count, size))
+
+    owned = vector_at(vector_total, 0, (mine * depth + deep) * shard, shard)
+    value_bias = vector_at(vector_part, 6, width + deep * shard, shard)[0]
+    query_bias = vector_at(vector_part, 6, 2 * width + deep * shard, shard)[0]
+    inner_bias = vector_at(vector_part, 7, deep * hidden_shard, hidden_shard)[0]
 
     return (
         output[None],

time: 270 us -> 256 us (0.948)
  waiting for transfers between devices: 115 us -> 101 us
  starting transfers between devices: 92.6 us -> 96.5 us
  other arithmetic: 5.91 us -> 3.11 us
    ppermute x12 -> x10, waiting for transfers between devices: 32.4 us -> 13.3 us  [shift(): lax.ppermute(value, axis, [(at, (at + by) % count) for at in range(count)])]
    ppermute x45 -> x38, starting transfers between devices: 70.3 us -> 77.8 us  [swap(): return lax.ppermute(value, axis, [(at, at ^ bit) for at in range(count)])]
    ppermute x45 -> x38, waiting for transfers between devices: 82.4 us -> 88.1 us  [swap(): return lax.ppermute(value, axis, [(at, at ^ bit) for at in range(count)])]
    ppermute x12 -> x10, starting transfers between devices: 19.6 us -> 15.1 us  [shift(): lax.ppermute(value, axis, [(at, (at + by) % count) for at in range(count)])]
    pallas_call x20 -> x19, Pallas kernels: 42.8 us -> 41.4 us  [local_call(): pl.pallas_call(kernel, name=getattr(kernel, 'func', kernel).__name__, out...]
    unnamed x48 -> x54, local copies, waits for them, and re-layouts: 5.73 us -> 5.97 us
  transfers between devices with their start and end apart: 61 -> 52, of which waited for: 24 -> 27; matrix products, arithmetic and copies ran while one was open for 4% -> 2% of each run, Pallas kernels for 11% -> 10%
where the time goes in v9:
time: 256 us
  waiting for transfers between devices  101 us (39%)
  starting transfers between devices  96.5 us (38%)
  Pallas kernels  41.4 us (16%)
  local copies, waits for them, and re-layouts  12.3 us (5%)
  other arithmetic  3.11 us (1%)
    ppermute x38, waiting for transfers between devices, swap(): return lax.ppermute(value, axis, [(at, at ^ bit) for at in range(count)])  88.1 us
    ppermute x38, starting transfers between devices, swap(): return lax.ppermute(value, axis, [(at, at ^ bit) for at in range(count)])  77.8 us
    pallas_call x19, Pallas kernels, local_call(): pl.pallas_call(kernel, name=getattr(kernel, 'func', kernel).__name__, out...  41.4 us
    ppermute x10, starting transfers between devices, shift(): lax.ppermute(value, axis, [(at, (at + by) % count) for at in range(count)])  15.1 us
    ppermute x10, waiting for transfers between devices, shift(): lax.ppermute(value, axis, [(at, (at + by) % count) for at in range(count)])  13.3 us
    unnamed x54, local copies, waits for them, and re-layouts  5.97 us
  transfers between devices with their start and end apart: 52, of which 27 were waited for; matrix products, arithmetic and copies ran while one was open for 2% of the time, Pallas kernels for 10%

profile of v9, /device:TPU:0, one launch (start us, length us, event | category | flops | bytes accessed | tf_op | source)
XLA Modules:
  0.0 255.9 jit_solution(4593908307419889423)
XLA Ops:
  5.0 2.6 collective-permute-start.1
  7.6 4.4 %collective-permute-done.1.refs_2_ = bf16[48,1408]{1,0:T(8,128)(2,1)S(1)} collective-permute-done((bf16[48,1408]{1,0:T(8,128)(2,1)S(1)}, bf16[48,1408]{1,0:T(8,128)(2,1)S(1)}, u32[]{:S(2)}, u32[]{:S(2)}) %collective-permute-start.1) | collective-permute-done | bytes 135200 | tf_op jit(solution)/shard_map/ppermute | solution.py:25
  12.0 2.4 collective-permute-done.2.refs_3_
  18.7 5.1 %collective-permute-start.7 = (bf16[272,576]{1,0:T(8,128)(2,1)S(1)}, bf16[272,576]{1,0:T(8,128)(2,1)S(1)}, u32[]{:S(2)}, u32[]{:S(2)}) collective-permute-start(bf16[272,576]{1,0:T(8,128)(2,1)S(1)} %get-tuple-element.110.refs_4_.refs_1_), channel_id=1, source_target_pairs={{0,2},{1,3},{2,0},{3,1},{4,6},{5,7},{6,4},{7,5},{8,10},{9,11},{10,... | collective-permute-start | bytes 940040 | tf_op jit(solution)/shard_map/ppermute | solution.py:25
  24.5 5.2 %collective-permute-done.4.refs_5_.refs_2_ = bf16[272,576]{1,0:T(8,128)(2,1)S(1)} collective-permute-done((bf16[272,576]{1,0:T(8,128)(2,1)S(1)}, bf16[272,576]{1,0:T(8,128)(2,1)S(1)}, u32[]{:S(2)}, u32[]{:S(2)}) %collective-permute-start.4) | collective-permute-done | bytes 313376 | tf_op jit(solution)/shard_map/ppermute | solution.py:25
  29.7 20.6 %collective-permute-start.6 = (bf16[128,768]{1,0:T(8,128)(2,1)S(1)}, bf16[128,768]{1,0:T(8,128)(2,1)S(1)}, u32[]{:S(2)}, u32[]{:S(2)}) collective-permute-start(bf16[128,768]{1,0:T(8,128)(2,1)S(1)} %collective-permute-done.3.refs_0_.refs_3_), channel_id=1, source_target_pairs={{0,16},{8,24},{16,0},{24,8},{1,17},{9,25},{17,1},{25,9},{2,18},{10... | collective-permute-start | bytes 589832 | tf_op jit(solution)/shard_map/ppermute | solution.py:25
  50.3 6.0 %collective-permute-done.7.refs_6_.refs_3_ = bf16[272,576]{1,0:T(8,128)(2,1)S(1)} collective-permute-done((bf16[272,576]{1,0:T(8,128)(2,1)S(1)}, bf16[272,576]{1,0:T(8,128)(2,1)S(1)}, u32[]{:S(2)}, u32[]{:S(2)}) %collective-permute-start.7) | collective-permute-done | bytes 313376 | tf_op jit(solution)/shard_map/ppermute | solution.py:25
  57.7 3.0 %project_kernel.1 = (bf16[512,576]{1,0:T(8,128)(2,1)S(1)}, bf16[512,384]{1,0:T(8,128)(2,1)S(1)}, bf16[768,576]{1,0:T(8,128)(2,1)S(1)}, bf16[512,768]{1,0:T(8,128)(2,1)S(1)}, f32[8,768]{1,0:T(8,128)S(1)}) custom-call(s32[6]{0:T(128)S(1)} %stack.33.meta_ref.place_ref, bf16[128,768]{1,0:T(8,128)(2,1)S(1)} %collective-permute-done.3.refs_0_.refs_3_, ...), custom_call_target="tpu_custom_call" | custom-call | flops 22649240 | bytes 235930 | tf_op jit(solution)/shard_map/project_kernel/pallas_call | solution.py:764
  62.3 6.4 %collective-permute-start.11 = (bf16[192,768]{1,0:T(8,128)(2,1)S(1)}, bf16[192,768]{1,0:T(8,128)(2,1)S(1)}, u32[]{:S(2)}, u32[]{:S(2)}) collective-permute-start(bf16[192,768]{1,0:T(8,128)(2,1)S(1)} %get-tuple-element.121.refs_8_), channel_id=1, source_target_pairs={{0,1},{1,0},{2,3},{3,2},{4,5},{5,4},{6,7},{7,6},{8,9},{9,8},{10,11... | collective-permute-start | bytes 884744 | tf_op jit(solution)/shard_map/ppermute | solution.py:25
  68.7 2.4 collective-permute-start.13
  71.1 6.8 %own_forward.1 = (f32[512,192]{1,0:T(8,128)S(1)}, f32[512,128]{1,0:T(8,128)S(1)}) custom-call(s32[6]{0:T(128)S(1)} %stack.33.meta_ref.place_ref, bf16[512,576]{1,0:T(8,128)(2,1)S(1)} %get-tuple-element.113.kvq_ref.refs_5_.refs_0_), custom_call_target="tpu_custom_call" | custom-call | flops 10066329 | bytes 62260 | tf_op jit(solution)/shard_map/own_forward/pallas_call | solution.py:764
  83.1 9.1 %collective-permute-done.12.refs_10_ = bf16[192,768]{1,0:T(8,128)(2,1)S(1)} collective-permute-done((bf16[192,768]{1,0:T(8,128)(2,1)S(1)}, bf16[192,768]{1,0:T(8,128)(2,1)S(1)}, u32[]{:S(2)}, u32[]{:S(2)}) %collective-permute-start.12) | collective-permute-done | bytes 294944 | tf_op jit(solution)/shard_map/ppermute | solution.py:25
  97.3 4.0 %collective-permute-start.17 = (bf16[128,768]{1,0:T(8,128)(2,1)S(1)}, bf16[128,768]{1,0:T(8,128)(2,1)S(1)}, u32[]{:S(2)}, u32[]{:S(2)}) collective-permute-start(bf16[128,768]{1,0:T(8,128)(2,1)S(1)} %add_convert_fusion.5), channel_id=1, source_target_pairs={{0,16},{8,24},{16,0},{24,8},{1,17},{9,25},{17,1},{25,9},{2,18},{10... | collective-permute-start | bytes 589832 | tf_op jit(solution)/shard_map/ppermute | solution.py:25
  101.7 10.9 %collective-permute-start.23 = (bf16[128,768]{1,0:T(8,128)(2,1)S(1)}, bf16[128,768]{1,0:T(8,128)(2,1)S(1)}, u32[]{:S(2)}, u32[]{:S(2)}) collective-permute-start(bf16[128,768]{1,0:T(8,128)(2,1)S(1)} %collective-permute-done.21.refs_4_.refs_5_), channel_id=1, source_target_pairs={{0,16},{8,24},{16,0},{24,8},{1,17},{9,25},{17,1},{25,9},{2,18},{10... | collective-permute-start | bytes 589832 | tf_op jit(solution)/shard_map/ppermute | solution.py:25
  114.2 2.7 %collective-permute-done.23.refs_6_ = bf16[128,768]{1,0:T(8,128)(2,1)S(1)} collective-permute-done((bf16[128,768]{1,0:T(8,128)(2,1)S(1)}, bf16[128,768]{1,0:T(8,128)(2,1)S(1)}, u32[]{:S(2)}, u32[]{:S(2)}) %collective-permute-start.23) | collective-permute-done | bytes 196640 | tf_op jit(solution)/shard_map/ppermute | solution.py:25
  120.7 4.8 %feed_kernel.1 = (f32[256,768]{1,0:T(8,128)S(1)}, bf16[256,768]{1,0:T(8,128)(2,1)S(1)}, bf16[512,768]{1,0:T(8,128)(2,1)S(1)}, bf16[512,768]{1,0:T(8,128)(2,1)S(1...) custom-call(s32[6]{0:T(128)S(1)} %stack.33.meta_ref.place_ref, ...), custom_call_target="tpu_custom_call" | custom-call | flops 90596968 | bytes 473242 | tf_op jit(solution)/shard_map/feed_kernel/pallas_call | solution.py:764
  125.7 3.8 %feed_grad_kernel.1 = (f32[4,192,768]{2,1,0:T(8,128)S(1)}, bf16[4,192,768]{2,1,0:T(8,128)(2,1)S(1)}, f32[256,768]{1,0:T(8,128)S(1)}, bf16[256,768]{1,0:T(8,128)(2,1)S(1)}) custom-call(s32[6]{0:T(128)S(1)} %stack.33.meta_ref.place_ref, bf16[512,768]{1,0:T(8,128)(2,1)S(1)} %get-tuple-element.129.refs_0_, bf16[512,768]{1,0:T(8,128)(2,1)S(1)} %get-tuple-element.130.refs_1_, ...), custom_call_target="tpu_custom_call" | custom-call | flops 90596968 | bytes 452199 | tf_op jit(solution)/shard_map/feed_grad_kernel/pallas_call | solution.py:764
  131.9 5.1 %collective-permute-done.28.refs_2_ = bf16[128,768]{1,0:T(8,128)(2,1)S(1)} collective-permute-done((bf16[128,768]{1,0:T(8,128)(2,1)S(1)}, bf16[128,768]{1,0:T(8,128)(2,1)S(1)}, u32[]{:S(2)}, u32[]{:S(2)}) %collective-permute-start.28) | collective-permute-done | bytes 196640 | tf_op jit(solution)/shard_map/ppermute | solution.py:25
  139.9 4.3 %collective-permute-done.29.refs_2_ = bf16[128,768]{1,0:T(8,128)(2,1)S(1)} collective-permute-done((bf16[128,768]{1,0:T(8,128)(2,1)S(1)}, bf16[128,768]{1,0:T(8,128)(2,1)S(1)}, u32[]{:S(2)}, u32[]{:S(2)}) %collective-permute-start.29) | collective-permute-done | bytes 196640 | tf_op jit(solution)/shard_map/ppermute | solution.py:25
  148.6 7.6 %collective-permute-start.36 = (bf16[512,384]{1,0:T(8,128)(2,1)S(1)}, bf16[512,384]{1,0:T(8,128)(2,1)S(1)}, u32[]{:S(2)}, u32[]{:S(2)}) collective-permute-start(bf16[512,384]{1,0:T(8,128)(2,1)S(1)} %bitcast.43), channel_id=1, source_target_pairs={{0,4},{4,0},{1,5},{5,1},{2,6},{6,2},{3,7},{7,3},{8,12},{12,8},{9,1... | collective-permute-start | bytes 1179656 | tf_op jit(solution)/shard_map/ppermute | solution.py:30
  159.0 3.1 %collective-permute-start.35 = (bf16[192,768]{1,0:T(8,128)(2,1)S(1)}, bf16[192,768]{1,0:T(8,128)(2,1)S(1)}, u32[]{:S(2)}, u32[]{:S(2)}) collective-permute-start(bf16[192,768]{1,0:T(8,128)(2,1)S(1)} %get-tuple-element.155), channel_id=1, source_target_pairs={{0,3},{1,2},{2,1},{3,0},{4,7},{5,6},{6,5},{7,4},{8,11},{9,10},{10,... | collective-permute-start | bytes 884744 | tf_op jit(solution)/shard_map/ppermute | solution.py:25
  163.2 6.8 %own_grad_kernel.1 = (f32[512,576]{1,0:T(8,128)S(1)}, f32[192,768]{1,0:T(8,128)S(1)}) custom-call(s32[6]{0:T(128)S(1)} %stack.33.meta_ref.place_ref, bf16[512,576]{1,0:T(8,128)(2,1)S(1)} %get-tuple-element.113.kvq_ref.refs_5_.refs_0_, bf16[512,192]{1,0:T(8,128)(2,1)S(1)} %get-tuple-element.146.refs_1_, f32[512,192]{1,0:T(8,128)S(1)} %get-tuple-element.144.refs_7_.refs_2_, ...), custom_call_target="tpu_custom_call" | custom-call | flops 25165824 | bytes 229377 | tf_op jit(solution)/shard_map/own_grad_kernel/pallas_call | solution.py:764
  178.3 5.9 %collective-permute-start.38 = (bf16[192,768]{1,0:T(8,128)(2,1)}, bf16[192,768]{1,0:T(8,128)(2,1)S(1)}, u32[]{:S(2)}, u32[]{:S(2)}) collective-permute-start(bf16[192,768]{1,0:T(8,128)(2,1)} %copy-done.12), channel_id=1, source_target_pairs={{0,1},{1,0},{2,3},{3,2},{4,5},{5,4},{6,7},{7,6},{8,9},{9,8},{10,11... | collective-permute-start | bytes 884744 | tf_op jit(solution)/shard_map/ppermute | solution.py:25
  185.4 12.0 %collective-permute-done.38 = bf16[192,768]{1,0:T(8,128)(2,1)S(1)} collective-permute-done((bf16[192,768]{1,0:T(8,128)(2,1)}, bf16[192,768]{1,0:T(8,128)(2,1)S(1)}, u32[]{:S(2)}, u32[]{:S(2)}) %collective-permute-start.38) | collective-permute-done | bytes 294944 | tf_op jit(solution)/shard_map/ppermute | solution.py:25
  197.4 2.7 %collective-permute-done.39 = bf16[192,768]{1,0:T(8,128)(2,1)S(1)} collective-permute-done((bf16[192,768]{1,0:T(8,128)(2,1)}, bf16[192,768]{1,0:T(8,128)(2,1)S(1)}, u32[]{:S(2)}, u32[]{:S(2)}) %collective-permute-start.39) | collective-permute-done | bytes 294944 | tf_op jit(solution)/shard_map/ppermute | solution.py:25
  205.9 2.3 collective-permute-start.44
  212.0 3.6 %collective-permute-done.44 = bf16[144,576]{1,0:T(8,128)(2,1)S(1)} collective-permute-done((bf16[144,576]{1,0:T(8,128)(2,1)}, bf16[144,576]{1,0:T(8,128)(2,1)S(1)}, u32[]{:S(2)}, u32[]{:S(2)}) %collective-permute-start.44) | collective-permute-done | bytes 165920 | tf_op jit(solution)/shard_map/ppermute | solution.py:25
  215.6 11.8 %collective-permute-done.43 = bf16[144,576]{1,0:T(8,128)(2,1)S(1)} collective-permute-done((bf16[144,576]{1,0:T(8,128)(2,1)}, bf16[144,576]{1,0:T(8,128)(2,1)S(1)}, u32[]{:S(2)}, u32[]{:S(2)}) %collective-permute-start.43) | collective-permute-done | bytes 165920 | tf_op jit(solution)/shard_map/ppermute | solution.py:25
  231.0 4.1 %collective-permute-done.46.arrived = bf16[144,576]{1,0:T(8,128)(2,1)S(1)} collective-permute-done((bf16[144,576]{1,0:T(8,128)(2,1)S(1)}, bf16[144,576]{1,0:T(8,128)(2,1)S(1)}, u32[]{:S(2)}, u32[]{:S(2)}) %collective-permute-start.46) | collective-permute-done | bytes 165920 | tf_op jit(solution)/shard_map/ppermute | solution.py:30
  236.6 3.8 %collective-permute-done.48.refs_1_ = bf16[192,768]{1,0:T(8,128)(2,1)S(1)} collective-permute-done((bf16[192,768]{1,0:T(8,128)(2,1)S(1)}, bf16[192,768]{1,0:T(8,128)(2,1)S(1)}, u32[]{:S(2)}, u32[]{:S(2)}) %collective-permute-start.48) | collective-permute-done | bytes 294944 | tf_op jit(solution)/shard_map/ppermute | solution.py:30
  246.2 3.8 %collective-permute-done.50.refs_2_ = bf16[64,1408]{1,0:T(8,128)(2,1)S(1)} collective-permute-done((bf16[64,1408]{1,0:T(8,128)(2,1)S(1)}, bf16[64,1408]{1,0:T(8,128)(2,1)S(1)}, u32[]{:S(2)}, u32[]{:S(2)}) %collective-permute-start.50) | collective-permute-done | bytes 180256 | tf_op jit(solution)/shard_map/ppermute | solution.py:25
  250.0 3.6 %collective-permute-done.51.refs_3_ = bf16[64,1408]{1,0:T(8,128)(2,1)S(1)} collective-permute-done((bf16[64,1408]{1,0:T(8,128)(2,1)S(1)}, bf16[64,1408]{1,0:T(8,128)(2,1)S(1)}, u32[]{:S(2)}, u32[]{:S(2)}) %collective-permute-start.51) | collective-permute-done | bytes 180256 | tf_op jit(solution)/shard_map/ppermute | solution.py:25
  (165 shorter events, 74.0 us)
Async XLA Ops:
  5.0 7.0 %collective-permute-start.1 = (bf16[48,1408]{1,0:T(8,128)(2,1)S(1)}, bf16[48,1408]{1,0:T(8,128)(2,1)S(1)}, u32[]{:S(2)}, u32[]{:S(2)}) collective-permute-start(bf16[48,1408]{1,0:T(8,128)(2,1)S(1)} %get-tuple-element.106), channel_id=1, source_target_pairs={{0,16},{8,24},{16,0},{24,8},{1,17},{9,25},{17,1},{25,9},{2,18},{10... | collective-permute-start | bytes 405512 | tf_op jit(solution)/shard_map/ppermute | solution.py:25
  16.3 13.4 %collective-permute-start.4 = (bf16[272,576]{1,0:T(8,128)(2,1)S(1)}, bf16[272,576]{1,0:T(8,128)(2,1)S(1)}, u32[]{:S(2)}, u32[]{:S(2)}) collective-permute-start(bf16[272,576]{1,0:T(8,128)(2,1)S(1)} %get-tuple-element.110.refs_4_.refs_1_), channel_id=1, source_target_pairs={{0,1},{1,0},{2,3},{3,2},{4,5},{5,4},{6,7},{7,6},{8,9},{9,8},{10,11... | collective-permute-start | bytes 940040 | tf_op jit(solution)/shard_map/ppermute | solution.py:25
  18.7 37.5 %collective-permute-start.7 = (bf16[272,576]{1,0:T(8,128)(2,1)S(1)}, bf16[272,576]{1,0:T(8,128)(2,1)S(1)}, u32[]{:S(2)}, u32[]{:S(2)}) collective-permute-start(bf16[272,576]{1,0:T(8,128)(2,1)S(1)} %get-tuple-element.110.refs_4_.refs_1_), channel_id=1, source_target_pairs={{0,2},{1,3},{2,0},{3,1},{4,6},{5,7},{6,4},{7,5},{8,10},{9,11},{10,... | collective-permute-start | bytes 940040 | tf_op jit(solution)/shard_map/ppermute | solution.py:25
  23.9 32.4 %collective-permute-start.8 = (bf16[272,576]{1,0:T(8,128)(2,1)S(1)}, bf16[272,576]{1,0:T(8,128)(2,1)S(1)}, u32[]{:S(2)}, u32[]{:S(2)}) collective-permute-start(bf16[272,576]{1,0:T(8,128)(2,1)S(1)} %get-tuple-element.110.refs_4_.refs_1_), channel_id=1, source_target_pairs={{0,3},{1,2},{2,1},{3,0},{4,7},{5,6},{6,5},{7,4},{8,11},{9,10},{10,... | collective-permute-start | bytes 940040 | tf_op jit(solution)/shard_map/ppermute | solution.py:25
  29.7 26.6 %collective-permute-start.6 = (bf16[128,768]{1,0:T(8,128)(2,1)S(1)}, bf16[128,768]{1,0:T(8,128)(2,1)S(1)}, u32[]{:S(2)}, u32[]{:S(2)}) collective-permute-start(bf16[128,768]{1,0:T(8,128)(2,1)S(1)} %collective-permute-done.3.refs_0_.refs_3_), channel_id=1, source_target_pairs={{0,16},{8,24},{16,0},{24,8},{1,17},{9,25},{17,1},{25,9},{2,18},{10... | collective-permute-start | bytes 589832 | tf_op jit(solution)/shard_map/ppermute | solution.py:25
  60.7 19.7 %collective-permute-start.10 = (bf16[512,384]{1,0:T(8,128)(2,1)S(1)}, bf16[512,384]{1,0:T(8,128)(2,1)S(1)}, u32[]{:S(2)}, u32[]{:S(2)}) collective-permute-start(bf16[512,384]{1,0:T(8,128)(2,1)S(1)} %get-tuple-element.114), channel_id=1, source_target_pairs={{0,4},{4,0},{1,5},{5,1},{2,6},{6,2},{3,7},{7,3},{8,12},{12,8},{9,1... | collective-permute-start | bytes 1179656 | tf_op jit(solution)/shard_map/ppermute | solution.py:30
  62.3 17.6 %collective-permute-start.11 = (bf16[192,768]{1,0:T(8,128)(2,1)S(1)}, bf16[192,768]{1,0:T(8,128)(2,1)S(1)}, u32[]{:S(2)}, u32[]{:S(2)}) collective-permute-start(bf16[192,768]{1,0:T(8,128)(2,1)S(1)} %get-tuple-element.121.refs_8_), channel_id=1, source_target_pairs={{0,1},{1,0},{2,3},{3,2},{4,5},{5,4},{6,7},{7,6},{8,9},{9,8},{10,11... | collective-permute-start | bytes 884744 | tf_op jit(solution)/shard_map/ppermute | solution.py:25
  68.7 23.5 %collective-permute-start.12 = (bf16[192,768]{1,0:T(8,128)(2,1)S(1)}, bf16[192,768]{1,0:T(8,128)(2,1)S(1)}, u32[]{:S(2)}, u32[]{:S(2)}) collective-permute-start(bf16[192,768]{1,0:T(8,128)(2,1)S(1)} %get-tuple-element.121.refs_8_), channel_id=1, source_target_pairs={{0,2},{1,3},{2,0},{3,1},{4,6},{5,7},{6,4},{7,5},{8,10},{9,11},{10,... | collective-permute-start | bytes 884744 | tf_op jit(solution)/shard_map/ppermute | solution.py:25
  68.7 23.5 %collective-permute-start.13 = (bf16[192,768]{1,0:T(8,128)(2,1)S(1)}, bf16[192,768]{1,0:T(8,128)(2,1)S(1)}, u32[]{:S(2)}, u32[]{:S(2)}) collective-permute-start(bf16[192,768]{1,0:T(8,128)(2,1)S(1)} %get-tuple-element.121.refs_8_), channel_id=1, source_target_pairs={{0,3},{1,2},{2,1},{3,0},{4,7},{5,6},{6,5},{7,4},{8,11},{9,10},{10,... | collective-permute-start | bytes 884744 | tf_op jit(solution)/shard_map/ppermute | solution.py:25
  79.9 12.3 %collective-permute-start.15 = (bf16[192,768]{1,0:T(8,128)(2,1)S(1)}, bf16[192,768]{1,0:T(8,128)(2,1)S(1)}, u32[]{:S(2)}, u32[]{:S(2)}) collective-permute-start(bf16[192,768]{1,0:T(8,128)(2,1)S(1)} %collective-permute-done.11.refs_9_), channel_id=1, source_target_pairs={{0,4},{4,0},{1,5},{5,1},{2,6},{6,2},{3,7},{7,3},{8,12},{12,8},{9,1... | collective-permute-start | bytes 884744 | tf_op jit(solution)/shard_map/ppermute | solution.py:30
  80.4 14.1 %collective-permute-start.14 = (bf16[192,768]{1,0:T(8,128)(2,1)S(1)}, bf16[192,768]{1,0:T(8,128)(2,1)S(1)}, u32[]{:S(2)}, u32[]{:S(2)}) collective-permute-start(bf16[192,768]{1,0:T(8,128)(2,1)S(1)} %get-tuple-element.121.refs_8_), channel_id=1, source_target_pairs={{0,4},{4,0},{1,5},{5,1},{2,6},{6,2},{3,7},{7,3},{8,12},{12,8},{9,1... | collective-permute-start | bytes 884744 | tf_op jit(solution)/shard_map/ppermute | solution.py:30
  97.3 15.4 %collective-permute-start.17 = (bf16[128,768]{1,0:T(8,128)(2,1)S(1)}, bf16[128,768]{1,0:T(8,128)(2,1)S(1)}, u32[]{:S(2)}, u32[]{:S(2)}) collective-permute-start(bf16[128,768]{1,0:T(8,128)(2,1)S(1)} %add_convert_fusion.5), channel_id=1, source_target_pairs={{0,16},{8,24},{16,0},{24,8},{1,17},{9,25},{17,1},{25,9},{2,18},{10... | collective-permute-start | bytes 589832 | tf_op jit(solution)/shard_map/ppermute | solution.py:25
  101.3 15.5 %collective-permute-start.25 = (bf16[192,768]{1,0:T(8,128)(2,1)S(1)}, bf16[192,768]{1,0:T(8,128)(2,1)S(1)}, u32[]{:S(2)}, u32[]{:S(2)}) collective-permute-start(bf16[192,768]{1,0:T(8,128)(2,1)S(1)} %collective-permute-done.12.refs_10_), channel_id=1, source_target_pairs={{0,4},{4,0},{1,5},{5,1},{2,6},{6,2},{3,7},{7,3},{8,12},{12,8},{9,1... | collective-permute-start | bytes 884744 | tf_op jit(solution)/shard_map/ppermute | solution.py:30
  101.7 15.1 %collective-permute-start.23 = (bf16[128,768]{1,0:T(8,128)(2,1)S(1)}, bf16[128,768]{1,0:T(8,128)(2,1)S(1)}, u32[]{:S(2)}, u32[]{:S(2)}) collective-permute-start(bf16[128,768]{1,0:T(8,128)(2,1)S(1)} %collective-permute-done.21.refs_4_.refs_5_), channel_id=1, source_target_pairs={{0,16},{8,24},{16,0},{24,8},{1,17},{9,25},{17,1},{25,9},{2,18},{10... | collective-permute-start | bytes 589832 | tf_op jit(solution)/shard_map/ppermute | solution.py:25
  129.5 28.8 %collective-permute-start.34 = (bf16[4,192,768]{2,1,0:T(8,128)(2,1)S(1)}, bf16[4,192,768]{2,1,0:T(8,128)(2,1)S(1)}, u32[]{:S(2)}, u32[]{:S(2)}) collective-permute-start(bf16[4,192,768]{2,1,0:T(8,128)(2,1)S(1)} %get-tuple-element.150), channel_id=1, source_target_pairs={{0,4},{4,0},{1,5},{5,1},{2,6},{6,2},{3,7},{7,3},{8,12},{12,8},{9,1... | collective-permute-start | bytes 3538952 | tf_op jit(solution)/shard_map/ppermute | solution.py:30
  145.7 16.4 %collective-permute-start.31 = (bf16[256,768]{1,0:T(8,128)(2,1)S(1)}, bf16[256,768]{1,0:T(8,128)(2,1)S(1)}, u32[]{:S(2)}, u32[]{:S(2)}) collective-permute-start(bf16[256,768]{1,0:T(8,128)(2,1)S(1)} %get-tuple-element.141), channel_id=1, source_target_pairs={{0,8},{8,0},{16,24},{24,16},{1,9},{9,1},{17,25},{25,17},{2,10},{10... | collective-permute-start | bytes 1179656 | tf_op jit(solution)/shard_map/ppermute | solution.py:25
  148.6 21.4 %collective-permute-start.36 = (bf16[512,384]{1,0:T(8,128)(2,1)S(1)}, bf16[512,384]{1,0:T(8,128)(2,1)S(1)}, u32[]{:S(2)}, u32[]{:S(2)}) collective-permute-start(bf16[512,384]{1,0:T(8,128)(2,1)S(1)} %bitcast.43), channel_id=1, source_target_pairs={{0,4},{4,0},{1,5},{5,1},{2,6},{6,2},{3,7},{7,3},{8,12},{12,8},{9,1... | collective-permute-start | bytes 1179656 | tf_op jit(solution)/shard_map/ppermute | solution.py:30
  159.0 11.0 %collective-permute-start.35 = (bf16[192,768]{1,0:T(8,128)(2,1)S(1)}, bf16[192,768]{1,0:T(8,128)(2,1)S(1)}, u32[]{:S(2)}, u32[]{:S(2)}) collective-permute-start(bf16[192,768]{1,0:T(8,128)(2,1)S(1)} %get-tuple-element.155), channel_id=1, source_target_pairs={{0,3},{1,2},{2,1},{3,0},{4,7},{5,6},{6,5},{7,4},{8,11},{9,10},{10,... | collective-permute-start | bytes 884744 | tf_op jit(solution)/shard_map/ppermute | solution.py:25
  162.1 7.9 %collective-permute-start.32 = (bf16[128,768]{1,0:T(8,128)(2,1)S(1)}, bf16[128,768]{1,0:T(8,128)(2,1)S(1)}, u32[]{:S(2)}, u32[]{:S(2)}) collective-permute-start(bf16[128,768]{1,0:T(8,128)(2,1)S(1)} %add_convert_fusion.3), channel_id=1, source_target_pairs={{0,16},{8,24},{16,0},{24,8},{1,17},{9,25},{17,1},{25,9},{2,18},{10... | collective-permute-start | bytes 589832 | tf_op jit(solution)/shard_map/ppermute | solution.py:25
  178.2 24.9 %collective-permute-start.40 = (bf16[4,128,576]{1,2,0:T(8,128)(2,1)}, bf16[4,128,576]{1,2,0:T(8,128)(2,1)}, u32[]{:S(2)}, u32[]{:S(2)}) collective-permute-start(bf16[4,128,576]{1,2,0:T(8,128)(2,1)} %copy.30), channel_id=1, source_target_pairs={{0,4},{4,0},{1,5},{5,1},{2,6},{6,2},{3,7},{7,3},{8,12},{12,8},{9,1... | collective-permute-start | bytes 1769480 | tf_op jit(solution)/shard_map/ppermute | solution.py:30
  178.3 19.1 %collective-permute-start.38 = (bf16[192,768]{1,0:T(8,128)(2,1)}, bf16[192,768]{1,0:T(8,128)(2,1)S(1)}, u32[]{:S(2)}, u32[]{:S(2)}) collective-permute-start(bf16[192,768]{1,0:T(8,128)(2,1)} %copy-done.12), channel_id=1, source_target_pairs={{0,1},{1,0},{2,3},{3,2},{4,5},{5,4},{6,7},{7,6},{8,9},{9,8},{10,11... | collective-permute-start | bytes 884744 | tf_op jit(solution)/shard_map/ppermute | solution.py:25
  184.2 16.0 %collective-permute-start.39 = (bf16[192,768]{1,0:T(8,128)(2,1)}, bf16[192,768]{1,0:T(8,128)(2,1)S(1)}, u32[]{:S(2)}, u32[]{:S(2)}) collective-permute-start(bf16[192,768]{1,0:T(8,128)(2,1)} %copy-done.11), channel_id=1, source_target_pairs={{0,2},{1,3},{2,0},{3,1},{4,6},{5,7},{6,4},{7,5},{8,10},{9,11},{10,... | collective-permute-start | bytes 884744 | tf_op jit(solution)/shard_map/ppermute | solution.py:25
  185.0 15.1 %collective-permute-start.41 = (bf16[128,768]{1,0:T(8,128)(2,1)S(1)}, bf16[128,768]{1,0:T(8,128)(2,1)S(1)}, u32[]{:S(2)}, u32[]{:S(2)}) collective-permute-start(bf16[128,768]{1,0:T(8,128)(2,1)S(1)} %add_convert_fusion.1), channel_id=1, source_target_pairs={{0,16},{8,24},{16,0},{24,8},{1,17},{9,25},{17,1},{25,9},{2,18},{10... | collective-permute-start | bytes 589832 | tf_op jit(solution)/shard_map/ppermute | solution.py:25
  205.9 9.7 %collective-permute-start.44 = (bf16[144,576]{1,0:T(8,128)(2,1)}, bf16[144,576]{1,0:T(8,128)(2,1)S(1)}, u32[]{:S(2)}, u32[]{:S(2)}) collective-permute-start(bf16[144,576]{1,0:T(8,128)(2,1)} %get-tuple-element.180), channel_id=1, source_target_pairs={{0,3},{1,2},{2,1},{3,0},{4,7},{5,6},{6,5},{7,4},{8,11},{9,10},{10,... | collective-permute-start | bytes 497672 | tf_op jit(solution)/shard_map/ppermute | solution.py:25
  208.3 19.1 %collective-permute-start.43 = (bf16[144,576]{1,0:T(8,128)(2,1)}, bf16[144,576]{1,0:T(8,128)(2,1)S(1)}, u32[]{:S(2)}, u32[]{:S(2)}) collective-permute-start(bf16[144,576]{1,0:T(8,128)(2,1)} %get-tuple-element.179), channel_id=1, source_target_pairs={{0,2},{1,3},{2,0},{3,1},{4,6},{5,7},{6,4},{7,5},{8,10},{9,11},{10,... | collective-permute-start | bytes 497672 | tf_op jit(solution)/shard_map/ppermute | solution.py:25
  208.3 19.1 %collective-permute-start.42 = (bf16[144,576]{1,0:T(8,128)(2,1)S(1)}, bf16[144,576]{1,0:T(8,128)(2,1)S(1)}, u32[]{:S(2)}, u32[]{:S(2)}) collective-permute-start(bf16[144,576]{1,0:T(8,128)(2,1)S(1)} %get-tuple-element.178), channel_id=1, source_target_pairs={{0,1},{1,0},{2,3},{3,2},{4,5},{5,4},{6,7},{7,6},{8,9},{9,8},{10,11... | collective-permute-start | bytes 497672 | tf_op jit(solution)/shard_map/ppermute | solution.py:25
  210.4 17.1 %collective-permute-start.45 = (bf16[128,768]{1,0:T(8,128)(2,1)}, bf16[128,768]{1,0:T(8,128)(2,1)S(1)}, u32[]{:S(2)}, u32[]{:S(2)}) collective-permute-start(bf16[128,768]{1,0:T(8,128)(2,1)} %copy-done.13), channel_id=1, source_target_pairs={{0,0},{1,8},{2,16},{3,24},{8,1},{9,9},{10,17},{11,25},{16,2},{17,1... | collective-permute-start | bytes 589832 | tf_op jit(solution)/shard_map/ppermute | solution.py:36
  227.5 7.6 %collective-permute-start.46 = (bf16[144,576]{1,0:T(8,128)(2,1)S(1)}, bf16[144,576]{1,0:T(8,128)(2,1)S(1)}, u32[]{:S(2)}, u32[]{:S(2)}) collective-permute-start(bf16[144,576]{1,0:T(8,128)(2,1)S(1)} %add_convert_fusion.6.mine), channel_id=1, source_target_pairs={{0,4},{4,0},{1,5},{5,1},{2,6},{6,2},{3,7},{7,3},{8,12},{12,8},{9,1... | collective-permute-start | bytes 497672 | tf_op jit(solution)/shard_map/ppermute | solution.py:30
  230.3 10.1 %collective-permute-start.48 = (bf16[192,768]{1,0:T(8,128)(2,1)S(1)}, bf16[192,768]{1,0:T(8,128)(2,1)S(1)}, u32[]{:S(2)}, u32[]{:S(2)}) collective-permute-start(bf16[192,768]{1,0:T(8,128)(2,1)S(1)} %add_convert_fusion.refs_0_), channel_id=1, source_target_pairs={{0,4},{4,0},{1,5},{5,1},{2,6},{6,2},{3,7},{7,3},{8,12},{12,8},{9,1... | collective-permute-start | bytes 884744 | tf_op jit(solution)/shard_map/ppermute | solution.py:30
  235.1 10.3 %collective-permute-start.47 = (bf16[128,768]{1,0:T(8,128)(2,1)S(1)}, bf16[128,768]{1,0:T(8,128)(2,1)S(1)}, u32[]{:S(2)}, u32[]{:S(2)}) collective-permute-start(bf16[128,768]{1,0:T(8,128)(2,1)S(1)} %add_convert_fusion.2), channel_id=1, source_target_pairs={{0,0},{1,8},{2,16},{3,24},{8,1},{9,9},{10,17},{11,25},{16,2},{17,1... | collective-permute-start | bytes 589832 | tf_op jit(solution)/shard_map/ppermute | solution.py:36
  241.9 8.1 %collective-permute-start.50 = (bf16[64,1408]{1,0:T(8,128)(2,1)S(1)}, bf16[64,1408]{1,0:T(8,128)(2,1)S(1)}, u32[]{:S(2)}, u32[]{:S(2)}) collective-permute-start(bf16[64,1408]{1,0:T(8,128)(2,1)S(1)} %get-tuple-element.187), channel_id=1, source_target_pairs={{0,16},{8,24},{16,0},{24,8},{1,17},{9,25},{17,1},{25,9},{2,18},{10... | collective-permute-start | bytes 540680 | tf_op jit(solution)/shard_map/ppermute | solution.py:25
  244.0 9.6 %collective-permute-start.51 = (bf16[64,1408]{1,0:T(8,128)(2,1)S(1)}, bf16[64,1408]{1,0:T(8,128)(2,1)S(1)}, u32[]{:S(2)}, u32[]{:S(2)}) collective-permute-start(bf16[64,1408]{1,0:T(8,128)(2,1)S(1)} %get-tuple-element.188), channel_id=1, source_target_pairs={{0,24},{8,16},{16,8},{24,0},{1,25},{9,17},{17,9},{25,1},{2,26},{10... | collective-permute-start | bytes 540680 | tf_op jit(solution)/shard_map/ppermute | solution.py:25
  (47 other events, 312.4 us)

commit v10 on v9

--- a/solution.py
+++ b/solution.py
@@ -347,10 +347,10 @@
 
 
 def stack_kernel(parts, depth, halves, meta_ref, *refs):
-    split, down_weight, out_weight, kvq_rows, feeds, vectors = take(
-        refs, parts, None, None, None, 1 if halves else 2, None
-    )
-    columns = kvq_rows.shape[1]
+    split, down_weight, out_weight, kvq_own, kvq_other, feed_own, feed_other, vectors, folded = (
+        take(refs, parts, *([None] * 8))
+    )
+    columns = kvq_own.shape[1]
     shard = split[0].shape[0]
     model = vectors.shape[1]
     width = columns // 3
@@ -358,7 +358,7 @@
     member = meta_ref[parts + 1]
 
     def placed(slot, start):
-        rows = split[slot][:, columns : -feeds[0].shape[1]]
+        rows = split[slot][:, columns : -feed_own.shape[1]]
         row = lax.broadcasted_iota(jnp.int32, (rows.shape[1], model), 0)
         column = lax.broadcasted_iota(jnp.int32, (rows.shape[1], model), 1)
         chosen = jnp.where((column == start + row) & (row < shard), 1.0, 0.0)
@@ -374,31 +374,39 @@
         placed(0, member * hidden_shard + at * shard)[8 + at : 9 + at]
         for at in range(hidden_shard // shard)
     )
-    for slot in range(parts):
-        kvq_rows[slot * shard : (slot + 1) * shard, :] = split[slot][:, :columns]
     vectors[8:16, : model - columns] = vectors[0:8, columns:]
-    first = parts * shard + 16
-    kvq_rows[parts * shard : first, :] = vectors[:, :columns].astype(LOW)
-    kvq_rows[first : first + shard, :] = out_weight[:, :columns].astype(LOW)
     rest = model - columns
+    folded[:shard, :] = out_weight[:, :columns]
     for at in range(columns // rest):
-        kvq_rows[first + shard :, at * rest : (at + 1) * rest] = out_weight[
-            at * 16 : (at + 1) * 16, columns:
-        ].astype(LOW)
-
-    def up(out):
-        for slot in range(parts):
-            out[slot * shard : (slot + 1) * shard, :] = split[slot][:, -out.shape[1] :]
-
-    def down(out):
-        out[...] = down_weight[...].astype(LOW)
+        folded[shard:, at * rest : (at + 1) * rest] = out_weight[at * 16 : (at + 1) * 16, columns:]
+    slots = parts // 2
+    extra = folded.shape[0] // 2
+
+    def kvq(half, out):
+        for slot in range(slots):
+            out[slot * shard : (slot + 1) * shard, :] = split[half * slots + slot][:, :columns]
+        start = slots * shard
+        out[start : start + extra, :] = folded[half * extra : (half + 1) * extra, :].astype(LOW)
+        out[start + extra :, :] = vectors[:, :columns].astype(LOW)
+
+    def feed(half, out):
+        if half:
+            out[...] = down_weight[...].astype(LOW)
+        else:
+            for slot in range(parts):
+                out[slot * shard : (slot + 1) * shard, :] = split[slot][:, -out.shape[1] :]
+
+    def emit(first):
+        kvq(first, kvq_own)
+        kvq(1 - first, kvq_other)
+        feed(first, feed_own)
+        feed(1 - first, feed_other)
 
     if halves:
-        pl.when(meta_ref[parts] == 0)(lambda: up(feeds[0]))
-        pl.when(meta_ref[parts] != 0)(lambda: down(feeds[0]))
+        pl.when(meta_ref[parts] == 0)(lambda: emit(0))
+        pl.when(meta_ref[parts] != 0)(lambda: emit(1))
     else:
-        up(feeds[0])
-        down(feeds[1])
+        emit(0)
 
 
 def split_kernel(parts, width, meta_ref, qkv_ref, up_ref, *refs):
@@ -448,19 +456,35 @@
     vectors[...] = sum(piece[shard:, : vectors.shape[1]].astype(WIDE) for piece in pieces)
 
 
-def project_kernel(parts, depth, meta_ref, *refs):
-    tokens, weight, kvq_ref, kv_ref, matrix_ref, norm_ref, vectors_ref = take(
-        refs, parts, depth, None, None, None, None, None
+def in_order(halves, parts, meta_ref, place, own, other):
+    if halves:
+        pl.when(meta_ref[parts] == 0)(lambda: place(own, other))
+        pl.when(meta_ref[parts] != 0)(lambda: place(other, own))
+    else:
+        place(own, other)
+
+
+def project_kernel(parts, depth, halves, meta_ref, *refs):
+    tokens, own, other, kvq_ref, kv_ref, matrix_ref, norm_ref, vectors_ref = take(
+        refs, parts, depth, depth, None, None, None, None, None
     )
     columns = kvq_ref.shape[1]
     rows = tokens[0].shape[0]
     shard = matrix_ref.shape[0] // (parts * depth)
-    for deep in range(depth):
-        member = meta_ref[parts + 1] ^ deep
-        for slot in range(parts):
-            start = pl.multiple_of((meta_ref[slot] * depth + member) * shard, 16)
-            matrix_ref[pl.ds(start, shard), :] = weight[deep][slot * shard : (slot + 1) * shard, :]
-    folded = sum(piece[parts * shard : parts * shard + 16, :].astype(WIDE) for piece in weight)
+    slots = parts // 2
+
+    def place(*pair):
+        for half, pieces in enumerate(pair):
+            for deep in range(depth):
+                member = meta_ref[parts + 1] ^ deep
+                for slot in range(slots):
+                    row = (meta_ref[half * slots + slot] * depth + member) * shard
+                    matrix_ref[pl.ds(pl.multiple_of(row, 16), shard), :] = pieces[deep][
+                        slot * shard : (slot + 1) * shard, :
+                    ]
+
+    in_order(halves, parts, meta_ref, place, own, other)
+    folded = sum(piece[-16:, :].astype(WIDE) for piece in own)
     vectors_ref[:, :columns] = folded[:8]
     vectors_ref[:, columns:] = folded[8:, : vectors_ref.shape[1] - columns]
     for slot, piece in enumerate(tokens):
@@ -479,19 +503,28 @@
     kv_ref[...] = low[:, : kv_ref.shape[1]]
 
 
-def mix_kernel(parts, depth, meta_ref, *refs):
-    low, weight, matrix, keep, send = take(refs, None, depth, None, None, None)
+def mix_kernel(parts, depth, halves, meta_ref, *refs):
+    low, own, other, matrix, keep, send = take(refs, None, depth, depth, None, None, None)
     shard = matrix.shape[0] // depth
-    columns = weight[0].shape[1]
+    columns = own[0].shape[1]
     rest = matrix.shape[1] - columns
-    first = parts * shard + 16
-    for deep in range(depth):
-        start = pl.multiple_of((meta_ref[parts + 1] ^ deep) * shard, 16)
-        matrix[pl.ds(start, shard), :columns] = weight[deep][first : first + shard, :]
-        for at in range(columns // rest):
-            matrix[pl.ds(start + at * 16, 16), columns:] = weight[deep][
-                first + shard :, at * rest : (at + 1) * rest
+    at_first = parts // 2 * shard
+    extra = own[0].shape[0] - at_first - 16
+
+    def place(first, second):
+        for deep in range(depth):
+            start = pl.multiple_of((meta_ref[parts + 1] ^ deep) * shard, 16)
+            split = at_first + shard - extra
+            matrix[pl.ds(start, extra), :columns] = first[deep][at_first : at_first + extra, :]
+            matrix[pl.ds(start + extra, shard - extra), :columns] = second[deep][
+                at_first:split, :
             ]
+            for at in range(columns // rest):
+                matrix[pl.ds(start + at * 16, 16), columns:] = second[deep][
+                    split : split + 16, at * rest : (at + 1) * rest
+                ]
+
+    in_order(halves, parts, meta_ref, place, own, other)
     emit_rows(matmul_nn(low[...], matrix[...]), keep, send)
 
 
@@ -652,6 +685,7 @@
     slots = parts // 2
     extra = kept.shape[1] - slots * shard
     whole[...] = matmul_tn(norm[...], kvq_grad[...])
+    sent[:, kept.shape[1] :] = jnp.zeros_like(sent[:, kept.shape[1] :])
 
     def emit(half, out):
         for deep in range(depth):
@@ -666,7 +700,8 @@
             for at in range(columns // rest):
                 piece = out_grad[pl.ds(start + at * 16, 16), columns:]
                 folded[shard:, at * rest : (at + 1) * rest] = piece
-            out[deep, slots * shard :] = folded[half * extra : (half + 1) * extra, :].astype(
+            first = slots * shard
+            out[deep, first : first + extra] = folded[half * extra : (half + 1) * extra, :].astype(
                 out.dtype
             )
 
@@ -689,10 +724,10 @@
     sends, folded = refs[:-1], refs[-1]
     rows = kept.shape[1]
     fold_vectors(sums, folded)
-    keep[:rows, :] = kept[0] + arrived[0].astype(WIDE)
+    keep[:rows, :] = kept[0] + arrived[0, :rows].astype(WIDE)
     keep[rows:, :] = folded[...]
     for deep, send in enumerate(sends, 1):
-        send[:rows, :] = (kept[deep] + arrived[deep].astype(WIDE)).astype(LOW)
+        send[:rows, :] = (kept[deep] + arrived[deep, :rows].astype(WIDE)).astype(LOW)
         send[rows:, :] = folded[...].astype(LOW)
 
 
@@ -821,21 +856,26 @@
         [pltpu.VMEM((shard, padded - 3 * width), WIDE)],
     )
     split_arrived = send_pieces(split[1:], "dp")
-    kvq_rows, *feeds = local_call(
+    folded_rows = shard * model // (3 * width)
+    half_rows = parts // 2 * shard + folded_rows // 2 + 16
+    kvq_mine, kvq_theirs, feed_mine, feed_theirs = local_call(
         functools.partial(stack_kernel, parts, depth, halves),
         (meta, split[0], *split_arrived, fc2_weight, out_weight),
-        [low_like(parts * shard + 16 + shard * model // (3 * width), 3 * width)]
-        + [low_like(hidden_shard, model)] * (1 if halves else 2),
-        [pltpu.VMEM((16, model), WIDE)],
-    )
-    kvq_pieces = gather_direct(kvq_rows, "fsdp")
+        [low_like(half_rows, 3 * width)] * 2 + [low_like(hidden_shard, model)] * 2,
+        [pltpu.VMEM((16, model), WIDE), pltpu.VMEM((folded_rows, 3 * width), WIDE)],
+    )
+    kvq_own = gather_direct(kvq_mine, "fsdp")
+    if halves:
+        kvq_other = [kvq_theirs] + [shift(piece, "ctx", 1) for piece in kvq_own[1:]]
+    else:
+        kvq_other = gather_direct(kvq_theirs, "fsdp")
 
     token_rows = transpose_homes(after(tokens[0].astype(LOW), *split_arrived))
-    pieces = gather_pieces(after(token_rows, kvq_pieces[1]), *kvq_pieces[2:])
+    pieces = gather_pieces(after(token_rows, kvq_own[-1]), *kvq_own[1:])
 
     kvq, kv, kvq_matrix, norm1_all, vectors = local_call(
-        functools.partial(project_kernel, parts, depth),
-        (meta, *pieces, *kvq_pieces),
+        functools.partial(project_kernel, parts, depth, halves),
+        (meta, *pieces, *kvq_own, *kvq_other),
         [
             low_like(group, 3 * width),
             low_like(group, 2 * width),
@@ -848,10 +888,10 @@
     kv_earlier = jnp.stack([shift(kv, "ctx", by) for by in range(1, contexts)])
 
     if halves:
-        own_half = gather_direct(after(feeds[0], *kvq_pieces[1:]), "fsdp")
+        own_half = gather_direct(after(feed_mine, *kvq_own[1:]), "fsdp")
     else:
-        own_half = gather_direct(feeds[0], "fsdp")
-        other_half = gather_direct(feeds[1], "fsdp")
+        own_half = gather_direct(feed_mine, "fsdp")
+        other_half = gather_direct(feed_theirs, "fsdp")
     grad_rows = transpose_homes(after(cotangent[0].astype(LOW), own_half[1]))
     branch_pieces = gather_pieces(grad_rows)
 
@@ -860,14 +900,13 @@
     low_square = pltpu.VMEM((group, group), LOW)
     acc, stat = local_call(
         functools.partial(own_forward, heads, rows),
-        (meta, kvq),
+        (meta, after(kvq, own_half[1])),
         [wide_like(group, width), wide_like(group, 128)],
         [wide_square, low_square],
         flops=2 * score_flops,
     )
     if halves:
-        other_half = [shift(after(feeds[0], kv_earlier, acc), "ctx", 1)]
-        other_half.append(shift(after(own_half[1], acc), "ctx", 1))
+        other_half = [feed_theirs, shift(after(own_half[1], acc), "ctx", 1)]
         other_half += [shift(piece, "ctx", 1) for piece in own_half[2:]]
     context, context_low, stat = local_call(
         functools.partial(earlier_forward, heads, parts),
@@ -877,8 +916,8 @@
         flops=2 * score_flops,
     )
     out_matrix, attended_keep, attended_send = local_call(
-        functools.partial(mix_kernel, parts, depth),
-        (meta, after(context_low, *own_half[2:], *other_half[:2]), *kvq_pieces),
+        functools.partial(mix_kernel, parts, depth, halves),
+        (meta, after(context_low, *own_half[2:], other_half[1]), *kvq_own, *kvq_other),
         [low_like(width, model), wide_like(2 * rows, model), low_like(2 * rows, model)],
         flops=2 * group * width * model,
     )
@@ -998,7 +1037,7 @@
     kept_share, sent_share = local_call(
         functools.partial(projection_grad_kernel, parts, depth, halves),
         (meta, norm1_all, after(kvq_grad, norm1_sum[1]), out_grad),
-        [wide_like(depth, share_rows, 3 * width), low_like(depth, share_rows, 3 * width)],
+        [wide_like(depth, share_rows, 3 * width), low_like(depth, share_rows + 16, 3 * width)],
         [
             pltpu.VMEM((model, 3 * width), WIDE),
             pltpu.VMEM((shard * model // (3 * width), 3 * width), WIDE),
@@ -1024,7 +1063,7 @@
             [pltpu.VMEM((16, 3 * width), WIDE)],
         )
         share_pieces = send_pieces(share_sends, "fsdp")
-        mine_half = sum_all(after(half_keep, share_pieces[0]), half_pieces).astype(LOW)
+        mine_half = sum_all(after(half_keep, input_part), half_pieces).astype(LOW)
         feed_totals = (mine_half, shift(mine_half, "ctx", 1))
         mine_share = sum_all(share_keep, share_pieces).astype(LOW)
         shares = (mine_share, shift(after(mine_share, input_rows), "ctx", 1))
@@ -1032,8 +1071,11 @@
         share_pieces = []
         feed_totals = direct_totals(kept_half, sent_half[0])
         shares = (
-            *direct_totals(kept_share, sent_share), sum_replicas(sum_doubling(sums, "fsdp"))
+            *direct_totals(kept_share, sent_share[:, :share_rows]), sum_replicas(sum_doubling(sums, "fsdp"))
         )
+    delta = row_sum(*fed_sum) + vectors[5:6] + attended
+    delta_rows = transpose_homes(after(delta.astype(LOW), shares[1]))
+    output = tokens[0] + delta_rows.astype(WIDE)
     *totals, out_total, down_total, vector_part = local_call(
         functools.partial(unfold_kernel, parts, halves),
         (meta, *shares, *feed_totals),
@@ -1050,9 +1092,6 @@
             wide_like(16, 3 * width),
         ],
     )
-    delta = row_sum(*fed_sum) + vectors[5:6] + attended
-    delta = after(delta.astype(LOW), shares[1])
-    output = tokens[0] + transpose_homes(delta).astype(WIDE)
     input_grad = cotangent[0] + input_rows.astype(WIDE)
 
     def vector_at(source, row, start, size):

time: 256 us -> 248 us (0.969)
  starting transfers between devices: 96.5 us -> 84 us
  waiting for transfers between devices: 101 us -> 109 us
  local copies, waits for them, and re-layouts: 12.3 us -> 5.66 us
    ppermute x38, starting transfers between devices: 77.8 us -> 62.8 us  [swap(): return lax.ppermute(value, axis, [(at, at ^ bit) for at in range(count)])]
    ppermute x10 -> x12, waiting for transfers between devices: 13.3 us -> 17.2 us  [shift(): lax.ppermute(value, axis, [(at, (at + by) % count) for at in range(count)])]
    ppermute x38, waiting for transfers between devices: 88.1 us -> 91.5 us  [swap(): return lax.ppermute(value, axis, [(at, at ^ bit) for at in range(count)])]
    ppermute x10 -> x12, starting transfers between devices: 15.1 us -> 18.4 us  [shift(): lax.ppermute(value, axis, [(at, (at + by) % count) for at in range(count)])]
    unnamed x54 -> x34, local copies, waits for them, and re-layouts: 5.97 us -> 2.84 us
  transfers between devices with their start and end apart: 52 -> 54, of which waited for: 27 -> 25; matrix products, arithmetic and copies ran while one was open for 2% -> 2% of each run, Pallas kernels for 10% -> 13%
where the time goes in v10:
time: 248 us
  waiting for transfers between devices  109 us (44%)
  starting transfers between devices  84 us (34%)
  Pallas kernels  43.5 us (18%)
  local copies, waits for them, and re-layouts  5.66 us (2%)
  other arithmetic  4.87 us (2%)
    ppermute x38, waiting for transfers between devices, swap(): return lax.ppermute(value, axis, [(at, at ^ bit) for at in range(count)])  91.5 us
    ppermute x38, starting transfers between devices, swap(): return lax.ppermute(value, axis, [(at, at ^ bit) for at in range(count)])  62.8 us
    pallas_call x19, Pallas kernels, local_call(): pl.pallas_call(kernel, name=getattr(kernel, 'func', kernel).__name__, out...  43.5 us
    ppermute x12, starting transfers between devices, shift(): lax.ppermute(value, axis, [(at, (at + by) % count) for at in range(count)])  18.4 us
    ppermute x12, waiting for transfers between devices, shift(): lax.ppermute(value, axis, [(at, (at + by) % count) for at in range(count)])  17.2 us
  transfers between devices with their start and end apart: 54, of which 25 were waited for; matrix products, arithmetic and copies ran while one was open for 2% of the time, Pallas kernels for 13%

profile of v10, /device:TPU:0, one launch (start us, length us, event | category | flops | bytes accessed | tf_op | source)
XLA Modules:
  0.0 247.8 jit_solution(1874227312148031497)
XLA Ops:
  5.0 2.6 %collective-permute-start.1 = (bf16[48,1408]{1,0:T(8,128)(2,1)S(1)}, bf16[48,1408]{1,0:T(8,128)(2,1)S(1)}, u32[]{:S(2)}, u32[]{:S(2)}) collective-permute-start(bf16[48,1408]{1,0:T(8,128)(2,1)S(1)} %get-tuple-element.108), channel_id=1, source_target_pairs={{0,16},{8,24},{16,0},{24,8},{1,17},{9,25},{17,1},{25,9},{2,18},{10... | collective-permute-start | bytes 405512 | tf_op jit(solution)/shard_map/ppermute | solution.py:25
  8.7 3.3 %collective-permute-done.1.refs_2_ = bf16[48,1408]{1,0:T(8,128)(2,1)S(1)} collective-permute-done((bf16[48,1408]{1,0:T(8,128)(2,1)S(1)}, bf16[48,1408]{1,0:T(8,128)(2,1)S(1)}, u32[]{:S(2)}, u32[]{:S(2)}) %collective-permute-start.1) | collective-permute-done | bytes 135200 | tf_op jit(solution)/shard_map/ppermute | solution.py:25
  16.1 6.0 %collective-permute-start.4 = (bf16[144,576]{1,0:T(8,128)(2,1)S(1)}, bf16[144,576]{1,0:T(8,128)(2,1)S(1)}, u32[]{:S(2)}, u32[]{:S(2)}) collective-permute-start(bf16[144,576]{1,0:T(8,128)(2,1)S(1)} %get-tuple-element.112.refs_4_.refs_1_), channel_id=1, source_target_pairs={{0,3},{1,2},{2,1},{3,0},{4,7},{5,6},{6,5},{7,4},{8,11},{9,10},{10,... | collective-permute-start | bytes 497672 | tf_op jit(solution)/shard_map/ppermute | solution.py:25
  22.1 8.6 %collective-permute-done.4.refs_7_.refs_4_ = bf16[144,576]{1,0:T(8,128)(2,1)S(1)} collective-permute-done((bf16[144,576]{1,0:T(8,128)(2,1)S(1)}, bf16[144,576]{1,0:T(8,128)(2,1)S(1)}, u32[]{:S(2)}, u32[]{:S(2)}) %collective-permute-start.4) | collective-permute-done | bytes 165920 | tf_op jit(solution)/shard_map/ppermute | solution.py:25
  30.7 4.8 %collective-permute-start.6 = (bf16[128,768]{1,0:T(8,128)(2,1)S(1)}, bf16[128,768]{1,0:T(8,128)(2,1)S(1)}, u32[]{:S(2)}, u32[]{:S(2)}) collective-permute-start(bf16[128,768]{1,0:T(8,128)(2,1)S(1)} %collective-permute-done.3.refs_0_.refs_3_), channel_id=1, source_target_pairs={{0,16},{8,24},{16,0},{24,8},{1,17},{9,25},{17,1},{25,9},{2,18},{10... | collective-permute-start | bytes 589832 | tf_op jit(solution)/shard_map/ppermute | solution.py:25
  35.5 4.3 %collective-permute-start.8 = (bf16[144,576]{1,0:T(8,128)(2,1)S(1)}, bf16[144,576]{1,0:T(8,128)(2,1)S(1)}, u32[]{:S(2)}, u32[]{:S(2)}) collective-permute-start(bf16[144,576]{1,0:T(8,128)(2,1)S(1)} %get-tuple-element.112.refs_4_.refs_1_), channel_id=1, source_target_pairs={{0,2},{1,3},{2,0},{3,1},{4,6},{5,7},{6,4},{7,5},{8,10},{9,11},{10,... | collective-permute-start | bytes 497672 | tf_op jit(solution)/shard_map/ppermute | solution.py:25
  41.3 7.1 %collective-permute-done.8.refs_6_.refs_3_ = bf16[144,576]{1,0:T(8,128)(2,1)S(1)} collective-permute-done((bf16[144,576]{1,0:T(8,128)(2,1)S(1)}, bf16[144,576]{1,0:T(8,128)(2,1)S(1)}, u32[]{:S(2)}, u32[]{:S(2)}) %collective-permute-start.8) | collective-permute-done | bytes 165920 | tf_op jit(solution)/shard_map/ppermute | solution.py:25
  50.6 5.4 %collective-permute-done.11.refs_10_.refs_7_ = bf16[144,576]{1,0:T(8,128)(2,1)S(1)} collective-permute-done((bf16[144,576]{1,0:T(8,128)(2,1)S(1)}, bf16[144,576]{1,0:T(8,128)(2,1)S(1)}, u32[]{:S(2)}, u32[]{:S(2)}) %collective-permute-start.11) | collective-permute-done | bytes 165920 | tf_op jit(solution)/shard_map/ppermute | solution.py:30
  56.0 3.5 %collective-permute-done.12.refs_11_.refs_8_ = bf16[144,576]{1,0:T(8,128)(2,1)S(1)} collective-permute-done((bf16[144,576]{1,0:T(8,128)(2,1)S(1)}, bf16[144,576]{1,0:T(8,128)(2,1)S(1)}, u32[]{:S(2)}, u32[]{:S(2)}) %collective-permute-start.12) | collective-permute-done | bytes 165920 | tf_op jit(solution)/shard_map/ppermute | solution.py:30
  59.5 3.1 %project_kernel.1 = (bf16[512,576]{1,0:T(8,128)(2,1)S(1)}, bf16[512,384]{1,0:T(8,128)(2,1)S(1)}, bf16[768,576]{1,0:T(8,128)(2,1)S(1)}, bf16[512,768]{1,0:T(8,128)(2,1)S(1)}, f32[8,768]{1,0:T(8,128)S(1)}) custom-call(s32[6]{0:T(128)S(1)} %stack.33.meta_ref.place_ref, bf16[128,768]{1,0:T(8,128)(2,1)S(1)} %collective-permute-done.3.refs_0_.refs_3_, ...), custom_call_target="tpu_custom_call" | custom-call | flops 22649240 | bytes 239617 | tf_op jit(solution)/shard_map/project_kernel/pallas_call | solution.py:799
  65.2 3.1 %collective-permute-start.16 = (bf16[192,768]{1,0:T(8,128)(2,1)S(1)}, bf16[192,768]{1,0:T(8,128)(2,1)S(1)}, u32[]{:S(2)}, u32[]{:S(2)}) collective-permute-start(bf16[192,768]{1,0:T(8,128)(2,1)S(1)} %get-tuple-element.119.refs_8_), channel_id=1, source_target_pairs={{0,3},{1,2},{2,1},{3,0},{4,7},{5,6},{6,5},{7,4},{8,11},{9,10},{10,... | collective-permute-start | bytes 884744 | tf_op jit(solution)/shard_map/ppermute | solution.py:25
  68.3 6.8 %own_forward.1 = (f32[512,192]{1,0:T(8,128)S(1)}, f32[512,128]{1,0:T(8,128)S(1)}) custom-call(s32[6]{0:T(128)S(1)} %stack.33.meta_ref.place_ref, bf16[512,576]{1,0:T(8,128)(2,1)S(1)} %get-tuple-element.120.kvq_ref.refs_5_.refs_0_), custom_call_target="tpu_custom_call" | custom-call | flops 10066329 | bytes 62260 | tf_op jit(solution)/shard_map/own_forward/pallas_call | solution.py:799
  76.8 10.3 %collective-permute-done.15.refs_10_ = bf16[192,768]{1,0:T(8,128)(2,1)S(1)} collective-permute-done((bf16[192,768]{1,0:T(8,128)(2,1)S(1)}, bf16[192,768]{1,0:T(8,128)(2,1)S(1)}, u32[]{:S(2)}, u32[]{:S(2)}) %collective-permute-start.15) | collective-permute-done | bytes 294944 | tf_op jit(solution)/shard_map/ppermute | solution.py:25
  89.9 7.3 %collective-permute-start.19 = (bf16[128,768]{1,0:T(8,128)(2,1)S(1)}, bf16[128,768]{1,0:T(8,128)(2,1)S(1)}, u32[]{:S(2)}, u32[]{:S(2)}) collective-permute-start(bf16[128,768]{1,0:T(8,128)(2,1)S(1)} %add_convert_fusion.5), channel_id=1, source_target_pairs={{0,16},{8,24},{16,0},{24,8},{1,17},{9,25},{17,1},{25,9},{2,18},{10... | collective-permute-start | bytes 589832 | tf_op jit(solution)/shard_map/ppermute | solution.py:25
  97.8 6.8 %collective-permute-start.25 = (bf16[128,768]{1,0:T(8,128)(2,1)S(1)}, bf16[128,768]{1,0:T(8,128)(2,1)S(1)}, u32[]{:S(2)}, u32[]{:S(2)}) collective-permute-start(bf16[128,768]{1,0:T(8,128)(2,1)S(1)} %collective-permute-done.23.refs_4_.refs_5_), channel_id=1, source_target_pairs={{0,16},{8,24},{16,0},{24,8},{1,17},{9,25},{17,1},{25,9},{2,18},{10... | collective-permute-start | bytes 589832 | tf_op jit(solution)/shard_map/ppermute | solution.py:25
  107.4 2.6 %collective-permute-done.25.refs_6_ = bf16[128,768]{1,0:T(8,128)(2,1)S(1)} collective-permute-done((bf16[128,768]{1,0:T(8,128)(2,1)S(1)}, bf16[128,768]{1,0:T(8,128)(2,1)S(1)}, u32[]{:S(2)}, u32[]{:S(2)}) %collective-permute-start.25) | collective-permute-done | bytes 196640 | tf_op jit(solution)/shard_map/ppermute | solution.py:25
  113.9 4.8 %feed_kernel.1 = (f32[256,768]{1,0:T(8,128)S(1)}, bf16[256,768]{1,0:T(8,128)(2,1)S(1)}, bf16[512,768]{1,0:T(8,128)(2,1)S(1)}, bf16[512,768]{1,0:T(8,128)(2,1)S(1...) custom-call(s32[6]{0:T(128)S(1)} %stack.33.meta_ref.place_ref, ...), custom_call_target="tpu_custom_call" | custom-call | flops 90596968 | bytes 473242 | tf_op jit(solution)/shard_map/feed_kernel/pallas_call | solution.py:799
  118.8 3.8 %feed_grad_kernel.1 = (f32[4,192,768]{2,1,0:T(8,128)S(1)}, bf16[4,192,768]{2,1,0:T(8,128)(2,1)S(1)}, f32[256,768]{1,0:T(8,128)S(1)}, bf16[256,768]{1,0:T(8,128)(2,1)S(1)}) custom-call(s32[6]{0:T(128)S(1)} %stack.33.meta_ref.place_ref, bf16[512,768]{1,0:T(8,128)(2,1)S(1)} %get-tuple-element.133.refs_0_, bf16[512,768]{1,0:T(8,128)(2,1)S(1)} %get-tuple-element.134.refs_1_, ...), custom_call_target="tpu_custom_call" | custom-call | flops 90596968 | bytes 452199 | tf_op jit(solution)/shard_map/feed_grad_kernel/pallas_call | solution.py:799
  124.9 5.3 %collective-permute-done.30.refs_2_ = bf16[128,768]{1,0:T(8,128)(2,1)S(1)} collective-permute-done((bf16[128,768]{1,0:T(8,128)(2,1)S(1)}, bf16[128,768]{1,0:T(8,128)(2,1)S(1)}, u32[]{:S(2)}, u32[]{:S(2)}) %collective-permute-start.30) | collective-permute-done | bytes 196640 | tf_op jit(solution)/shard_map/ppermute | solution.py:25
  132.9 4.5 %collective-permute-done.31.refs_2_ = bf16[128,768]{1,0:T(8,128)(2,1)S(1)} collective-permute-done((bf16[128,768]{1,0:T(8,128)(2,1)S(1)}, bf16[128,768]{1,0:T(8,128)(2,1)S(1)}, u32[]{:S(2)}, u32[]{:S(2)}) %collective-permute-start.31) | collective-permute-done | bytes 196640 | tf_op jit(solution)/shard_map/ppermute | solution.py:25
  141.8 7.7 %collective-permute-start.38 = (bf16[512,384]{1,0:T(8,128)(2,1)S(1)}, bf16[512,384]{1,0:T(8,128)(2,1)S(1)}, u32[]{:S(2)}, u32[]{:S(2)}) collective-permute-start(bf16[512,384]{1,0:T(8,128)(2,1)S(1)} %bitcast.43), channel_id=1, source_target_pairs={{0,4},{4,0},{1,5},{5,1},{2,6},{6,2},{3,7},{7,3},{8,12},{12,8},{9,1... | collective-permute-start | bytes 1179656 | tf_op jit(solution)/shard_map/ppermute | solution.py:30
  156.6 6.8 %own_grad_kernel.1 = (f32[512,576]{1,0:T(8,128)S(1)}, f32[192,768]{1,0:T(8,128)S(1)}) custom-call(s32[6]{0:T(128)S(1)} %stack.33.meta_ref.place_ref, bf16[512,576]{1,0:T(8,128)(2,1)S(1)} %get-tuple-element.120.kvq_ref.refs_5_.refs_0_, bf16[512,192]{1,0:T(8,128)(2,1)S(1)} %get-tuple-element.150.refs_1_, f32[512,192]{1,0:T(8,128)S(1)} %get-tuple-element.148.refs_7_.refs_2_, ...), custom_call_target="tpu_custom_call" | custom-call | flops 25165824 | bytes 229377 | tf_op jit(solution)/shard_map/own_grad_kernel/pallas_call | solution.py:799
  167.4 2.8 %projection_grad_kernel.1 = (f32[4,128,576]{2,1,0:T(8,128)S(1)}, bf16[4,144,576]{2,1,0:T(8,128)(2,1)}) custom-call(s32[6]{0:T(128)S(1)} %stack.33.meta_ref.place_ref, bf16[512,768]{1,0:T(8,128)(2,1)S(1)} %get-tuple-element.146.refs_0_, bf16[512,576]{1,0:T(8,128)(2,1)S(1)} %get-tuple-element.165.refs_1_, f32[192,768]{1,0:T(8,128)S(1)} %get-tuple-element.166.refs_2_), custom_call_target="tpu_custom_call" | custom-call | flops 22649240 | bytes 190465 | tf_op jit(solution)/shard_map/projection_grad_kernel/pallas_call | solution.py:799
  170.4 6.5 %collective-permute-start.40 = (bf16[192,768]{1,0:T(8,128)(2,1)}, bf16[192,768]{1,0:T(8,128)(2,1)}, u32[]{:S(2)}, u32[]{:S(2)}) collective-permute-start(bf16[192,768]{1,0:T(8,128)(2,1)} %get-tuple-element.169), channel_id=1, source_target_pairs={{0,1},{1,0},{2,3},{3,2},{4,5},{5,4},{6,7},{7,6},{8,9},{9,8},{10,11... | collective-permute-start | bytes 884744 | tf_op jit(solution)/shard_map/ppermute | solution.py:25
  180.0 10.1 %collective-permute-done.40 = bf16[192,768]{1,0:T(8,128)(2,1)} collective-permute-done((bf16[192,768]{1,0:T(8,128)(2,1)}, bf16[192,768]{1,0:T(8,128)(2,1)}, u32[]{:S(2)}, u32[]{:S(2)}) %collective-permute-start.40) | collective-permute-done | bytes 294944 | tf_op jit(solution)/shard_map/ppermute | solution.py:25
  190.1 2.8 %collective-permute-done.41 = bf16[192,768]{1,0:T(8,128)(2,1)} collective-permute-done((bf16[192,768]{1,0:T(8,128)(2,1)}, bf16[192,768]{1,0:T(8,128)(2,1)}, u32[]{:S(2)}, u32[]{:S(2)}) %collective-permute-start.41) | collective-permute-done | bytes 294944 | tf_op jit(solution)/shard_map/ppermute | solution.py:25
  196.4 3.5 %collective-permute-start.46 = (bf16[144,576]{1,0:T(8,128)(2,1)S(1)}, bf16[144,576]{1,0:T(8,128)(2,1)S(1)}, u32[]{:S(2)}, u32[]{:S(2)}) collective-permute-start(bf16[144,576]{1,0:T(8,128)(2,1)S(1)} %get-tuple-element.184), channel_id=1, source_target_pairs={{0,3},{1,2},{2,1},{3,0},{4,7},{5,6},{6,5},{7,4},{8,11},{9,10},{10,... | collective-permute-start | bytes 497672 | tf_op jit(solution)/shard_map/ppermute | solution.py:25
  205.1 3.1 %collective-permute-done.46 = bf16[144,576]{1,0:T(8,128)(2,1)S(1)} collective-permute-done((bf16[144,576]{1,0:T(8,128)(2,1)S(1)}, bf16[144,576]{1,0:T(8,128)(2,1)S(1)}, u32[]{:S(2)}, u32[]{:S(2)}) %collective-permute-start.46) | collective-permute-done | bytes 165920 | tf_op jit(solution)/shard_map/ppermute | solution.py:25
  208.2 15.4 %collective-permute-done.45 = bf16[144,576]{1,0:T(8,128)(2,1)S(1)} collective-permute-done((bf16[144,576]{1,0:T(8,128)(2,1)S(1)}, bf16[144,576]{1,0:T(8,128)(2,1)S(1)}, u32[]{:S(2)}, u32[]{:S(2)}) %collective-permute-start.45) | collective-permute-done | bytes 165920 | tf_op jit(solution)/shard_map/ppermute | solution.py:25
  225.5 4.9 %collective-permute-done.48.arrived = bf16[144,576]{1,0:T(8,128)(2,1)S(1)} collective-permute-done((bf16[144,576]{1,0:T(8,128)(2,1)S(1)}, bf16[144,576]{1,0:T(8,128)(2,1)S(1)}, u32[]{:S(2)}, u32[]{:S(2)}) %collective-permute-start.48) | collective-permute-done | bytes 165920 | tf_op jit(solution)/shard_map/ppermute | solution.py:30
  236.5 2.8 %collective-permute-done.52.refs_2_ = bf16[64,1408]{1,0:T(8,128)(2,1)S(1)} collective-permute-done((bf16[64,1408]{1,0:T(8,128)(2,1)S(1)}, bf16[64,1408]{1,0:T(8,128)(2,1)S(1)}, u32[]{:S(2)}, u32[]{:S(2)}) %collective-permute-start.52) | collective-permute-done | bytes 180256 | tf_op jit(solution)/shard_map/ppermute | solution.py:25
  239.3 5.5 %collective-permute-done.53.refs_3_ = bf16[64,1408]{1,0:T(8,128)(2,1)S(1)} collective-permute-done((bf16[64,1408]{1,0:T(8,128)(2,1)S(1)}, bf16[64,1408]{1,0:T(8,128)(2,1)S(1)}, u32[]{:S(2)}, u32[]{:S(2)}) %collective-permute-start.53) | collective-permute-done | bytes 180256 | tf_op jit(solution)/shard_map/ppermute | solution.py:25
  (147 shorter events, 71.0 us)
Async XLA Ops:
  14.4 16.3 %collective-permute-start.3 = (bf16[128,768]{1,0:T(8,128)(2,1)S(1)}, bf16[128,768]{1,0:T(8,128)(2,1)S(1)}, u32[]{:S(2)}, u32[]{:S(2)}) collective-permute-start(bf16[128,768]{1,0:T(8,128)(2,1)S(1)} %bitcast_convert_fusion.1), channel_id=1, source_target_pairs={{0,0},{1,8},{2,16},{3,24},{8,1},{9,9},{10,17},{11,25},{16,2},{17,1... | collective-permute-start | bytes 589832 | tf_op jit(solution)/shard_map/ppermute | solution.py:36
  16.1 14.6 %collective-permute-start.4 = (bf16[144,576]{1,0:T(8,128)(2,1)S(1)}, bf16[144,576]{1,0:T(8,128)(2,1)S(1)}, u32[]{:S(2)}, u32[]{:S(2)}) collective-permute-start(bf16[144,576]{1,0:T(8,128)(2,1)S(1)} %get-tuple-element.112.refs_4_.refs_1_), channel_id=1, source_target_pairs={{0,3},{1,2},{2,1},{3,0},{4,7},{5,6},{6,5},{7,4},{8,11},{9,10},{10,... | collective-permute-start | bytes 497672 | tf_op jit(solution)/shard_map/ppermute | solution.py:25
  22.1 17.7 %collective-permute-start.7 = (bf16[144,576]{1,0:T(8,128)(2,1)S(1)}, bf16[144,576]{1,0:T(8,128)(2,1)S(1)}, u32[]{:S(2)}, u32[]{:S(2)}) collective-permute-start(bf16[144,576]{1,0:T(8,128)(2,1)S(1)} %get-tuple-element.112.refs_4_.refs_1_), channel_id=1, source_target_pairs={{0,1},{1,0},{2,3},{3,2},{4,5},{5,4},{6,7},{7,6},{8,9},{9,8},{10,11... | collective-permute-start | bytes 497672 | tf_op jit(solution)/shard_map/ppermute | solution.py:25
  30.7 17.8 %collective-permute-start.6 = (bf16[128,768]{1,0:T(8,128)(2,1)S(1)}, bf16[128,768]{1,0:T(8,128)(2,1)S(1)}, u32[]{:S(2)}, u32[]{:S(2)}) collective-permute-start(bf16[128,768]{1,0:T(8,128)(2,1)S(1)} %collective-permute-done.3.refs_0_.refs_3_), channel_id=1, source_target_pairs={{0,16},{8,24},{16,0},{24,8},{1,17},{9,25},{17,1},{25,9},{2,18},{10... | collective-permute-start | bytes 589832 | tf_op jit(solution)/shard_map/ppermute | solution.py:25
  35.5 12.9 %collective-permute-start.8 = (bf16[144,576]{1,0:T(8,128)(2,1)S(1)}, bf16[144,576]{1,0:T(8,128)(2,1)S(1)}, u32[]{:S(2)}, u32[]{:S(2)}) collective-permute-start(bf16[144,576]{1,0:T(8,128)(2,1)S(1)} %get-tuple-element.112.refs_4_.refs_1_), channel_id=1, source_target_pairs={{0,2},{1,3},{2,0},{3,1},{4,6},{5,7},{6,4},{7,5},{8,10},{9,11},{10,... | collective-permute-start | bytes 497672 | tf_op jit(solution)/shard_map/ppermute | solution.py:25
  39.8 10.2 %collective-permute-start.10 = (bf16[144,576]{1,0:T(8,128)(2,1)S(1)}, bf16[144,576]{1,0:T(8,128)(2,1)S(1)}, u32[]{:S(2)}, u32[]{:S(2)}) collective-permute-start(bf16[144,576]{1,0:T(8,128)(2,1)S(1)} %collective-permute-done.7.refs_5_.refs_2_), channel_id=1, source_target_pairs={{0,4},{4,0},{1,5},{5,1},{2,6},{6,2},{3,7},{7,3},{8,12},{12,8},{9,1... | collective-permute-start | bytes 497672 | tf_op jit(solution)/shard_map/ppermute | solution.py:30
  41.3 18.1 %collective-permute-start.5 = (bf16[128,768]{1,0:T(8,128)(2,1)S(1)}, bf16[128,768]{1,0:T(8,128)(2,1)S(1)}, u32[]{:S(2)}, u32[]{:S(2)}) collective-permute-start(bf16[128,768]{1,0:T(8,128)(2,1)S(1)} %collective-permute-done.3.refs_0_.refs_3_), channel_id=1, source_target_pairs={{0,8},{8,0},{16,24},{24,16},{1,9},{9,1},{17,25},{25,17},{2,10},{10... | collective-permute-start | bytes 589832 | tf_op jit(solution)/shard_map/ppermute | solution.py:25
  48.5 11.0 %collective-permute-start.9 = (bf16[128,768]{1,0:T(8,128)(2,1)S(1)}, bf16[128,768]{1,0:T(8,128)(2,1)S(1)}, u32[]{:S(2)}, u32[]{:S(2)}) collective-permute-start(bf16[128,768]{1,0:T(8,128)(2,1)S(1)} %collective-permute-done.6.refs_2_), channel_id=1, source_target_pairs={{0,8},{8,0},{16,24},{24,16},{1,9},{9,1},{17,25},{25,17},{2,10},{10... | collective-permute-start | bytes 589832 | tf_op jit(solution)/shard_map/ppermute | solution.py:25
  48.5 19.8 %collective-permute-start.14 = (bf16[192,768]{1,0:T(8,128)(2,1)S(1)}, bf16[192,768]{1,0:T(8,128)(2,1)S(1)}, u32[]{:S(2)}, u32[]{:S(2)}) collective-permute-start(bf16[192,768]{1,0:T(8,128)(2,1)S(1)} %get-tuple-element.119.refs_8_), channel_id=1, source_target_pairs={{0,1},{1,0},{2,3},{3,2},{4,5},{5,4},{6,7},{7,6},{8,9},{9,8},{10,11... | collective-permute-start | bytes 884744 | tf_op jit(solution)/shard_map/ppermute | solution.py:25
  62.6 13.1 %collective-permute-start.13 = (bf16[512,384]{1,0:T(8,128)(2,1)S(1)}, bf16[512,384]{1,0:T(8,128)(2,1)S(1)}, u32[]{:S(2)}, u32[]{:S(2)}) collective-permute-start(bf16[512,384]{1,0:T(8,128)(2,1)S(1)} %get-tuple-element.117), channel_id=1, source_target_pairs={{0,4},{4,0},{1,5},{5,1},{2,6},{6,2},{3,7},{7,3},{8,12},{12,8},{9,1... | collective-permute-start | bytes 1179656 | tf_op jit(solution)/shard_map/ppermute | solution.py:30
  64.2 22.9 %collective-permute-start.15 = (bf16[192,768]{1,0:T(8,128)(2,1)S(1)}, bf16[192,768]{1,0:T(8,128)(2,1)S(1)}, u32[]{:S(2)}, u32[]{:S(2)}) collective-permute-start(bf16[192,768]{1,0:T(8,128)(2,1)S(1)} %get-tuple-element.119.refs_8_), channel_id=1, source_target_pairs={{0,2},{1,3},{2,0},{3,1},{4,6},{5,7},{6,4},{7,5},{8,10},{9,11},{10,... | collective-permute-start | bytes 884744 | tf_op jit(solution)/shard_map/ppermute | solution.py:25
  65.2 21.9 %collective-permute-start.16 = (bf16[192,768]{1,0:T(8,128)(2,1)S(1)}, bf16[192,768]{1,0:T(8,128)(2,1)S(1)}, u32[]{:S(2)}, u32[]{:S(2)}) collective-permute-start(bf16[192,768]{1,0:T(8,128)(2,1)S(1)} %get-tuple-element.119.refs_8_), channel_id=1, source_target_pairs={{0,3},{1,2},{2,1},{3,0},{4,7},{5,6},{6,5},{7,4},{8,11},{9,10},{10,... | collective-permute-start | bytes 884744 | tf_op jit(solution)/shard_map/ppermute | solution.py:25
  75.1 12.0 %collective-permute-start.17 = (bf16[192,768]{1,0:T(8,128)(2,1)S(1)}, bf16[192,768]{1,0:T(8,128)(2,1)S(1)}, u32[]{:S(2)}, u32[]{:S(2)}) collective-permute-start(bf16[192,768]{1,0:T(8,128)(2,1)S(1)} %collective-permute-done.14.refs_9_), channel_id=1, source_target_pairs={{0,4},{4,0},{1,5},{5,1},{2,6},{6,2},{3,7},{7,3},{8,12},{12,8},{9,1... | collective-permute-start | bytes 884744 | tf_op jit(solution)/shard_map/ppermute | solution.py:30
  88.2 9.6 %collective-permute-start.23 = (bf16[128,768]{1,0:T(8,128)(2,1)S(1)}, bf16[128,768]{1,0:T(8,128)(2,1)S(1)}, u32[]{:S(2)}, u32[]{:S(2)}) collective-permute-start(bf16[128,768]{1,0:T(8,128)(2,1)S(1)} %bitcast_convert_fusion), channel_id=1, source_target_pairs={{0,0},{1,8},{2,16},{3,24},{8,1},{9,9},{10,17},{11,25},{16,2},{17,1... | collective-permute-start | bytes 589832 | tf_op jit(solution)/shard_map/ppermute | solution.py:36
  89.9 14.6 %collective-permute-start.19 = (bf16[128,768]{1,0:T(8,128)(2,1)S(1)}, bf16[128,768]{1,0:T(8,128)(2,1)S(1)}, u32[]{:S(2)}, u32[]{:S(2)}) collective-permute-start(bf16[128,768]{1,0:T(8,128)(2,1)S(1)} %add_convert_fusion.5), channel_id=1, source_target_pairs={{0,16},{8,24},{16,0},{24,8},{1,17},{9,25},{17,1},{25,9},{2,18},{10... | collective-permute-start | bytes 589832 | tf_op jit(solution)/shard_map/ppermute | solution.py:25
  97.3 12.8 %collective-permute-start.27 = (bf16[192,768]{1,0:T(8,128)(2,1)S(1)}, bf16[192,768]{1,0:T(8,128)(2,1)S(1)}, u32[]{:S(2)}, u32[]{:S(2)}) collective-permute-start(bf16[192,768]{1,0:T(8,128)(2,1)S(1)} %collective-permute-done.15.refs_10_), channel_id=1, source_target_pairs={{0,4},{4,0},{1,5},{5,1},{2,6},{6,2},{3,7},{7,3},{8,12},{12,8},{9,1... | collective-permute-start | bytes 884744 | tf_op jit(solution)/shard_map/ppermute | solution.py:30
  97.8 12.2 %collective-permute-start.25 = (bf16[128,768]{1,0:T(8,128)(2,1)S(1)}, bf16[128,768]{1,0:T(8,128)(2,1)S(1)}, u32[]{:S(2)}, u32[]{:S(2)}) collective-permute-start(bf16[128,768]{1,0:T(8,128)(2,1)S(1)} %collective-permute-done.23.refs_4_.refs_5_), channel_id=1, source_target_pairs={{0,16},{8,24},{16,0},{24,8},{1,17},{9,25},{17,1},{25,9},{2,18},{10... | collective-permute-start | bytes 589832 | tf_op jit(solution)/shard_map/ppermute | solution.py:25
  122.6 28.8 %collective-permute-start.36 = (bf16[4,192,768]{2,1,0:T(8,128)(2,1)S(1)}, bf16[4,192,768]{2,1,0:T(8,128)(2,1)S(1)}, u32[]{:S(2)}, u32[]{:S(2)}) collective-permute-start(bf16[4,192,768]{2,1,0:T(8,128)(2,1)S(1)} %get-tuple-element.154), channel_id=1, source_target_pairs={{0,4},{4,0},{1,5},{5,1},{2,6},{6,2},{3,7},{7,3},{8,12},{12,8},{9,1... | collective-permute-start | bytes 3538952 | tf_op jit(solution)/shard_map/ppermute | solution.py:30
  138.8 16.0 %collective-permute-start.33 = (bf16[256,768]{1,0:T(8,128)(2,1)S(1)}, bf16[256,768]{1,0:T(8,128)(2,1)S(1)}, u32[]{:S(2)}, u32[]{:S(2)}) collective-permute-start(bf16[256,768]{1,0:T(8,128)(2,1)S(1)} %get-tuple-element.145), channel_id=1, source_target_pairs={{0,8},{8,0},{16,24},{24,16},{1,9},{9,1},{17,25},{25,17},{2,10},{10... | collective-permute-start | bytes 1179656 | tf_op jit(solution)/shard_map/ppermute | solution.py:25
  141.8 21.8 %collective-permute-start.38 = (bf16[512,384]{1,0:T(8,128)(2,1)S(1)}, bf16[512,384]{1,0:T(8,128)(2,1)S(1)}, u32[]{:S(2)}, u32[]{:S(2)}) collective-permute-start(bf16[512,384]{1,0:T(8,128)(2,1)S(1)} %bitcast.43), channel_id=1, source_target_pairs={{0,4},{4,0},{1,5},{5,1},{2,6},{6,2},{3,7},{7,3},{8,12},{12,8},{9,1... | collective-permute-start | bytes 1179656 | tf_op jit(solution)/shard_map/ppermute | solution.py:30
  153.0 10.5 %collective-permute-start.37 = (bf16[192,768]{1,0:T(8,128)(2,1)S(1)}, bf16[192,768]{1,0:T(8,128)(2,1)S(1)}, u32[]{:S(2)}, u32[]{:S(2)}) collective-permute-start(bf16[192,768]{1,0:T(8,128)(2,1)S(1)} %get-tuple-element.159), channel_id=1, source_target_pairs={{0,3},{1,2},{2,1},{3,0},{4,7},{5,6},{6,5},{7,4},{8,11},{9,10},{10,... | collective-permute-start | bytes 884744 | tf_op jit(solution)/shard_map/ppermute | solution.py:25
  170.2 24.9 %collective-permute-start.42 = (bf16[4,144,576]{2,1,0:T(8,128)(2,1)}, bf16[4,144,576]{2,1,0:T(8,128)(2,1)}, u32[]{:S(2)}, u32[]{:S(2)}) collective-permute-start(bf16[4,144,576]{2,1,0:T(8,128)(2,1)} %get-tuple-element.173), channel_id=1, source_target_pairs={{0,4},{4,0},{1,5},{5,1},{2,6},{6,2},{3,7},{7,3},{8,12},{12,8},{9,1... | collective-permute-start | bytes 1990664 | tf_op jit(solution)/shard_map/ppermute | solution.py:30
  170.4 19.7 %collective-permute-start.40 = (bf16[192,768]{1,0:T(8,128)(2,1)}, bf16[192,768]{1,0:T(8,128)(2,1)}, u32[]{:S(2)}, u32[]{:S(2)}) collective-permute-start(bf16[192,768]{1,0:T(8,128)(2,1)} %get-tuple-element.169), channel_id=1, source_target_pairs={{0,1},{1,0},{2,3},{3,2},{4,5},{5,4},{6,7},{7,6},{8,9},{9,8},{10,11... | collective-permute-start | bytes 884744 | tf_op jit(solution)/shard_map/ppermute | solution.py:25
  176.9 16.1 %collective-permute-start.41 = (bf16[192,768]{1,0:T(8,128)(2,1)}, bf16[192,768]{1,0:T(8,128)(2,1)}, u32[]{:S(2)}, u32[]{:S(2)}) collective-permute-start(bf16[192,768]{1,0:T(8,128)(2,1)} %get-tuple-element.171), channel_id=1, source_target_pairs={{0,2},{1,3},{2,0},{3,1},{4,6},{5,7},{6,4},{7,5},{8,10},{9,11},{10,... | collective-permute-start | bytes 884744 | tf_op jit(solution)/shard_map/ppermute | solution.py:25
  178.3 14.7 %collective-permute-start.43 = (bf16[128,768]{1,0:T(8,128)(2,1)}, bf16[128,768]{1,0:T(8,128)(2,1)}, u32[]{:S(2)}, u32[]{:S(2)}) collective-permute-start(bf16[128,768]{1,0:T(8,128)(2,1)} %add_convert_fusion.1), channel_id=1, source_target_pairs={{0,16},{8,24},{16,0},{24,8},{1,17},{9,25},{17,1},{25,9},{2,18},{10... | collective-permute-start | bytes 589832 | tf_op jit(solution)/shard_map/ppermute | solution.py:25
  194.3 29.5 %collective-permute-start.47 = (bf16[128,768]{1,0:T(8,128)(2,1)S(1)}, bf16[128,768]{1,0:T(8,128)(2,1)S(1)}, u32[]{:S(2)}, u32[]{:S(2)}) collective-permute-start(bf16[128,768]{1,0:T(8,128)(2,1)S(1)} %get-tuple-element.185), channel_id=1, source_target_pairs={{0,0},{1,8},{2,16},{3,24},{8,1},{9,9},{10,17},{11,25},{16,2},{17,1... | collective-permute-start | bytes 589832 | tf_op jit(solution)/shard_map/ppermute | solution.py:36
  196.4 11.8 %collective-permute-start.46 = (bf16[144,576]{1,0:T(8,128)(2,1)S(1)}, bf16[144,576]{1,0:T(8,128)(2,1)S(1)}, u32[]{:S(2)}, u32[]{:S(2)}) collective-permute-start(bf16[144,576]{1,0:T(8,128)(2,1)S(1)} %get-tuple-element.184), channel_id=1, source_target_pairs={{0,3},{1,2},{2,1},{3,0},{4,7},{5,6},{6,5},{7,4},{8,11},{9,10},{10,... | collective-permute-start | bytes 497672 | tf_op jit(solution)/shard_map/ppermute | solution.py:25
  199.9 23.8 %collective-permute-start.45 = (bf16[144,576]{1,0:T(8,128)(2,1)S(1)}, bf16[144,576]{1,0:T(8,128)(2,1)S(1)}, u32[]{:S(2)}, u32[]{:S(2)}) collective-permute-start(bf16[144,576]{1,0:T(8,128)(2,1)S(1)} %get-tuple-element.183), channel_id=1, source_target_pairs={{0,2},{1,3},{2,0},{3,1},{4,6},{5,7},{6,4},{7,5},{8,10},{9,11},{10,... | collective-permute-start | bytes 497672 | tf_op jit(solution)/shard_map/ppermute | solution.py:25
  201.8 21.9 %collective-permute-start.44 = (bf16[144,576]{1,0:T(8,128)(2,1)S(1)}, bf16[144,576]{1,0:T(8,128)(2,1)S(1)}, u32[]{:S(2)}, u32[]{:S(2)}) collective-permute-start(bf16[144,576]{1,0:T(8,128)(2,1)S(1)} %get-tuple-element.182), channel_id=1, source_target_pairs={{0,1},{1,0},{2,3},{3,2},{4,5},{5,4},{6,7},{7,6},{8,9},{9,8},{10,11... | collective-permute-start | bytes 497672 | tf_op jit(solution)/shard_map/ppermute | solution.py:25
  203.5 21.9 %collective-permute-start.50 = (bf16[192,768]{1,0:T(8,128)(2,1)S(1)}, bf16[192,768]{1,0:T(8,128)(2,1)S(1)}, u32[]{:S(2)}, u32[]{:S(2)}) collective-permute-start(bf16[192,768]{1,0:T(8,128)(2,1)S(1)} %add_convert_fusion.refs_0_), channel_id=1, source_target_pairs={{0,4},{4,0},{1,5},{5,1},{2,6},{6,2},{3,7},{7,3},{8,12},{12,8},{9,1... | collective-permute-start | bytes 884744 | tf_op jit(solution)/shard_map/ppermute | solution.py:30
  231.9 12.8 %collective-permute-start.53 = (bf16[64,1408]{1,0:T(8,128)(2,1)S(1)}, bf16[64,1408]{1,0:T(8,128)(2,1)S(1)}, u32[]{:S(2)}, u32[]{:S(2)}) collective-permute-start(bf16[64,1408]{1,0:T(8,128)(2,1)S(1)} %get-tuple-element.192), channel_id=1, source_target_pairs={{0,24},{8,16},{16,8},{24,0},{1,25},{9,17},{17,9},{25,1},{2,26},{10... | collective-permute-start | bytes 540680 | tf_op jit(solution)/shard_map/ppermute | solution.py:25
  234.6 12.5 %collective-permute-start.49 = (bf16[128,768]{1,0:T(8,128)(2,1)S(1)}, bf16[128,768]{1,0:T(8,128)(2,1)S(1)}, u32[]{:S(2)}, u32[]{:S(2)}) collective-permute-start(bf16[128,768]{1,0:T(8,128)(2,1)S(1)} %add_convert_fusion.2), channel_id=1, source_target_pairs={{0,0},{1,8},{2,16},{3,24},{8,1},{9,9},{10,17},{11,25},{16,2},{17,1... | collective-permute-start | bytes 589832 | tf_op jit(solution)/shard_map/ppermute | solution.py:36
  (39 other events, 324.4 us)

commit v11 on v10

--- a/solution.py
+++ b/solution.py
@@ -434,7 +434,7 @@
 
 
 def join_kernel(parts, width, meta_ref, *refs):
-    pieces, out_ref, up_ref, vectors = take(refs, parts, None, None, None)
+    pieces, up, out_ref, up_ref, vectors = take(refs, parts, parts, None, None, None)
     model = parts * width
     shard = out_ref.shape[0]
     hidden = up_ref.shape[1] // parts
@@ -449,11 +449,9 @@
                     out_ref[:, start : start + width] = pieces[slot][
                         :shard, at * width : (at + 1) * width
                     ].astype(WIDE)
-                up_ref[:, owner * hidden : (owner + 1) * hidden] = pieces[slot][
-                    :shard, -hidden:
-                ].astype(WIDE)
-
-    vectors[...] = sum(piece[shard:, : vectors.shape[1]].astype(WIDE) for piece in pieces)
+                up_ref[:, owner * hidden : (owner + 1) * hidden] = up[slot][...].astype(WIDE)
+
+    vectors[...] = sum(piece[shard:, :].astype(WIDE) for piece in pieces)
 
 
 def in_order(halves, parts, meta_ref, place, own, other):
@@ -731,12 +729,23 @@
         send[rows:, :] = folded[...].astype(LOW)
 
 
+def unfold_feed_kernel(parts, halves, meta_ref, mine, other, *refs):
+    pieces, down_ref = refs[:parts], refs[parts]
+    shard = pieces[0].shape[0]
+
+    def place(up, down):
+        for slot in range(parts):
+            pieces[slot][...] = up[slot * shard : (slot + 1) * shard, :].astype(LOW)
+        down_ref[...] = down[...].astype(WIDE)
+
+    in_order(halves, parts, meta_ref, place, mine, other)
+
+
 def unfold_kernel(parts, halves, meta_ref, mine, arrived, *refs):
-    sums, mine_feed, other_feed, pieces, out_ref, down_ref, vectors, folded = take(
-        refs, 0 if halves else 1, None, None, parts, None, None, None, None
+    sums, pieces, out_ref, vectors, folded = take(
+        refs, 0 if halves else 1, parts, None, None, None
     )
     shard, columns = pieces[0].shape[0] - 16, vectors.shape[1]
-    hidden = mine_feed.shape[1]
     rest = out_ref.shape[1] - columns
     slots = parts // 2
     extra = folded.shape[0] // 2
@@ -749,15 +758,8 @@
         start = slots * shard
         folded[half * extra : (half + 1) * extra, :] = ref[start : start + extra, :].astype(WIDE)
 
-    def feeds(up, down):
-        for slot in range(parts):
-            pieces[slot][:shard, -hidden:] = up[slot * shard : (slot + 1) * shard, :].astype(LOW)
-        down_ref[...] = down[...].astype(WIDE)
-
     if halves:
         first = meta_ref[parts] == 0
-        pl.when(first)(lambda: feeds(mine_feed, other_feed))
-        pl.when(jnp.logical_not(first))(lambda: feeds(other_feed, mine_feed))
         for half in range(2):
             pl.when(first)(functools.partial(unfold, half, arrived if half else mine))
             pl.when(jnp.logical_not(first))(
@@ -766,14 +768,11 @@
         start = slots * shard + extra
         vectors[...] = mine[start:, :].astype(WIDE) + arrived[start:, :].astype(WIDE)
     else:
-        feeds(mine_feed, other_feed)
         unfold(0, mine)
         unfold(1, arrived)
         fold_vectors(sums[0], vectors)
     for piece in pieces:
-        piece[shard:, :columns] = vectors[...].astype(LOW)
-        piece[shard:, columns:] = jnp.zeros_like(piece[shard:, columns:])
-        piece[:shard, columns:-hidden] = jnp.zeros_like(piece[:shard, columns:-hidden])
+        piece[shard:, :] = vectors[...].astype(LOW)
     out_ref[:, :columns] = folded[:shard, :]
     for at in range(columns // rest):
         out_ref[at * 16 : (at + 1) * 16, columns:] = folded[shard:, at * rest : (at + 1) * rest]
@@ -871,7 +870,7 @@
         kvq_other = gather_direct(kvq_theirs, "fsdp")
 
     token_rows = transpose_homes(after(tokens[0].astype(LOW), *split_arrived))
-    pieces = gather_pieces(after(token_rows, kvq_own[-1]), *kvq_own[1:])
+    pieces = gather_pieces(after(token_rows, kvq_own[-1]), *kvq_own[1:], kvq_other[-1])
 
     kvq, kv, kvq_matrix, norm1_all, vectors = local_call(
         functools.partial(project_kernel, parts, depth, halves),
@@ -900,14 +899,15 @@
     low_square = pltpu.VMEM((group, group), LOW)
     acc, stat = local_call(
         functools.partial(own_forward, heads, rows),
-        (meta, after(kvq, own_half[1])),
+        (meta, after(kvq, own_half[2])),
         [wide_like(group, width), wide_like(group, 128)],
         [wide_square, low_square],
         flops=2 * score_flops,
     )
     if halves:
-        other_half = [feed_theirs, shift(after(own_half[1], acc), "ctx", 1)]
-        other_half += [shift(piece, "ctx", 1) for piece in own_half[2:]]
+        other_half = [feed_theirs, shift(own_half[1], "ctx", 1)]
+        other_half.append(shift(after(own_half[2], acc), "ctx", 1))
+        other_half += [shift(piece, "ctx", 1) for piece in own_half[3:]]
     context, context_low, stat = local_call(
         functools.partial(earlier_forward, heads, parts),
         (meta, kvq, kv_earlier, after(acc, own_half[1]), stat),
@@ -917,7 +917,7 @@
     )
     out_matrix, attended_keep, attended_send = local_call(
         functools.partial(mix_kernel, parts, depth, halves),
-        (meta, after(context_low, *own_half[2:], other_half[1]), *kvq_own, *kvq_other),
+        (meta, after(context_low, *own_half[1:], other_half[2]), *kvq_own, *kvq_other),
         [low_like(width, model), wide_like(2 * rows, model), low_like(2 * rows, model)],
         flops=2 * group * width * model,
     )
@@ -1076,16 +1076,22 @@
     delta = row_sum(*fed_sum) + vectors[5:6] + attended
     delta_rows = transpose_homes(after(delta.astype(LOW), shares[1]))
     output = tokens[0] + delta_rows.astype(WIDE)
-    *totals, out_total, down_total, vector_part = local_call(
+    *up_totals, down_total = local_call(
+        functools.partial(unfold_feed_kernel, parts, halves),
+        (meta, *feed_totals),
+        [low_like(shard, hidden_part)] * parts + [wide_like(hidden_shard, model)],
+    )
+    up_arrived = send_pieces(up_totals[1:], "dp")
+    *totals, out_total, vector_part = local_call(
         functools.partial(unfold_kernel, parts, halves),
-        (meta, *shares, *feed_totals),
-        [low_like(shard + 16, padded + hidden_part)] * parts
-        + [wide_like(shard, model), wide_like(hidden_shard, model), wide_like(16, 3 * width)],
+        (meta, after(shares[0], *up_arrived), *shares[1:]),
+        [low_like(shard + 16, 3 * width)] * parts
+        + [wide_like(shard, model), wide_like(16, 3 * width)],
         [pltpu.VMEM((shard * model // (3 * width), 3 * width), WIDE)],
     )
     qkv_total, up_total, vector_total = local_call(
         functools.partial(join_kernel, parts, width),
-        (meta, totals[0], *send_pieces(totals[1:], "dp")),
+        (meta, totals[0], *send_pieces(totals[1:], "dp"), up_totals[0], *up_arrived),
         [
             wide_like(shard, 3 * model),
             wide_like(shard, parts * hidden_part),

time: 248 us -> 240 us (0.968)
  waiting for transfers between devices: 109 us -> 91.9 us
  starting transfers between devices: 84 us -> 91 us
    ppermute x38 -> x41, waiting for transfers between devices: 91.5 us -> 68.9 us  [swap(): return lax.ppermute(value, axis, [(at, at ^ bit) for at in range(count)])]
    ppermute x12, starting transfers between devices: 18.4 us -> 28.8 us  [shift(): lax.ppermute(value, axis, [(at, (at + by) % count) for at in range(count)])]
    ppermute x12, waiting for transfers between devices: 17.2 us -> 23 us  [shift(): lax.ppermute(value, axis, [(at, (at + by) % count) for at in range(count)])]
    ppermute x38 -> x41, starting transfers between devices: 62.8 us -> 59.6 us  [swap(): return lax.ppermute(value, axis, [(at, at ^ bit) for at in range(count)])]
    pallas_call x19 -> x20, Pallas kernels: 43.5 us -> 44.8 us  [local_call(): pl.pallas_call(kernel, name=getattr(kernel, 'func', kernel).__name__, out...]
  transfers between devices with their start and end apart: 54 -> 57, of which waited for: 25 -> 26; matrix products, arithmetic and copies ran while one was open for 2% -> 2% of each run, Pallas kernels for 13% -> 15%
where the time goes in v11:
time: 240 us; the launch traced here: 239 us
  waiting for transfers between devices  91.9 us (38%)
  starting transfers between devices  91 us (38%)
  Pallas kernels  44.8 us (19%)
  local copies, waits for them, and re-layouts  5.65 us (2%)
  other arithmetic  4.87 us (2%)
    ppermute x41, waiting for transfers between devices, swap(): return lax.ppermute(value, axis, [(at, at ^ bit) for at in range(count)])  68.9 us
    ppermute x41, starting transfers between devices, swap(): return lax.ppermute(value, axis, [(at, at ^ bit) for at in range(count)])  59.6 us
    pallas_call x20, Pallas kernels, local_call(): pl.pallas_call(kernel, name=getattr(kernel, 'func', kernel).__name__, out...  44.8 us
    ppermute x12, starting transfers between devices, shift(): lax.ppermute(value, axis, [(at, (at + by) % count) for at in range(count)])  28.8 us
    ppermute x12, waiting for transfers between devices, shift(): lax.ppermute(value, axis, [(at, (at + by) % count) for at in range(count)])  23 us
  transfers between devices with their start and end apart: 57, of which 26 were waited for; matrix products, arithmetic and copies ran while one was open for 2% of the time, Pallas kernels for 15%

profile of v11, /device:TPU:0, one launch (start us, length us, event | category | flops | bytes accessed | tf_op | source)
XLA Modules:
  0.0 239.4 jit_solution(6164025359893451660)
XLA Ops:
  8.7 3.3 %collective-permute-done.1.refs_2_ = bf16[48,1408]{1,0:T(8,128)(2,1)S(1)} collective-permute-done((bf16[48,1408]{1,0:T(8,128)(2,1)S(1)}, bf16[48,1408]{1,0:T(8,128)(2,1)S(1)}, u32[]{:S(2)}, u32[]{:S(2)}) %collective-permute-start.1) | collective-permute-done | bytes 135200 | tf_op jit(solution)/shard_map/ppermute | solution.py:25
  16.1 6.0 %collective-permute-start.4 = (bf16[144,576]{1,0:T(8,128)(2,1)S(1)}, bf16[144,576]{1,0:T(8,128)(2,1)S(1)}, u32[]{:S(2)}, u32[]{:S(2)}) collective-permute-start(bf16[144,576]{1,0:T(8,128)(2,1)S(1)} %get-tuple-element.117.refs_4_.refs_1_), channel_id=1, source_target_pairs={{0,3},{1,2},{2,1},{3,0},{4,7},{5,6},{6,5},{7,4},{8,11},{9,10},{10,... | collective-permute-start | bytes 497672 | tf_op jit(solution)/shard_map/ppermute | solution.py:25
  22.1 8.2 %collective-permute-done.4.refs_7_.refs_4_ = bf16[144,576]{1,0:T(8,128)(2,1)S(1)} collective-permute-done((bf16[144,576]{1,0:T(8,128)(2,1)S(1)}, bf16[144,576]{1,0:T(8,128)(2,1)S(1)}, u32[]{:S(2)}, u32[]{:S(2)}) %collective-permute-start.4) | collective-permute-done | bytes 165920 | tf_op jit(solution)/shard_map/ppermute | solution.py:25
  30.3 5.2 %collective-permute-start.6 = (bf16[128,768]{1,0:T(8,128)(2,1)S(1)}, bf16[128,768]{1,0:T(8,128)(2,1)S(1)}, u32[]{:S(2)}, u32[]{:S(2)}) collective-permute-start(bf16[128,768]{1,0:T(8,128)(2,1)S(1)} %collective-permute-done.3.refs_0_.refs_3_), channel_id=1, source_target_pairs={{0,16},{8,24},{16,0},{24,8},{1,17},{9,25},{17,1},{25,9},{2,18},{10... | collective-permute-start | bytes 589832 | tf_op jit(solution)/shard_map/ppermute | solution.py:25
  35.5 2.7 %collective-permute-start.7 = (bf16[144,576]{1,0:T(8,128)(2,1)S(1)}, bf16[144,576]{1,0:T(8,128)(2,1)S(1)}, u32[]{:S(2)}, u32[]{:S(2)}) collective-permute-start(bf16[144,576]{1,0:T(8,128)(2,1)S(1)} %get-tuple-element.117.refs_4_.refs_1_), channel_id=1, source_target_pairs={{0,1},{1,0},{2,3},{3,2},{4,5},{5,4},{6,7},{7,6},{8,9},{9,8},{10,11... | collective-permute-start | bytes 497672 | tf_op jit(solution)/shard_map/ppermute | solution.py:25
  41.3 5.5 %collective-permute-done.7.refs_5_.refs_2_ = bf16[144,576]{1,0:T(8,128)(2,1)S(1)} collective-permute-done((bf16[144,576]{1,0:T(8,128)(2,1)S(1)}, bf16[144,576]{1,0:T(8,128)(2,1)S(1)}, u32[]{:S(2)}, u32[]{:S(2)}) %collective-permute-start.7) | collective-permute-done | bytes 165920 | tf_op jit(solution)/shard_map/ppermute | solution.py:25
  46.9 2.6 %collective-permute-start.14 = (bf16[192,768]{1,0:T(8,128)(2,1)S(1)}, bf16[192,768]{1,0:T(8,128)(2,1)S(1)}, u32[]{:S(2)}, u32[]{:S(2)}) collective-permute-start(bf16[192,768]{1,0:T(8,128)(2,1)S(1)} %get-tuple-element.124.refs_8_), channel_id=1, source_target_pairs={{0,2},{1,3},{2,0},{3,1},{4,6},{5,7},{6,4},{7,5},{8,10},{9,11},{10,... | collective-permute-start | bytes 884744 | tf_op jit(solution)/shard_map/ppermute | solution.py:25
  51.6 5.5 %collective-permute-done.11.refs_9_.refs_6_ = bf16[144,576]{1,0:T(8,128)(2,1)S(1)} collective-permute-done((bf16[144,576]{1,0:T(8,128)(2,1)S(1)}, bf16[144,576]{1,0:T(8,128)(2,1)S(1)}, u32[]{:S(2)}, u32[]{:S(2)}) %collective-permute-start.11) | collective-permute-done | bytes 165920 | tf_op jit(solution)/shard_map/ppermute | solution.py:30
  57.0 3.2 %collective-permute-done.12.refs_10_.refs_7_ = bf16[144,576]{1,0:T(8,128)(2,1)S(1)} collective-permute-done((bf16[144,576]{1,0:T(8,128)(2,1)S(1)}, bf16[144,576]{1,0:T(8,128)(2,1)S(1)}, u32[]{:S(2)}, u32[]{:S(2)}) %collective-permute-start.12) | collective-permute-done | bytes 165920 | tf_op jit(solution)/shard_map/ppermute | solution.py:30
  60.2 3.1 %project_kernel.1 = (bf16[512,576]{1,0:T(8,128)(2,1)S(1)}, bf16[512,384]{1,0:T(8,128)(2,1)S(1)}, bf16[768,576]{1,0:T(8,128)(2,1)S(1)}, bf16[512,768]{1,0:T(8,128)(2,1)S(1)}, f32[8,768]{1,0:T(8,128)S(1)}) custom-call(s32[6]{0:T(128)S(1)} %stack.33.meta_ref.place_ref, bf16[128,768]{1,0:T(8,128)(2,1)S(1)} %collective-permute-done.3.refs_0_.refs_3_, ...), custom_call_target="tpu_custom_call" | custom-call | flops 22649240 | bytes 239617 | tf_op jit(solution)/shard_map/project_kernel/pallas_call | solution.py:798
  64.9 3.4 %collective-permute-start.15 = (bf16[192,768]{1,0:T(8,128)(2,1)S(1)}, bf16[192,768]{1,0:T(8,128)(2,1)S(1)}, u32[]{:S(2)}, u32[]{:S(2)}) collective-permute-start(bf16[192,768]{1,0:T(8,128)(2,1)S(1)} %get-tuple-element.124.refs_8_), channel_id=1, source_target_pairs={{0,1},{1,0},{2,3},{3,2},{4,5},{5,4},{6,7},{7,6},{8,9},{9,8},{10,11... | collective-permute-start | bytes 884744 | tf_op jit(solution)/shard_map/ppermute | solution.py:25
  68.3 6.8 %own_forward.1 = (f32[512,192]{1,0:T(8,128)S(1)}, f32[512,128]{1,0:T(8,128)S(1)}) custom-call(s32[6]{0:T(128)S(1)} %stack.33.meta_ref.place_ref, bf16[512,576]{1,0:T(8,128)(2,1)S(1)} %get-tuple-element.125.kvq_ref.refs_5_.refs_0_), custom_call_target="tpu_custom_call" | custom-call | flops 10066329 | bytes 62260 | tf_op jit(solution)/shard_map/own_forward/pallas_call | solution.py:798
  75.7 5.1 %collective-permute-done.15.refs_9_ = bf16[192,768]{1,0:T(8,128)(2,1)S(1)} collective-permute-done((bf16[192,768]{1,0:T(8,128)(2,1)S(1)}, bf16[192,768]{1,0:T(8,128)(2,1)S(1)}, u32[]{:S(2)}, u32[]{:S(2)}) %collective-permute-start.15) | collective-permute-done | bytes 294944 | tf_op jit(solution)/shard_map/ppermute | solution.py:25
  85.7 3.2 %collective-permute-start.19 = (bf16[128,768]{1,0:T(8,128)(2,1)S(1)}, bf16[128,768]{1,0:T(8,128)(2,1)S(1)}, u32[]{:S(2)}, u32[]{:S(2)}) collective-permute-start(bf16[128,768]{1,0:T(8,128)(2,1)S(1)} %add_convert_fusion.5), channel_id=1, source_target_pairs={{0,16},{8,24},{16,0},{24,8},{1,17},{9,25},{17,1},{25,9},{2,18},{10... | collective-permute-start | bytes 589832 | tf_op jit(solution)/shard_map/ppermute | solution.py:25
  89.0 4.8 %collective-permute-start.27 = (bf16[192,768]{1,0:T(8,128)(2,1)S(1)}, bf16[192,768]{1,0:T(8,128)(2,1)S(1)}, u32[]{:S(2)}, u32[]{:S(2)}) collective-permute-start(bf16[192,768]{1,0:T(8,128)(2,1)S(1)} %collective-permute-done.15.refs_9_), channel_id=1, source_target_pairs={{0,4},{4,0},{1,5},{5,1},{2,6},{6,2},{3,7},{7,3},{8,12},{12,8},{9,1... | collective-permute-start | bytes 884744 | tf_op jit(solution)/shard_map/ppermute | solution.py:30
  93.7 5.4 %collective-permute-start.25 = (bf16[128,768]{1,0:T(8,128)(2,1)S(1)}, bf16[128,768]{1,0:T(8,128)(2,1)S(1)}, u32[]{:S(2)}, u32[]{:S(2)}) collective-permute-start(bf16[128,768]{1,0:T(8,128)(2,1)S(1)} %collective-permute-done.23.refs_4_.refs_5_), channel_id=1, source_target_pairs={{0,16},{8,24},{16,0},{24,8},{1,17},{9,25},{17,1},{25,9},{2,18},{10... | collective-permute-start | bytes 589832 | tf_op jit(solution)/shard_map/ppermute | solution.py:25
  100.6 5.5 %collective-permute-start.28 = (bf16[192,768]{1,0:T(8,128)(2,1)S(1)}, bf16[192,768]{1,0:T(8,128)(2,1)S(1)}, u32[]{:S(2)}, u32[]{:S(2)}) collective-permute-start(bf16[192,768]{1,0:T(8,128)(2,1)S(1)} %collective-permute-done.16.refs_11_), channel_id=1, source_target_pairs={{0,4},{4,0},{1,5},{5,1},{2,6},{6,2},{3,7},{7,3},{8,12},{12,8},{9,1... | collective-permute-start | bytes 884744 | tf_op jit(solution)/shard_map/ppermute | solution.py:30
  107.1 6.2 %collective-permute-done.28.refs_15_ = bf16[192,768]{1,0:T(8,128)(2,1)S(1)} collective-permute-done((bf16[192,768]{1,0:T(8,128)(2,1)S(1)}, bf16[192,768]{1,0:T(8,128)(2,1)S(1)}, u32[]{:S(2)}, u32[]{:S(2)}) %collective-permute-start.28) | collective-permute-done | bytes 294944 | tf_op jit(solution)/shard_map/ppermute | solution.py:30
  113.3 4.8 %feed_kernel.1 = (f32[256,768]{1,0:T(8,128)S(1)}, bf16[256,768]{1,0:T(8,128)(2,1)S(1)}, bf16[512,768]{1,0:T(8,128)(2,1)S(1)}, bf16[512,768]{1,0:T(8,128)(2,1)S(1...) custom-call(s32[6]{0:T(128)S(1)} %stack.33.meta_ref.place_ref, ...), custom_call_target="tpu_custom_call" | custom-call | flops 90596968 | bytes 473242 | tf_op jit(solution)/shard_map/feed_kernel/pallas_call | solution.py:798
  118.1 3.8 %feed_grad_kernel.1 = (f32[4,192,768]{2,1,0:T(8,128)S(1)}, bf16[4,192,768]{2,1,0:T(8,128)(2,1)S(1)}, f32[256,768]{1,0:T(8,128)S(1)}, bf16[256,768]{1,0:T(8,128)(2,1)S(1)}) custom-call(s32[6]{0:T(128)S(1)} %stack.33.meta_ref.place_ref, bf16[512,768]{1,0:T(8,128)(2,1)S(1)} %get-tuple-element.138.refs_0_, bf16[512,768]{1,0:T(8,128)(2,1)S(1)} %get-tuple-element.139.refs_1_, ...), custom_call_target="tpu_custom_call" | custom-call | flops 90596968 | bytes 452199 | tf_op jit(solution)/shard_map/feed_grad_kernel/pallas_call | solution.py:798
  125.2 5.7 %collective-permute-done.30.refs_2_ = bf16[128,768]{1,0:T(8,128)(2,1)S(1)} collective-permute-done((bf16[128,768]{1,0:T(8,128)(2,1)S(1)}, bf16[128,768]{1,0:T(8,128)(2,1)S(1)}, u32[]{:S(2)}, u32[]{:S(2)}) %collective-permute-start.30) | collective-permute-done | bytes 196640 | tf_op jit(solution)/shard_map/ppermute | solution.py:25
  133.1 5.0 %collective-permute-done.31.refs_2_ = bf16[128,768]{1,0:T(8,128)(2,1)S(1)} collective-permute-done((bf16[128,768]{1,0:T(8,128)(2,1)S(1)}, bf16[128,768]{1,0:T(8,128)(2,1)S(1)}, u32[]{:S(2)}, u32[]{:S(2)}) %collective-permute-start.31) | collective-permute-done | bytes 196640 | tf_op jit(solution)/shard_map/ppermute | solution.py:25
  142.5 6.5 %collective-permute-start.38 = (bf16[512,384]{1,0:T(8,128)(2,1)S(1)}, bf16[512,384]{1,0:T(8,128)(2,1)S(1)}, u32[]{:S(2)}, u32[]{:S(2)}) collective-permute-start(bf16[512,384]{1,0:T(8,128)(2,1)S(1)} %bitcast.43), channel_id=1, source_target_pairs={{0,4},{4,0},{1,5},{5,1},{2,6},{6,2},{3,7},{7,3},{8,12},{12,8},{9,1... | collective-permute-start | bytes 1179656 | tf_op jit(solution)/shard_map/ppermute | solution.py:30
  153.9 6.8 %own_grad_kernel.1 = (f32[512,576]{1,0:T(8,128)S(1)}, f32[192,768]{1,0:T(8,128)S(1)}) custom-call(s32[6]{0:T(128)S(1)} %stack.33.meta_ref.place_ref, bf16[512,576]{1,0:T(8,128)(2,1)S(1)} %get-tuple-element.125.kvq_ref.refs_5_.refs_0_, bf16[512,192]{1,0:T(8,128)(2,1)S(1)} %get-tuple-element.155.refs_1_, f32[512,192]{1,0:T(8,128)S(1)} %get-tuple-element.153.refs_7_.refs_2_, ...), custom_call_target="tpu_custom_call" | custom-call | flops 25165824 | bytes 229377 | tf_op jit(solution)/shard_map/own_grad_kernel/pallas_call | solution.py:798
  164.7 3.4 %collective-permute-start.40 = (bf16[192,768]{1,0:T(8,128)(2,1)}, bf16[192,768]{1,0:T(8,128)(2,1)}, u32[]{:S(2)}, u32[]{:S(2)}) collective-permute-start(bf16[192,768]{1,0:T(8,128)(2,1)} %get-tuple-element.174), channel_id=1, source_target_pairs={{0,1},{1,0},{2,3},{3,2},{4,5},{5,4},{6,7},{7,6},{8,9},{9,8},{10,11... | collective-permute-start | bytes 884744 | tf_op jit(solution)/shard_map/ppermute | solution.py:25
  168.9 2.8 %projection_grad_kernel.1 = (f32[4,128,576]{2,1,0:T(8,128)S(1)}, bf16[4,144,576]{2,1,0:T(8,128)(2,1)}) custom-call(s32[6]{0:T(128)S(1)} %stack.33.meta_ref.place_ref, bf16[512,768]{1,0:T(8,128)(2,1)S(1)} %get-tuple-element.151.refs_0_, bf16[512,576]{1,0:T(8,128)(2,1)S(1)} %get-tuple-element.170.refs_1_, f32[192,768]{1,0:T(8,128)S(1)} %get-tuple-element.171.refs_2_), custom_call_target="tpu_custom_call" | custom-call | flops 22649240 | bytes 190465 | tf_op jit(solution)/shard_map/projection_grad_kernel/pallas_call | solution.py:798
  174.8 5.9 %collective-permute-done.43.refs_2_ = bf16[128,768]{1,0:T(8,128)(2,1)} collective-permute-done((bf16[128,768]{1,0:T(8,128)(2,1)}, bf16[128,768]{1,0:T(8,128)(2,1)}, u32[]{:S(2)}, u32[]{:S(2)}) %collective-permute-start.43) | collective-permute-done | bytes 196640 | tf_op jit(solution)/shard_map/ppermute | solution.py:25
  182.1 2.7 %collective-permute-done.41 = bf16[192,768]{1,0:T(8,128)(2,1)} collective-permute-done((bf16[192,768]{1,0:T(8,128)(2,1)}, bf16[192,768]{1,0:T(8,128)(2,1)}, u32[]{:S(2)}, u32[]{:S(2)}) %collective-permute-start.41) | collective-permute-done | bytes 294944 | tf_op jit(solution)/shard_map/ppermute | solution.py:25
  187.6 3.7 %collective-permute-done.42.arrived = bf16[4,144,576]{2,1,0:T(8,128)(2,1)} collective-permute-done((bf16[4,144,576]{2,1,0:T(8,128)(2,1)}, bf16[4,144,576]{2,1,0:T(8,128)(2,1)}, u32[]{:S(2)}, u32[]{:S(2)}) %collective-permute-start.42) | collective-permute-done | bytes 663584 | tf_op jit(solution)/shard_map/ppermute | solution.py:30
  203.8 11.8 %collective-permute-done.45 = bf16[144,576]{1,0:T(8,128)(2,1)S(1)} collective-permute-done((bf16[144,576]{1,0:T(8,128)(2,1)S(1)}, bf16[144,576]{1,0:T(8,128)(2,1)S(1)}, u32[]{:S(2)}, u32[]{:S(2)}) %collective-permute-start.45) | collective-permute-done | bytes 165920 | tf_op jit(solution)/shard_map/ppermute | solution.py:25
  223.3 6.2 %collective-permute-start.55 = (bf16[64,576]{1,0:T(8,128)(2,1)S(1)}, bf16[64,576]{1,0:T(8,128)(2,1)S(1)}, u32[]{:S(2)}, u32[]{:S(2)}) collective-permute-start(bf16[64,576]{1,0:T(8,128)(2,1)S(1)} %get-tuple-element.200), channel_id=1, source_target_pairs={{0,16},{8,24},{16,0},{24,8},{1,17},{9,25},{17,1},{25,9},{2,18},{10... | collective-permute-start | bytes 221192 | tf_op jit(solution)/shard_map/ppermute | solution.py:25
  230.9 3.1 %collective-permute-done.55.refs_2_ = bf16[64,576]{1,0:T(8,128)(2,1)S(1)} collective-permute-done((bf16[64,576]{1,0:T(8,128)(2,1)S(1)}, bf16[64,576]{1,0:T(8,128)(2,1)S(1)}, u32[]{:S(2)}, u32[]{:S(2)}) %collective-permute-start.55) | collective-permute-done | bytes 73760 | tf_op jit(solution)/shard_map/ppermute | solution.py:25
  (154 shorter events, 80.4 us)
Async XLA Ops:
  14.4 15.9 %collective-permute-start.3 = (bf16[128,768]{1,0:T(8,128)(2,1)S(1)}, bf16[128,768]{1,0:T(8,128)(2,1)S(1)}, u32[]{:S(2)}, u32[]{:S(2)}) collective-permute-start(bf16[128,768]{1,0:T(8,128)(2,1)S(1)} %bitcast_convert_fusion.1), channel_id=1, source_target_pairs={{0,0},{1,8},{2,16},{3,24},{8,1},{9,9},{10,17},{11,25},{16,2},{17,1... | collective-permute-start | bytes 589832 | tf_op jit(solution)/shard_map/ppermute | solution.py:36
  16.1 14.2 %collective-permute-start.4 = (bf16[144,576]{1,0:T(8,128)(2,1)S(1)}, bf16[144,576]{1,0:T(8,128)(2,1)S(1)}, u32[]{:S(2)}, u32[]{:S(2)}) collective-permute-start(bf16[144,576]{1,0:T(8,128)(2,1)S(1)} %get-tuple-element.117.refs_4_.refs_1_), channel_id=1, source_target_pairs={{0,3},{1,2},{2,1},{3,0},{4,7},{5,6},{6,5},{7,4},{8,11},{9,10},{10,... | collective-permute-start | bytes 497672 | tf_op jit(solution)/shard_map/ppermute | solution.py:25
  30.3 16.5 %collective-permute-start.6 = (bf16[128,768]{1,0:T(8,128)(2,1)S(1)}, bf16[128,768]{1,0:T(8,128)(2,1)S(1)}, u32[]{:S(2)}, u32[]{:S(2)}) collective-permute-start(bf16[128,768]{1,0:T(8,128)(2,1)S(1)} %collective-permute-done.3.refs_0_.refs_3_), channel_id=1, source_target_pairs={{0,16},{8,24},{16,0},{24,8},{1,17},{9,25},{17,1},{25,9},{2,18},{10... | collective-permute-start | bytes 589832 | tf_op jit(solution)/shard_map/ppermute | solution.py:25
  35.5 11.4 %collective-permute-start.7 = (bf16[144,576]{1,0:T(8,128)(2,1)S(1)}, bf16[144,576]{1,0:T(8,128)(2,1)S(1)}, u32[]{:S(2)}, u32[]{:S(2)}) collective-permute-start(bf16[144,576]{1,0:T(8,128)(2,1)S(1)} %get-tuple-element.117.refs_4_.refs_1_), channel_id=1, source_target_pairs={{0,1},{1,0},{2,3},{3,2},{4,5},{5,4},{6,7},{7,6},{8,9},{9,8},{10,11... | collective-permute-start | bytes 497672 | tf_op jit(solution)/shard_map/ppermute | solution.py:25
  41.3 18.9 %collective-permute-start.5 = (bf16[128,768]{1,0:T(8,128)(2,1)S(1)}, bf16[128,768]{1,0:T(8,128)(2,1)S(1)}, u32[]{:S(2)}, u32[]{:S(2)}) collective-permute-start(bf16[128,768]{1,0:T(8,128)(2,1)S(1)} %collective-permute-done.3.refs_0_.refs_3_), channel_id=1, source_target_pairs={{0,8},{8,0},{16,24},{24,16},{1,9},{9,1},{17,25},{25,17},{2,10},{10... | collective-permute-start | bytes 589832 | tf_op jit(solution)/shard_map/ppermute | solution.py:25
  46.8 13.4 %collective-permute-start.10 = (bf16[128,768]{1,0:T(8,128)(2,1)S(1)}, bf16[128,768]{1,0:T(8,128)(2,1)S(1)}, u32[]{:S(2)}, u32[]{:S(2)}) collective-permute-start(bf16[128,768]{1,0:T(8,128)(2,1)S(1)} %collective-permute-done.6.refs_2_), channel_id=1, source_target_pairs={{0,8},{8,0},{16,24},{24,16},{1,9},{9,1},{17,25},{25,17},{2,10},{10... | collective-permute-start | bytes 589832 | tf_op jit(solution)/shard_map/ppermute | solution.py:25
  46.9 21.4 %collective-permute-start.14 = (bf16[192,768]{1,0:T(8,128)(2,1)S(1)}, bf16[192,768]{1,0:T(8,128)(2,1)S(1)}, u32[]{:S(2)}, u32[]{:S(2)}) collective-permute-start(bf16[192,768]{1,0:T(8,128)(2,1)S(1)} %get-tuple-element.124.refs_8_), channel_id=1, source_target_pairs={{0,2},{1,3},{2,0},{3,1},{4,6},{5,7},{6,4},{7,5},{8,10},{9,11},{10,... | collective-permute-start | bytes 884744 | tf_op jit(solution)/shard_map/ppermute | solution.py:25
  63.3 17.5 %collective-permute-start.13 = (bf16[512,384]{1,0:T(8,128)(2,1)S(1)}, bf16[512,384]{1,0:T(8,128)(2,1)S(1)}, u32[]{:S(2)}, u32[]{:S(2)}) collective-permute-start(bf16[512,384]{1,0:T(8,128)(2,1)S(1)} %get-tuple-element.122), channel_id=1, source_target_pairs={{0,4},{4,0},{1,5},{5,1},{2,6},{6,2},{3,7},{7,3},{8,12},{12,8},{9,1... | collective-permute-start | bytes 1179656 | tf_op jit(solution)/shard_map/ppermute | solution.py:30
  64.9 15.9 %collective-permute-start.15 = (bf16[192,768]{1,0:T(8,128)(2,1)S(1)}, bf16[192,768]{1,0:T(8,128)(2,1)S(1)}, u32[]{:S(2)}, u32[]{:S(2)}) collective-permute-start(bf16[192,768]{1,0:T(8,128)(2,1)S(1)} %get-tuple-element.124.refs_8_), channel_id=1, source_target_pairs={{0,1},{1,0},{2,3},{3,2},{4,5},{5,4},{6,7},{7,6},{8,9},{9,8},{10,11... | collective-permute-start | bytes 884744 | tf_op jit(solution)/shard_map/ppermute | solution.py:25
  68.3 13.7 %collective-permute-start.16 = (bf16[192,768]{1,0:T(8,128)(2,1)S(1)}, bf16[192,768]{1,0:T(8,128)(2,1)S(1)}, u32[]{:S(2)}, u32[]{:S(2)}) collective-permute-start(bf16[192,768]{1,0:T(8,128)(2,1)S(1)} %get-tuple-element.124.refs_8_), channel_id=1, source_target_pairs={{0,3},{1,2},{2,1},{3,0},{4,7},{5,6},{6,5},{7,4},{8,11},{9,10},{10,... | collective-permute-start | bytes 884744 | tf_op jit(solution)/shard_map/ppermute | solution.py:25
  84.0 9.8 %collective-permute-start.23 = (bf16[128,768]{1,0:T(8,128)(2,1)S(1)}, bf16[128,768]{1,0:T(8,128)(2,1)S(1)}, u32[]{:S(2)}, u32[]{:S(2)}) collective-permute-start(bf16[128,768]{1,0:T(8,128)(2,1)S(1)} %bitcast_convert_fusion), channel_id=1, source_target_pairs={{0,0},{1,8},{2,16},{3,24},{8,1},{9,9},{10,17},{11,25},{16,2},{17,1... | collective-permute-start | bytes 589832 | tf_op jit(solution)/shard_map/ppermute | solution.py:36
  85.7 13.4 %collective-permute-start.19 = (bf16[128,768]{1,0:T(8,128)(2,1)S(1)}, bf16[128,768]{1,0:T(8,128)(2,1)S(1)}, u32[]{:S(2)}, u32[]{:S(2)}) collective-permute-start(bf16[128,768]{1,0:T(8,128)(2,1)S(1)} %add_convert_fusion.5), channel_id=1, source_target_pairs={{0,16},{8,24},{16,0},{24,8},{1,17},{9,25},{17,1},{25,9},{2,18},{10... | collective-permute-start | bytes 589832 | tf_op jit(solution)/shard_map/ppermute | solution.py:25
  89.0 17.6 %collective-permute-start.27 = (bf16[192,768]{1,0:T(8,128)(2,1)S(1)}, bf16[192,768]{1,0:T(8,128)(2,1)S(1)}, u32[]{:S(2)}, u32[]{:S(2)}) collective-permute-start(bf16[192,768]{1,0:T(8,128)(2,1)S(1)} %collective-permute-done.15.refs_9_), channel_id=1, source_target_pairs={{0,4},{4,0},{1,5},{5,1},{2,6},{6,2},{3,7},{7,3},{8,12},{12,8},{9,1... | collective-permute-start | bytes 884744 | tf_op jit(solution)/shard_map/ppermute | solution.py:30
  93.7 12.3 %collective-permute-start.25 = (bf16[128,768]{1,0:T(8,128)(2,1)S(1)}, bf16[128,768]{1,0:T(8,128)(2,1)S(1)}, u32[]{:S(2)}, u32[]{:S(2)}) collective-permute-start(bf16[128,768]{1,0:T(8,128)(2,1)S(1)} %collective-permute-done.23.refs_4_.refs_5_), channel_id=1, source_target_pairs={{0,16},{8,24},{16,0},{24,8},{1,17},{9,25},{17,1},{25,9},{2,18},{10... | collective-permute-start | bytes 589832 | tf_op jit(solution)/shard_map/ppermute | solution.py:25
  100.6 12.7 %collective-permute-start.28 = (bf16[192,768]{1,0:T(8,128)(2,1)S(1)}, bf16[192,768]{1,0:T(8,128)(2,1)S(1)}, u32[]{:S(2)}, u32[]{:S(2)}) collective-permute-start(bf16[192,768]{1,0:T(8,128)(2,1)S(1)} %collective-permute-done.16.refs_11_), channel_id=1, source_target_pairs={{0,4},{4,0},{1,5},{5,1},{2,6},{6,2},{3,7},{7,3},{8,12},{12,8},{9,1... | collective-permute-start | bytes 884744 | tf_op jit(solution)/shard_map/ppermute | solution.py:30
  122.0 28.7 %collective-permute-start.36 = (bf16[4,192,768]{2,1,0:T(8,128)(2,1)S(1)}, bf16[4,192,768]{2,1,0:T(8,128)(2,1)S(1)}, u32[]{:S(2)}, u32[]{:S(2)}) collective-permute-start(bf16[4,192,768]{2,1,0:T(8,128)(2,1)S(1)} %get-tuple-element.159), channel_id=1, source_target_pairs={{0,4},{4,0},{1,5},{5,1},{2,6},{6,2},{3,7},{7,3},{8,12},{12,8},{9,1... | collective-permute-start | bytes 3538952 | tf_op jit(solution)/shard_map/ppermute | solution.py:30
  139.6 13.7 %collective-permute-start.33 = (bf16[256,768]{1,0:T(8,128)(2,1)S(1)}, bf16[256,768]{1,0:T(8,128)(2,1)S(1)}, u32[]{:S(2)}, u32[]{:S(2)}) collective-permute-start(bf16[256,768]{1,0:T(8,128)(2,1)S(1)} %get-tuple-element.150), channel_id=1, source_target_pairs={{0,8},{8,0},{16,24},{24,16},{1,9},{9,1},{17,25},{25,17},{2,10},{10... | collective-permute-start | bytes 1179656 | tf_op jit(solution)/shard_map/ppermute | solution.py:25
  142.5 20.0 %collective-permute-start.38 = (bf16[512,384]{1,0:T(8,128)(2,1)S(1)}, bf16[512,384]{1,0:T(8,128)(2,1)S(1)}, u32[]{:S(2)}, u32[]{:S(2)}) collective-permute-start(bf16[512,384]{1,0:T(8,128)(2,1)S(1)} %bitcast.43), channel_id=1, source_target_pairs={{0,4},{4,0},{1,5},{5,1},{2,6},{6,2},{3,7},{7,3},{8,12},{12,8},{9,1... | collective-permute-start | bytes 1179656 | tf_op jit(solution)/shard_map/ppermute | solution.py:30
  152.3 10.2 %collective-permute-start.37 = (bf16[192,768]{1,0:T(8,128)(2,1)S(1)}, bf16[192,768]{1,0:T(8,128)(2,1)S(1)}, u32[]{:S(2)}, u32[]{:S(2)}) collective-permute-start(bf16[192,768]{1,0:T(8,128)(2,1)S(1)} %get-tuple-element.164), channel_id=1, source_target_pairs={{0,3},{1,2},{2,1},{3,0},{4,7},{5,6},{6,5},{7,4},{8,11},{9,10},{10,... | collective-permute-start | bytes 884744 | tf_op jit(solution)/shard_map/ppermute | solution.py:25
  153.3 9.2 %collective-permute-start.34 = (bf16[128,768]{1,0:T(8,128)(2,1)S(1)}, bf16[128,768]{1,0:T(8,128)(2,1)S(1)}, u32[]{:S(2)}, u32[]{:S(2)}) collective-permute-start(bf16[128,768]{1,0:T(8,128)(2,1)S(1)} %add_convert_fusion.3), channel_id=1, source_target_pairs={{0,16},{8,24},{16,0},{24,8},{1,17},{9,25},{17,1},{25,9},{2,18},{10... | collective-permute-start | bytes 589832 | tf_op jit(solution)/shard_map/ppermute | solution.py:25
  164.7 17.4 %collective-permute-start.40 = (bf16[192,768]{1,0:T(8,128)(2,1)}, bf16[192,768]{1,0:T(8,128)(2,1)}, u32[]{:S(2)}, u32[]{:S(2)}) collective-permute-start(bf16[192,768]{1,0:T(8,128)(2,1)} %get-tuple-element.174), channel_id=1, source_target_pairs={{0,1},{1,0},{2,3},{3,2},{4,5},{5,4},{6,7},{7,6},{8,9},{9,8},{10,11... | collective-permute-start | bytes 884744 | tf_op jit(solution)/shard_map/ppermute | solution.py:25
  168.1 16.7 %collective-permute-start.41 = (bf16[192,768]{1,0:T(8,128)(2,1)}, bf16[192,768]{1,0:T(8,128)(2,1)}, u32[]{:S(2)}, u32[]{:S(2)}) collective-permute-start(bf16[192,768]{1,0:T(8,128)(2,1)} %get-tuple-element.176), channel_id=1, source_target_pairs={{0,2},{1,3},{2,0},{3,1},{4,6},{5,7},{6,4},{7,5},{8,10},{9,11},{10,... | collective-permute-start | bytes 884744 | tf_op jit(solution)/shard_map/ppermute | solution.py:25
  171.7 19.7 %collective-permute-start.42 = (bf16[4,144,576]{2,1,0:T(8,128)(2,1)}, bf16[4,144,576]{2,1,0:T(8,128)(2,1)}, u32[]{:S(2)}, u32[]{:S(2)}) collective-permute-start(bf16[4,144,576]{2,1,0:T(8,128)(2,1)} %get-tuple-element.178), channel_id=1, source_target_pairs={{0,4},{4,0},{1,5},{5,1},{2,6},{6,2},{3,7},{7,3},{8,12},{12,8},{9,1... | collective-permute-start | bytes 1990664 | tf_op jit(solution)/shard_map/ppermute | solution.py:30
  186.0 11.9 %collective-permute-start.50 = (bf16[192,768]{1,0:T(8,128)(2,1)S(1)}, bf16[192,768]{1,0:T(8,128)(2,1)S(1)}, u32[]{:S(2)}, u32[]{:S(2)}) collective-permute-start(bf16[192,768]{1,0:T(8,128)(2,1)S(1)} %add_convert_fusion.mine), channel_id=1, source_target_pairs={{0,4},{4,0},{1,5},{5,1},{2,6},{6,2},{3,7},{7,3},{8,12},{12,8},{9,1... | collective-permute-start | bytes 884744 | tf_op jit(solution)/shard_map/ppermute | solution.py:30
  192.6 9.4 %collective-permute-start.46 = (bf16[144,576]{1,0:T(8,128)(2,1)S(1)}, bf16[144,576]{1,0:T(8,128)(2,1)S(1)}, u32[]{:S(2)}, u32[]{:S(2)}) collective-permute-start(bf16[144,576]{1,0:T(8,128)(2,1)S(1)} %get-tuple-element.189), channel_id=1, source_target_pairs={{0,3},{1,2},{2,1},{3,0},{4,7},{5,6},{6,5},{7,4},{8,11},{9,10},{10,... | collective-permute-start | bytes 497672 | tf_op jit(solution)/shard_map/ppermute | solution.py:25
  194.3 21.3 %collective-permute-start.45 = (bf16[144,576]{1,0:T(8,128)(2,1)S(1)}, bf16[144,576]{1,0:T(8,128)(2,1)S(1)}, u32[]{:S(2)}, u32[]{:S(2)}) collective-permute-start(bf16[144,576]{1,0:T(8,128)(2,1)S(1)} %get-tuple-element.188), channel_id=1, source_target_pairs={{0,2},{1,3},{2,0},{3,1},{4,6},{5,7},{6,4},{7,5},{8,10},{9,11},{10,... | collective-permute-start | bytes 497672 | tf_op jit(solution)/shard_map/ppermute | solution.py:25
  196.1 19.5 %collective-permute-start.44 = (bf16[144,576]{1,0:T(8,128)(2,1)S(1)}, bf16[144,576]{1,0:T(8,128)(2,1)S(1)}, u32[]{:S(2)}, u32[]{:S(2)}) collective-permute-start(bf16[144,576]{1,0:T(8,128)(2,1)S(1)} %get-tuple-element.187), channel_id=1, source_target_pairs={{0,1},{1,0},{2,3},{3,2},{4,5},{5,4},{6,7},{7,6},{8,9},{9,8},{10,11... | collective-permute-start | bytes 497672 | tf_op jit(solution)/shard_map/ppermute | solution.py:25
  197.2 18.5 %collective-permute-start.47 = (bf16[128,768]{1,0:T(8,128)(2,1)S(1)}, bf16[128,768]{1,0:T(8,128)(2,1)S(1)}, u32[]{:S(2)}, u32[]{:S(2)}) collective-permute-start(bf16[128,768]{1,0:T(8,128)(2,1)S(1)} %get-tuple-element.190), channel_id=1, source_target_pairs={{0,0},{1,8},{2,16},{3,24},{8,1},{9,9},{10,17},{11,25},{16,2},{17,1... | collective-permute-start | bytes 589832 | tf_op jit(solution)/shard_map/ppermute | solution.py:36
  199.3 18.7 %collective-permute-start.51 = (bf16[48,768]{1,0:T(8,128)(2,1)S(1)}, bf16[48,768]{1,0:T(8,128)(2,1)S(1)}, u32[]{:S(2)}, u32[]{:S(2)}) collective-permute-start(bf16[48,768]{1,0:T(8,128)(2,1)S(1)} %get-tuple-element.194), channel_id=1, source_target_pairs={{0,8},{8,0},{16,24},{24,16},{1,9},{9,1},{17,25},{25,17},{2,10},{10... | collective-permute-start | bytes 221192 | tf_op jit(solution)/shard_map/ppermute | solution.py:25
  202.1 16.0 %collective-permute-start.52 = (bf16[48,768]{1,0:T(8,128)(2,1)S(1)}, bf16[48,768]{1,0:T(8,128)(2,1)S(1)}, u32[]{:S(2)}, u32[]{:S(2)}) collective-permute-start(bf16[48,768]{1,0:T(8,128)(2,1)S(1)} %get-tuple-element.195), channel_id=1, source_target_pairs={{0,16},{8,24},{16,0},{24,8},{1,17},{9,25},{17,1},{25,9},{2,18},{10... | collective-permute-start | bytes 221192 | tf_op jit(solution)/shard_map/ppermute | solution.py:25
  221.3 17.2 %collective-permute-start.49 = (bf16[128,768]{1,0:T(8,128)(2,1)S(1)}, bf16[128,768]{1,0:T(8,128)(2,1)S(1)}, u32[]{:S(2)}, u32[]{:S(2)}) collective-permute-start(bf16[128,768]{1,0:T(8,128)(2,1)S(1)} %add_convert_fusion.2), channel_id=1, source_target_pairs={{0,0},{1,8},{2,16},{3,24},{8,1},{9,9},{10,17},{11,25},{16,2},{17,1... | collective-permute-start | bytes 589832 | tf_op jit(solution)/shard_map/ppermute | solution.py:36
  223.3 10.7 %collective-permute-start.55 = (bf16[64,576]{1,0:T(8,128)(2,1)S(1)}, bf16[64,576]{1,0:T(8,128)(2,1)S(1)}, u32[]{:S(2)}, u32[]{:S(2)}) collective-permute-start(bf16[64,576]{1,0:T(8,128)(2,1)S(1)} %get-tuple-element.200), channel_id=1, source_target_pairs={{0,16},{8,24},{16,0},{24,8},{1,17},{9,25},{17,1},{25,9},{2,18},{10... | collective-permute-start | bytes 221192 | tf_op jit(solution)/shard_map/ppermute | solution.py:25
  (42 other events, 325.5 us)

commit v12 on v11

--- a/solution.py
+++ b/solution.py
@@ -869,8 +869,8 @@
     else:
         kvq_other = gather_direct(kvq_theirs, "fsdp")
 
-    token_rows = transpose_homes(after(tokens[0].astype(LOW), *split_arrived))
-    pieces = gather_pieces(after(token_rows, kvq_own[-1]), *kvq_own[1:], kvq_other[-1])
+    token_rows = transpose_homes(after(tokens[0].astype(LOW), kvq_mine))
+    pieces = gather_pieces(after(token_rows, kvq_own[-1]), *kvq_own[1:], kvq_other[1], kvq_other[-1])
 
     kvq, kv, kvq_matrix, norm1_all, vectors = local_call(
         functools.partial(project_kernel, parts, depth, halves),
@@ -1058,30 +1058,30 @@
         shape = (share_rows + 16, 3 * width)
         share_keep, *share_sends = local_call(
             fold_share_kernel,
-            (meta, after(kept_share, *half_pieces[:-1]), shift(sent_share, "ctx", 1), sums),
+            (meta, after(kept_share, input_rows, *half_pieces[:-1]), shift(sent_share, "ctx", 1), sums),
             [wide_like(*shape)] + [low_like(*shape)] * (depth - 1),
             [pltpu.VMEM((16, 3 * width), WIDE)],
         )
         share_pieces = send_pieces(share_sends, "fsdp")
-        mine_half = sum_all(after(half_keep, input_part), half_pieces).astype(LOW)
+        mine_half = sum_all(after(half_keep, input_rows), half_pieces).astype(LOW)
         feed_totals = (mine_half, shift(mine_half, "ctx", 1))
         mine_share = sum_all(share_keep, share_pieces).astype(LOW)
-        shares = (mine_share, shift(after(mine_share, input_rows), "ctx", 1))
+        shares = (mine_share, shift(mine_share, "ctx", 1))
     else:
         share_pieces = []
         feed_totals = direct_totals(kept_half, sent_half[0])
         shares = (
             *direct_totals(kept_share, sent_share[:, :share_rows]), sum_replicas(sum_doubling(sums, "fsdp"))
         )
-    delta = row_sum(*fed_sum) + vectors[5:6] + attended
-    delta_rows = transpose_homes(after(delta.astype(LOW), shares[1]))
-    output = tokens[0] + delta_rows.astype(WIDE)
     *up_totals, down_total = local_call(
         functools.partial(unfold_feed_kernel, parts, halves),
         (meta, *feed_totals),
         [low_like(shard, hidden_part)] * parts + [wide_like(hidden_shard, model)],
     )
     up_arrived = send_pieces(up_totals[1:], "dp")
+    delta = row_sum(*fed_sum) + vectors[5:6] + attended
+    delta_rows = transpose_homes(after(delta.astype(LOW), up_arrived[0], *share_pieces))
+    output = tokens[0] + delta_rows.astype(WIDE)
     *totals, out_total, vector_part = local_call(
         functools.partial(unfold_kernel, parts, halves),
         (meta, after(shares[0], *up_arrived), *shares[1:]),

time: 240 us -> 240 us (level)
  starting transfers between devices: 91 us -> 98.4 us
  waiting for transfers between devices: 91.9 us -> 87.3 us
    ppermute x41, waiting for transfers between devices: 68.9 us -> 61.5 us  [swap(): return lax.ppermute(value, axis, [(at, at ^ bit) for at in range(count)])]
    ppermute x12, starting transfers between devices: 28.8 us -> 35.8 us  [shift(): lax.ppermute(value, axis, [(at, (at + by) % count) for at in range(count)])]
    ppermute x12, waiting for transfers between devices: 23 us -> 25.8 us  [shift(): lax.ppermute(value, axis, [(at, (at + by) % count) for at in range(count)])]
  transfers between devices with their start and end apart: 57 -> 57, of which waited for: 26 -> 23; matrix products, arithmetic and copies ran while one was open for 2% -> 2% of each run, Pallas kernels for 15% -> 14%
where the time goes in v12:
time: 240 us
  starting transfers between devices  98.4 us (41%)
  waiting for transfers between devices  87.3 us (36%)
  Pallas kernels  43.5 us (18%)
  local copies, waits for them, and re-layouts  6.35 us (3%)
  other arithmetic  3.13 us (1%)
    ppermute x41, waiting for transfers between devices, swap(): return lax.ppermute(value, axis, [(at, at ^ bit) for at in range(count)])  61.5 us
    ppermute x41, starting transfers between devices, swap(): return lax.ppermute(value, axis, [(at, at ^ bit) for at in range(count)])  60 us
    pallas_call x20, Pallas kernels, local_call(): pl.pallas_call(kernel, name=getattr(kernel, 'func', kernel).__name__, out...  43.5 us
    ppermute x12, starting transfers between devices, shift(): lax.ppermute(value, axis, [(at, (at + by) % count) for at in range(count)])  35.8 us
    ppermute x12, waiting for transfers between devices, shift(): lax.ppermute(value, axis, [(at, (at + by) % count) for at in range(count)])  25.8 us
  transfers between devices with their start and end apart: 57, of which 23 were waited for; matrix products, arithmetic and copies ran while one was open for 2% of the time, Pallas kernels for 14%

profile of v12, /device:TPU:0, one launch (start us, length us, event | category | flops | bytes accessed | tf_op | source)
XLA Modules:
  0.0 239.7 jit_solution(4616047757488785791)
XLA Ops:
  5.0 2.6 %collective-permute-start.1 = (bf16[48,1408]{1,0:T(8,128)(2,1)S(1)}, bf16[48,1408]{1,0:T(8,128)(2,1)S(1)}, u32[]{:S(2)}, u32[]{:S(2)}) collective-permute-start(bf16[48,1408]{1,0:T(8,128)(2,1)S(1)} %get-tuple-element.113), channel_id=1, source_target_pairs={{0,16},{8,24},{16,0},{24,8},{1,17},{9,25},{17,1},{25,9},{2,18},{10... | collective-permute-start | bytes 405512 | tf_op jit(solution)/shard_map/ppermute | solution.py:25
  8.7 3.3 %collective-permute-done.1.refs_2_ = bf16[48,1408]{1,0:T(8,128)(2,1)S(1)} collective-permute-done((bf16[48,1408]{1,0:T(8,128)(2,1)S(1)}, bf16[48,1408]{1,0:T(8,128)(2,1)S(1)}, u32[]{:S(2)}, u32[]{:S(2)}) %collective-permute-start.1) | collective-permute-done | bytes 135200 | tf_op jit(solution)/shard_map/ppermute | solution.py:25
  16.1 6.0 %collective-permute-start.4 = (bf16[144,576]{1,0:T(8,128)(2,1)S(1)}, bf16[144,576]{1,0:T(8,128)(2,1)S(1)}, u32[]{:S(2)}, u32[]{:S(2)}) collective-permute-start(bf16[144,576]{1,0:T(8,128)(2,1)S(1)} %get-tuple-element.115.refs_4_.refs_1_), channel_id=1, source_target_pairs={{0,3},{1,2},{2,1},{3,0},{4,7},{5,6},{6,5},{7,4},{8,11},{9,10},{10,... | collective-permute-start | bytes 497672 | tf_op jit(solution)/shard_map/ppermute | solution.py:25
  22.1 9.6 %collective-permute-done.4.refs_7_.refs_4_ = bf16[144,576]{1,0:T(8,128)(2,1)S(1)} collective-permute-done((bf16[144,576]{1,0:T(8,128)(2,1)S(1)}, bf16[144,576]{1,0:T(8,128)(2,1)S(1)}, u32[]{:S(2)}, u32[]{:S(2)}) %collective-permute-start.4) | collective-permute-done | bytes 165920 | tf_op jit(solution)/shard_map/ppermute | solution.py:25
  31.7 4.8 %collective-permute-start.6 = (bf16[128,768]{1,0:T(8,128)(2,1)S(1)}, bf16[128,768]{1,0:T(8,128)(2,1)S(1)}, u32[]{:S(2)}, u32[]{:S(2)}) collective-permute-start(bf16[128,768]{1,0:T(8,128)(2,1)S(1)} %collective-permute-done.3.refs_0_.refs_3_), channel_id=1, source_target_pairs={{0,16},{8,24},{16,0},{24,8},{1,17},{9,25},{17,1},{25,9},{2,18},{10... | collective-permute-start | bytes 589832 | tf_op jit(solution)/shard_map/ppermute | solution.py:25
  36.6 4.3 %collective-permute-start.8 = (bf16[144,576]{1,0:T(8,128)(2,1)S(1)}, bf16[144,576]{1,0:T(8,128)(2,1)S(1)}, u32[]{:S(2)}, u32[]{:S(2)}) collective-permute-start(bf16[144,576]{1,0:T(8,128)(2,1)S(1)} %get-tuple-element.115.refs_4_.refs_1_), channel_id=1, source_target_pairs={{0,2},{1,3},{2,0},{3,1},{4,6},{5,7},{6,4},{7,5},{8,10},{9,11},{10,... | collective-permute-start | bytes 497672 | tf_op jit(solution)/shard_map/ppermute | solution.py:25
  42.9 6.6 %collective-permute-done.8.refs_6_.refs_3_ = bf16[144,576]{1,0:T(8,128)(2,1)S(1)} collective-permute-done((bf16[144,576]{1,0:T(8,128)(2,1)S(1)}, bf16[144,576]{1,0:T(8,128)(2,1)S(1)}, u32[]{:S(2)}, u32[]{:S(2)}) %collective-permute-start.8) | collective-permute-done | bytes 165920 | tf_op jit(solution)/shard_map/ppermute | solution.py:25
  52.8 5.2 %collective-permute-done.12.refs_10_.refs_7_ = bf16[144,576]{1,0:T(8,128)(2,1)S(1)} collective-permute-done((bf16[144,576]{1,0:T(8,128)(2,1)S(1)}, bf16[144,576]{1,0:T(8,128)(2,1)S(1)}, u32[]{:S(2)}, u32[]{:S(2)}) %collective-permute-start.12) | collective-permute-done | bytes 165920 | tf_op jit(solution)/shard_map/ppermute | solution.py:30
  58.0 3.1 %project_kernel.1 = (bf16[512,576]{1,0:T(8,128)(2,1)S(1)}, bf16[512,384]{1,0:T(8,128)(2,1)S(1)}, bf16[768,576]{1,0:T(8,128)(2,1)S(1)}, bf16[512,768]{1,0:T(8,128)(2,1)S(1)}, f32[8,768]{1,0:T(8,128)S(1)}) custom-call(s32[6]{0:T(128)S(1)} %stack.33.meta_ref.place_ref, bf16[128,768]{1,0:T(8,128)(2,1)S(1)} %collective-permute-done.3.refs_0_.refs_3_, ...), custom_call_target="tpu_custom_call" | custom-call | flops 22649240 | bytes 239617 | tf_op jit(solution)/shard_map/project_kernel/pallas_call | solution.py:798
  63.8 3.1 %collective-permute-start.16 = (bf16[192,768]{1,0:T(8,128)(2,1)S(1)}, bf16[192,768]{1,0:T(8,128)(2,1)S(1)}, u32[]{:S(2)}, u32[]{:S(2)}) collective-permute-start(bf16[192,768]{1,0:T(8,128)(2,1)S(1)} %get-tuple-element.123.refs_8_), channel_id=1, source_target_pairs={{0,3},{1,2},{2,1},{3,0},{4,7},{5,6},{6,5},{7,4},{8,11},{9,10},{10,... | collective-permute-start | bytes 884744 | tf_op jit(solution)/shard_map/ppermute | solution.py:25
  66.9 6.8 %own_forward.1 = (f32[512,192]{1,0:T(8,128)S(1)}, f32[512,128]{1,0:T(8,128)S(1)}) custom-call(s32[6]{0:T(128)S(1)} %stack.33.meta_ref.place_ref, bf16[512,576]{1,0:T(8,128)(2,1)S(1)} %get-tuple-element.124.kvq_ref.refs_5_.refs_0_), custom_call_target="tpu_custom_call" | custom-call | flops 10066329 | bytes 62260 | tf_op jit(solution)/shard_map/own_forward/pallas_call | solution.py:798
  75.4 3.8 %collective-permute-done.16.refs_11_ = bf16[192,768]{1,0:T(8,128)(2,1)S(1)} collective-permute-done((bf16[192,768]{1,0:T(8,128)(2,1)S(1)}, bf16[192,768]{1,0:T(8,128)(2,1)S(1)}, u32[]{:S(2)}, u32[]{:S(2)}) %collective-permute-start.16) | collective-permute-done | bytes 294944 | tf_op jit(solution)/shard_map/ppermute | solution.py:25
  86.4 8.3 %collective-permute-start.27 = (bf16[192,768]{1,0:T(8,128)(2,1)S(1)}, bf16[192,768]{1,0:T(8,128)(2,1)S(1)}, u32[]{:S(2)}, u32[]{:S(2)}) collective-permute-start(bf16[192,768]{1,0:T(8,128)(2,1)S(1)} %collective-permute-done.15.refs_9_), channel_id=1, source_target_pairs={{0,4},{4,0},{1,5},{5,1},{2,6},{6,2},{3,7},{7,3},{8,12},{12,8},{9,1... | collective-permute-start | bytes 884744 | tf_op jit(solution)/shard_map/ppermute | solution.py:30
  94.7 2.5 %collective-permute-start.25 = (bf16[128,768]{1,0:T(8,128)(2,1)S(1)}, bf16[128,768]{1,0:T(8,128)(2,1)S(1)}, u32[]{:S(2)}, u32[]{:S(2)}) collective-permute-start(bf16[128,768]{1,0:T(8,128)(2,1)S(1)} %collective-permute-done.23.refs_4_.refs_5_), channel_id=1, source_target_pairs={{0,16},{8,24},{16,0},{24,8},{1,17},{9,25},{17,1},{25,9},{2,18},{10... | collective-permute-start | bytes 589832 | tf_op jit(solution)/shard_map/ppermute | solution.py:25
  98.1 8.4 %collective-permute-start.28 = (bf16[192,768]{1,0:T(8,128)(2,1)S(1)}, bf16[192,768]{1,0:T(8,128)(2,1)S(1)}, u32[]{:S(2)}, u32[]{:S(2)}) collective-permute-start(bf16[192,768]{1,0:T(8,128)(2,1)S(1)} %collective-permute-done.16.refs_11_), channel_id=1, source_target_pairs={{0,4},{4,0},{1,5},{5,1},{2,6},{6,2},{3,7},{7,3},{8,12},{12,8},{9,1... | collective-permute-start | bytes 884744 | tf_op jit(solution)/shard_map/ppermute | solution.py:30
  107.5 6.7 %collective-permute-done.28.refs_15_ = bf16[192,768]{1,0:T(8,128)(2,1)S(1)} collective-permute-done((bf16[192,768]{1,0:T(8,128)(2,1)S(1)}, bf16[192,768]{1,0:T(8,128)(2,1)S(1)}, u32[]{:S(2)}, u32[]{:S(2)}) %collective-permute-start.28) | collective-permute-done | bytes 294944 | tf_op jit(solution)/shard_map/ppermute | solution.py:30
  114.3 4.8 %feed_kernel.1 = (f32[256,768]{1,0:T(8,128)S(1)}, bf16[256,768]{1,0:T(8,128)(2,1)S(1)}, bf16[512,768]{1,0:T(8,128)(2,1)S(1)}, bf16[512,768]{1,0:T(8,128)(2,1)S(1...) custom-call(s32[6]{0:T(128)S(1)} %stack.33.meta_ref.place_ref, ...), custom_call_target="tpu_custom_call" | custom-call | flops 90596968 | bytes 473242 | tf_op jit(solution)/shard_map/feed_kernel/pallas_call | solution.py:798
  119.2 3.8 %feed_grad_kernel.1 = (f32[4,192,768]{2,1,0:T(8,128)S(1)}, bf16[4,192,768]{2,1,0:T(8,128)(2,1)S(1)}, f32[256,768]{1,0:T(8,128)S(1)}, bf16[256,768]{1,0:T(8,128)(2,1)S(1)}) custom-call(s32[6]{0:T(128)S(1)} %stack.33.meta_ref.place_ref, bf16[512,768]{1,0:T(8,128)(2,1)S(1)} %get-tuple-element.137.refs_0_, bf16[512,768]{1,0:T(8,128)(2,1)S(1)} %get-tuple-element.138.refs_1_, ...), custom_call_target="tpu_custom_call" | custom-call | flops 90596968 | bytes 452199 | tf_op jit(solution)/shard_map/feed_grad_kernel/pallas_call | solution.py:798
  125.6 6.3 %collective-permute-done.30.refs_2_ = bf16[128,768]{1,0:T(8,128)(2,1)S(1)} collective-permute-done((bf16[128,768]{1,0:T(8,128)(2,1)S(1)}, bf16[128,768]{1,0:T(8,128)(2,1)S(1)}, u32[]{:S(2)}, u32[]{:S(2)}) %collective-permute-start.30) | collective-permute-done | bytes 196640 | tf_op jit(solution)/shard_map/ppermute | solution.py:25
  133.6 5.6 %collective-permute-done.31.refs_2_ = bf16[128,768]{1,0:T(8,128)(2,1)S(1)} collective-permute-done((bf16[128,768]{1,0:T(8,128)(2,1)S(1)}, bf16[128,768]{1,0:T(8,128)(2,1)S(1)}, u32[]{:S(2)}, u32[]{:S(2)}) %collective-permute-start.31) | collective-permute-done | bytes 196640 | tf_op jit(solution)/shard_map/ppermute | solution.py:25
  143.6 6.4 %collective-permute-start.38 = (bf16[512,384]{1,0:T(8,128)(2,1)S(1)}, bf16[512,384]{1,0:T(8,128)(2,1)S(1)}, u32[]{:S(2)}, u32[]{:S(2)}) collective-permute-start(bf16[512,384]{1,0:T(8,128)(2,1)S(1)} %bitcast.43), channel_id=1, source_target_pairs={{0,4},{4,0},{1,5},{5,1},{2,6},{6,2},{3,7},{7,3},{8,12},{12,8},{9,1... | collective-permute-start | bytes 1179656 | tf_op jit(solution)/shard_map/ppermute | solution.py:30
  155.3 6.8 %own_grad_kernel.1 = (f32[512,576]{1,0:T(8,128)S(1)}, f32[192,768]{1,0:T(8,128)S(1)}) custom-call(s32[6]{0:T(128)S(1)} %stack.33.meta_ref.place_ref, bf16[512,576]{1,0:T(8,128)(2,1)S(1)} %get-tuple-element.124.kvq_ref.refs_5_.refs_0_, bf16[512,192]{1,0:T(8,128)(2,1)S(1)} %get-tuple-element.158.refs_1_, f32[512,192]{1,0:T(8,128)S(1)} %get-tuple-element.152.refs_7_.refs_2_, ...), custom_call_target="tpu_custom_call" | custom-call | flops 25165824 | bytes 229377 | tf_op jit(solution)/shard_map/own_grad_kernel/pallas_call | solution.py:798
  167.5 5.0 %collective-permute-start.43 = (bf16[192,768]{1,0:T(8,128)(2,1)S(1)}, bf16[192,768]{1,0:T(8,128)(2,1)S(1)}, u32[]{:S(2)}, u32[]{:S(2)}) collective-permute-start(bf16[192,768]{1,0:T(8,128)(2,1)S(1)} %get-tuple-element.183), channel_id=1, source_target_pairs={{0,2},{1,3},{2,0},{3,1},{4,6},{5,7},{6,4},{7,5},{8,10},{9,11},{10,... | collective-permute-start | bytes 884744 | tf_op jit(solution)/shard_map/ppermute | solution.py:25
  172.6 2.8 %projection_grad_kernel.1 = (f32[4,128,576]{2,1,0:T(8,128)S(1)}, bf16[4,144,576]{2,1,0:T(8,128)(2,1)}) custom-call(s32[6]{0:T(128)S(1)} %stack.33.meta_ref.place_ref, bf16[512,768]{1,0:T(8,128)(2,1)S(1)} %get-tuple-element.167.refs_0_, bf16[512,576]{1,0:T(8,128)(2,1)S(1)} %get-tuple-element.170.refs_1_, f32[192,768]{1,0:T(8,128)S(1)} %get-tuple-element.171.refs_2_), custom_call_target="tpu_custom_call" | custom-call | flops 22649240 | bytes 190465 | tf_op jit(solution)/shard_map/projection_grad_kernel/pallas_call | solution.py:798
  178.8 8.0 %collective-permute-done.43 = bf16[192,768]{1,0:T(8,128)(2,1)S(1)} collective-permute-done((bf16[192,768]{1,0:T(8,128)(2,1)S(1)}, bf16[192,768]{1,0:T(8,128)(2,1)S(1)}, u32[]{:S(2)}, u32[]{:S(2)}) %collective-permute-start.43) | collective-permute-done | bytes 294944 | tf_op jit(solution)/shard_map/ppermute | solution.py:25
  188.7 5.0 %collective-permute-done.46.arrived = bf16[4,144,576]{2,1,0:T(8,128)(2,1)S(1)} collective-permute-done((bf16[4,144,576]{2,1,0:T(8,128)(2,1)}, bf16[4,144,576]{2,1,0:T(8,128)(2,1)S(1)}, u32[]{:S(2)}, u32[]{:S(2)}) %collective-permute-start.46) | collective-permute-done | bytes 663584 | tf_op jit(solution)/shard_map/ppermute | solution.py:30
  195.2 6.8 %collective-permute-start.47 = (bf16[144,576]{1,0:T(8,128)(2,1)S(1)}, bf16[144,576]{1,0:T(8,128)(2,1)S(1)}, u32[]{:S(2)}, u32[]{:S(2)}) collective-permute-start(bf16[144,576]{1,0:T(8,128)(2,1)S(1)} %get-tuple-element.188), channel_id=1, source_target_pairs={{0,1},{1,0},{2,3},{3,2},{4,5},{5,4},{6,7},{7,6},{8,9},{9,8},{10,11... | collective-permute-start | bytes 497672 | tf_op jit(solution)/shard_map/ppermute | solution.py:25
  206.9 3.7 %collective-permute-start.51 = (bf16[48,768]{1,0:T(8,128)(2,1)S(1)}, bf16[48,768]{1,0:T(8,128)(2,1)S(1)}, u32[]{:S(2)}, u32[]{:S(2)}) collective-permute-start(bf16[48,768]{1,0:T(8,128)(2,1)S(1)} %get-tuple-element.193), channel_id=1, source_target_pairs={{0,16},{8,24},{16,0},{24,8},{1,17},{9,25},{17,1},{25,9},{2,18},{10... | collective-permute-start | bytes 221192 | tf_op jit(solution)/shard_map/ppermute | solution.py:25
  211.4 6.9 %collective-permute-done.48 = bf16[144,576]{1,0:T(8,128)(2,1)S(1)} collective-permute-done((bf16[144,576]{1,0:T(8,128)(2,1)S(1)}, bf16[144,576]{1,0:T(8,128)(2,1)S(1)}, u32[]{:S(2)}, u32[]{:S(2)}) %collective-permute-start.48) | collective-permute-done | bytes 165920 | tf_op jit(solution)/shard_map/ppermute | solution.py:25
  221.4 3.3 %collective-permute-done.53.arrived = bf16[144,576]{1,0:T(8,128)(2,1)S(1)} collective-permute-done((bf16[144,576]{1,0:T(8,128)(2,1)S(1)}, bf16[144,576]{1,0:T(8,128)(2,1)S(1)}, u32[]{:S(2)}, u32[]{:S(2)}) %collective-permute-start.53) | collective-permute-done | bytes 165920 | tf_op jit(solution)/shard_map/ppermute | solution.py:30
  226.1 3.2 %collective-permute-start.54 = (bf16[64,576]{1,0:T(8,128)(2,1)S(1)}, bf16[64,576]{1,0:T(8,128)(2,1)S(1)}, u32[]{:S(2)}, u32[]{:S(2)}) collective-permute-start(bf16[64,576]{1,0:T(8,128)(2,1)S(1)} %get-tuple-element.197), channel_id=1, source_target_pairs={{0,8},{8,0},{16,24},{24,16},{1,9},{9,1},{17,25},{25,17},{2,10},{10... | collective-permute-start | bytes 221192 | tf_op jit(solution)/shard_map/ppermute | solution.py:25
  229.2 3.7 %collective-permute-start.55 = (bf16[64,576]{1,0:T(8,128)(2,1)S(1)}, bf16[64,576]{1,0:T(8,128)(2,1)S(1)}, u32[]{:S(2)}, u32[]{:S(2)}) collective-permute-start(bf16[64,576]{1,0:T(8,128)(2,1)S(1)} %get-tuple-element.198), channel_id=1, source_target_pairs={{0,16},{8,24},{16,0},{24,8},{1,17},{9,25},{17,1},{25,9},{2,18},{10... | collective-permute-start | bytes 221192 | tf_op jit(solution)/shard_map/ppermute | solution.py:25
  (150 shorter events, 71.4 us)
Async XLA Ops:
  15.4 16.3 %collective-permute-start.3 = (bf16[128,768]{1,0:T(8,128)(2,1)S(1)}, bf16[128,768]{1,0:T(8,128)(2,1)S(1)}, u32[]{:S(2)}, u32[]{:S(2)}) collective-permute-start(bf16[128,768]{1,0:T(8,128)(2,1)S(1)} %bitcast_convert_fusion.1), channel_id=1, source_target_pairs={{0,0},{1,8},{2,16},{3,24},{8,1},{9,9},{10,17},{11,25},{16,2},{17,1... | collective-permute-start | bytes 589832 | tf_op jit(solution)/shard_map/ppermute | solution.py:36
  16.1 15.6 %collective-permute-start.4 = (bf16[144,576]{1,0:T(8,128)(2,1)S(1)}, bf16[144,576]{1,0:T(8,128)(2,1)S(1)}, u32[]{:S(2)}, u32[]{:S(2)}) collective-permute-start(bf16[144,576]{1,0:T(8,128)(2,1)S(1)} %get-tuple-element.115.refs_4_.refs_1_), channel_id=1, source_target_pairs={{0,3},{1,2},{2,1},{3,0},{4,7},{5,6},{6,5},{7,4},{8,11},{9,10},{10,... | collective-permute-start | bytes 497672 | tf_op jit(solution)/shard_map/ppermute | solution.py:25
  22.1 18.7 %collective-permute-start.7 = (bf16[144,576]{1,0:T(8,128)(2,1)S(1)}, bf16[144,576]{1,0:T(8,128)(2,1)S(1)}, u32[]{:S(2)}, u32[]{:S(2)}) collective-permute-start(bf16[144,576]{1,0:T(8,128)(2,1)S(1)} %get-tuple-element.115.refs_4_.refs_1_), channel_id=1, source_target_pairs={{0,1},{1,0},{2,3},{3,2},{4,5},{5,4},{6,7},{7,6},{8,9},{9,8},{10,11... | collective-permute-start | bytes 497672 | tf_op jit(solution)/shard_map/ppermute | solution.py:25
  31.7 19.2 %collective-permute-start.6 = (bf16[128,768]{1,0:T(8,128)(2,1)S(1)}, bf16[128,768]{1,0:T(8,128)(2,1)S(1)}, u32[]{:S(2)}, u32[]{:S(2)}) collective-permute-start(bf16[128,768]{1,0:T(8,128)(2,1)S(1)} %collective-permute-done.3.refs_0_.refs_3_), channel_id=1, source_target_pairs={{0,16},{8,24},{16,0},{24,8},{1,17},{9,25},{17,1},{25,9},{2,18},{10... | collective-permute-start | bytes 589832 | tf_op jit(solution)/shard_map/ppermute | solution.py:25
  36.6 12.9 %collective-permute-start.8 = (bf16[144,576]{1,0:T(8,128)(2,1)S(1)}, bf16[144,576]{1,0:T(8,128)(2,1)S(1)}, u32[]{:S(2)}, u32[]{:S(2)}) collective-permute-start(bf16[144,576]{1,0:T(8,128)(2,1)S(1)} %get-tuple-element.115.refs_4_.refs_1_), channel_id=1, source_target_pairs={{0,2},{1,3},{2,0},{3,1},{4,6},{5,7},{6,4},{7,5},{8,10},{9,11},{10,... | collective-permute-start | bytes 497672 | tf_op jit(solution)/shard_map/ppermute | solution.py:25
  40.9 8.7 %collective-permute-start.9 = (bf16[144,576]{1,0:T(8,128)(2,1)S(1)}, bf16[144,576]{1,0:T(8,128)(2,1)S(1)}, u32[]{:S(2)}, u32[]{:S(2)}) collective-permute-start(bf16[144,576]{1,0:T(8,128)(2,1)S(1)} %collective-permute-done.7.refs_5_.refs_2_), channel_id=1, source_target_pairs={{0,4},{4,0},{1,5},{5,1},{2,6},{6,2},{3,7},{7,3},{8,12},{12,8},{9,1... | collective-permute-start | bytes 497672 | tf_op jit(solution)/shard_map/ppermute | solution.py:30
  42.9 15.2 %collective-permute-start.5 = (bf16[128,768]{1,0:T(8,128)(2,1)S(1)}, bf16[128,768]{1,0:T(8,128)(2,1)S(1)}, u32[]{:S(2)}, u32[]{:S(2)}) collective-permute-start(bf16[128,768]{1,0:T(8,128)(2,1)S(1)} %collective-permute-done.3.refs_0_.refs_3_), channel_id=1, source_target_pairs={{0,8},{8,0},{16,24},{24,16},{1,9},{9,1},{17,25},{25,17},{2,10},{10... | collective-permute-start | bytes 589832 | tf_op jit(solution)/shard_map/ppermute | solution.py:25
  51.0 15.9 %collective-permute-start.14 = (bf16[192,768]{1,0:T(8,128)(2,1)S(1)}, bf16[192,768]{1,0:T(8,128)(2,1)S(1)}, u32[]{:S(2)}, u32[]{:S(2)}) collective-permute-start(bf16[192,768]{1,0:T(8,128)(2,1)S(1)} %get-tuple-element.123.refs_8_), channel_id=1, source_target_pairs={{0,2},{1,3},{2,0},{3,1},{4,6},{5,7},{6,4},{7,5},{8,10},{9,11},{10,... | collective-permute-start | bytes 884744 | tf_op jit(solution)/shard_map/ppermute | solution.py:25
  61.2 13.1 %collective-permute-start.13 = (bf16[512,384]{1,0:T(8,128)(2,1)S(1)}, bf16[512,384]{1,0:T(8,128)(2,1)S(1)}, u32[]{:S(2)}, u32[]{:S(2)}) collective-permute-start(bf16[512,384]{1,0:T(8,128)(2,1)S(1)} %get-tuple-element.121), channel_id=1, source_target_pairs={{0,4},{4,0},{1,5},{5,1},{2,6},{6,2},{3,7},{7,3},{8,12},{12,8},{9,1... | collective-permute-start | bytes 1179656 | tf_op jit(solution)/shard_map/ppermute | solution.py:30
  62.8 11.5 %collective-permute-start.15 = (bf16[192,768]{1,0:T(8,128)(2,1)S(1)}, bf16[192,768]{1,0:T(8,128)(2,1)S(1)}, u32[]{:S(2)}, u32[]{:S(2)}) collective-permute-start(bf16[192,768]{1,0:T(8,128)(2,1)S(1)} %get-tuple-element.123.refs_8_), channel_id=1, source_target_pairs={{0,1},{1,0},{2,3},{3,2},{4,5},{5,4},{6,7},{7,6},{8,9},{9,8},{10,11... | collective-permute-start | bytes 884744 | tf_op jit(solution)/shard_map/ppermute | solution.py:25
  63.8 15.4 %collective-permute-start.16 = (bf16[192,768]{1,0:T(8,128)(2,1)S(1)}, bf16[192,768]{1,0:T(8,128)(2,1)S(1)}, u32[]{:S(2)}, u32[]{:S(2)}) collective-permute-start(bf16[192,768]{1,0:T(8,128)(2,1)S(1)} %get-tuple-element.123.refs_8_), channel_id=1, source_target_pairs={{0,3},{1,2},{2,1},{3,0},{4,7},{5,6},{6,5},{7,4},{8,11},{9,10},{10,... | collective-permute-start | bytes 884744 | tf_op jit(solution)/shard_map/ppermute | solution.py:25
  82.7 12.0 %collective-permute-start.23 = (bf16[128,768]{1,0:T(8,128)(2,1)S(1)}, bf16[128,768]{1,0:T(8,128)(2,1)S(1)}, u32[]{:S(2)}, u32[]{:S(2)}) collective-permute-start(bf16[128,768]{1,0:T(8,128)(2,1)S(1)} %bitcast_convert_fusion), channel_id=1, source_target_pairs={{0,0},{1,8},{2,16},{3,24},{8,1},{9,9},{10,17},{11,25},{16,2},{17,1... | collective-permute-start | bytes 589832 | tf_op jit(solution)/shard_map/ppermute | solution.py:36
  84.4 12.7 %collective-permute-start.19 = (bf16[128,768]{1,0:T(8,128)(2,1)S(1)}, bf16[128,768]{1,0:T(8,128)(2,1)S(1)}, u32[]{:S(2)}, u32[]{:S(2)}) collective-permute-start(bf16[128,768]{1,0:T(8,128)(2,1)S(1)} %add_convert_fusion.5), channel_id=1, source_target_pairs={{0,16},{8,24},{16,0},{24,8},{1,17},{9,25},{17,1},{25,9},{2,18},{10... | collective-permute-start | bytes 589832 | tf_op jit(solution)/shard_map/ppermute | solution.py:25
  86.4 20.6 %collective-permute-start.27 = (bf16[192,768]{1,0:T(8,128)(2,1)S(1)}, bf16[192,768]{1,0:T(8,128)(2,1)S(1)}, u32[]{:S(2)}, u32[]{:S(2)}) collective-permute-start(bf16[192,768]{1,0:T(8,128)(2,1)S(1)} %collective-permute-done.15.refs_9_), channel_id=1, source_target_pairs={{0,4},{4,0},{1,5},{5,1},{2,6},{6,2},{3,7},{7,3},{8,12},{12,8},{9,1... | collective-permute-start | bytes 884744 | tf_op jit(solution)/shard_map/ppermute | solution.py:30
  94.7 12.1 %collective-permute-start.25 = (bf16[128,768]{1,0:T(8,128)(2,1)S(1)}, bf16[128,768]{1,0:T(8,128)(2,1)S(1)}, u32[]{:S(2)}, u32[]{:S(2)}) collective-permute-start(bf16[128,768]{1,0:T(8,128)(2,1)S(1)} %collective-permute-done.23.refs_4_.refs_5_), channel_id=1, source_target_pairs={{0,16},{8,24},{16,0},{24,8},{1,17},{9,25},{17,1},{25,9},{2,18},{10... | collective-permute-start | bytes 589832 | tf_op jit(solution)/shard_map/ppermute | solution.py:25
  98.0 9.4 %collective-permute-start.21 = (bf16[128,768]{1,0:T(8,128)(2,1)S(1)}, bf16[128,768]{1,0:T(8,128)(2,1)S(1)}, u32[]{:S(2)}, u32[]{:S(2)}) collective-permute-start(bf16[128,768]{1,0:T(8,128)(2,1)S(1)} %get-tuple-element.134.refs_0_), channel_id=1, source_target_pairs={{0,16},{8,24},{16,0},{24,8},{1,17},{9,25},{17,1},{25,9},{2,18},{10... | collective-permute-start | bytes 589832 | tf_op jit(solution)/shard_map/ppermute | solution.py:25
  98.1 16.2 %collective-permute-start.28 = (bf16[192,768]{1,0:T(8,128)(2,1)S(1)}, bf16[192,768]{1,0:T(8,128)(2,1)S(1)}, u32[]{:S(2)}, u32[]{:S(2)}) collective-permute-start(bf16[192,768]{1,0:T(8,128)(2,1)S(1)} %collective-permute-done.16.refs_11_), channel_id=1, source_target_pairs={{0,4},{4,0},{1,5},{5,1},{2,6},{6,2},{3,7},{7,3},{8,12},{12,8},{9,1... | collective-permute-start | bytes 884744 | tf_op jit(solution)/shard_map/ppermute | solution.py:30
  123.0 28.7 %collective-permute-start.36 = (bf16[4,192,768]{2,1,0:T(8,128)(2,1)S(1)}, bf16[4,192,768]{2,1,0:T(8,128)(2,1)S(1)}, u32[]{:S(2)}, u32[]{:S(2)}) collective-permute-start(bf16[4,192,768]{2,1,0:T(8,128)(2,1)S(1)} %get-tuple-element.156), channel_id=1, source_target_pairs={{0,4},{4,0},{1,5},{5,1},{2,6},{6,2},{3,7},{7,3},{8,12},{12,8},{9,1... | collective-permute-start | bytes 3538952 | tf_op jit(solution)/shard_map/ppermute | solution.py:30
  140.6 13.7 %collective-permute-start.33 = (bf16[256,768]{1,0:T(8,128)(2,1)S(1)}, bf16[256,768]{1,0:T(8,128)(2,1)S(1)}, u32[]{:S(2)}, u32[]{:S(2)}) collective-permute-start(bf16[256,768]{1,0:T(8,128)(2,1)S(1)} %get-tuple-element.149), channel_id=1, source_target_pairs={{0,8},{8,0},{16,24},{24,16},{1,9},{9,1},{17,25},{25,17},{2,10},{10... | collective-permute-start | bytes 1179656 | tf_op jit(solution)/shard_map/ppermute | solution.py:25
  143.6 19.3 %collective-permute-start.38 = (bf16[512,384]{1,0:T(8,128)(2,1)S(1)}, bf16[512,384]{1,0:T(8,128)(2,1)S(1)}, u32[]{:S(2)}, u32[]{:S(2)}) collective-permute-start(bf16[512,384]{1,0:T(8,128)(2,1)S(1)} %bitcast.43), channel_id=1, source_target_pairs={{0,4},{4,0},{1,5},{5,1},{2,6},{6,2},{3,7},{7,3},{8,12},{12,8},{9,1... | collective-permute-start | bytes 1179656 | tf_op jit(solution)/shard_map/ppermute | solution.py:30
  152.6 10.3 %collective-permute-start.37 = (bf16[192,768]{1,0:T(8,128)(2,1)S(1)}, bf16[192,768]{1,0:T(8,128)(2,1)S(1)}, u32[]{:S(2)}, u32[]{:S(2)}) collective-permute-start(bf16[192,768]{1,0:T(8,128)(2,1)S(1)} %get-tuple-element.162), channel_id=1, source_target_pairs={{0,3},{1,2},{2,1},{3,0},{4,7},{5,6},{6,5},{7,4},{8,11},{9,10},{10,... | collective-permute-start | bytes 884744 | tf_op jit(solution)/shard_map/ppermute | solution.py:25
  167.5 19.2 %collective-permute-start.43 = (bf16[192,768]{1,0:T(8,128)(2,1)S(1)}, bf16[192,768]{1,0:T(8,128)(2,1)S(1)}, u32[]{:S(2)}, u32[]{:S(2)}) collective-permute-start(bf16[192,768]{1,0:T(8,128)(2,1)S(1)} %get-tuple-element.183), channel_id=1, source_target_pairs={{0,2},{1,3},{2,0},{3,1},{4,6},{5,7},{6,4},{7,5},{8,10},{9,11},{10,... | collective-permute-start | bytes 884744 | tf_op jit(solution)/shard_map/ppermute | solution.py:25
  172.5 14.2 %collective-permute-start.42 = (bf16[192,768]{1,0:T(8,128)(2,1)S(1)}, bf16[192,768]{1,0:T(8,128)(2,1)S(1)}, u32[]{:S(2)}, u32[]{:S(2)}) collective-permute-start(bf16[192,768]{1,0:T(8,128)(2,1)S(1)} %get-tuple-element.181), channel_id=1, source_target_pairs={{0,1},{1,0},{2,3},{3,2},{4,5},{5,4},{6,7},{7,6},{8,9},{9,8},{10,11... | collective-permute-start | bytes 884744 | tf_op jit(solution)/shard_map/ppermute | solution.py:25
  177.0 16.7 %collective-permute-start.46 = (bf16[4,144,576]{2,1,0:T(8,128)(2,1)}, bf16[4,144,576]{2,1,0:T(8,128)(2,1)S(1)}, u32[]{:S(2)}, u32[]{:S(2)}) collective-permute-start(bf16[4,144,576]{2,1,0:T(8,128)(2,1)} %get-tuple-element.186), channel_id=1, source_target_pairs={{0,4},{4,0},{1,5},{5,1},{2,6},{6,2},{3,7},{7,3},{8,12},{12,8},{9,1... | collective-permute-start | bytes 1990664 | tf_op jit(solution)/shard_map/ppermute | solution.py:30
  186.9 17.5 %collective-permute-start.44 = (bf16[192,768]{1,0:T(8,128)(2,1)S(1)}, bf16[192,768]{1,0:T(8,128)(2,1)}, u32[]{:S(2)}, u32[]{:S(2)}) collective-permute-start(bf16[192,768]{1,0:T(8,128)(2,1)S(1)} %add_convert_fusion.mine), channel_id=1, source_target_pairs={{0,4},{4,0},{1,5},{5,1},{2,6},{6,2},{3,7},{7,3},{8,12},{12,8},{9,1... | collective-permute-start | bytes 884744 | tf_op jit(solution)/shard_map/ppermute | solution.py:30
  195.2 16.2 %collective-permute-start.47 = (bf16[144,576]{1,0:T(8,128)(2,1)S(1)}, bf16[144,576]{1,0:T(8,128)(2,1)S(1)}, u32[]{:S(2)}, u32[]{:S(2)}) collective-permute-start(bf16[144,576]{1,0:T(8,128)(2,1)S(1)} %get-tuple-element.188), channel_id=1, source_target_pairs={{0,1},{1,0},{2,3},{3,2},{4,5},{5,4},{6,7},{7,6},{8,9},{9,8},{10,11... | collective-permute-start | bytes 497672 | tf_op jit(solution)/shard_map/ppermute | solution.py:25
  202.0 16.4 %collective-permute-start.48 = (bf16[144,576]{1,0:T(8,128)(2,1)S(1)}, bf16[144,576]{1,0:T(8,128)(2,1)S(1)}, u32[]{:S(2)}, u32[]{:S(2)}) collective-permute-start(bf16[144,576]{1,0:T(8,128)(2,1)S(1)} %get-tuple-element.189), channel_id=1, source_target_pairs={{0,2},{1,3},{2,0},{3,1},{4,6},{5,7},{6,4},{7,5},{8,10},{9,11},{10,... | collective-permute-start | bytes 497672 | tf_op jit(solution)/shard_map/ppermute | solution.py:25
  203.0 15.3 %collective-permute-start.49 = (bf16[144,576]{1,0:T(8,128)(2,1)S(1)}, bf16[144,576]{1,0:T(8,128)(2,1)S(1)}, u32[]{:S(2)}, u32[]{:S(2)}) collective-permute-start(bf16[144,576]{1,0:T(8,128)(2,1)S(1)} %get-tuple-element.190), channel_id=1, source_target_pairs={{0,3},{1,2},{2,1},{3,0},{4,7},{5,6},{6,5},{7,4},{8,11},{9,10},{10,... | collective-permute-start | bytes 497672 | tf_op jit(solution)/shard_map/ppermute | solution.py:25
  206.9 14.6 %collective-permute-start.51 = (bf16[48,768]{1,0:T(8,128)(2,1)S(1)}, bf16[48,768]{1,0:T(8,128)(2,1)S(1)}, u32[]{:S(2)}, u32[]{:S(2)}) collective-permute-start(bf16[48,768]{1,0:T(8,128)(2,1)S(1)} %get-tuple-element.193), channel_id=1, source_target_pairs={{0,16},{8,24},{16,0},{24,8},{1,17},{9,25},{17,1},{25,9},{2,18},{10... | collective-permute-start | bytes 221192 | tf_op jit(solution)/shard_map/ppermute | solution.py:25
  210.6 10.8 %collective-permute-start.52 = (bf16[48,768]{1,0:T(8,128)(2,1)S(1)}, bf16[48,768]{1,0:T(8,128)(2,1)S(1)}, u32[]{:S(2)}, u32[]{:S(2)}) collective-permute-start(bf16[48,768]{1,0:T(8,128)(2,1)S(1)} %get-tuple-element.194), channel_id=1, source_target_pairs={{0,24},{8,16},{16,8},{24,0},{1,25},{9,17},{17,9},{25,1},{2,26},{10... | collective-permute-start | bytes 221192 | tf_op jit(solution)/shard_map/ppermute | solution.py:25
  218.4 15.9 %collective-permute-start.50 = (bf16[128,768]{1,0:T(8,128)(2,1)S(1)}, bf16[128,768]{1,0:T(8,128)(2,1)S(1)}, u32[]{:S(2)}, u32[]{:S(2)}) collective-permute-start(bf16[128,768]{1,0:T(8,128)(2,1)S(1)} %add_convert_fusion.2), channel_id=1, source_target_pairs={{0,0},{1,8},{2,16},{3,24},{8,1},{9,9},{10,17},{11,25},{16,2},{17,1... | collective-permute-start | bytes 589832 | tf_op jit(solution)/shard_map/ppermute | solution.py:36
  226.1 9.0 %collective-permute-start.54 = (bf16[64,576]{1,0:T(8,128)(2,1)S(1)}, bf16[64,576]{1,0:T(8,128)(2,1)S(1)}, u32[]{:S(2)}, u32[]{:S(2)}) collective-permute-start(bf16[64,576]{1,0:T(8,128)(2,1)S(1)} %get-tuple-element.197), channel_id=1, source_target_pairs={{0,8},{8,0},{16,24},{24,16},{1,9},{9,1},{17,25},{25,17},{2,10},{10... | collective-permute-start | bytes 221192 | tf_op jit(solution)/shard_map/ppermute | solution.py:25
  (40 other events, 276.8 us)

commit v13 on v12

--- a/solution.py
+++ b/solution.py
@@ -1054,11 +1054,14 @@
     )
 
     input_rows = transpose_homes(input_part)
+    delta = row_sum(*fed_sum) + vectors[5:6] + attended
+    delta_rows = transpose_homes(after(delta.astype(LOW), input_part))
+    output = tokens[0] + delta_rows.astype(WIDE)
     if halves:
         shape = (share_rows + 16, 3 * width)
         share_keep, *share_sends = local_call(
             fold_share_kernel,
-            (meta, after(kept_share, input_rows, *half_pieces[:-1]), shift(sent_share, "ctx", 1), sums),
+            (meta, after(kept_share, input_rows, delta_rows, *half_pieces[:-1]), shift(sent_share, "ctx", 1), sums),
             [wide_like(*shape)] + [low_like(*shape)] * (depth - 1),
             [pltpu.VMEM((16, 3 * width), WIDE)],
         )
@@ -1079,9 +1082,6 @@
         [low_like(shard, hidden_part)] * parts + [wide_like(hidden_shard, model)],
     )
     up_arrived = send_pieces(up_totals[1:], "dp")
-    delta = row_sum(*fed_sum) + vectors[5:6] + attended
-    delta_rows = transpose_homes(after(delta.astype(LOW), up_arrived[0], *share_pieces))
-    output = tokens[0] + delta_rows.astype(WIDE)
     *totals, out_total, vector_part = local_call(
         functools.partial(unfold_kernel, parts, halves),
         (meta, after(shares[0], *up_arrived), *shares[1:]),

time: 240 us -> 239 us (level)
    ppermute x41, starting transfers between devices: 60 us -> 52.6 us  [swap(): return lax.ppermute(value, axis, [(at, at ^ bit) for at in range(count)])]
    ppermute x41, waiting for transfers between devices: 61.5 us -> 67.1 us  [swap(): return lax.ppermute(value, axis, [(at, at ^ bit) for at in range(count)])]
    ppermute x12, waiting for transfers between devices: 25.8 us -> 21.8 us  [shift(): lax.ppermute(value, axis, [(at, (at + by) % count) for at in range(count)])]
    ppermute x12, starting transfers between devices: 35.8 us -> 39 us  [shift(): lax.ppermute(value, axis, [(at, (at + by) % count) for at in range(count)])]
  transfers between devices with their start and end apart: 57 -> 57, of which waited for: 23 -> 23; matrix products, arithmetic and copies ran while one was open for 2% -> 2% of each run, Pallas kernels for 14% -> 13%
where the time goes in v13:
time: 239 us; the launch traced here: 238 us
  starting transfers between devices  96.7 us (40%)
  waiting for transfers between devices  88.9 us (37%)
  Pallas kernels  42.2 us (18%)
  local copies, waits for them, and re-layouts  4.92 us (2%)
  other arithmetic  4.73 us (2%)
    ppermute x41, waiting for transfers between devices, swap(): return lax.ppermute(value, axis, [(at, at ^ bit) for at in range(count)])  67.1 us
    ppermute x41, starting transfers between devices, swap(): return lax.ppermute(value, axis, [(at, at ^ bit) for at in range(count)])  52.6 us
    pallas_call x20, Pallas kernels, local_call(): pl.pallas_call(kernel, name=getattr(kernel, 'func', kernel).__name__, out...  42.2 us
    ppermute x12, starting transfers between devices, shift(): lax.ppermute(value, axis, [(at, (at + by) % count) for at in range(count)])  39 us
    ppermute x12, waiting for transfers between devices, shift(): lax.ppermute(value, axis, [(at, (at + by) % count) for at in range(count)])  21.8 us
    ppermute x4, starting transfers between devices, transpose_homes(): return lax.ppermute(value, ('dp', 'fsdp'), pairs)  5.01 us
  transfers between devices with their start and end apart: 57, of which 23 were waited for; matrix products, arithmetic and copies ran while one was open for 2% of the time, Pallas kernels for 13%

profile of v13, /device:TPU:0, one launch (start us, length us, event | category | flops | bytes accessed | tf_op | source)
XLA Modules:
  0.0 238.5 jit_solution(18034457213597330323)
XLA Ops:
  5.0 2.6 %collective-permute-start.1 = (bf16[48,1408]{1,0:T(8,128)(2,1)S(1)}, bf16[48,1408]{1,0:T(8,128)(2,1)S(1)}, u32[]{:S(2)}, u32[]{:S(2)}) collective-permute-start(bf16[48,1408]{1,0:T(8,128)(2,1)S(1)} %get-tuple-element.113), channel_id=1, source_target_pairs={{0,16},{8,24},{16,0},{24,8},{1,17},{9,25},{17,1},{25,9},{2,18},{10... | collective-permute-start | bytes 405512 | tf_op jit(solution)/shard_map/ppermute | solution.py:25
  8.7 3.3 %collective-permute-done.1.refs_2_ = bf16[48,1408]{1,0:T(8,128)(2,1)S(1)} collective-permute-done((bf16[48,1408]{1,0:T(8,128)(2,1)S(1)}, bf16[48,1408]{1,0:T(8,128)(2,1)S(1)}, u32[]{:S(2)}, u32[]{:S(2)}) %collective-permute-start.1) | collective-permute-done | bytes 135200 | tf_op jit(solution)/shard_map/ppermute | solution.py:25
  16.1 6.0 %collective-permute-start.4 = (bf16[144,576]{1,0:T(8,128)(2,1)S(1)}, bf16[144,576]{1,0:T(8,128)(2,1)S(1)}, u32[]{:S(2)}, u32[]{:S(2)}) collective-permute-start(bf16[144,576]{1,0:T(8,128)(2,1)S(1)} %get-tuple-element.115.refs_4_.refs_1_), channel_id=1, source_target_pairs={{0,3},{1,2},{2,1},{3,0},{4,7},{5,6},{6,5},{7,4},{8,11},{9,10},{10,... | collective-permute-start | bytes 497672 | tf_op jit(solution)/shard_map/ppermute | solution.py:25
  22.1 9.6 %collective-permute-done.4.refs_7_.refs_4_ = bf16[144,576]{1,0:T(8,128)(2,1)S(1)} collective-permute-done((bf16[144,576]{1,0:T(8,128)(2,1)S(1)}, bf16[144,576]{1,0:T(8,128)(2,1)S(1)}, u32[]{:S(2)}, u32[]{:S(2)}) %collective-permute-start.4) | collective-permute-done | bytes 165920 | tf_op jit(solution)/shard_map/ppermute | solution.py:25
  31.7 4.8 %collective-permute-start.6 = (bf16[128,768]{1,0:T(8,128)(2,1)S(1)}, bf16[128,768]{1,0:T(8,128)(2,1)S(1)}, u32[]{:S(2)}, u32[]{:S(2)}) collective-permute-start(bf16[128,768]{1,0:T(8,128)(2,1)S(1)} %collective-permute-done.3.refs_0_.refs_3_), channel_id=1, source_target_pairs={{0,16},{8,24},{16,0},{24,8},{1,17},{9,25},{17,1},{25,9},{2,18},{10... | collective-permute-start | bytes 589832 | tf_op jit(solution)/shard_map/ppermute | solution.py:25
  36.6 4.3 %collective-permute-start.8 = (bf16[144,576]{1,0:T(8,128)(2,1)S(1)}, bf16[144,576]{1,0:T(8,128)(2,1)S(1)}, u32[]{:S(2)}, u32[]{:S(2)}) collective-permute-start(bf16[144,576]{1,0:T(8,128)(2,1)S(1)} %get-tuple-element.115.refs_4_.refs_1_), channel_id=1, source_target_pairs={{0,2},{1,3},{2,0},{3,1},{4,6},{5,7},{6,4},{7,5},{8,10},{9,11},{10,... | collective-permute-start | bytes 497672 | tf_op jit(solution)/shard_map/ppermute | solution.py:25
  42.9 6.6 %collective-permute-done.8.refs_6_.refs_3_ = bf16[144,576]{1,0:T(8,128)(2,1)S(1)} collective-permute-done((bf16[144,576]{1,0:T(8,128)(2,1)S(1)}, bf16[144,576]{1,0:T(8,128)(2,1)S(1)}, u32[]{:S(2)}, u32[]{:S(2)}) %collective-permute-start.8) | collective-permute-done | bytes 165920 | tf_op jit(solution)/shard_map/ppermute | solution.py:25
  52.8 5.2 %collective-permute-done.12.refs_10_.refs_7_ = bf16[144,576]{1,0:T(8,128)(2,1)S(1)} collective-permute-done((bf16[144,576]{1,0:T(8,128)(2,1)S(1)}, bf16[144,576]{1,0:T(8,128)(2,1)S(1)}, u32[]{:S(2)}, u32[]{:S(2)}) %collective-permute-start.12) | collective-permute-done | bytes 165920 | tf_op jit(solution)/shard_map/ppermute | solution.py:30
  58.0 3.1 %project_kernel.1 = (bf16[512,576]{1,0:T(8,128)(2,1)S(1)}, bf16[512,384]{1,0:T(8,128)(2,1)S(1)}, bf16[768,576]{1,0:T(8,128)(2,1)S(1)}, bf16[512,768]{1,0:T(8,128)(2,1)S(1)}, f32[8,768]{1,0:T(8,128)S(1)}) custom-call(s32[6]{0:T(128)S(1)} %stack.33.meta_ref.place_ref, bf16[128,768]{1,0:T(8,128)(2,1)S(1)} %collective-permute-done.3.refs_0_.refs_3_, ...), custom_call_target="tpu_custom_call" | custom-call | flops 22649240 | bytes 239617 | tf_op jit(solution)/shard_map/project_kernel/pallas_call | solution.py:798
  63.8 3.1 %collective-permute-start.16 = (bf16[192,768]{1,0:T(8,128)(2,1)S(1)}, bf16[192,768]{1,0:T(8,128)(2,1)S(1)}, u32[]{:S(2)}, u32[]{:S(2)}) collective-permute-start(bf16[192,768]{1,0:T(8,128)(2,1)S(1)} %get-tuple-element.123.refs_8_), channel_id=1, source_target_pairs={{0,3},{1,2},{2,1},{3,0},{4,7},{5,6},{6,5},{7,4},{8,11},{9,10},{10,... | collective-permute-start | bytes 884744 | tf_op jit(solution)/shard_map/ppermute | solution.py:25
  66.9 6.8 %own_forward.1 = (f32[512,192]{1,0:T(8,128)S(1)}, f32[512,128]{1,0:T(8,128)S(1)}) custom-call(s32[6]{0:T(128)S(1)} %stack.33.meta_ref.place_ref, bf16[512,576]{1,0:T(8,128)(2,1)S(1)} %get-tuple-element.124.kvq_ref.refs_5_.refs_0_), custom_call_target="tpu_custom_call" | custom-call | flops 10066329 | bytes 62260 | tf_op jit(solution)/shard_map/own_forward/pallas_call | solution.py:798
  75.4 3.8 %collective-permute-done.16.refs_11_ = bf16[192,768]{1,0:T(8,128)(2,1)S(1)} collective-permute-done((bf16[192,768]{1,0:T(8,128)(2,1)S(1)}, bf16[192,768]{1,0:T(8,128)(2,1)S(1)}, u32[]{:S(2)}, u32[]{:S(2)}) %collective-permute-start.16) | collective-permute-done | bytes 294944 | tf_op jit(solution)/shard_map/ppermute | solution.py:25
  86.4 8.3 %collective-permute-start.27 = (bf16[192,768]{1,0:T(8,128)(2,1)S(1)}, bf16[192,768]{1,0:T(8,128)(2,1)S(1)}, u32[]{:S(2)}, u32[]{:S(2)}) collective-permute-start(bf16[192,768]{1,0:T(8,128)(2,1)S(1)} %collective-permute-done.15.refs_9_), channel_id=1, source_target_pairs={{0,4},{4,0},{1,5},{5,1},{2,6},{6,2},{3,7},{7,3},{8,12},{12,8},{9,1... | collective-permute-start | bytes 884744 | tf_op jit(solution)/shard_map/ppermute | solution.py:30
  94.7 2.5 %collective-permute-start.25 = (bf16[128,768]{1,0:T(8,128)(2,1)S(1)}, bf16[128,768]{1,0:T(8,128)(2,1)S(1)}, u32[]{:S(2)}, u32[]{:S(2)}) collective-permute-start(bf16[128,768]{1,0:T(8,128)(2,1)S(1)} %collective-permute-done.23.refs_4_.refs_5_), channel_id=1, source_target_pairs={{0,16},{8,24},{16,0},{24,8},{1,17},{9,25},{17,1},{25,9},{2,18},{10... | collective-permute-start | bytes 589832 | tf_op jit(solution)/shard_map/ppermute | solution.py:25
  98.1 8.4 %collective-permute-start.28 = (bf16[192,768]{1,0:T(8,128)(2,1)S(1)}, bf16[192,768]{1,0:T(8,128)(2,1)S(1)}, u32[]{:S(2)}, u32[]{:S(2)}) collective-permute-start(bf16[192,768]{1,0:T(8,128)(2,1)S(1)} %collective-permute-done.16.refs_11_), channel_id=1, source_target_pairs={{0,4},{4,0},{1,5},{5,1},{2,6},{6,2},{3,7},{7,3},{8,12},{12,8},{9,1... | collective-permute-start | bytes 884744 | tf_op jit(solution)/shard_map/ppermute | solution.py:30
  107.5 6.7 %collective-permute-done.28.refs_15_ = bf16[192,768]{1,0:T(8,128)(2,1)S(1)} collective-permute-done((bf16[192,768]{1,0:T(8,128)(2,1)S(1)}, bf16[192,768]{1,0:T(8,128)(2,1)S(1)}, u32[]{:S(2)}, u32[]{:S(2)}) %collective-permute-start.28) | collective-permute-done | bytes 294944 | tf_op jit(solution)/shard_map/ppermute | solution.py:30
  114.3 4.8 %feed_kernel.1 = (f32[256,768]{1,0:T(8,128)S(1)}, bf16[256,768]{1,0:T(8,128)(2,1)S(1)}, bf16[512,768]{1,0:T(8,128)(2,1)S(1)}, bf16[512,768]{1,0:T(8,128)(2,1)S(1...) custom-call(s32[6]{0:T(128)S(1)} %stack.33.meta_ref.place_ref, ...), custom_call_target="tpu_custom_call" | custom-call | flops 90596968 | bytes 473242 | tf_op jit(solution)/shard_map/feed_kernel/pallas_call | solution.py:798
  119.2 3.8 %feed_grad_kernel.1 = (f32[4,192,768]{2,1,0:T(8,128)S(1)}, bf16[4,192,768]{2,1,0:T(8,128)(2,1)S(1)}, f32[256,768]{1,0:T(8,128)S(1)}, bf16[256,768]{1,0:T(8,128)(2,1)S(1)}) custom-call(s32[6]{0:T(128)S(1)} %stack.33.meta_ref.place_ref, bf16[512,768]{1,0:T(8,128)(2,1)S(1)} %get-tuple-element.137.refs_0_, bf16[512,768]{1,0:T(8,128)(2,1)S(1)} %get-tuple-element.138.refs_1_, ...), custom_call_target="tpu_custom_call" | custom-call | flops 90596968 | bytes 452199 | tf_op jit(solution)/shard_map/feed_grad_kernel/pallas_call | solution.py:798
  125.6 6.3 %collective-permute-done.30.refs_2_ = bf16[128,768]{1,0:T(8,128)(2,1)S(1)} collective-permute-done((bf16[128,768]{1,0:T(8,128)(2,1)S(1)}, bf16[128,768]{1,0:T(8,128)(2,1)S(1)}, u32[]{:S(2)}, u32[]{:S(2)}) %collective-permute-start.30) | collective-permute-done | bytes 196640 | tf_op jit(solution)/shard_map/ppermute | solution.py:25
  133.6 5.6 %collective-permute-done.31.refs_2_ = bf16[128,768]{1,0:T(8,128)(2,1)S(1)} collective-permute-done((bf16[128,768]{1,0:T(8,128)(2,1)S(1)}, bf16[128,768]{1,0:T(8,128)(2,1)S(1)}, u32[]{:S(2)}, u32[]{:S(2)}) %collective-permute-start.31) | collective-permute-done | bytes 196640 | tf_op jit(solution)/shard_map/ppermute | solution.py:25
  143.6 6.4 %collective-permute-start.38 = (bf16[512,384]{1,0:T(8,128)(2,1)S(1)}, bf16[512,384]{1,0:T(8,128)(2,1)S(1)}, u32[]{:S(2)}, u32[]{:S(2)}) collective-permute-start(bf16[512,384]{1,0:T(8,128)(2,1)S(1)} %bitcast.43), channel_id=1, source_target_pairs={{0,4},{4,0},{1,5},{5,1},{2,6},{6,2},{3,7},{7,3},{8,12},{12,8},{9,1... | collective-permute-start | bytes 1179656 | tf_op jit(solution)/shard_map/ppermute | solution.py:30
  155.2 6.8 %own_grad_kernel.1 = (f32[512,576]{1,0:T(8,128)S(1)}, f32[192,768]{1,0:T(8,128)S(1)}) custom-call(s32[6]{0:T(128)S(1)} %stack.33.meta_ref.place_ref, bf16[512,576]{1,0:T(8,128)(2,1)S(1)} %get-tuple-element.124.kvq_ref.refs_5_.refs_0_, bf16[512,192]{1,0:T(8,128)(2,1)S(1)} %get-tuple-element.153.refs_1_, f32[512,192]{1,0:T(8,128)S(1)} %get-tuple-element.151.refs_7_.refs_2_, ...), custom_call_target="tpu_custom_call" | custom-call | flops 25165824 | bytes 229377 | tf_op jit(solution)/shard_map/own_grad_kernel/pallas_call | solution.py:798
  166.8 5.1 %collective-permute-start.43 = (bf16[192,768]{1,0:T(8,128)(2,1)S(1)}, bf16[192,768]{1,0:T(8,128)(2,1)S(1)}, u32[]{:S(2)}, u32[]{:S(2)}) collective-permute-start(bf16[192,768]{1,0:T(8,128)(2,1)S(1)} %get-tuple-element.181), channel_id=1, source_target_pairs={{0,1},{1,0},{2,3},{3,2},{4,5},{5,4},{6,7},{7,6},{8,9},{9,8},{10,11... | collective-permute-start | bytes 884744 | tf_op jit(solution)/shard_map/ppermute | solution.py:25
  178.1 3.0 %collective-permute-start.41 = (bf16[128,768]{1,0:T(8,128)(2,1)}, bf16[128,768]{1,0:T(8,128)(2,1)}, u32[]{:S(2)}, u32[]{:S(2)}) collective-permute-start(bf16[128,768]{1,0:T(8,128)(2,1)} %add_convert_fusion.2), channel_id=1, source_target_pairs={{0,0},{1,8},{2,16},{3,24},{8,1},{9,9},{10,17},{11,25},{16,2},{17,1... | collective-permute-start | bytes 589832 | tf_op jit(solution)/shard_map/ppermute | solution.py:36
  181.1 3.1 %collective-permute-done.43 = bf16[192,768]{1,0:T(8,128)(2,1)S(1)} collective-permute-done((bf16[192,768]{1,0:T(8,128)(2,1)S(1)}, bf16[192,768]{1,0:T(8,128)(2,1)S(1)}, u32[]{:S(2)}, u32[]{:S(2)}) %collective-permute-start.43) | collective-permute-done | bytes 294944 | tf_op jit(solution)/shard_map/ppermute | solution.py:25
  184.1 13.1 %collective-permute-done.44 = bf16[192,768]{1,0:T(8,128)(2,1)S(1)} collective-permute-done((bf16[192,768]{1,0:T(8,128)(2,1)S(1)}, bf16[192,768]{1,0:T(8,128)(2,1)S(1)}, u32[]{:S(2)}, u32[]{:S(2)}) %collective-permute-start.44) | collective-permute-done | bytes 294944 | tf_op jit(solution)/shard_map/ppermute | solution.py:25
  199.5 5.6 %collective-permute-start.47 = (bf16[144,576]{1,0:T(8,128)(2,1)S(1)}, bf16[144,576]{1,0:T(8,128)(2,1)S(1)}, u32[]{:S(2)}, u32[]{:S(2)}) collective-permute-start(bf16[144,576]{1,0:T(8,128)(2,1)S(1)} %get-tuple-element.189), channel_id=1, source_target_pairs={{0,2},{1,3},{2,0},{3,1},{4,6},{5,7},{6,4},{7,5},{8,10},{9,11},{10,... | collective-permute-start | bytes 497672 | tf_op jit(solution)/shard_map/ppermute | solution.py:25
  208.7 2.9 %collective-permute-start.50 = (bf16[48,768]{1,0:T(8,128)(2,1)S(1)}, bf16[48,768]{1,0:T(8,128)(2,1)S(1)}, u32[]{:S(2)}, u32[]{:S(2)}) collective-permute-start(bf16[48,768]{1,0:T(8,128)(2,1)S(1)} %get-tuple-element.192), channel_id=1, source_target_pairs={{0,8},{8,0},{16,24},{24,16},{1,9},{9,1},{17,25},{25,17},{2,10},{10... | collective-permute-start | bytes 221192 | tf_op jit(solution)/shard_map/ppermute | solution.py:25
  211.6 2.9 %collective-permute-start.51 = (bf16[48,768]{1,0:T(8,128)(2,1)S(1)}, bf16[48,768]{1,0:T(8,128)(2,1)S(1)}, u32[]{:S(2)}, u32[]{:S(2)}) collective-permute-start(bf16[48,768]{1,0:T(8,128)(2,1)S(1)} %get-tuple-element.193), channel_id=1, source_target_pairs={{0,16},{8,24},{16,0},{24,8},{1,17},{9,25},{17,1},{25,9},{2,18},{10... | collective-permute-start | bytes 221192 | tf_op jit(solution)/shard_map/ppermute | solution.py:25
  214.6 3.7 %collective-permute-done.47 = bf16[144,576]{1,0:T(8,128)(2,1)S(1)} collective-permute-done((bf16[144,576]{1,0:T(8,128)(2,1)S(1)}, bf16[144,576]{1,0:T(8,128)(2,1)S(1)}, u32[]{:S(2)}, u32[]{:S(2)}) %collective-permute-start.47) | collective-permute-done | bytes 165920 | tf_op jit(solution)/shard_map/ppermute | solution.py:25
  218.4 5.2 %collective-permute-start.53 = (bf16[144,576]{1,0:T(8,128)(2,1)S(1)}, bf16[144,576]{1,0:T(8,128)(2,1)S(1)}, u32[]{:S(2)}, u32[]{:S(2)}) collective-permute-start(bf16[144,576]{1,0:T(8,128)(2,1)S(1)} %add_convert_fusion.6.mine), channel_id=1, source_target_pairs={{0,4},{4,0},{1,5},{5,1},{2,6},{6,2},{3,7},{7,3},{8,12},{12,8},{9,1... | collective-permute-start | bytes 497672 | tf_op jit(solution)/shard_map/ppermute | solution.py:30
  224.4 4.3 %collective-permute-done.53.arrived = bf16[144,576]{1,0:T(8,128)(2,1)S(1)} collective-permute-done((bf16[144,576]{1,0:T(8,128)(2,1)S(1)}, bf16[144,576]{1,0:T(8,128)(2,1)S(1)}, u32[]{:S(2)}, u32[]{:S(2)}) %collective-permute-start.53) | collective-permute-done | bytes 165920 | tf_op jit(solution)/shard_map/ppermute | solution.py:30
  (138 shorter events, 69.8 us)
Async XLA Ops:
  15.4 16.3 %collective-permute-start.3 = (bf16[128,768]{1,0:T(8,128)(2,1)S(1)}, bf16[128,768]{1,0:T(8,128)(2,1)S(1)}, u32[]{:S(2)}, u32[]{:S(2)}) collective-permute-start(bf16[128,768]{1,0:T(8,128)(2,1)S(1)} %bitcast_convert_fusion.1), channel_id=1, source_target_pairs={{0,0},{1,8},{2,16},{3,24},{8,1},{9,9},{10,17},{11,25},{16,2},{17,1... | collective-permute-start | bytes 589832 | tf_op jit(solution)/shard_map/ppermute | solution.py:36
  16.1 15.6 %collective-permute-start.4 = (bf16[144,576]{1,0:T(8,128)(2,1)S(1)}, bf16[144,576]{1,0:T(8,128)(2,1)S(1)}, u32[]{:S(2)}, u32[]{:S(2)}) collective-permute-start(bf16[144,576]{1,0:T(8,128)(2,1)S(1)} %get-tuple-element.115.refs_4_.refs_1_), channel_id=1, source_target_pairs={{0,3},{1,2},{2,1},{3,0},{4,7},{5,6},{6,5},{7,4},{8,11},{9,10},{10,... | collective-permute-start | bytes 497672 | tf_op jit(solution)/shard_map/ppermute | solution.py:25
  22.1 18.8 %collective-permute-start.7 = (bf16[144,576]{1,0:T(8,128)(2,1)S(1)}, bf16[144,576]{1,0:T(8,128)(2,1)S(1)}, u32[]{:S(2)}, u32[]{:S(2)}) collective-permute-start(bf16[144,576]{1,0:T(8,128)(2,1)S(1)} %get-tuple-element.115.refs_4_.refs_1_), channel_id=1, source_target_pairs={{0,1},{1,0},{2,3},{3,2},{4,5},{5,4},{6,7},{7,6},{8,9},{9,8},{10,11... | collective-permute-start | bytes 497672 | tf_op jit(solution)/shard_map/ppermute | solution.py:25
  31.7 19.2 %collective-permute-start.6 = (bf16[128,768]{1,0:T(8,128)(2,1)S(1)}, bf16[128,768]{1,0:T(8,128)(2,1)S(1)}, u32[]{:S(2)}, u32[]{:S(2)}) collective-permute-start(bf16[128,768]{1,0:T(8,128)(2,1)S(1)} %collective-permute-done.3.refs_0_.refs_3_), channel_id=1, source_target_pairs={{0,16},{8,24},{16,0},{24,8},{1,17},{9,25},{17,1},{25,9},{2,18},{10... | collective-permute-start | bytes 589832 | tf_op jit(solution)/shard_map/ppermute | solution.py:25
  36.6 12.9 %collective-permute-start.8 = (bf16[144,576]{1,0:T(8,128)(2,1)S(1)}, bf16[144,576]{1,0:T(8,128)(2,1)S(1)}, u32[]{:S(2)}, u32[]{:S(2)}) collective-permute-start(bf16[144,576]{1,0:T(8,128)(2,1)S(1)} %get-tuple-element.115.refs_4_.refs_1_), channel_id=1, source_target_pairs={{0,2},{1,3},{2,0},{3,1},{4,6},{5,7},{6,4},{7,5},{8,10},{9,11},{10,... | collective-permute-start | bytes 497672 | tf_op jit(solution)/shard_map/ppermute | solution.py:25
  42.9 15.2 %collective-permute-start.5 = (bf16[128,768]{1,0:T(8,128)(2,1)S(1)}, bf16[128,768]{1,0:T(8,128)(2,1)S(1)}, u32[]{:S(2)}, u32[]{:S(2)}) collective-permute-start(bf16[128,768]{1,0:T(8,128)(2,1)S(1)} %collective-permute-done.3.refs_0_.refs_3_), channel_id=1, source_target_pairs={{0,8},{8,0},{16,24},{24,16},{1,9},{9,1},{17,25},{25,17},{2,10},{10... | collective-permute-start | bytes 589832 | tf_op jit(solution)/shard_map/ppermute | solution.py:25
  51.0 15.9 %collective-permute-start.14 = (bf16[192,768]{1,0:T(8,128)(2,1)S(1)}, bf16[192,768]{1,0:T(8,128)(2,1)S(1)}, u32[]{:S(2)}, u32[]{:S(2)}) collective-permute-start(bf16[192,768]{1,0:T(8,128)(2,1)S(1)} %get-tuple-element.123.refs_8_), channel_id=1, source_target_pairs={{0,2},{1,3},{2,0},{3,1},{4,6},{5,7},{6,4},{7,5},{8,10},{9,11},{10,... | collective-permute-start | bytes 884744 | tf_op jit(solution)/shard_map/ppermute | solution.py:25
  61.2 13.1 %collective-permute-start.13 = (bf16[512,384]{1,0:T(8,128)(2,1)S(1)}, bf16[512,384]{1,0:T(8,128)(2,1)S(1)}, u32[]{:S(2)}, u32[]{:S(2)}) collective-permute-start(bf16[512,384]{1,0:T(8,128)(2,1)S(1)} %get-tuple-element.121), channel_id=1, source_target_pairs={{0,4},{4,0},{1,5},{5,1},{2,6},{6,2},{3,7},{7,3},{8,12},{12,8},{9,1... | collective-permute-start | bytes 1179656 | tf_op jit(solution)/shard_map/ppermute | solution.py:30
  62.8 11.5 %collective-permute-start.15 = (bf16[192,768]{1,0:T(8,128)(2,1)S(1)}, bf16[192,768]{1,0:T(8,128)(2,1)S(1)}, u32[]{:S(2)}, u32[]{:S(2)}) collective-permute-start(bf16[192,768]{1,0:T(8,128)(2,1)S(1)} %get-tuple-element.123.refs_8_), channel_id=1, source_target_pairs={{0,1},{1,0},{2,3},{3,2},{4,5},{5,4},{6,7},{7,6},{8,9},{9,8},{10,11... | collective-permute-start | bytes 884744 | tf_op jit(solution)/shard_map/ppermute | solution.py:25
  63.8 15.4 %collective-permute-start.16 = (bf16[192,768]{1,0:T(8,128)(2,1)S(1)}, bf16[192,768]{1,0:T(8,128)(2,1)S(1)}, u32[]{:S(2)}, u32[]{:S(2)}) collective-permute-start(bf16[192,768]{1,0:T(8,128)(2,1)S(1)} %get-tuple-element.123.refs_8_), channel_id=1, source_target_pairs={{0,3},{1,2},{2,1},{3,0},{4,7},{5,6},{6,5},{7,4},{8,11},{9,10},{10,... | collective-permute-start | bytes 884744 | tf_op jit(solution)/shard_map/ppermute | solution.py:25
  82.7 12.0 %collective-permute-start.23 = (bf16[128,768]{1,0:T(8,128)(2,1)S(1)}, bf16[128,768]{1,0:T(8,128)(2,1)S(1)}, u32[]{:S(2)}, u32[]{:S(2)}) collective-permute-start(bf16[128,768]{1,0:T(8,128)(2,1)S(1)} %bitcast_convert_fusion), channel_id=1, source_target_pairs={{0,0},{1,8},{2,16},{3,24},{8,1},{9,9},{10,17},{11,25},{16,2},{17,1... | collective-permute-start | bytes 589832 | tf_op jit(solution)/shard_map/ppermute | solution.py:36
  84.4 12.7 %collective-permute-start.19 = (bf16[128,768]{1,0:T(8,128)(2,1)S(1)}, bf16[128,768]{1,0:T(8,128)(2,1)S(1)}, u32[]{:S(2)}, u32[]{:S(2)}) collective-permute-start(bf16[128,768]{1,0:T(8,128)(2,1)S(1)} %add_convert_fusion.5), channel_id=1, source_target_pairs={{0,16},{8,24},{16,0},{24,8},{1,17},{9,25},{17,1},{25,9},{2,18},{10... | collective-permute-start | bytes 589832 | tf_op jit(solution)/shard_map/ppermute | solution.py:25
  86.4 20.6 %collective-permute-start.27 = (bf16[192,768]{1,0:T(8,128)(2,1)S(1)}, bf16[192,768]{1,0:T(8,128)(2,1)S(1)}, u32[]{:S(2)}, u32[]{:S(2)}) collective-permute-start(bf16[192,768]{1,0:T(8,128)(2,1)S(1)} %collective-permute-done.15.refs_9_), channel_id=1, source_target_pairs={{0,4},{4,0},{1,5},{5,1},{2,6},{6,2},{3,7},{7,3},{8,12},{12,8},{9,1... | collective-permute-start | bytes 884744 | tf_op jit(solution)/shard_map/ppermute | solution.py:30
  94.7 12.1 %collective-permute-start.25 = (bf16[128,768]{1,0:T(8,128)(2,1)S(1)}, bf16[128,768]{1,0:T(8,128)(2,1)S(1)}, u32[]{:S(2)}, u32[]{:S(2)}) collective-permute-start(bf16[128,768]{1,0:T(8,128)(2,1)S(1)} %collective-permute-done.23.refs_4_.refs_5_), channel_id=1, source_target_pairs={{0,16},{8,24},{16,0},{24,8},{1,17},{9,25},{17,1},{25,9},{2,18},{10... | collective-permute-start | bytes 589832 | tf_op jit(solution)/shard_map/ppermute | solution.py:25
  98.1 16.2 %collective-permute-start.28 = (bf16[192,768]{1,0:T(8,128)(2,1)S(1)}, bf16[192,768]{1,0:T(8,128)(2,1)S(1)}, u32[]{:S(2)}, u32[]{:S(2)}) collective-permute-start(bf16[192,768]{1,0:T(8,128)(2,1)S(1)} %collective-permute-done.16.refs_11_), channel_id=1, source_target_pairs={{0,4},{4,0},{1,5},{5,1},{2,6},{6,2},{3,7},{7,3},{8,12},{12,8},{9,1... | collective-permute-start | bytes 884744 | tf_op jit(solution)/shard_map/ppermute | solution.py:30
  123.0 28.7 %collective-permute-start.36 = (bf16[4,192,768]{2,1,0:T(8,128)(2,1)S(1)}, bf16[4,192,768]{2,1,0:T(8,128)(2,1)S(1)}, u32[]{:S(2)}, u32[]{:S(2)}) collective-permute-start(bf16[4,192,768]{2,1,0:T(8,128)(2,1)S(1)} %get-tuple-element.157), channel_id=1, source_target_pairs={{0,4},{4,0},{1,5},{5,1},{2,6},{6,2},{3,7},{7,3},{8,12},{12,8},{9,1... | collective-permute-start | bytes 3538952 | tf_op jit(solution)/shard_map/ppermute | solution.py:30
  140.6 13.8 %collective-permute-start.33 = (bf16[256,768]{1,0:T(8,128)(2,1)S(1)}, bf16[256,768]{1,0:T(8,128)(2,1)S(1)}, u32[]{:S(2)}, u32[]{:S(2)}) collective-permute-start(bf16[256,768]{1,0:T(8,128)(2,1)S(1)} %get-tuple-element.149), channel_id=1, source_target_pairs={{0,8},{8,0},{16,24},{24,16},{1,9},{9,1},{17,25},{25,17},{2,10},{10... | collective-permute-start | bytes 1179656 | tf_op jit(solution)/shard_map/ppermute | solution.py:25
  143.6 19.3 %collective-permute-start.38 = (bf16[512,384]{1,0:T(8,128)(2,1)S(1)}, bf16[512,384]{1,0:T(8,128)(2,1)S(1)}, u32[]{:S(2)}, u32[]{:S(2)}) collective-permute-start(bf16[512,384]{1,0:T(8,128)(2,1)S(1)} %bitcast.43), channel_id=1, source_target_pairs={{0,4},{4,0},{1,5},{5,1},{2,6},{6,2},{3,7},{7,3},{8,12},{12,8},{9,1... | collective-permute-start | bytes 1179656 | tf_op jit(solution)/shard_map/ppermute | solution.py:30
  152.6 10.3 %collective-permute-start.37 = (bf16[192,768]{1,0:T(8,128)(2,1)S(1)}, bf16[192,768]{1,0:T(8,128)(2,1)S(1)}, u32[]{:S(2)}, u32[]{:S(2)}) collective-permute-start(bf16[192,768]{1,0:T(8,128)(2,1)S(1)} %get-tuple-element.162), channel_id=1, source_target_pairs={{0,3},{1,2},{2,1},{3,0},{4,7},{5,6},{6,5},{7,4},{8,11},{9,10},{10,... | collective-permute-start | bytes 884744 | tf_op jit(solution)/shard_map/ppermute | solution.py:25
  166.1 9.5 %collective-permute-start.40 = (bf16[128,768]{1,0:T(8,128)(2,1)S(1)}, bf16[128,768]{1,0:T(8,128)(2,1)S(1)}, u32[]{:S(2)}, u32[]{:S(2)}) collective-permute-start(bf16[128,768]{1,0:T(8,128)(2,1)S(1)} %add_convert_fusion.1), channel_id=1, source_target_pairs={{0,16},{8,24},{16,0},{24,8},{1,17},{9,25},{17,1},{25,9},{2,18},{10... | collective-permute-start | bytes 589832 | tf_op jit(solution)/shard_map/ppermute | solution.py:25
  166.8 17.3 %collective-permute-start.43 = (bf16[192,768]{1,0:T(8,128)(2,1)S(1)}, bf16[192,768]{1,0:T(8,128)(2,1)S(1)}, u32[]{:S(2)}, u32[]{:S(2)}) collective-permute-start(bf16[192,768]{1,0:T(8,128)(2,1)S(1)} %get-tuple-element.181), channel_id=1, source_target_pairs={{0,1},{1,0},{2,3},{3,2},{4,5},{5,4},{6,7},{7,6},{8,9},{9,8},{10,11... | collective-permute-start | bytes 884744 | tf_op jit(solution)/shard_map/ppermute | solution.py:25
  171.9 25.3 %collective-permute-start.44 = (bf16[192,768]{1,0:T(8,128)(2,1)S(1)}, bf16[192,768]{1,0:T(8,128)(2,1)S(1)}, u32[]{:S(2)}, u32[]{:S(2)}) collective-permute-start(bf16[192,768]{1,0:T(8,128)(2,1)S(1)} %get-tuple-element.183), channel_id=1, source_target_pairs={{0,2},{1,3},{2,0},{3,1},{4,6},{5,7},{6,4},{7,5},{8,10},{9,11},{10,... | collective-permute-start | bytes 884744 | tf_op jit(solution)/shard_map/ppermute | solution.py:25
  173.8 24.8 %collective-permute-start.45 = (bf16[4,144,576]{2,1,0:T(8,128)(2,1)S(1)}, bf16[4,144,576]{2,1,0:T(8,128)(2,1)S(1)}, u32[]{:S(2)}, u32[]{:S(2)}) collective-permute-start(bf16[4,144,576]{2,1,0:T(8,128)(2,1)S(1)} %get-tuple-element.185), channel_id=1, source_target_pairs={{0,4},{4,0},{1,5},{5,1},{2,6},{6,2},{3,7},{7,3},{8,12},{12,8},{9,1... | collective-permute-start | bytes 1990664 | tf_op jit(solution)/shard_map/ppermute | solution.py:30
  178.1 20.6 %collective-permute-start.41 = (bf16[128,768]{1,0:T(8,128)(2,1)}, bf16[128,768]{1,0:T(8,128)(2,1)}, u32[]{:S(2)}, u32[]{:S(2)}) collective-permute-start(bf16[128,768]{1,0:T(8,128)(2,1)} %add_convert_fusion.2), channel_id=1, source_target_pairs={{0,0},{1,8},{2,16},{3,24},{8,1},{9,9},{10,17},{11,25},{16,2},{17,1... | collective-permute-start | bytes 589832 | tf_op jit(solution)/shard_map/ppermute | solution.py:36
  197.4 9.9 %collective-permute-start.49 = (bf16[192,768]{1,0:T(8,128)(2,1)S(1)}, bf16[192,768]{1,0:T(8,128)(2,1)S(1)}, u32[]{:S(2)}, u32[]{:S(2)}) collective-permute-start(bf16[192,768]{1,0:T(8,128)(2,1)S(1)} %add_convert_fusion.mine), channel_id=1, source_target_pairs={{0,4},{4,0},{1,5},{5,1},{2,6},{6,2},{3,7},{7,3},{8,12},{12,8},{9,1... | collective-permute-start | bytes 884744 | tf_op jit(solution)/shard_map/ppermute | solution.py:30
  199.4 15.0 %collective-permute-start.48 = (bf16[144,576]{1,0:T(8,128)(2,1)S(1)}, bf16[144,576]{1,0:T(8,128)(2,1)S(1)}, u32[]{:S(2)}, u32[]{:S(2)}) collective-permute-start(bf16[144,576]{1,0:T(8,128)(2,1)S(1)} %get-tuple-element.190), channel_id=1, source_target_pairs={{0,3},{1,2},{2,1},{3,0},{4,7},{5,6},{6,5},{7,4},{8,11},{9,10},{10,... | collective-permute-start | bytes 497672 | tf_op jit(solution)/shard_map/ppermute | solution.py:25
  199.5 18.8 %collective-permute-start.47 = (bf16[144,576]{1,0:T(8,128)(2,1)S(1)}, bf16[144,576]{1,0:T(8,128)(2,1)S(1)}, u32[]{:S(2)}, u32[]{:S(2)}) collective-permute-start(bf16[144,576]{1,0:T(8,128)(2,1)S(1)} %get-tuple-element.189), channel_id=1, source_target_pairs={{0,2},{1,3},{2,0},{3,1},{4,6},{5,7},{6,4},{7,5},{8,10},{9,11},{10,... | collective-permute-start | bytes 497672 | tf_op jit(solution)/shard_map/ppermute | solution.py:25
  205.1 13.2 %collective-permute-start.46 = (bf16[144,576]{1,0:T(8,128)(2,1)S(1)}, bf16[144,576]{1,0:T(8,128)(2,1)S(1)}, u32[]{:S(2)}, u32[]{:S(2)}) collective-permute-start(bf16[144,576]{1,0:T(8,128)(2,1)S(1)} %get-tuple-element.188), channel_id=1, source_target_pairs={{0,1},{1,0},{2,3},{3,2},{4,5},{5,4},{6,7},{7,6},{8,9},{9,8},{10,11... | collective-permute-start | bytes 497672 | tf_op jit(solution)/shard_map/ppermute | solution.py:25
  208.7 15.7 %collective-permute-start.50 = (bf16[48,768]{1,0:T(8,128)(2,1)S(1)}, bf16[48,768]{1,0:T(8,128)(2,1)S(1)}, u32[]{:S(2)}, u32[]{:S(2)}) collective-permute-start(bf16[48,768]{1,0:T(8,128)(2,1)S(1)} %get-tuple-element.192), channel_id=1, source_target_pairs={{0,8},{8,0},{16,24},{24,16},{1,9},{9,1},{17,25},{25,17},{2,10},{10... | collective-permute-start | bytes 221192 | tf_op jit(solution)/shard_map/ppermute | solution.py:25
  211.6 12.8 %collective-permute-start.51 = (bf16[48,768]{1,0:T(8,128)(2,1)S(1)}, bf16[48,768]{1,0:T(8,128)(2,1)S(1)}, u32[]{:S(2)}, u32[]{:S(2)}) collective-permute-start(bf16[48,768]{1,0:T(8,128)(2,1)S(1)} %get-tuple-element.193), channel_id=1, source_target_pairs={{0,16},{8,24},{16,0},{24,8},{1,17},{9,25},{17,1},{25,9},{2,18},{10... | collective-permute-start | bytes 221192 | tf_op jit(solution)/shard_map/ppermute | solution.py:25
  214.4 9.9 %collective-permute-start.52 = (bf16[48,768]{1,0:T(8,128)(2,1)S(1)}, bf16[48,768]{1,0:T(8,128)(2,1)S(1)}, u32[]{:S(2)}, u32[]{:S(2)}) collective-permute-start(bf16[48,768]{1,0:T(8,128)(2,1)S(1)} %get-tuple-element.194), channel_id=1, source_target_pairs={{0,24},{8,16},{16,8},{24,0},{1,25},{9,17},{17,9},{25,1},{2,26},{10... | collective-permute-start | bytes 221192 | tf_op jit(solution)/shard_map/ppermute | solution.py:25
  218.4 10.3 %collective-permute-start.53 = (bf16[144,576]{1,0:T(8,128)(2,1)S(1)}, bf16[144,576]{1,0:T(8,128)(2,1)S(1)}, u32[]{:S(2)}, u32[]{:S(2)}) collective-permute-start(bf16[144,576]{1,0:T(8,128)(2,1)S(1)} %add_convert_fusion.6.mine), channel_id=1, source_target_pairs={{0,4},{4,0},{1,5},{5,1},{2,6},{6,2},{3,7},{7,3},{8,12},{12,8},{9,1... | collective-permute-start | bytes 497672 | tf_op jit(solution)/shard_map/ppermute | solution.py:30
  (34 other events, 239.9 us)
